TPU v7x, 256 devices: a whole 4x4x8 slice. The times are simulated.
256 devices in a mesh: pt: 32 (over y, z), comp: 8 (over x, core).
Axes of the slice: x: 4, y: 4, z: 8, core: 2. Of those that a mesh axis runs over, the one named last changes fastest.
Arguments:
- points: bfloat16 [16384, 1024], P(('pt', 'comp')), may hold values from -64 to 64
- means: bfloat16 [16384, 1024], P('comp'), may hold values from -2 to 2
- log_weights: float32 [16384], P('comp'), may hold values from -3 to 3
- inv_var: float32 [1024], replicated, may hold values from 0.03 to 0.3
Outputs:
- resp: bfloat16 [16384, 16384], P(('pt', 'comp'))
- counts: float32 [16384], P('comp')
- new_means_t: float32 [1024, 16384], P('pt', 'comp')
- loglik: float32 [16384], P(('pt', 'comp'))
All inputs are finite; a program needn't handle non-finite values.
Results may differ from a plain program's by a relative error of at most 0.0074.
Values may be sent and summed in bfloat16 or wider, within the bound.
No kernel may reach another device: no remote copies, remote signals or barrier semaphores. Data moves between devices by JAX's collectives and lax.ppermute only.
A program may use at most 128 MiB of HBM per device.

v0:
```python
import math

import jax
import jax.numpy as jnp
from jax import lax
from jax.sharding import PartitionSpec as P


def body(points, means, log_weights, inv_var):
    width = points.shape[1]
    gathered = lax.all_gather(points, "comp", axis=0, tiled=True)
    means_f = means.astype(jnp.float32)
    scaled = (means_f * inv_var[None, :]).astype(jnp.bfloat16)
    half_norm = 0.5 * jnp.sum(means_f * means_f * inv_var[None, :], axis=1)
    score = lax.dot_general(
        gathered, scaled, (((1,), (1,)), ((), ())), preferred_element_type=jnp.float32
    )
    score = score - half_norm[None, :] + log_weights[None, :]
    full_rows = lax.all_to_all(score, "comp", split_axis=0, concat_axis=1, tiled=True)
    peak = jnp.max(full_rows, axis=1)
    total = jnp.sum(jnp.exp(full_rows - peak[:, None]), axis=1)
    own_lse = peak + jnp.log(total)
    resp_rows = jnp.exp(full_rows - own_lse[:, None]).astype(jnp.bfloat16)
    resp = lax.all_to_all(resp_rows, "comp", split_axis=1, concat_axis=0, tiled=True)
    points_f = points.astype(jnp.float32)
    const_term = 0.5 * jnp.sum(jnp.log(inv_var)) - 0.5 * width * math.log(2.0 * math.pi)
    loglik = own_lse - 0.5 * jnp.sum(points_f * points_f * inv_var[None, :], axis=1) + const_term
    counts = lax.psum(jnp.sum(resp.astype(jnp.float32), axis=0), "pt")
    columns = width // lax.axis_size("pt")
    sums_t = lax.psum_scatter(
        lax.dot_general(
            gathered, resp, (((0,), (0,)), ((), ())), preferred_element_type=jnp.float32
        ),
        "pt",
        scatter_dimension=0,
        tiled=True,
    )
    mean_cols = lax.dynamic_slice_in_dim(means_f, lax.axis_index("pt") * columns, columns, 1).T
    new_means_t = (sums_t + mean_cols) / (counts[None, :] + 1.0)
    return (resp_rows, counts, new_means_t, loglik)


def solution(mesh):
    placed = (P(("pt", "comp"), None), P("comp", None), P("comp"), P())
    return jax.shard_map(
        body,
        mesh=mesh,
        in_specs=placed,
        out_specs=(P(("pt", "comp"), None), P("comp"), P("pt", "comp"), P(("pt", "comp"))),
        check_vma=False,
    )
```

profile of v0, /device:TPU:32, one launch (start us, length us, event | category | flops | bytes accessed | tf_op | source)
XLA Modules:
  0.0 392.0 jit_solution(1333219688482594108)
XLA Ops:
  7.2 0.7 all-gather.2.cloned.1.call-update
  7.9 3.4 multiply_reduce_fusion
  11.3 27.1 %all-gather.2.cloned.1.call-done = bf16[512,1024]{1,0:T(8,128)(2,1)} async-done(((bf16[64,1024]{1,0:T(8,128)(2,1)}), bf16[512,1024]{1,0:T(8,128)(2,1)}) %all-gather.2.cloned.1.call-update) | async-done | bytes 1048592 | tf_op jit(solution)/shard_map/all_gather | solution.py:11
  38.4 6.8 %subtract_add_fusion = f32[2048,512]{0,1:T(8,128)} fusion(bf16[512,1024]{1,0:T(8,128)(2,1)} %all-gather.2.cloned.1.call-done, f32[1024]{0:T(1024)S(1)} %copy-done.1, bf16[2048,1024]{1,0:T(8,128)(2,1)} %param.5, f32[2048]{0:T(1024)S(1)} %copy-done.4, f32[2048]{0:T(1024)S(1)} %broadcast_multiply_fusion), kind=kOutput, calls=%fused_computation.12 | convolution fusion | flops 2155872256 | bytes 9457664 | tf_op jit(solution)/shard_map/dot_general | solution.py:15
  45.2 4.7 %all-to-all-start = ((f32[8,64,2048]{2,1,0:T(8,128)}), f32[8,64,2048]{2,1,0:T(8,128)}, u32[]{:S(2)}, u32[]{:S(2)}) async-start(f32[8,64,2048]{2,1,0:T(8,128)} %bitcast.32), calls=%async_computation | async-start | bytes 8388608 | tf_op jit(solution)/shard_map/all_to_all | solution.py:19
  49.9 0.6 log_reduce_fusion
  51.2 0.1 multiply_reduce_fusion.1
  51.4 48.2 %all-to-all-done = f32[8,64,2048]{2,1,0:T(8,128)} async-done(((f32[8,64,2048]{2,1,0:T(8,128)}), f32[8,64,2048]{2,1,0:T(8,128)}, u32[]{:S(2)}, u32[]{:S(2)}) %all-to-all-start) | async-done | bytes 4194336 | tf_op jit(solution)/shard_map/all_to_all | solution.py:19
  99.6 2.6 reduce_max.9
  102.1 2.9 fusion.4
  105.1 0.5 subtract_add_fusion.1
  105.6 2.9 fusion.2
  108.5 30.0 %all_to_all.35 = bf16[64,8,2048]{2,0,1:T(8,128)(2,1)S(1)} all-to-all(bf16[64,8,2048]{2,0,1:T(8,128)(2,1)S(1)} %fusion.2), channel_id=1, replica_groups=mesh['pt'=32,'comp'=8] {'comp'}, dimensions={1} | all-to-all | bytes 4194304 | tf_op jit(solution)/shard_map/all_to_all | solution.py:24
  138.5 5.6 %convolution_bitcast_fusion = f32[1024,2048]{0,1:T(8,128)} fusion(bf16[512,2048]{1,0:T(8,128)(2,1)S(1)} %bitcast.31, bf16[512,1024]{1,0:T(8,128)(2,1)S(1)} %copy-done.3), kind=kOutput, calls=%fused_computation.2 | convolution fusion | flops 2147483648 | bytes 11534336 | tf_op jit(solution)/shard_map/dot_general | solution.py:31
  144.1 9.1 %copy.12 = f32[1024,2048]{1,0:T(8,128)} copy(f32[1024,2048]{0,1:T(8,128)} %convolution_bitcast_fusion) | data formatting | bytes 16777216
  153.2 6.4 %convert_element_type.19 = f32[2048,1024]{1,0:T(8,128)} convert(bf16[2048,1024]{1,0:T(8,128)(2,1)} %param.5) | non-fusion elementwise | flops 2097152 | bytes 12582912 | tf_op jit(solution)/shard_map/convert_element_type | solution.py:12
  159.7 2.5 copy.14
  162.2 1.9 exponential_convert_fusion
  164.1 0.4 convert_reduce_fusion
  164.5 73.2 %psum.7 = f32[2048]{0:T(1024)S(1)} all-reduce(f32[2048]{0:T(1024)S(1)} %convert_reduce_fusion), channel_id=1, replica_groups=mesh['pt'=32,'comp'=8] {'pt'}, use_global_device_ids=true, to_apply=%region_4.0 | all-reduce | flops 2048 | bytes 16384 | tf_op jit(solution)/shard_map/psum | solution.py:28
  237.7 143.4 %reduce-scatter.4.cloned.1.call-done = f32[32,2048]{1,0:T(8,128)} async-done(((f32[1024,2048]{1,0:T(8,128)}), f32[32,2048]{1,0:T(8,128)}) %reduce-scatter.4.cloned.1.call-update) | async-done | bytes 262160
  381.0 1.3 copy.13
  382.3 1.8 fusion.7
  384.2 1.0 copy.11
  (15 shorter events, 0.1 us)
Async XLA Ops:
  7.2 31.2 %copy-start.1 = (f32[1024]{0:T(1024)S(1)}, f32[1024]{0:T(1024)}, u32[]{:S(2)}) copy-start(f32[1024]{0:T(1024)} %param.7) | copy-start | bytes 12292
  7.2 31.2 %copy-start.4 = (f32[2048]{0:T(1024)S(1)}, f32[2048]{0:T(1024)}, u32[]{:S(2)}) copy-start(f32[2048]{0:T(1024)} %param.6) | copy-start | bytes 24580
  7.2 31.2 %all-gather.2.cloned.1.call-start = ((), (), s32[]{:S(2)}) async-start(), calls=%async_computation.3 | async-start | bytes 1179648 | tf_op jit(solution)/shard_map/all_gather | solution.py:11
  45.2 6.0 %copy-start = (bf16[64,1024]{1,0:T(8,128)(2,1)S(1)}, bf16[64,1024]{1,0:T(8,128)(2,1)}, u32[]{:S(2)}) copy-start(bf16[64,1024]{1,0:T(8,128)(2,1)} %param.4) | copy-start | bytes 393220
  45.2 54.4 %all-to-all-start = ((f32[8,64,2048]{2,1,0:T(8,128)}), f32[8,64,2048]{2,1,0:T(8,128)}, u32[]{:S(2)}, u32[]{:S(2)}) async-start(f32[8,64,2048]{2,1,0:T(8,128)} %bitcast.32), calls=%async_computation | async-start | bytes 8388608 | tf_op jit(solution)/shard_map/all_to_all | solution.py:19
  49.9 331.1 %reduce-scatter.4.cloned.1.call-start = ((), (), s32[]{:S(2)}) async-start(), calls=%async_computation.4 | async-start | bytes 8650752
  105.6 32.9 %copy-start.3 = (bf16[512,1024]{1,0:T(8,128)(2,1)S(1)}, bf16[512,1024]{1,0:T(8,128)(2,1)}, u32[]{:S(2)}) copy-start(bf16[512,1024]{1,0:T(8,128)(2,1)} %all-gather.2.cloned.1.call-done) | copy-start | bytes 3145732
  237.6 147.5 %copy-start.2 = (f32[2048]{0:T(1024)}, f32[2048]{0:T(1024)S(1)}, u32[]{:S(2)}) copy-start(f32[2048]{0:T(1024)S(1)} %psum.7) | copy-start | bytes 24580
Sparse Core Ops, SparseCore 0:
  9.9 28.4 all-gather.1
  153.4 227.6 reduce-scatter.3
where the time goes:
time: 394 us; the launch traced here: 392 us
  waiting for transfers between devices  219 us (56%)
  blocking collectives  103 us (26%)
  other arithmetic  23.6 us (6%)
  between operations  14.8 us (4%)
  local copies, waits for them, and re-layouts  13.9 us (4%)
  matrix products  12.4 us (3%)
  starting transfers between devices  4.76 us (1%)
    unnamed x3, waiting for transfers between devices  144 us
    psum x1, blocking collectives, body(): counts = lax.psum(jnp.sum(resp.astype(jnp.float32), axis=0), 'pt')  73.2 us
    all_to_all x1, waiting for transfers between devices, body(): lax.all_to_all(score, 'comp', split_axis=0, concat_axis=1, tiled=True)  48.2 us
    all_to_all x1, blocking collectives, body(): lax.all_to_all(resp_rows, 'comp', split_axis=1, concat_axis=0, tiled=True)  30 us
    all_gather x1, waiting for transfers between devices, body(): gathered = lax.all_gather(points, 'comp', axis=0, tiled=True)  27.1 us
    unnamed x13, local copies, waits for them, and re-layouts  11.5 us
  transfers between devices with their start and end apart: 3, of which 3 were waited for; matrix products, arithmetic and copies ran while one was open for 4% of the time, Pallas kernels for 0%

commit v1 on v0

v1 whole, which is shorter than its diff:
```python
import functools
import math

import jax
import jax.numpy as jnp
from jax import lax
from jax.experimental import pallas as pl
from jax.experimental.pallas import tpu as pltpu
from jax.sharding import Mesh
from jax.sharding import PartitionSpec as P

BF = jnp.bfloat16
F32 = jnp.float32
VMEM_LIMIT = 48 * 1024 * 1024
VMEM = pltpu.VMEM
SIZES = {"y": 4, "z": 8, "x": 4, "c": 2}


def shift(value, axis, step):
    n = SIZES[axis]
    return lax.ppermute(value, axis, [(i, (i + step) % n) for i in range(n)])


def params():
    return pltpu.CompilerParams(vmem_limit_bytes=VMEM_LIMIT)


def whole():
    return pl.BlockSpec(memory_space=VMEM)


def scalar():
    return pl.BlockSpec(memory_space=pltpu.SMEM)


def place_kernel(at, own, before, after, far, out):
    x = at[0]
    for step, piece in ((0, own), (3, before), (1, after), (2, far)):
        slot = lax.rem(x + step, 4)
        out[pl.ds(pl.multiple_of(slot * 64, 64), 64), :] = piece[...]


def place(at, own, before, after, far):
    return pl.pallas_call(
        place_kernel,
        out_shape=jax.ShapeDtypeStruct((256, 1024), BF),
        in_specs=[scalar()] + [whole()] * 4,
        out_specs=whole(),
        compiler_params=params(),
    )(at, own, before, after, far)


def gather_x(at, own):
    return place(at, own, shift(own, "x", 1), shift(own, "x", -1), shift(own, "x", 2))


def column(row):
    return jnp.transpose(jnp.broadcast_to(row, (128, 128)))[:, 0:1]


def score_kernel(at, own, other, scaled, bias, score, share, rows, peak, total):
    step = pl.program_id(0)
    c = at[1]

    @pl.when(step == 0)
    def _():
        rows[pl.ds(pl.multiple_of(c * 256, 256), 256), :] = own[...]
        rows[pl.ds(pl.multiple_of((1 - c) * 256, 256), 256), :] = other[...]
        peak[...] = jnp.full_like(peak, -jnp.inf)
        total[...] = jnp.zeros_like(total)

    tile = lax.dot_general(
        rows[...], scaled[...], (((1,), (1,)), ((), ())), preferred_element_type=F32
    )
    tile = tile + bias[...]
    score[...] = tile
    top = jnp.maximum(peak[...], jnp.max(tile, axis=1, keepdims=True))
    total[...] = total[...] * jnp.exp(peak[...] - top) + jnp.sum(
        jnp.exp(tile - top), axis=1, keepdims=True
    )
    peak[...] = top

    @pl.when(step == pl.num_programs(0) - 1)
    def _():
        lse = peak[...] + jnp.log(total[...])
        for b in range(4):
            part = jnp.broadcast_to(lse[b * 128 : (b + 1) * 128], (128, 128))
            line = jnp.transpose(part)[0:1, :]
            share[:, b, :] = jnp.broadcast_to(line, (32, 128))


def scores(at, own, other, scaled, bias_row):
    width = 512
    return pl.pallas_call(
        score_kernel,
        grid=(2048 // width,),
        out_shape=(
            jax.ShapeDtypeStruct((512, 2048), F32),
            jax.ShapeDtypeStruct((32, 4, 128), F32),
        ),
        in_specs=[
            scalar(),
            pl.BlockSpec((256, 1024), lambda i: (0, 0)),
            pl.BlockSpec((256, 1024), lambda i: (0, 0)),
            pl.BlockSpec((width, 1024), lambda i: (i, 0)),
            pl.BlockSpec((1, width), lambda i: (0, i)),
        ],
        out_specs=(
            pl.BlockSpec((512, width), lambda i: (0, i)),
            pl.BlockSpec((32, 4, 128), lambda i: (0, 0, 0)),
        ),
        scratch_shapes=[VMEM((512, 1024), BF), VMEM((512, 1), F32), VMEM((512, 1), F32)],
        compiler_params=params(),
        cost_estimate=pl.CostEstimate(
            flops=2 * 512 * 2048 * 1024, bytes_accessed=9 << 20, transcendentals=1 << 20
        ),
    )(at, own, other, scaled, bias_row)


def joined(shares):
    top = jnp.max(shares, axis=0)
    return top + jnp.log(jnp.sum(jnp.exp(shares - top[None]), axis=0))


def resp_kernel(at, shares, score, out):
    step = pl.program_id(0)
    del at
    lse = joined(shares[0, :, pl.ds(step, 1), :])
    out[...] = jnp.exp(score[...] - column(lse)).astype(BF)


def responsibilities(at, shares, score):
    return pl.pallas_call(
        resp_kernel,
        grid_spec=pltpu.PrefetchScalarGridSpec(
            num_scalar_prefetch=1,
            grid=(4,),
            in_specs=[
                pl.BlockSpec((1, 8, 4, 128), lambda i, at: (at[2], 0, 0, 0)),
                pl.BlockSpec((128, 2048), lambda i, at: (i, 0)),
            ],
            out_specs=pl.BlockSpec((128, 2048), lambda i, at: (i, 0)),
        ),
        out_shape=jax.ShapeDtypeStruct((512, 2048), BF),
        compiler_params=params(),
        cost_estimate=pl.CostEstimate(flops=1 << 21, bytes_accessed=6 << 20, transcendentals=1 << 20),
    )(at, shares, score)


def sums_kernel(at, shares, scaled, bias, *refs):
    pieces = refs[:8]
    sums, counts = refs[8:10]
    rows, weights, lse, sems = refs[10:]
    copies = [
        pltpu.make_async_copy(piece, rows.at[pl.ds(i * 256, 256)], sems.at[i])
        for i, piece in enumerate(pieces)
    ]
    for copy in copies:
        copy.start()
    y, c = at[2], at[1]
    for yy in range(4):
        lse[pl.ds(yy * 4, 4), :] = joined(shares[yy])
    count = jnp.zeros((512, 1), F32)
    for i in range(8):
        copies[i].wait()
        there = lax.rem(y + (0, 3, 1, 2)[i // 2], 4)
        core = c if i % 2 == 0 else 1 - c
        line = there * 4 + core * 2
        part = jnp.concatenate([lse[pl.ds(line, 1), :], lse[pl.ds(line + 1, 1), :]], axis=1)
        score = lax.dot_general(
            scaled[...], rows[i * 256 : (i + 1) * 256, :], (((1,), (1,)), ((), ())),
            preferred_element_type=F32,
        )
        weight = jnp.exp(score + bias[...] - part).astype(BF)
        weights[:, i * 256 : (i + 1) * 256] = weight
        count = count + jnp.sum(weight.astype(F32), axis=1, keepdims=True)
    for j in range(4):
        block = lax.dot_general(
            weights[...], rows[:, j * 256 : (j + 1) * 256], (((1,), (0,)), ((), ())),
            preferred_element_type=F32,
        )
        sums[j * 256 : (j + 1) * 256, :] = jnp.transpose(block).astype(BF)
    for b in range(4):
        part = jnp.broadcast_to(count[b * 128 : (b + 1) * 128], (128, 128))
        counts[:, b, :] = jnp.broadcast_to(jnp.transpose(part)[0:1, :], (32, 128))


def partial_sums(at, shares, scaled, bias_col, pieces):
    return pl.pallas_call(
        sums_kernel,
        grid_spec=pltpu.PrefetchScalarGridSpec(
            num_scalar_prefetch=1,
            grid=(1,),
            in_specs=[
                pl.BlockSpec((4, 8, 4, 128), lambda i, at: (0, 0, 0, 0)),
                pl.BlockSpec((512, 1024), lambda i, at: (at[2], 0)),
                pl.BlockSpec((512, 1), lambda i, at: (at[2], 0)),
            ]
            + [pl.BlockSpec(memory_space=pl.ANY)] * 8,
            out_specs=(
                pl.BlockSpec((1024, 512), lambda i, at: (0, 0)),
                pl.BlockSpec((32, 4, 128), lambda i, at: (0, 0, 0)),
            ),
            scratch_shapes=[
                VMEM((2048, 1024), BF),
                VMEM((512, 2048), BF),
                VMEM((16, 128), F32),
                pltpu.SemaphoreType.DMA((8,)),
            ],
        ),
        out_shape=(
            jax.ShapeDtypeStruct((1024, 512), BF),
            jax.ShapeDtypeStruct((32, 4, 128), F32),
        ),
        compiler_params=params(),
        cost_estimate=pl.CostEstimate(
            flops=4 * 512 * 2048 * 1024, bytes_accessed=8 << 20, transcendentals=1 << 20
        ),
    )(at, shares, scaled, bias_col, *pieces)


def body(points, means, log_weights, inv_var):
    x, c, y, z = (lax.axis_index(a) for a in "xcyz")
    at = jnp.stack([x, c, y]).astype(jnp.int32)

    far = shift(points, "y", 2)
    own = gather_x(at, points)
    other = shift(own, "c", 1)

    means_f = means.astype(F32)
    scaled = (means_f * inv_var[None, :]).astype(BF)
    half_norm = 0.5 * jnp.sum(means_f * means_f * inv_var[None, :], axis=1)
    bias = log_weights - half_norm

    score, share = scores(at, own, other, scaled, bias.reshape(1, 2048))

    before = shift(own, "y", 1)
    after = shift(own, "y", -1)
    far = gather_x(at, far)
    pieces = []
    for mine in (before, after, far):
        pieces += [mine, shift(mine, "c", 1)]

    shares = lax.all_to_all(share, ("y", "x", "c"), split_axis=0, concat_axis=0, tiled=True)
    shares = shares.reshape(4, 8, 4, 128)

    resp = responsibilities(at, shares, score)
    resp_rows = lax.all_to_all(resp, ("c", "x"), split_axis=0, concat_axis=0, tiled=True)
    resp_rows = resp_rows.reshape(2, 4, 64, 2048).transpose(2, 1, 0, 3).reshape(64, 16384)

    sums, counts = partial_sums(at, shares, scaled, bias[:, None], [own, other] + pieces)
    counts = lax.all_to_all(counts, ("y", "z"), split_axis=0, concat_axis=0, tiled=True)
    sums = lax.all_to_all(sums, ("y", "z"), split_axis=0, concat_axis=0, tiled=True)
    counts = jnp.sum(counts.reshape(4, 8, 512), axis=1).reshape(2048)
    sums = jnp.sum(sums.reshape(4, 8, 32, 512).astype(F32), axis=1)
    sums = sums.transpose(1, 0, 2).reshape(32, 2048)
    mean_cols = lax.dynamic_slice_in_dim(means, (y * 8 + z) * 32, 32, 1).T.astype(F32)
    new_means_t = (sums + mean_cols) / (counts[None, :] + 1.0)

    lse = joined(lax.dynamic_index_in_dim(shares, y, 0, keepdims=False)).reshape(8, 64)
    own_lse = lax.dynamic_index_in_dim(lse, c * 4 + x, 0, keepdims=False)
    points_f = points.astype(F32)
    const_term = 0.5 * jnp.sum(jnp.log(inv_var)) - 0.5 * 1024 * math.log(2.0 * math.pi)
    loglik = own_lse - 0.5 * jnp.sum(points_f * points_f * inv_var[None, :], axis=1) + const_term
    return (resp_rows, counts, new_means_t, loglik)


def solution(mesh):
    axes = ("y", "z", "x", "c")
    mesh = Mesh(mesh.devices.reshape(4, 8, 4, 2), axes)
    comp, pt = ("x", "c"), ("y", "z")
    return jax.shard_map(
        body,
        mesh=mesh,
        in_specs=(P(axes, None), P(comp, None), P(comp), P()),
        out_specs=(P(axes, None), P(comp), P(pt, comp), P(axes)),
        check_vma=False,
    )
```

time: 394 us -> 166 us (0.42)
  waiting for transfers between devices: 219 us -> 51.2 us
  blocking collectives: 103 us -> 29.7 us
  starting transfers between devices: 4.76 us -> 32.8 us
  Pallas kernels: 0 us -> 26.1 us
  other arithmetic: 23.6 us -> 7.94 us
  between operations: 14.8 us -> 1.5 us
  matrix products: 12.4 us -> 0 us
    unnamed x3 -> x0, waiting for transfers between devices: 144 us -> none
    psum x1 -> x0, blocking collectives: 73.2 us -> none  [body(): counts = lax.psum(jnp.sum(resp.astype(jnp.float32), axis=0), 'pt')]
    all_gather x1 -> x0, waiting for transfers between devices: 27.1 us -> none  [body(): gathered = lax.all_gather(points, 'comp', axis=0, tiled=True)]
    pallas_call x0 -> x5, Pallas kernels: none -> 26.1 us  [the longest x1 11.8 us: partial_sums(): pl.pallas_call(sums_kernel, grid_spec=pltpu.PrefetchScalarGridSpec(num_sc...]
    ppermute x0 -> x13, waiting for transfers between devices: none -> 24.8 us  [shift(): return lax.ppermute(value, axis, [(i, (i + step) % n) for i in range(n)])]
    all_to_all x1 -> x3, waiting for transfers between devices: 48.2 us -> 26.3 us  [the longest x1 15.2 us: body(): lax.all_to_all(sums, ('y', 'z'), split_axis=0, concat_axis=0, tiled=True)]
    ppermute x0 -> x13, starting transfers between devices: none -> 14.4 us  [shift(): return lax.ppermute(value, axis, [(i, (i + step) % n) for i in range(n)])]
    all_to_all x1 -> x3, starting transfers between devices: 4.68 us -> 18.5 us  [the longest x1 9.43 us: body(): lax.all_to_all(counts, ('y', 'z'), split_axis=0, concat_axis=0, tiled=True)]
  transfers between devices with their start and end apart: 3 -> 16, of which waited for: 3 -> 9; matrix products, arithmetic and copies ran while one was open for 4% -> 12% of each run, Pallas kernels for 0% -> 8%
where the time goes in v1:
time: 166 us; the launch traced here: 165 us
  waiting for transfers between devices  51.2 us (31%)
  starting transfers between devices  32.8 us (20%)
  blocking collectives  29.7 us (18%)
  Pallas kernels  26.1 us (16%)
  local copies, waits for them, and re-layouts  15.6 us (9%)
  other arithmetic  7.94 us (5%)
    all_to_all x1, blocking collectives, body(): lax.all_to_all(resp, ('c', 'x'), split_axis=0, concat_axis=0, tiled=True)  29.7 us
    ppermute x13, waiting for transfers between devices, shift(): return lax.ppermute(value, axis, [(i, (i + step) % n) for i in range(n)])  24.8 us
    all_to_all x1, waiting for transfers between devices, body(): lax.all_to_all(sums, ('y', 'z'), split_axis=0, concat_axis=0, tiled=True)  15.2 us
    ppermute x13, starting transfers between devices, shift(): return lax.ppermute(value, axis, [(i, (i + step) % n) for i in range(n)])  14.4 us
    pallas_call x1, Pallas kernels, partial_sums(): pl.pallas_call(sums_kernel, grid_spec=pltpu.PrefetchScalarGridSpec(num_sc...  11.8 us
    all_to_all x1, starting transfers between devices, body(): lax.all_to_all(counts, ('y', 'z'), split_axis=0, concat_axis=0, tiled=True)  9.43 us
    pallas_call x1, Pallas kernels, scores(): pl.pallas_call(score_kernel, grid=(2048 // width,), out_shape=(jax.ShapeD...  9.08 us
    reshape x2, local copies, waits for them, and re-layouts, body(): resp_rows.reshape(2, 4, 64, 2048).transpose(2, 1, 0, 3).reshape(64, 16384)  7.99 us
  transfers between devices with their start and end apart: 16, of which 9 were waited for; matrix products, arithmetic and copies ran while one was open for 12% of the time, Pallas kernels for 8%

profile of v1, /device:TPU:32, one launch (start us, length us, event | category | flops | bytes accessed | tf_op | source)
XLA Modules:
  0.0 164.9 jit_solution(18052054546920175576)
XLA Ops:
  2.2 1.7 %collective-permute-start.1 = (bf16[64,1024]{1,0:T(8,128)(2,1)}, bf16[64,1024]{1,0:T(8,128)(2,1)S(1)}, u32[]{:S(2)}, u32[]{:S(2)}) collective-permute-start(bf16[64,1024]{1,0:T(8,128)(2,1)} %own.1), channel_id=1, source_target_pairs={{0,6},{2,0},{4,2},{6,4},{1,7},{3,1},{5,3},{7,5},{8,14},{10,8},{12,... | collective-permute-start | bytes 393224 | tf_op jit(solution)/shard_map/ppermute | solution.py:21
  3.9 1.8 %collective-permute-start.2 = (bf16[64,1024]{1,0:T(8,128)(2,1)}, bf16[64,1024]{1,0:T(8,128)(2,1)S(1)}, u32[]{:S(2)}, u32[]{:S(2)}) collective-permute-start(bf16[64,1024]{1,0:T(8,128)(2,1)} %own.1), channel_id=1, source_target_pairs={{0,4},{2,6},{4,0},{6,2},{1,5},{3,7},{5,1},{7,3},{8,12},{10,14},{12... | collective-permute-start | bytes 393224 | tf_op jit(solution)/shard_map/ppermute | solution.py:21
  7.4 2.2 %collective-permute-done.1.after = bf16[64,1024]{1,0:T(8,128)(2,1)S(1)} collective-permute-done((bf16[64,1024]{1,0:T(8,128)(2,1)}, bf16[64,1024]{1,0:T(8,128)(2,1)S(1)}, u32[]{:S(2)}, u32[]{:S(2)}) %collective-permute-start.1) | collective-permute-done | bytes 131104 | tf_op jit(solution)/shard_map/ppermute | solution.py:21
  14.3 1.7 %collective-permute-start.6 = (bf16[256,1024]{1,0:T(8,128)(2,1)S(1)}, bf16[256,1024]{1,0:T(8,128)(2,1)S(1)}, u32[]{:S(2)}, u32[]{:S(2)}) collective-permute-start(bf16[256,1024]{1,0:T(8,128)(2,1)S(1)} %shard_map.75.own.refs_0_), channel_id=1, source_target_pairs={{0,192},{64,0},{128,64},{192,128},{1,193},{65,1},{129,65},{193,129... | collective-permute-start | bytes 1572872 | tf_op jit(solution)/shard_map/ppermute | solution.py:21
  16.0 2.0 %collective-permute-start.8 = (bf16[64,1024]{1,0:T(8,128)(2,1)S(1)}, bf16[64,1024]{1,0:T(8,128)(2,1)S(1)}, u32[]{:S(2)}, u32[]{:S(2)}) collective-permute-start(bf16[64,1024]{1,0:T(8,128)(2,1)S(1)} %copy-done.1), channel_id=1, source_target_pairs={{0,128},{64,192},{128,0},{192,64},{1,129},{65,193},{129,1},{193,65... | collective-permute-start | bytes 393224 | tf_op jit(solution)/shard_map/ppermute | solution.py:21
  18.0 13.0 %collective-permute-done.8.own = bf16[64,1024]{1,0:T(8,128)(2,1)S(1)} collective-permute-done((bf16[64,1024]{1,0:T(8,128)(2,1)S(1)}, bf16[64,1024]{1,0:T(8,128)(2,1)S(1)}, u32[]{:S(2)}, u32[]{:S(2)}) %collective-permute-start.8) | collective-permute-done | bytes 131104 | tf_op jit(solution)/shard_map/ppermute | solution.py:21
  31.3 2.9 %collective-permute-start.10 = (bf16[64,1024]{1,0:T(8,128)(2,1)S(1)}, bf16[64,1024]{1,0:T(8,128)(2,1)S(1)}, u32[]{:S(2)}, u32[]{:S(2)}) collective-permute-start(bf16[64,1024]{1,0:T(8,128)(2,1)S(1)} %collective-permute-done.8.own), channel_id=1, source_target_pairs={{0,6},{2,0},{4,2},{6,4},{1,7},{3,1},{5,3},{7,5},{8,14},{10,8},{12,... | collective-permute-start | bytes 393224 | tf_op jit(solution)/shard_map/ppermute | solution.py:21
  34.2 4.3 %collective-permute-done.9.before = bf16[64,1024]{1,0:T(8,128)(2,1)S(1)} collective-permute-done((bf16[64,1024]{1,0:T(8,128)(2,1)S(1)}, bf16[64,1024]{1,0:T(8,128)(2,1)S(1)}, u32[]{:S(2)}, u32[]{:S(2)}) %collective-permute-start.9) | collective-permute-done | bytes 131104 | tf_op jit(solution)/shard_map/ppermute | solution.py:21
  38.6 2.1 %collective-permute-done.11.far = bf16[64,1024]{1,0:T(8,128)(2,1)S(1)} collective-permute-done((bf16[64,1024]{1,0:T(8,128)(2,1)S(1)}, bf16[64,1024]{1,0:T(8,128)(2,1)S(1)}, u32[]{:S(2)}, u32[]{:S(2)}) %collective-permute-start.11) | collective-permute-done | bytes 131104 | tf_op jit(solution)/shard_map/ppermute | solution.py:21
  42.0 5.6 %fusion.2 = (f32[2048]{0:T(1024)S(1)}, bf16[2048,1024]{1,0:T(8,128)(2,1)}) fusion(bf16[2048,1024]{1,0:T(8,128)(2,1)} %param.5, f32[1024]{0:T(1024)} %param.7), kind=kLoop, calls=%fused_computation.4 | loop fusion | flops 12580864 | bytes 8400896 | tf_op jit(solution)/shard_map/reduce_sum | solution.py:232
  47.6 9.1 %shard_map.76 = (f32[512,2048]{1,0:T(8,128)S(1)}, f32[32,4,128]{2,1,0:T(4,128)}) custom-call(s32[3]{0:T(128)S(1)} %pad_add_fusion.at, bf16[256,1024]{1,0:T(8,128)(2,1)S(1)} %shard_map.75.own.refs_0_, bf16[256,1024]{1,0:T(8,128)(2,1)S(1)} %collective-permute-done.3.other.refs_1_, bf16[2048,1024]{1,0:T(8,128)(2,1)} %get-tuple-element.13.scaled, ...), custom_call_target="tpu_custom_call" | custom-call | flops 2147483648 | bytes 9437184 | tf_op jit(solution)/shard_map/pallas_call | solution.py:94
  56.7 2.0 %copy-done = f32[512,2048]{1,0:T(8,128)} copy-done((f32[512,2048]{1,0:T(8,128)}, f32[512,2048]{1,0:T(8,128)S(1)}, u32[]{:S(2)}) %copy-start) | copy-done | bytes 4194328
  58.7 4.0 %all-to-all-start = ((f32[32,4,128]{2,1,0:T(4,128)}), f32[32,4,128]{2,1,0:T(4,128)S(1)}, u32[]{:S(2)}, u32[]{:S(2)}) async-start(f32[32,4,128]{2,1,0:T(4,128)} %get-tuple-element.8), calls=%async_computation | async-start | bytes 131072 | tf_op jit(solution)/shard_map/all_to_all | solution.py:244
  64.1 6.1 %all-to-all-done = f32[32,4,128]{2,1,0:T(4,128)S(1)} async-done(((f32[32,4,128]{2,1,0:T(4,128)}), f32[32,4,128]{2,1,0:T(4,128)S(1)}, u32[]{:S(2)}, u32[]{:S(2)}) %all-to-all-start) | async-done | bytes 65568 | tf_op jit(solution)/shard_map/all_to_all | solution.py:244
  70.2 11.8 %shard_map.79 = (bf16[1024,512]{1,0:T(8,128)(2,1)}, f32[32,4,128]{2,1,0:T(4,128)}) custom-call(s32[3]{0:T(128)S(1)} %pad_add_fusion.at, f32[4,8,4,128]{3,2,1,0:T(4,128)S(1)} %bitcast.37, bf16[2048,1024]{1,0:T(8,128)(2,1)} %get-tuple-element.13.scaled, f32[2048,1]{1,0:T(8,128)} %copy.17.bias, bf16[256,1024]{1,0:T(8,128)(2,1)S(1)} %shard_map.75.own.refs_0_, ...), custom_call_target="tpu_custom_call" | custom-call | flops 4294967296 | bytes 8388608 | tf_op jit(solution)/shard_map/pallas_call | solution.py:189
  82.1 9.4 %all-to-all-start.2 = ((f32[32,4,128]{2,1,0:T(4,128)}), f32[32,4,128]{2,1,0:T(4,128)S(1)}, u32[]{:S(2)}, u32[]{:S(2)}) async-start(f32[32,4,128]{2,1,0:T(4,128)} %get-tuple-element.10), calls=%async_computation.2 | async-start | bytes 131072 | tf_op jit(solution)/shard_map/all_to_all | solution.py:252
  91.5 4.0 %shard_map.77 = bf16[512,2048]{1,0:T(8,128)(2,1)S(1)} custom-call(s32[3]{0:T(128)S(1)} %pad_add_fusion.at, f32[4,8,4,128]{3,2,1,0:T(4,128)S(1)} %bitcast.38, f32[512,2048]{1,0:T(8,128)} %copy-done), custom_call_target="tpu_custom_call" | custom-call | flops 2097152 | bytes 6291456 | tf_op jit(solution)/shard_map/pallas_call | solution.py:133
  95.6 5.1 %all-to-all-done.2 = f32[32,4,128]{2,1,0:T(4,128)S(1)} async-done(((f32[32,4,128]{2,1,0:T(4,128)}), f32[32,4,128]{2,1,0:T(4,128)S(1)}, u32[]{:S(2)}, u32[]{:S(2)}) %all-to-all-start.2) | async-done | bytes 65568 | tf_op jit(solution)/shard_map/all_to_all | solution.py:252
  100.6 29.7 %all_to_all.28 = bf16[8,64,2048]{2,1,0:T(8,128)(2,1)} all-to-all(bf16[8,64,2048]{2,1,0:T(8,128)(2,1)S(1)} %bitcast.36), channel_id=1, replica_groups=mesh['y'=4,'z'=8,'x'=4,'c'=2] {'c','x'}, dimensions={0} | all-to-all | bytes 4194304 | tf_op jit(solution)/shard_map/all_to_all | solution.py:248
  130.4 5.0 %all-to-all-start.3 = ((bf16[32,32,512]{2,1,0:T(8,128)(2,1)}), bf16[32,32,512]{2,1,0:T(8,128)(2,1)S(1)}, u32[]{:S(2)}, u32[]{:S(2)}) async-start(bf16[32,32,512]{2,1,0:T(8,128)(2,1)} %bitcast.9), calls=%async_computation.3 | async-start | bytes 2097152 | tf_op jit(solution)/shard_map/all_to_all | solution.py:253
  135.4 2.0 %constant_dynamic-slice_fusion.1 = bf16[2048,32]{1,0:T(8,128)(2,1)} fusion(bf16[2048,1024]{1,0:T(8,128)(2,1)} %param.5, s32[]{:T(128)S(6)} %select_n.11), kind=kLoop, calls=%fused_computation.19 | loop fusion | bytes 262148 | tf_op jit(solution)/shard_map/dynamic_slice | solution.py:257
  140.9 3.5 %copy.24 = bf16[2,4,64,2048]{3,0,1,2:T(2,128)(2,1)} copy(bf16[2,4,64,2048]{3,2,1,0:T(8,128)(2,1)S(1)} %bitcast.43) | data formatting | bytes 4194304 | tf_op jit(solution)/shard_map/reshape | solution.py:249
  144.4 4.5 %reshape.55 = bf16[64,16384]{1,0:T(8,128)(2,1)} reshape(bf16[64,4,2,2048]{3,2,1,0:T(2,128)(2,1)} %bitcast.44) | data formatting | bytes 4194304 | tf_op jit(solution)/shard_map/reshape | solution.py:249
  148.9 15.2 %all-to-all-done.3 = bf16[32,32,512]{2,1,0:T(8,128)(2,1)S(1)} async-done(((bf16[32,32,512]{2,1,0:T(8,128)(2,1)}), bf16[32,32,512]{2,1,0:T(8,128)(2,1)S(1)}, u32[]{:S(2)}, u32[]{:S(2)}) %all-to-all-start.3) | async-done | bytes 1048608 | tf_op jit(solution)/shard_map/all_to_all | solution.py:253
  (50 shorter events, 14.5 us)
Async XLA Ops:
  0.6 6.7 %collective-permute-start = (bf16[64,1024]{1,0:T(8,128)(2,1)}, bf16[64,1024]{1,0:T(8,128)(2,1)S(1)}, u32[]{:S(2)}, u32[]{:S(2)}) collective-permute-start(bf16[64,1024]{1,0:T(8,128)(2,1)} %own.1), channel_id=1, source_target_pairs={{0,2},{2,4},{4,6},{6,0},{1,3},{3,5},{5,7},{7,1},{8,10},{10,12},{12... | collective-permute-start | bytes 393224 | tf_op jit(solution)/shard_map/ppermute | solution.py:21
  2.2 7.4 %collective-permute-start.1 = (bf16[64,1024]{1,0:T(8,128)(2,1)}, bf16[64,1024]{1,0:T(8,128)(2,1)S(1)}, u32[]{:S(2)}, u32[]{:S(2)}) collective-permute-start(bf16[64,1024]{1,0:T(8,128)(2,1)} %own.1), channel_id=1, source_target_pairs={{0,6},{2,0},{4,2},{6,4},{1,7},{3,1},{5,3},{7,5},{8,14},{10,8},{12,... | collective-permute-start | bytes 393224 | tf_op jit(solution)/shard_map/ppermute | solution.py:21
  3.9 7.2 %collective-permute-start.2 = (bf16[64,1024]{1,0:T(8,128)(2,1)}, bf16[64,1024]{1,0:T(8,128)(2,1)S(1)}, u32[]{:S(2)}, u32[]{:S(2)}) collective-permute-start(bf16[64,1024]{1,0:T(8,128)(2,1)} %own.1), channel_id=1, source_target_pairs={{0,4},{2,6},{4,0},{6,2},{1,5},{3,7},{5,1},{7,3},{8,12},{10,14},{12... | collective-permute-start | bytes 393224 | tf_op jit(solution)/shard_map/ppermute | solution.py:21
  11.2 0.9 copy-start.1
  12.7 28.8 %collective-permute-start.4 = (bf16[256,1024]{1,0:T(8,128)(2,1)S(1)}, bf16[256,1024]{1,0:T(8,128)(2,1)S(1)}, u32[]{:S(2)}, u32[]{:S(2)}) collective-permute-start(bf16[256,1024]{1,0:T(8,128)(2,1)S(1)} %shard_map.75.own.refs_0_), channel_id=1, source_target_pairs={{0,64},{64,128},{128,192},{192,0},{1,65},{65,129},{129,193},{193,1... | collective-permute-start | bytes 1572872 | tf_op jit(solution)/shard_map/ppermute | solution.py:21
  14.3 27.6 %collective-permute-start.6 = (bf16[256,1024]{1,0:T(8,128)(2,1)S(1)}, bf16[256,1024]{1,0:T(8,128)(2,1)S(1)}, u32[]{:S(2)}, u32[]{:S(2)}) collective-permute-start(bf16[256,1024]{1,0:T(8,128)(2,1)S(1)} %shard_map.75.own.refs_0_), channel_id=1, source_target_pairs={{0,192},{64,0},{128,64},{192,128},{1,193},{65,1},{129,65},{193,129... | collective-permute-start | bytes 1572872 | tf_op jit(solution)/shard_map/ppermute | solution.py:21
  16.0 15.0 %collective-permute-start.8 = (bf16[64,1024]{1,0:T(8,128)(2,1)S(1)}, bf16[64,1024]{1,0:T(8,128)(2,1)S(1)}, u32[]{:S(2)}, u32[]{:S(2)}) collective-permute-start(bf16[64,1024]{1,0:T(8,128)(2,1)S(1)} %copy-done.1), channel_id=1, source_target_pairs={{0,128},{64,192},{128,0},{192,64},{1,129},{65,193},{129,1},{193,65... | collective-permute-start | bytes 393224 | tf_op jit(solution)/shard_map/ppermute | solution.py:21
  31.0 7.6 %collective-permute-start.9 = (bf16[64,1024]{1,0:T(8,128)(2,1)S(1)}, bf16[64,1024]{1,0:T(8,128)(2,1)S(1)}, u32[]{:S(2)}, u32[]{:S(2)}) collective-permute-start(bf16[64,1024]{1,0:T(8,128)(2,1)S(1)} %collective-permute-done.8.own), channel_id=1, source_target_pairs={{0,2},{2,4},{4,6},{6,0},{1,3},{3,5},{5,7},{7,1},{8,10},{10,12},{12... | collective-permute-start | bytes 393224 | tf_op jit(solution)/shard_map/ppermute | solution.py:21
  31.3 7.2 %collective-permute-start.10 = (bf16[64,1024]{1,0:T(8,128)(2,1)S(1)}, bf16[64,1024]{1,0:T(8,128)(2,1)S(1)}, u32[]{:S(2)}, u32[]{:S(2)}) collective-permute-start(bf16[64,1024]{1,0:T(8,128)(2,1)S(1)} %collective-permute-done.8.own), channel_id=1, source_target_pairs={{0,6},{2,0},{4,2},{6,4},{1,7},{3,1},{5,3},{7,5},{8,14},{10,8},{12,... | collective-permute-start | bytes 393224 | tf_op jit(solution)/shard_map/ppermute | solution.py:21
  34.2 6.5 %collective-permute-start.11 = (bf16[64,1024]{1,0:T(8,128)(2,1)S(1)}, bf16[64,1024]{1,0:T(8,128)(2,1)S(1)}, u32[]{:S(2)}, u32[]{:S(2)}) collective-permute-start(bf16[64,1024]{1,0:T(8,128)(2,1)S(1)} %collective-permute-done.8.own), channel_id=1, source_target_pairs={{0,4},{2,6},{4,0},{6,2},{1,5},{3,7},{5,1},{7,3},{8,12},{10,14},{12... | collective-permute-start | bytes 393224 | tf_op jit(solution)/shard_map/ppermute | solution.py:21
  38.6 9.1 %collective-permute-start.3 = (bf16[256,1024]{1,0:T(8,128)(2,1)S(1)}, bf16[256,1024]{1,0:T(8,128)(2,1)S(1)}, u32[]{:S(2)}, u32[]{:S(2)}) collective-permute-start(bf16[256,1024]{1,0:T(8,128)(2,1)S(1)} %shard_map.75.own.refs_0_), channel_id=1, source_target_pairs={{0,1},{1,0},{2,3},{3,2},{4,5},{5,4},{6,7},{7,6},{8,9},{9,8},{10,11... | collective-permute-start | bytes 1572872 | tf_op jit(solution)/shard_map/ppermute | solution.py:21
  41.3 6.3 %copy-start.6 = (f32[2048]{0:T(1024)S(1)}, f32[2048]{0:T(1024)}, u32[]{:S(2)}) copy-start(f32[2048]{0:T(1024)} %param.6) | copy-start | bytes 24580
  41.3 28.9 %collective-permute-start.12 = (bf16[256,1024]{1,0:T(8,128)(2,1)S(1)}, bf16[256,1024]{1,0:T(8,128)(2,1)}, u32[]{:S(2)}, u32[]{:S(2)}) collective-permute-start(bf16[256,1024]{1,0:T(8,128)(2,1)S(1)} %shard_map.78.refs_6_), channel_id=1, source_target_pairs={{0,1},{1,0},{2,3},{3,2},{4,5},{5,4},{6,7},{7,6},{8,9},{9,8},{10,11... | collective-permute-start | bytes 1572872 | tf_op jit(solution)/shard_map/ppermute | solution.py:21
  41.4 28.8 %collective-permute-start.5 = (bf16[256,1024]{1,0:T(8,128)(2,1)S(1)}, bf16[256,1024]{1,0:T(8,128)(2,1)}, u32[]{:S(2)}, u32[]{:S(2)}) collective-permute-start(bf16[256,1024]{1,0:T(8,128)(2,1)S(1)} %collective-permute-done.4.refs_2_), channel_id=1, source_target_pairs={{0,1},{1,0},{2,3},{3,2},{4,5},{5,4},{6,7},{7,6},{8,9},{9,8},{10,11... | collective-permute-start | bytes 1572872 | tf_op jit(solution)/shard_map/ppermute | solution.py:21
  41.9 28.3 %collective-permute-start.7 = (bf16[256,1024]{1,0:T(8,128)(2,1)S(1)}, bf16[256,1024]{1,0:T(8,128)(2,1)}, u32[]{:S(2)}, u32[]{:S(2)}) collective-permute-start(bf16[256,1024]{1,0:T(8,128)(2,1)S(1)} %collective-permute-done.6.refs_4_), channel_id=1, source_target_pairs={{0,1},{1,0},{2,3},{3,2},{4,5},{5,4},{6,7},{7,6},{8,9},{9,8},{10,11... | collective-permute-start | bytes 1572872 | tf_op jit(solution)/shard_map/ppermute | solution.py:21
  56.7 2.0 %copy-start = (f32[512,2048]{1,0:T(8,128)}, f32[512,2048]{1,0:T(8,128)S(1)}, u32[]{:S(2)}) copy-start(f32[512,2048]{1,0:T(8,128)S(1)} %get-tuple-element.9.score) | copy-start | bytes 12582916
  58.7 11.5 %all-to-all-start = ((f32[32,4,128]{2,1,0:T(4,128)}), f32[32,4,128]{2,1,0:T(4,128)S(1)}, u32[]{:S(2)}, u32[]{:S(2)}) async-start(f32[32,4,128]{2,1,0:T(4,128)} %get-tuple-element.8), calls=%async_computation | async-start | bytes 131072 | tf_op jit(solution)/shard_map/all_to_all | solution.py:244
  82.1 18.6 %all-to-all-start.2 = ((f32[32,4,128]{2,1,0:T(4,128)}), f32[32,4,128]{2,1,0:T(4,128)S(1)}, u32[]{:S(2)}, u32[]{:S(2)}) async-start(f32[32,4,128]{2,1,0:T(4,128)} %get-tuple-element.10), calls=%async_computation.2 | async-start | bytes 131072 | tf_op jit(solution)/shard_map/all_to_all | solution.py:252
  95.6 43.1 %copy-start.4 = (f32[1024]{0:T(1024)S(1)}, f32[1024]{0:T(1024)}, u32[]{:S(2)}) copy-start(f32[1024]{0:T(1024)} %param.7) | copy-start | bytes 12292
  95.6 44.4 %copy-start.2 = (bf16[64,1024]{1,0:T(8,128)(2,1)S(1)}, bf16[64,1024]{1,0:T(8,128)(2,1)}, u32[]{:S(2)}) copy-start(bf16[64,1024]{1,0:T(8,128)(2,1)} %own.1) | copy-start | bytes 393220
  130.4 10.5 %copy-start.3 = (bf16[8,64,2048]{2,1,0:T(8,128)(2,1)S(1)}, bf16[8,64,2048]{2,1,0:T(8,128)(2,1)}, u32[]{:S(2)}) copy-start(bf16[8,64,2048]{2,1,0:T(8,128)(2,1)} %all_to_all.28) | copy-start | bytes 6291460
  130.4 33.7 %all-to-all-start.3 = ((bf16[32,32,512]{2,1,0:T(8,128)(2,1)}), bf16[32,32,512]{2,1,0:T(8,128)(2,1)S(1)}, u32[]{:S(2)}, u32[]{:S(2)}) async-start(bf16[32,32,512]{2,1,0:T(8,128)(2,1)} %bitcast.9), calls=%async_computation.3 | async-start | bytes 2097152 | tf_op jit(solution)/shard_map/all_to_all | solution.py:253
  140.8 8.0 %copy-start.5 = (f32[1,4,4,128]{3,1,2,0:T(4,128)}, f32[1,4,4,128]{3,1,2,0:T(4,128)S(1)}, u32[]{:S(2)}) copy-start(f32[1,4,4,128]{3,1,2,0:T(4,128)S(1)} %copy.22) | copy-start | bytes 24580

commit v2 on v1

v2 whole, which is shorter than its diff:
```python
import functools
import math

import jax
import jax.numpy as jnp
from jax import lax
from jax.experimental import pallas as pl
from jax.experimental.pallas import tpu as pltpu
from jax.sharding import Mesh
from jax.sharding import PartitionSpec as P

BF = jnp.bfloat16
F32 = jnp.float32
VMEM_LIMIT = 24 * 1024 * 1024
VMEM = pltpu.VMEM
SIZES = {"y": 4, "z": 8, "x": 4, "c": 2}


def shift(value, axis, step):
    n = SIZES[axis]
    return lax.ppermute(value, axis, [(i, (i + step) % n) for i in range(n)])


def swap(value, axis, bit):
    n = SIZES[axis]
    return lax.ppermute(value, axis, [(i, i ^ bit) for i in range(n)])


def params():
    return pltpu.CompilerParams(vmem_limit_bytes=VMEM_LIMIT)


def whole():
    return pl.BlockSpec(memory_space=VMEM)


def scalar():
    return pl.BlockSpec(memory_space=pltpu.SMEM)


def anywhere(n=1):
    return [pl.BlockSpec(memory_space=pl.ANY)] * n


def hbm(n=1):
    return [pl.BlockSpec(memory_space=pltpu.HBM)] * n


def hand_on_kernel(value, *refs):
    refs[-1][...] = value[...]


def hand_on(value, *first):
    return pl.pallas_call(
        hand_on_kernel,
        out_shape=jax.ShapeDtypeStruct(value.shape, value.dtype),
        in_specs=[whole()] + anywhere(len(first)),
        out_specs=whole(),
        compiler_params=params(),
    )(value, *first)


def place_kernel(at, own, before, after, far, *refs):
    out = refs[-1]
    x = at[0]
    for step, piece in ((0, own), (3, before), (1, after), (2, far)):
        slot = lax.rem(x + step, 4)
        out[pl.ds(pl.multiple_of(slot * 64, 64), 64), :] = piece[...]


def gather_x(at, own, ahead):
    parts = (own, shift(own, "x", 1), shift(own, "x", -1), shift(own, "x", 2))
    return pl.pallas_call(
        place_kernel,
        out_shape=jax.ShapeDtypeStruct((256, 1024), BF),
        in_specs=[scalar()] + [whole()] * 4 + anywhere(len(ahead)),
        out_specs=whole(),
        compiler_params=params(),
    )(at, *parts, *ahead)


def column(row):
    return jnp.transpose(jnp.broadcast_to(row, (128, 128)))[:, 0:1]


def line(col):
    return jnp.transpose(jnp.broadcast_to(col, (128, 128)))[0:1, :]


def score_kernel(at, own, other, scaled, bias, score, share, rows, peak, total):
    step = pl.program_id(0)
    c = at[1]

    @pl.when(step == 0)
    def _():
        rows[pl.ds(pl.multiple_of(c * 256, 256), 256), :] = own[...]
        rows[pl.ds(pl.multiple_of((1 - c) * 256, 256), 256), :] = other[...]
        peak[...] = jnp.full_like(peak, -jnp.inf)
        total[...] = jnp.zeros_like(total)

    for r in range(2):
        cut = slice(r * 256, r * 256 + 256)
        tile = lax.dot_general(
            rows[cut, :], scaled[...], (((1,), (1,)), ((), ())), preferred_element_type=F32
        )
        tile = tile + bias[...]
        score[cut, :] = tile
        lanes = [tile[:, i : i + 128] for i in range(0, tile.shape[1], 128)]
        old = peak[cut, :]
        top = functools.reduce(jnp.maximum, lanes, old)
        added = functools.reduce(jnp.add, [jnp.exp(lane - top) for lane in lanes])
        total[cut, :] = total[cut, :] * jnp.exp(old - top) + added
        peak[cut, :] = top

    @pl.when(step == pl.num_programs(0) - 1)
    def _():
        for b in range(4):
            cut = slice(b * 128, b * 128 + 128)
            top = jnp.max(peak[cut, :], axis=1, keepdims=True)
            mass = jnp.sum(total[cut, :] * jnp.exp(peak[cut, :] - top), axis=1, keepdims=True)
            share[:, b, :] = jnp.broadcast_to(line(top + jnp.log(mass)), (32, 128))


def scores(at, own, other, scaled, bias_row):
    width = 512
    return pl.pallas_call(
        score_kernel,
        grid=(2048 // width,),
        out_shape=(
            pltpu.HBM((512, 2048), F32),
            jax.ShapeDtypeStruct((32, 4, 128), F32),
        ),
        in_specs=[
            scalar(),
            pl.BlockSpec((256, 1024), lambda i: (0, 0)),
            pl.BlockSpec((256, 1024), lambda i: (0, 0)),
            pl.BlockSpec((width, 1024), lambda i: (i, 0)),
            pl.BlockSpec((1, width), lambda i: (0, i)),
        ],
        out_specs=(
            pl.BlockSpec((512, width), lambda i: (0, i)),
            pl.BlockSpec((32, 4, 128), lambda i: (0, 0, 0)),
        ),
        scratch_shapes=[VMEM((512, 1024), BF), VMEM((512, 128), F32), VMEM((512, 128), F32)],
        compiler_params=params(),
        cost_estimate=pl.CostEstimate(
            flops=2 * 512 * 2048 * 1024, bytes_accessed=9 << 20, transcendentals=1 << 20
        ),
    )(at, own, other, scaled, bias_row)


def joined(shares):
    top = jnp.max(shares, axis=0)
    return top + jnp.log(jnp.sum(jnp.exp(shares - top[None]), axis=0))


def sums_kernel(at, shares, scaled, bias, *refs):
    pieces = refs[:8]
    sums, counts = refs[8:10]
    rows, weights, lse, sems = refs[10:]
    copies = [
        pltpu.make_async_copy(piece, rows.at[pl.ds(i * 256, 256)], sems.at[i])
        for i, piece in enumerate(pieces)
    ]
    for copy in copies:
        copy.start()
    y, c = at[2], at[1]
    for yy in range(4):
        lse[pl.ds(yy * 4, 4), :] = joined(shares[yy])
    count = jnp.zeros((512, 128), F32)
    for i in range(8):
        there = lax.rem(y + (0, 3, 1, 2)[i // 2], 4)
        core = c if i % 2 == 0 else 1 - c
        at_row = there * 4 + core * 2
        norm = jnp.concatenate([lse[pl.ds(at_row, 1), :], lse[pl.ds(at_row + 1, 1), :]], axis=1)
        cut = slice(i * 256, i * 256 + 256)
        copies[i].wait()
        score = lax.dot_general(
            scaled[...], rows[cut, :], (((1,), (1,)), ((), ())), preferred_element_type=F32
        )
        weight = jnp.exp(score + bias[...] - norm).astype(BF)
        weights[:, cut] = weight
        count = count + weight[:, :128].astype(F32) + weight[:, 128:].astype(F32)
    count = jnp.sum(count, axis=1, keepdims=True)
    counts[...] = jnp.zeros_like(counts)
    for b in range(4):
        counts[pl.ds(y * 4 + b, 1), :] = line(count[b * 128 : b * 128 + 128])
    for j in range(4):
        cut = slice(j * 256, j * 256 + 256)
        block = lax.dot_general(
            weights[...], rows[:, cut], (((1,), (0,)), ((), ())), preferred_element_type=F32
        )
        sums[cut, :] = jnp.transpose(block.astype(BF))


def partial_sums(at, shares, scaled, bias_col, pieces):
    return pl.pallas_call(
        sums_kernel,
        grid_spec=pltpu.PrefetchScalarGridSpec(
            num_scalar_prefetch=1,
            grid=(1,),
            in_specs=[
                pl.BlockSpec((4, 8, 4, 128), lambda i, at: (0, 0, 0, 0)),
                pl.BlockSpec((512, 1024), lambda i, at: (at[2], 0)),
                pl.BlockSpec((512, 1), lambda i, at: (at[2], 0)),
            ]
            + anywhere(8),
            out_specs=(
                pl.BlockSpec((1024, 512), lambda i, at: (0, 0)),
                pl.BlockSpec((16, 128), lambda i, at: (0, 0)),
            ),
            scratch_shapes=[
                VMEM((2048, 1024), BF),
                VMEM((512, 2048), BF),
                VMEM((16, 128), F32),
                pltpu.SemaphoreType.DMA((8,)),
            ],
        ),
        out_shape=(
            pltpu.HBM((1024, 512), BF),
            jax.ShapeDtypeStruct((16, 128), F32),
        ),
        compiler_params=params(),
        cost_estimate=pl.CostEstimate(
            flops=4 * 512 * 2048 * 1024, bytes_accessed=8 << 20, transcendentals=1 << 20
        ),
    )(at, shares, scaled, bias_col, *pieces)


def resp_kernel(at, shares, counts, score, *refs):
    outs, passed, norm, held, sems = refs[:8], refs[8], refs[9], refs[10], refs[11]
    x, c, y = at[0], at[1], at[2]
    copies = []
    for j in range(8):
        core = 1 - c if j < 4 else c
        start = pl.multiple_of(core * 256 + lax.rem(x + j % 4, 4) * 64, 64)
        copies.append(
            (start, pltpu.make_async_copy(score.at[pl.ds(start, 64)], held.at[j], sems.at[j]))
        )
    for _, copy in copies:
        copy.start()
    passed[...] = counts[...]
    lse = joined(shares[y])
    for b in range(4):
        norm[b * 128 : b * 128 + 128, :] = jnp.transpose(
            jnp.broadcast_to(lse[b : b + 1, :], (128, 128))
        )
    for j, (start, copy) in enumerate(copies):
        copy.wait()
        outs[j][...] = jnp.exp(held[j] - norm[pl.ds(start, 64), 0:1]).astype(BF)


def responsibilities(at, shares, counts, score):
    return pl.pallas_call(
        resp_kernel,
        in_specs=[scalar(), whole(), whole()] + hbm(),
        out_specs=[whole()] * 9,
        scratch_shapes=[
            VMEM((512, 128), F32),
            VMEM((8, 64, 2048), F32),
            pltpu.SemaphoreType.DMA((8,)),
        ],
        out_shape=[jax.ShapeDtypeStruct((64, 2048), BF)] * 8
        + [jax.ShapeDtypeStruct((16, 128), F32)],
        compiler_params=params(),
        cost_estimate=pl.CostEstimate(flops=1 << 21, bytes_accessed=6 << 20, transcendentals=1 << 20),
    )(at, shares, counts, pltpu.with_memory_space_constraint(score, pltpu.HBM))


def lay_kernel(at, *refs):
    pieces, out, sems = refs[:8], refs[8], refs[9]
    x, c = at[0], at[1]
    copies = []
    for j in range(8):
        core = 1 - c if j < 4 else c
        comp = lax.rem(x + 4 - j % 4, 4) * 2 + core
        spot = out.at[:, pl.ds(pl.multiple_of(comp * 2048, 2048), 2048)]
        copies.append(pltpu.make_async_copy(pieces[j], spot, sems.at[j]))
    for copy in copies:
        copy.start()
    for copy in copies:
        copy.wait()


def lay_out(at, pieces):
    return pl.pallas_call(
        lay_kernel,
        in_specs=[scalar()] + anywhere(8),
        out_specs=pl.BlockSpec(memory_space=pl.ANY),
        scratch_shapes=[pltpu.SemaphoreType.DMA((8,))],
        out_shape=jax.ShapeDtypeStruct((64, 16384), BF),
        compiler_params=params(),
    )(at, *pieces)


def body(points, means, log_weights, inv_var):
    x, c, y, z = (lax.axis_index(a) for a in "xcyz")
    at = jnp.stack([x, c, y]).astype(jnp.int32)

    far = shift(points, "y", 2)
    means_f = means.astype(F32)
    scaled = (means_f * inv_var[None, :]).astype(BF)
    scaled = pltpu.with_memory_space_constraint(scaled, pltpu.HBM)
    half_norm = 0.5 * jnp.sum(means_f * means_f * inv_var[None, :], axis=1)
    bias = log_weights - half_norm
    bias_row, bias_col = bias.reshape(1, 2048), bias[:, None]

    own = gather_x(at, points, (bias_row, bias_col, far))
    other = shift(own, "c", 1)
    before = shift(own, "y", 1)
    after = shift(own, "y", -1)
    score, share = scores(at, own, other, scaled, bias_row)

    shares = lax.all_to_all(share, ("y", "x", "c"), split_axis=0, concat_axis=0, tiled=True)
    far = gather_x(at, far, (shares,))
    shares = shares.reshape(4, 8, 4, 128)
    pieces = [own, other]
    for mine in (before, after, far):
        pieces += [mine, shift(mine, "c", 1)]

    sums, counts = partial_sums(at, shares, scaled, bias_col, pieces)
    sums = lax.all_to_all(sums, ("y", "z"), split_axis=0, concat_axis=0, tiled=True)

    *blocks, counts = responsibilities(at, shares, counts, score)
    theirs = [swap(b, "c", 1) for b in blocks[:4]]
    held = theirs + list(blocks[4:])
    held = [shift(b, "x", j % 4) if j % 4 else b for j, b in enumerate(held)]
    resp_rows = lay_out(at, held)

    counts = hand_on(counts, *theirs, held[5])
    counts = sum([shift(counts, "z", i) for i in range(1, 8)], counts)
    counts = hand_on(counts, held[1], held[3], held[6], held[7])
    counts = sum([shift(counts, "y", i) for i in range(1, 4)], counts)
    counts = counts.reshape(2048)

    sums = jnp.sum(sums.reshape(4, 8, 32, 512).astype(F32), axis=1)
    sums = sums.transpose(1, 0, 2).reshape(32, 2048)
    mean_cols = lax.dynamic_slice_in_dim(means, (y * 8 + z) * 32, 32, 1).T.astype(F32)
    new_means_t = (sums + mean_cols) / (counts[None, :] + 1.0)

    lse = joined(lax.dynamic_index_in_dim(shares, y, 0, keepdims=False)).reshape(8, 64)
    own_lse = lax.dynamic_index_in_dim(lse, c * 4 + x, 0, keepdims=False)
    points_f = points.astype(F32)
    const_term = 0.5 * jnp.sum(jnp.log(inv_var)) - 0.5 * 1024 * math.log(2.0 * math.pi)
    loglik = own_lse - 0.5 * jnp.sum(points_f * points_f * inv_var[None, :], axis=1) + const_term
    return (resp_rows, counts, new_means_t, loglik)


def solution(mesh):
    axes = ("y", "z", "x", "c")
    mesh = Mesh(mesh.devices.reshape(4, 8, 4, 2), axes)
    comp, pt = ("x", "c"), ("y", "z")
    return jax.shard_map(
        body,
        mesh=mesh,
        in_specs=(P(axes, None), P(comp, None), P(comp), P()),
        out_specs=(P(axes, None), P(comp), P(pt, comp), P(axes)),
        check_vma=False,
    )
```

time: 166 us -> 129 us (0.78)
  the two profiles are of different devices: /device:TPU:32 before, /device:TPU:2 now
where the time goes in v2:
time: 129 us; the launch traced here: 128 us
  starting transfers between devices  62.4 us (48%)
  waiting for transfers between devices  25.4 us (20%)
  Pallas kernels  25.1 us (19%)
  other arithmetic  9.83 us (8%)
  local copies, waits for them, and re-layouts  3.74 us (3%)
  between operations  1.52 us (1%)
    ppermute x29, starting transfers between devices, shift(): return lax.ppermute(value, axis, [(i, (i + step) % n) for i in range(n)])  46.6 us
    ppermute x29, waiting for transfers between devices, shift(): return lax.ppermute(value, axis, [(i, (i + step) % n) for i in range(n)])  19.7 us
    pallas_call x1, Pallas kernels, partial_sums(): pl.pallas_call(sums_kernel, grid_spec=pltpu.PrefetchScalarGridSpec(num_sc...  11.3 us
    all_to_all x1, starting transfers between devices, body(): lax.all_to_all(sums, ('y', 'z'), split_axis=0, concat_axis=0, tiled=True)  9.7 us
    pallas_call x1, Pallas kernels, scores(): pl.pallas_call(score_kernel, grid=(2048 // width,), out_shape=(pltpu.HBM(...  7.2 us
    convert_element_type x1, other arithmetic, body(): scaled = (means_f * inv_var[None, :]).astype(BF)  5.69 us
    all_to_all x1, waiting for transfers between devices, body(): lax.all_to_all(share, ('y', 'x', 'c'), split_axis=0, concat_axis=0, tiled...  5.66 us
    all_to_all x1, starting transfers between devices, body(): lax.all_to_all(share, ('y', 'x', 'c'), split_axis=0, concat_axis=0, tiled...  4.99 us
  transfers between devices with their start and end apart: 35, of which 8 were waited for; matrix products, arithmetic and copies ran while one was open for 9% of the time, Pallas kernels for 10%

profile of v2, /device:TPU:2, one launch (start us, length us, event | category | flops | bytes accessed | tf_op | source)
XLA Modules:
  0.0 128.0 jit_solution(1079414871590736566)
XLA Ops:
  0.7 3.3 %collective-permute-start.3 = (bf16[64,1024]{1,0:T(8,128)(2,1)}, bf16[64,1024]{1,0:T(8,128)(2,1)S(1)}, u32[]{:S(2)}, u32[]{:S(2)}) collective-permute-start(bf16[64,1024]{1,0:T(8,128)(2,1)} %own.1), channel_id=1, source_target_pairs={{0,128},{64,192},{128,0},{192,64},{1,129},{65,193},{129,1},{193,65... | collective-permute-start | bytes 393224 | tf_op jit(solution)/shard_map/ppermute | solution.py:21
  6.0 2.1 %collective-permute-start.2 = (bf16[64,1024]{1,0:T(8,128)(2,1)}, bf16[64,1024]{1,0:T(8,128)(2,1)S(1)}, u32[]{:S(2)}, u32[]{:S(2)}) collective-permute-start(bf16[64,1024]{1,0:T(8,128)(2,1)} %own.1), channel_id=1, source_target_pairs={{0,4},{2,6},{4,0},{6,2},{1,5},{3,7},{5,1},{7,3},{8,12},{10,14},{12... | collective-permute-start | bytes 393224 | tf_op jit(solution)/shard_map/ppermute | solution.py:21
  8.1 5.7 %fusion.2 = (bf16[2048,1024]{1,0:T(8,128)(2,1)}, f32[2048]{0:T(1024)S(1)}) fusion(bf16[2048,1024]{1,0:T(8,128)(2,1)} %param.5, f32[1024]{0:T(1024)} %param.7), kind=kLoop, calls=%fused_computation.4 | loop fusion | flops 12580864 | bytes 8400896 | tf_op jit(solution)/shard_map/convert_element_type | solution.py:302
  15.7 2.6 %collective-permute-start.7 = (bf16[256,1024]{1,0:T(8,128)(2,1)S(1)}, bf16[256,1024]{1,0:T(8,128)(2,1)}, u32[]{:S(2)}, u32[]{:S(2)}) collective-permute-start(bf16[256,1024]{1,0:T(8,128)(2,1)S(1)} %shard_map.75.own.refs_0_), channel_id=1, source_target_pairs={{0,192},{64,0},{128,64},{192,128},{1,193},{65,1},{129,65},{193,129... | collective-permute-start | bytes 1572872 | tf_op jit(solution)/shard_map/ppermute | solution.py:21
  22.3 7.2 %shard_map.76 = (f32[512,2048]{1,0:T(8,128)}, f32[32,4,128]{2,1,0:T(4,128)}) custom-call(s32[3]{0:T(128)S(1)} %pad_add_fusion.at, bf16[256,1024]{1,0:T(8,128)(2,1)S(1)} %shard_map.75.own.refs_0_, bf16[256,1024]{1,0:T(8,128)(2,1)S(1)} %collective-permute-done.4.other.refs_1_, bf16[2048,1024]{1,0:T(8,128)(2,1)} %get-tuple-element.32.scaled, f32[1,2048]{1,0:T(1,128)S(1)} %bitcast.38), custom_call_target="tpu_custom_call" | custom-call | flops 2147483648 | bytes 9437184 | tf_op jit(solution)/shard_map/pallas_call | solution.py:126
  29.5 5.0 %all-to-all-start = ((f32[32,4,128]{2,1,0:T(4,128)}), f32[32,4,128]{2,1,0:T(4,128)S(1)}, u32[]{:S(2)}, u32[]{:S(2)}) async-start(f32[32,4,128]{2,1,0:T(4,128)} %get-tuple-element.17), calls=%async_computation | async-start | bytes 131072 | tf_op jit(solution)/shard_map/all_to_all | solution.py:314
  35.1 5.7 %all-to-all-done.refs_0_ = f32[32,4,128]{2,1,0:T(4,128)S(1)} async-done(((f32[32,4,128]{2,1,0:T(4,128)}), f32[32,4,128]{2,1,0:T(4,128)S(1)}, u32[]{:S(2)}, u32[]{:S(2)}) %all-to-all-start) | async-done | bytes 65568 | tf_op jit(solution)/shard_map/all_to_all | solution.py:314
  41.8 1.8 %collective-permute-done.12.refs_7_ = bf16[256,1024]{1,0:T(8,128)(2,1)S(1)} collective-permute-done((bf16[256,1024]{1,0:T(8,128)(2,1)S(1)}, bf16[256,1024]{1,0:T(8,128)(2,1)S(1)}, u32[]{:S(2)}, u32[]{:S(2)}) %collective-permute-start.12) | collective-permute-done | bytes 524320 | tf_op jit(solution)/shard_map/ppermute | solution.py:21
  43.6 11.3 %shard_map.78 = (bf16[1024,512]{1,0:T(8,128)(2,1)}, f32[16,128]{1,0:T(8,128)S(1)}) custom-call(s32[3]{0:T(128)S(1)} %pad_add_fusion.at, f32[4,8,4,128]{3,2,1,0:T(4,128)S(1)} %bitcast.32, bf16[2048,1024]{1,0:T(8,128)(2,1)} %get-tuple-element.32.scaled, f32[2048,1]{1,0:T(8,128)S(1)} %copy.15.refs_1_.bias, bf16[256,1024]{1,0:T(8,128)(2,1)S(1)} %shard_map.75.own.refs_0_, ...), custom_call_target="tpu_custom_call" | custom-call | flops 4294967296 | bytes 8388608 | tf_op jit(solution)/shard_map/pallas_call | solution.py:197
  54.8 9.7 %all-to-all-start.1 = ((bf16[32,32,512]{2,1,0:T(8,128)(2,1)}), bf16[32,32,512]{2,1,0:T(8,128)(2,1)}, u32[]{:S(2)}, u32[]{:S(2)}) async-start(bf16[32,32,512]{2,1,0:T(8,128)(2,1)} %bitcast.40), calls=%async_computation.1 | async-start | bytes 2097152 | tf_op jit(solution)/shard_map/all_to_all | solution.py:322
  64.6 3.6 %shard_map.79 = (bf16[64,2048]{1,0:T(8,128)(2,1)}, bf16[64,2048]{1,0:T(8,128)(2,1)}, bf16[64,2048]{1,0:T(8,128)(2,1)S(1)}, bf16[64,2048]{1,0:T(8,128)(2,1)S(1)},...) custom-call(s32[3]{0:T(128)S(1)} %pad_add_fusion.at, ...), custom_call_target="tpu_custom_call" | custom-call | flops 2097152 | bytes 6291456 | tf_op jit(solution)/shard_map/pallas_call | solution.py:254
  69.8 2.0 %constant_dynamic-slice_fusion.1 = bf16[2048,32]{1,0:T(8,128)(2,1)} fusion(bf16[2048,1024]{1,0:T(8,128)(2,1)} %param.5, s32[]{:T(128)S(6)} %select_n.11), kind=kLoop, calls=%fused_computation.20 | loop fusion | bytes 262148 | tf_op jit(solution)/shard_map/dynamic_slice | solution.py:338
  71.9 5.6 %collective-permute-done.20.refs_5_.refs_4_ = bf16[64,2048]{1,0:T(8,128)(2,1)S(1)} collective-permute-done((bf16[64,2048]{1,0:T(8,128)(2,1)S(1)}, bf16[64,2048]{1,0:T(8,128)(2,1)S(1)}, u32[]{:S(2)}, u32[]{:S(2)}) %collective-permute-start.20) | collective-permute-done | bytes 262176 | tf_op jit(solution)/shard_map/ppermute | solution.py:21
  77.6 1.7 %collective-permute-start.23 = (f32[16,128]{1,0:T(8,128)S(1)}, f32[16,128]{1,0:T(8,128)S(1)}, u32[]{:S(2)}, u32[]{:S(2)}) collective-permute-start(f32[16,128]{1,0:T(8,128)S(1)} %shard_map.81), channel_id=1, source_target_pairs={{0,8},{8,16},{16,24},{24,32},{32,40},{40,48},{48,56},{56,0},{1,9},... | collective-permute-start | bytes 24584 | tf_op jit(solution)/shard_map/ppermute | solution.py:21
  81.8 2.4 %collective-permute-start.24 = (f32[16,128]{1,0:T(8,128)S(1)}, f32[16,128]{1,0:T(8,128)S(1)}, u32[]{:S(2)}, u32[]{:S(2)}) collective-permute-start(f32[16,128]{1,0:T(8,128)S(1)} %shard_map.81), channel_id=1, source_target_pairs={{0,16},{8,24},{16,32},{24,40},{32,48},{40,56},{48,0},{56,8},{1,17}... | collective-permute-start | bytes 24584 | tf_op jit(solution)/shard_map/ppermute | solution.py:21
  84.2 2.7 %collective-permute-start.25 = (f32[16,128]{1,0:T(8,128)S(1)}, f32[16,128]{1,0:T(8,128)S(1)}, u32[]{:S(2)}, u32[]{:S(2)}) collective-permute-start(f32[16,128]{1,0:T(8,128)S(1)} %shard_map.81), channel_id=1, source_target_pairs={{0,24},{8,32},{16,40},{24,48},{32,56},{40,0},{48,8},{56,16},{1,25}... | collective-permute-start | bytes 24584 | tf_op jit(solution)/shard_map/ppermute | solution.py:21
  86.9 2.4 %collective-permute-start.26 = (f32[16,128]{1,0:T(8,128)S(1)}, f32[16,128]{1,0:T(8,128)S(1)}, u32[]{:S(2)}, u32[]{:S(2)}) collective-permute-start(f32[16,128]{1,0:T(8,128)S(1)} %shard_map.81), channel_id=1, source_target_pairs={{0,32},{8,40},{16,48},{24,56},{32,0},{40,8},{48,16},{56,24},{1,33}... | collective-permute-start | bytes 24584 | tf_op jit(solution)/shard_map/ppermute | solution.py:21
  89.3 2.7 %collective-permute-start.27 = (f32[16,128]{1,0:T(8,128)S(1)}, f32[16,128]{1,0:T(8,128)S(1)}, u32[]{:S(2)}, u32[]{:S(2)}) collective-permute-start(f32[16,128]{1,0:T(8,128)S(1)} %shard_map.81), channel_id=1, source_target_pairs={{0,40},{8,48},{16,56},{24,0},{32,8},{40,16},{48,24},{56,32},{1,41}... | collective-permute-start | bytes 24584 | tf_op jit(solution)/shard_map/ppermute | solution.py:21
  91.9 3.6 %collective-permute-start.28 = (f32[16,128]{1,0:T(8,128)S(1)}, f32[16,128]{1,0:T(8,128)S(1)}, u32[]{:S(2)}, u32[]{:S(2)}) collective-permute-start(f32[16,128]{1,0:T(8,128)S(1)} %shard_map.81), channel_id=1, source_target_pairs={{0,48},{8,56},{16,0},{24,8},{32,16},{40,24},{48,32},{56,40},{1,49}... | collective-permute-start | bytes 24584 | tf_op jit(solution)/shard_map/ppermute | solution.py:21
  102.0 2.8 %collective-permute-start.17 = (bf16[64,2048]{1,0:T(8,128)(2,1)S(1)}, bf16[64,2048]{1,0:T(8,128)(2,1)S(1)}, u32[]{:S(2)}, u32[]{:S(2)}) collective-permute-start(bf16[64,2048]{1,0:T(8,128)(2,1)S(1)} %collective-permute-done.16.refs_2_), channel_id=1, source_target_pairs={{0,4},{2,6},{4,0},{6,2},{1,5},{3,7},{5,1},{7,3},{8,12},{10,14},{12... | collective-permute-start | bytes 786440 | tf_op jit(solution)/shard_map/ppermute | solution.py:21
  106.4 3.1 %collective-permute-done.22.refs_7_.refs_3_ = bf16[64,2048]{1,0:T(8,128)(2,1)S(1)} collective-permute-done((bf16[64,2048]{1,0:T(8,128)(2,1)S(1)}, bf16[64,2048]{1,0:T(8,128)(2,1)S(1)}, u32[]{:S(2)}, u32[]{:S(2)}) %collective-permute-start.22) | collective-permute-done | bytes 262176 | tf_op jit(solution)/shard_map/ppermute | solution.py:21
  110.8 6.1 %collective-permute-done.19.refs_3_.refs_1_ = bf16[64,2048]{1,0:T(8,128)(2,1)S(1)} collective-permute-done((bf16[64,2048]{1,0:T(8,128)(2,1)S(1)}, bf16[64,2048]{1,0:T(8,128)(2,1)S(1)}, u32[]{:S(2)}, u32[]{:S(2)}) %collective-permute-start.19) | collective-permute-done | bytes 262176 | tf_op jit(solution)/shard_map/ppermute | solution.py:21
  118.6 2.7 %collective-permute-start.31 = (f32[16,128]{1,0:T(8,128)S(1)}, f32[16,128]{1,0:T(8,128)S(1)}, u32[]{:S(2)}, u32[]{:S(2)}) collective-permute-start(f32[16,128]{1,0:T(8,128)S(1)} %shard_map.82), channel_id=1, source_target_pairs={{0,128},{64,192},{128,0},{192,64},{1,129},{65,193},{129,1},{193,65... | collective-permute-start | bytes 24584 | tf_op jit(solution)/shard_map/ppermute | solution.py:21
  123.2 1.9 %shard_map.80 = bf16[64,16384]{1,0:T(8,128)(2,1)} custom-call(s32[3]{0:T(128)S(1)} %pad_add_fusion.at, bf16[64,2048]{1,0:T(8,128)(2,1)S(1)} %collective-permute-done.13.refs_0_, bf16[64,2048]{1,0:T(8,128)(2,1)S(1)} %collective-permute-done.15.refs_1_.refs_0_, bf16[64,2048]{1,0:T(8,128)(2,1)S(1)} %collective-permute-done.17.refs_2_, ...), custom_call_target="tpu_custom_call" | custom-call | tf_op jit(solution)/shard_map/pallas_call | solution.py:286
  (78 shorter events, 28.8 us)
Async XLA Ops:
  0.7 13.6 %collective-permute-start.3 = (bf16[64,1024]{1,0:T(8,128)(2,1)}, bf16[64,1024]{1,0:T(8,128)(2,1)S(1)}, u32[]{:S(2)}, u32[]{:S(2)}) collective-permute-start(bf16[64,1024]{1,0:T(8,128)(2,1)} %own.1), channel_id=1, source_target_pairs={{0,128},{64,192},{128,0},{192,64},{1,129},{65,193},{129,1},{193,65... | collective-permute-start | bytes 393224 | tf_op jit(solution)/shard_map/ppermute | solution.py:21
  3.9 10.3 %collective-permute-start = (bf16[64,1024]{1,0:T(8,128)(2,1)}, bf16[64,1024]{1,0:T(8,128)(2,1)S(1)}, u32[]{:S(2)}, u32[]{:S(2)}) collective-permute-start(bf16[64,1024]{1,0:T(8,128)(2,1)} %own.1), channel_id=1, source_target_pairs={{0,2},{2,4},{4,6},{6,0},{1,3},{3,5},{5,7},{7,1},{8,10},{10,12},{12... | collective-permute-start | bytes 393224 | tf_op jit(solution)/shard_map/ppermute | solution.py:21
  5.4 8.8 %collective-permute-start.1 = (bf16[64,1024]{1,0:T(8,128)(2,1)}, bf16[64,1024]{1,0:T(8,128)(2,1)S(1)}, u32[]{:S(2)}, u32[]{:S(2)}) collective-permute-start(bf16[64,1024]{1,0:T(8,128)(2,1)} %own.1), channel_id=1, source_target_pairs={{0,6},{2,0},{4,2},{6,4},{1,7},{3,1},{5,3},{7,5},{8,14},{10,8},{12,... | collective-permute-start | bytes 393224 | tf_op jit(solution)/shard_map/ppermute | solution.py:21
  6.0 8.3 %collective-permute-start.2 = (bf16[64,1024]{1,0:T(8,128)(2,1)}, bf16[64,1024]{1,0:T(8,128)(2,1)S(1)}, u32[]{:S(2)}, u32[]{:S(2)}) collective-permute-start(bf16[64,1024]{1,0:T(8,128)(2,1)} %own.1), channel_id=1, source_target_pairs={{0,4},{2,6},{4,0},{6,2},{1,5},{3,7},{5,1},{7,3},{8,12},{10,14},{12... | collective-permute-start | bytes 393224 | tf_op jit(solution)/shard_map/ppermute | solution.py:21
  15.0 19.6 %collective-permute-start.5 = (bf16[256,1024]{1,0:T(8,128)(2,1)S(1)}, bf16[256,1024]{1,0:T(8,128)(2,1)S(1)}, u32[]{:S(2)}, u32[]{:S(2)}) collective-permute-start(bf16[256,1024]{1,0:T(8,128)(2,1)S(1)} %shard_map.75.own.refs_0_), channel_id=1, source_target_pairs={{0,64},{64,128},{128,192},{192,0},{1,65},{65,129},{129,193},{193,1... | collective-permute-start | bytes 1572872 | tf_op jit(solution)/shard_map/ppermute | solution.py:21
  15.7 19.0 %collective-permute-start.7 = (bf16[256,1024]{1,0:T(8,128)(2,1)S(1)}, bf16[256,1024]{1,0:T(8,128)(2,1)}, u32[]{:S(2)}, u32[]{:S(2)}) collective-permute-start(bf16[256,1024]{1,0:T(8,128)(2,1)S(1)} %shard_map.75.own.refs_0_), channel_id=1, source_target_pairs={{0,192},{64,0},{128,64},{192,128},{1,193},{65,1},{129,65},{193,129... | collective-permute-start | bytes 1572872 | tf_op jit(solution)/shard_map/ppermute | solution.py:21
  18.3 16.8 %collective-permute-start.10 = (bf16[64,1024]{1,0:T(8,128)(2,1)S(1)}, bf16[64,1024]{1,0:T(8,128)(2,1)S(1)}, u32[]{:S(2)}, u32[]{:S(2)}) collective-permute-start(bf16[64,1024]{1,0:T(8,128)(2,1)S(1)} %collective-permute-done.3.refs_2_.own), channel_id=1, source_target_pairs={{0,6},{2,0},{4,2},{6,4},{1,7},{3,1},{5,3},{7,5},{8,14},{10,8},{12,... | collective-permute-start | bytes 393224 | tf_op jit(solution)/shard_map/ppermute | solution.py:21
  19.7 15.4 %collective-permute-start.11 = (bf16[64,1024]{1,0:T(8,128)(2,1)S(1)}, bf16[64,1024]{1,0:T(8,128)(2,1)S(1)}, u32[]{:S(2)}, u32[]{:S(2)}) collective-permute-start(bf16[64,1024]{1,0:T(8,128)(2,1)S(1)} %collective-permute-done.3.refs_2_.own), channel_id=1, source_target_pairs={{0,4},{2,6},{4,0},{6,2},{1,5},{3,7},{5,1},{7,3},{8,12},{10,14},{12... | collective-permute-start | bytes 393224 | tf_op jit(solution)/shard_map/ppermute | solution.py:21
  20.8 14.3 %collective-permute-start.9 = (bf16[64,1024]{1,0:T(8,128)(2,1)S(1)}, bf16[64,1024]{1,0:T(8,128)(2,1)S(1)}, u32[]{:S(2)}, u32[]{:S(2)}) collective-permute-start(bf16[64,1024]{1,0:T(8,128)(2,1)S(1)} %collective-permute-done.3.refs_2_.own), channel_id=1, source_target_pairs={{0,2},{2,4},{4,6},{6,0},{1,3},{3,5},{5,7},{7,1},{8,10},{10,12},{12... | collective-permute-start | bytes 393224 | tf_op jit(solution)/shard_map/ppermute | solution.py:21
  29.5 11.3 %all-to-all-start = ((f32[32,4,128]{2,1,0:T(4,128)}), f32[32,4,128]{2,1,0:T(4,128)S(1)}, u32[]{:S(2)}, u32[]{:S(2)}) async-start(f32[32,4,128]{2,1,0:T(4,128)} %get-tuple-element.17), calls=%async_computation | async-start | bytes 131072 | tf_op jit(solution)/shard_map/all_to_all | solution.py:314
  54.8 71.0 %all-to-all-start.1 = ((bf16[32,32,512]{2,1,0:T(8,128)(2,1)}), bf16[32,32,512]{2,1,0:T(8,128)(2,1)}, u32[]{:S(2)}, u32[]{:S(2)}) async-start(bf16[32,32,512]{2,1,0:T(8,128)(2,1)} %bitcast.40), calls=%async_computation.1 | async-start | bytes 2097152 | tf_op jit(solution)/shard_map/all_to_all | solution.py:322
  69.3 8.3 %collective-permute-start.20 = (bf16[64,2048]{1,0:T(8,128)(2,1)S(1)}, bf16[64,2048]{1,0:T(8,128)(2,1)S(1)}, u32[]{:S(2)}, u32[]{:S(2)}) collective-permute-start(bf16[64,2048]{1,0:T(8,128)(2,1)S(1)} %get-tuple-element.25), channel_id=1, source_target_pairs={{0,2},{2,4},{4,6},{6,0},{1,3},{3,5},{5,7},{7,1},{8,10},{10,12},{12... | collective-permute-start | bytes 786440 | tf_op jit(solution)/shard_map/ppermute | solution.py:21
  77.6 14.4 %collective-permute-start.23 = (f32[16,128]{1,0:T(8,128)S(1)}, f32[16,128]{1,0:T(8,128)S(1)}, u32[]{:S(2)}, u32[]{:S(2)}) collective-permute-start(f32[16,128]{1,0:T(8,128)S(1)} %shard_map.81), channel_id=1, source_target_pairs={{0,8},{8,16},{16,24},{24,32},{32,40},{40,48},{48,56},{56,0},{1,9},... | collective-permute-start | bytes 24584 | tf_op jit(solution)/shard_map/ppermute | solution.py:21
  81.8 13.8 %collective-permute-start.24 = (f32[16,128]{1,0:T(8,128)S(1)}, f32[16,128]{1,0:T(8,128)S(1)}, u32[]{:S(2)}, u32[]{:S(2)}) collective-permute-start(f32[16,128]{1,0:T(8,128)S(1)} %shard_map.81), channel_id=1, source_target_pairs={{0,16},{8,24},{16,32},{24,40},{32,48},{40,56},{48,0},{56,8},{1,17}... | collective-permute-start | bytes 24584 | tf_op jit(solution)/shard_map/ppermute | solution.py:21
  84.2 12.9 %collective-permute-start.25 = (f32[16,128]{1,0:T(8,128)S(1)}, f32[16,128]{1,0:T(8,128)S(1)}, u32[]{:S(2)}, u32[]{:S(2)}) collective-permute-start(f32[16,128]{1,0:T(8,128)S(1)} %shard_map.81), channel_id=1, source_target_pairs={{0,24},{8,32},{16,40},{24,48},{32,56},{40,0},{48,8},{56,16},{1,25}... | collective-permute-start | bytes 24584 | tf_op jit(solution)/shard_map/ppermute | solution.py:21
  86.9 11.5 %collective-permute-start.26 = (f32[16,128]{1,0:T(8,128)S(1)}, f32[16,128]{1,0:T(8,128)S(1)}, u32[]{:S(2)}, u32[]{:S(2)}) collective-permute-start(f32[16,128]{1,0:T(8,128)S(1)} %shard_map.81), channel_id=1, source_target_pairs={{0,32},{8,40},{16,48},{24,56},{32,0},{40,8},{48,16},{56,24},{1,33}... | collective-permute-start | bytes 24584 | tf_op jit(solution)/shard_map/ppermute | solution.py:21
  89.3 10.6 %collective-permute-start.27 = (f32[16,128]{1,0:T(8,128)S(1)}, f32[16,128]{1,0:T(8,128)S(1)}, u32[]{:S(2)}, u32[]{:S(2)}) collective-permute-start(f32[16,128]{1,0:T(8,128)S(1)} %shard_map.81), channel_id=1, source_target_pairs={{0,40},{8,48},{16,56},{24,0},{32,8},{40,16},{48,24},{56,32},{1,41}... | collective-permute-start | bytes 24584 | tf_op jit(solution)/shard_map/ppermute | solution.py:21
  91.9 9.3 %collective-permute-start.28 = (f32[16,128]{1,0:T(8,128)S(1)}, f32[16,128]{1,0:T(8,128)S(1)}, u32[]{:S(2)}, u32[]{:S(2)}) collective-permute-start(f32[16,128]{1,0:T(8,128)S(1)} %shard_map.81), channel_id=1, source_target_pairs={{0,48},{8,56},{16,0},{24,8},{32,16},{40,24},{48,32},{56,40},{1,49}... | collective-permute-start | bytes 24584 | tf_op jit(solution)/shard_map/ppermute | solution.py:21
  95.5 10.8 %collective-permute-start.21 = (bf16[64,2048]{1,0:T(8,128)(2,1)S(1)}, bf16[64,2048]{1,0:T(8,128)(2,1)S(1)}, u32[]{:S(2)}, u32[]{:S(2)}) collective-permute-start(bf16[64,2048]{1,0:T(8,128)(2,1)S(1)} %get-tuple-element.26), channel_id=1, source_target_pairs={{0,4},{2,6},{4,0},{6,2},{1,5},{3,7},{5,1},{7,3},{8,12},{10,14},{12... | collective-permute-start | bytes 786440 | tf_op jit(solution)/shard_map/ppermute | solution.py:21
  97.1 12.4 %collective-permute-start.22 = (bf16[64,2048]{1,0:T(8,128)(2,1)S(1)}, bf16[64,2048]{1,0:T(8,128)(2,1)S(1)}, u32[]{:S(2)}, u32[]{:S(2)}) collective-permute-start(bf16[64,2048]{1,0:T(8,128)(2,1)S(1)} %get-tuple-element.27), channel_id=1, source_target_pairs={{0,6},{2,0},{4,2},{6,4},{1,7},{3,1},{5,3},{7,5},{8,14},{10,8},{12,... | collective-permute-start | bytes 786440 | tf_op jit(solution)/shard_map/ppermute | solution.py:21
  99.8 11.0 %collective-permute-start.15 = (bf16[64,2048]{1,0:T(8,128)(2,1)S(1)}, bf16[64,2048]{1,0:T(8,128)(2,1)S(1)}, u32[]{:S(2)}, u32[]{:S(2)}) collective-permute-start(bf16[64,2048]{1,0:T(8,128)(2,1)S(1)} %collective-permute-done.14.refs_1_), channel_id=1, source_target_pairs={{0,2},{2,4},{4,6},{6,0},{1,3},{3,5},{5,7},{7,1},{8,10},{10,12},{12... | collective-permute-start | bytes 786440 | tf_op jit(solution)/shard_map/ppermute | solution.py:21
  101.3 15.7 %collective-permute-start.19 = (bf16[64,2048]{1,0:T(8,128)(2,1)S(1)}, bf16[64,2048]{1,0:T(8,128)(2,1)S(1)}, u32[]{:S(2)}, u32[]{:S(2)}) collective-permute-start(bf16[64,2048]{1,0:T(8,128)(2,1)S(1)} %collective-permute-done.18.refs_3_), channel_id=1, source_target_pairs={{0,6},{2,0},{4,2},{6,4},{1,7},{3,1},{5,3},{7,5},{8,14},{10,8},{12,... | collective-permute-start | bytes 786440 | tf_op jit(solution)/shard_map/ppermute | solution.py:21
  102.0 21.2 %collective-permute-start.17 = (bf16[64,2048]{1,0:T(8,128)(2,1)S(1)}, bf16[64,2048]{1,0:T(8,128)(2,1)S(1)}, u32[]{:S(2)}, u32[]{:S(2)}) collective-permute-start(bf16[64,2048]{1,0:T(8,128)(2,1)S(1)} %collective-permute-done.16.refs_2_), channel_id=1, source_target_pairs={{0,4},{2,6},{4,0},{6,2},{1,5},{3,7},{5,1},{7,3},{8,12},{10,14},{12... | collective-permute-start | bytes 786440 | tf_op jit(solution)/shard_map/ppermute | solution.py:21
  117.0 8.2 %collective-permute-start.30 = (f32[16,128]{1,0:T(8,128)S(1)}, f32[16,128]{1,0:T(8,128)S(1)}, u32[]{:S(2)}, u32[]{:S(2)}) collective-permute-start(f32[16,128]{1,0:T(8,128)S(1)} %shard_map.82), channel_id=1, source_target_pairs={{0,64},{64,128},{128,192},{192,0},{1,65},{65,129},{129,193},{193,1... | collective-permute-start | bytes 24584 | tf_op jit(solution)/shard_map/ppermute | solution.py:21
  (14 other events, 91.8 us)

commit v3 on v2

--- a/solution.py
+++ b/solution.py
@@ -44,20 +44,6 @@
 
 def hbm(n=1):
     return [pl.BlockSpec(memory_space=pltpu.HBM)] * n
-
-
-def hand_on_kernel(value, *refs):
-    refs[-1][...] = value[...]
-
-
-def hand_on(value, *first):
-    return pl.pallas_call(
-        hand_on_kernel,
-        out_shape=jax.ShapeDtypeStruct(value.shape, value.dtype),
-        in_specs=[whole()] + anywhere(len(first)),
-        out_specs=whole(),
-        compiler_params=params(),
-    )(value, *first)
 
 
 def place_kernel(at, own, before, after, far, *refs):
@@ -156,8 +142,8 @@
 
 def sums_kernel(at, shares, scaled, bias, *refs):
     pieces = refs[:8]
-    sums, counts = refs[8:10]
-    rows, weights, lse, sems = refs[10:]
+    sums = refs[8]
+    rows, weights, lse, sems = refs[9:]
     copies = [
         pltpu.make_async_copy(piece, rows.at[pl.ds(i * 256, 256)], sems.at[i])
         for i, piece in enumerate(pieces)
@@ -182,15 +168,18 @@
         weights[:, cut] = weight
         count = count + weight[:, :128].astype(F32) + weight[:, 128:].astype(F32)
     count = jnp.sum(count, axis=1, keepdims=True)
-    counts[...] = jnp.zeros_like(counts)
-    for b in range(4):
-        counts[pl.ds(y * 4 + b, 1), :] = line(count[b * 128 : b * 128 + 128])
+    count = jnp.concatenate([line(count[b : b + 128]) for b in range(0, 512, 128)], axis=1)
+    high = count.astype(BF).astype(F32)
+    tail = jnp.concatenate([high, count - high, jnp.zeros((6, 512), F32)], axis=0).astype(BF)
+    sums[:, 32:40, :] = jnp.broadcast_to(tail[None], (32, 8, 512))
     for j in range(4):
-        cut = slice(j * 256, j * 256 + 256)
         block = lax.dot_general(
-            weights[...], rows[:, cut], (((1,), (0,)), ((), ())), preferred_element_type=F32
-        )
-        sums[cut, :] = jnp.transpose(block.astype(BF))
+            weights[...],
+            rows[:, j * 256 : j * 256 + 256],
+            (((1,), (0,)), ((), ())),
+            preferred_element_type=F32,
+        )
+        sums[j * 8 : j * 8 + 8, 0:32, :] = jnp.transpose(block.astype(BF)).reshape(8, 32, 512)
 
 
 def partial_sums(at, shares, scaled, bias_col, pieces):
@@ -205,10 +194,7 @@
                 pl.BlockSpec((512, 1), lambda i, at: (at[2], 0)),
             ]
             + anywhere(8),
-            out_specs=(
-                pl.BlockSpec((1024, 512), lambda i, at: (0, 0)),
-                pl.BlockSpec((16, 128), lambda i, at: (0, 0)),
-            ),
+            out_specs=pl.BlockSpec((32, 40, 512), lambda i, at: (0, 0, 0)),
             scratch_shapes=[
                 VMEM((2048, 1024), BF),
                 VMEM((512, 2048), BF),
@@ -216,10 +202,7 @@
                 pltpu.SemaphoreType.DMA((8,)),
             ],
         ),
-        out_shape=(
-            pltpu.HBM((1024, 512), BF),
-            jax.ShapeDtypeStruct((16, 128), F32),
-        ),
+        out_shape=pltpu.HBM((32, 40, 512), BF),
         compiler_params=params(),
         cost_estimate=pl.CostEstimate(
             flops=4 * 512 * 2048 * 1024, bytes_accessed=8 << 20, transcendentals=1 << 20
@@ -227,8 +210,9 @@
     )(at, shares, scaled, bias_col, *pieces)
 
 
-def resp_kernel(at, shares, counts, score, *refs):
-    outs, passed, norm, held, sems = refs[:8], refs[8], refs[9], refs[10], refs[11]
+def resp_kernel(at, shares, score, first, *refs):
+    del first
+    outs, norm, held, sems = refs[:8], refs[8], refs[9], refs[10]
     x, c, y = at[0], at[1], at[2]
     copies = []
     for j in range(8):
@@ -239,7 +223,6 @@
         )
     for _, copy in copies:
         copy.start()
-    passed[...] = counts[...]
     lse = joined(shares[y])
     for b in range(4):
         norm[b * 128 : b * 128 + 128, :] = jnp.transpose(
@@ -250,21 +233,20 @@
         outs[j][...] = jnp.exp(held[j] - norm[pl.ds(start, 64), 0:1]).astype(BF)
 
 
-def responsibilities(at, shares, counts, score):
+def responsibilities(at, shares, score, first):
     return pl.pallas_call(
         resp_kernel,
-        in_specs=[scalar(), whole(), whole()] + hbm(),
-        out_specs=[whole()] * 9,
+        in_specs=[scalar(), whole()] + hbm(2),
+        out_specs=[whole()] * 8,
         scratch_shapes=[
             VMEM((512, 128), F32),
             VMEM((8, 64, 2048), F32),
             pltpu.SemaphoreType.DMA((8,)),
         ],
-        out_shape=[jax.ShapeDtypeStruct((64, 2048), BF)] * 8
-        + [jax.ShapeDtypeStruct((16, 128), F32)],
+        out_shape=[jax.ShapeDtypeStruct((64, 2048), BF)] * 8,
         compiler_params=params(),
         cost_estimate=pl.CostEstimate(flops=1 << 21, bytes_accessed=6 << 20, transcendentals=1 << 20),
-    )(at, shares, counts, pltpu.with_memory_space_constraint(score, pltpu.HBM))
+    )(at, shares, pltpu.with_memory_space_constraint(score, pltpu.HBM), first)
 
 
 def lay_kernel(at, *refs):
@@ -318,23 +300,18 @@
     for mine in (before, after, far):
         pieces += [mine, shift(mine, "c", 1)]
 
-    sums, counts = partial_sums(at, shares, scaled, bias_col, pieces)
-    sums = lax.all_to_all(sums, ("y", "z"), split_axis=0, concat_axis=0, tiled=True)
-
-    *blocks, counts = responsibilities(at, shares, counts, score)
+    sums = partial_sums(at, shares, scaled, bias_col, pieces)
+    sent = lax.all_to_all(sums, ("y", "z"), split_axis=0, concat_axis=0, tiled=True)
+
+    blocks = responsibilities(at, shares, score, sums)
     theirs = [swap(b, "c", 1) for b in blocks[:4]]
     held = theirs + list(blocks[4:])
     held = [shift(b, "x", j % 4) if j % 4 else b for j, b in enumerate(held)]
     resp_rows = lay_out(at, held)
 
-    counts = hand_on(counts, *theirs, held[5])
-    counts = sum([shift(counts, "z", i) for i in range(1, 8)], counts)
-    counts = hand_on(counts, held[1], held[3], held[6], held[7])
-    counts = sum([shift(counts, "y", i) for i in range(1, 4)], counts)
-    counts = counts.reshape(2048)
-
-    sums = jnp.sum(sums.reshape(4, 8, 32, 512).astype(F32), axis=1)
-    sums = sums.transpose(1, 0, 2).reshape(32, 2048)
+    sums = jnp.sum(sent.reshape(4, 8, 40, 512).astype(F32), axis=1)
+    counts = (sums[:, 32, :] + sums[:, 33, :]).reshape(2048)
+    sums = sums[:, :32, :].transpose(1, 0, 2).reshape(32, 2048)
     mean_cols = lax.dynamic_slice_in_dim(means, (y * 8 + z) * 32, 32, 1).T.astype(F32)
     new_means_t = (sums + mean_cols) / (counts[None, :] + 1.0)
 

time: 129 us -> 107 us (0.83)
  the two profiles are of different devices: /device:TPU:2 before, /device:TPU:32 now
where the time goes in v3:
time: 107 us; the launch traced here: 106 us
  starting transfers between devices  37.6 us (35%)
  waiting for transfers between devices  28.9 us (27%)
  Pallas kernels  25.3 us (24%)
  other arithmetic  9.4 us (9%)
  local copies, waits for them, and re-layouts  3.77 us (4%)
  between operations  1.58 us (1%)
    ppermute x19, starting transfers between devices, shift(): return lax.ppermute(value, axis, [(i, (i + step) % n) for i in range(n)])  22.2 us
    ppermute x19, waiting for transfers between devices, shift(): return lax.ppermute(value, axis, [(i, (i + step) % n) for i in range(n)])  22 us
    pallas_call x1, Pallas kernels, partial_sums(): pl.pallas_call(sums_kernel, grid_spec=pltpu.PrefetchScalarGridSpec(num_sc...  11.3 us
    all_to_all x1, starting transfers between devices, body(): lax.all_to_all(sums, ('y', 'z'), split_axis=0, concat_axis=0, tiled=True)  9.6 us
    pallas_call x1, Pallas kernels, scores(): pl.pallas_call(score_kernel, grid=(2048 // width,), out_shape=(pltpu.HBM(...  7.28 us
    all_to_all x1, waiting for transfers between devices, body(): lax.all_to_all(share, ('y', 'x', 'c'), split_axis=0, concat_axis=0, tiled...  6.86 us
    convert_element_type x1, other arithmetic, body(): scaled = (means_f * inv_var[None, :]).astype(BF)  5.65 us
    all_to_all x1, starting transfers between devices, body(): lax.all_to_all(share, ('y', 'x', 'c'), split_axis=0, concat_axis=0, tiled...  4.69 us
  transfers between devices with their start and end apart: 25, of which 6 were waited for; matrix products, arithmetic and copies ran while one was open for 10% of the time, Pallas kernels for 13%

profile of v3, /device:TPU:32, one launch (start us, length us, event | category | flops | bytes accessed | tf_op | source)
XLA Modules:
  0.0 106.5 jit_solution(14523824693742624258)
XLA Ops:
  0.7 3.3 %collective-permute-start.3 = (bf16[64,1024]{1,0:T(8,128)(2,1)}, bf16[64,1024]{1,0:T(8,128)(2,1)S(1)}, u32[]{:S(2)}, u32[]{:S(2)}) collective-permute-start(bf16[64,1024]{1,0:T(8,128)(2,1)} %own.1), channel_id=1, source_target_pairs={{0,128},{64,192},{128,0},{192,64},{1,129},{65,193},{129,1},{193,65... | collective-permute-start | bytes 393224 | tf_op jit(solution)/shard_map/ppermute | solution.py:21
  3.9 1.5 %collective-permute-start = (bf16[64,1024]{1,0:T(8,128)(2,1)}, bf16[64,1024]{1,0:T(8,128)(2,1)S(1)}, u32[]{:S(2)}, u32[]{:S(2)}) collective-permute-start(bf16[64,1024]{1,0:T(8,128)(2,1)} %own.1), channel_id=1, source_target_pairs={{0,2},{2,4},{4,6},{6,0},{1,3},{3,5},{5,7},{7,1},{8,10},{10,12},{12... | collective-permute-start | bytes 393224 | tf_op jit(solution)/shard_map/ppermute | solution.py:21
  5.4 1.7 %collective-permute-start.1 = (bf16[64,1024]{1,0:T(8,128)(2,1)}, bf16[64,1024]{1,0:T(8,128)(2,1)S(1)}, u32[]{:S(2)}, u32[]{:S(2)}) collective-permute-start(bf16[64,1024]{1,0:T(8,128)(2,1)} %own.1), channel_id=1, source_target_pairs={{0,6},{2,0},{4,2},{6,4},{1,7},{3,1},{5,3},{7,5},{8,14},{10,8},{12,... | collective-permute-start | bytes 393224 | tf_op jit(solution)/shard_map/ppermute | solution.py:21
  7.2 1.8 %collective-permute-start.2 = (bf16[64,1024]{1,0:T(8,128)(2,1)}, bf16[64,1024]{1,0:T(8,128)(2,1)S(1)}, u32[]{:S(2)}, u32[]{:S(2)}) collective-permute-start(bf16[64,1024]{1,0:T(8,128)(2,1)} %own.1), channel_id=1, source_target_pairs={{0,4},{2,6},{4,0},{6,2},{1,5},{3,7},{5,1},{7,3},{8,12},{10,14},{12... | collective-permute-start | bytes 393224 | tf_op jit(solution)/shard_map/ppermute | solution.py:21
  9.0 5.6 %fusion.2 = (bf16[2048,1024]{1,0:T(8,128)(2,1)}, f32[2048]{0:T(1024)S(1)}) fusion(bf16[2048,1024]{1,0:T(8,128)(2,1)} %param.5, f32[1024]{0:T(1024)} %param.7), kind=kLoop, calls=%fused_computation.4 | loop fusion | flops 12580864 | bytes 8400896 | tf_op jit(solution)/shard_map/convert_element_type | solution.py:284
  16.6 2.6 %collective-permute-start.7 = (bf16[256,1024]{1,0:T(8,128)(2,1)S(1)}, bf16[256,1024]{1,0:T(8,128)(2,1)}, u32[]{:S(2)}, u32[]{:S(2)}) collective-permute-start(bf16[256,1024]{1,0:T(8,128)(2,1)S(1)} %shard_map.75.own.refs_0_), channel_id=1, source_target_pairs={{0,192},{64,0},{128,64},{192,128},{1,193},{65,1},{129,65},{193,129... | collective-permute-start | bytes 1572872 | tf_op jit(solution)/shard_map/ppermute | solution.py:21
  20.3 1.5 %collective-permute-start.11 = (bf16[64,1024]{1,0:T(8,128)(2,1)S(1)}, bf16[64,1024]{1,0:T(8,128)(2,1)S(1)}, u32[]{:S(2)}, u32[]{:S(2)}) collective-permute-start(bf16[64,1024]{1,0:T(8,128)(2,1)S(1)} %collective-permute-done.3.refs_2_.own), channel_id=1, source_target_pairs={{0,4},{2,6},{4,0},{6,2},{1,5},{3,7},{5,1},{7,3},{8,12},{10,14},{12... | collective-permute-start | bytes 393224 | tf_op jit(solution)/shard_map/ppermute | solution.py:21
  22.3 7.3 %shard_map.76 = (f32[512,2048]{1,0:T(8,128)}, f32[32,4,128]{2,1,0:T(4,128)}) custom-call(s32[3]{0:T(128)S(1)} %pad_add_fusion.at, bf16[256,1024]{1,0:T(8,128)(2,1)S(1)} %shard_map.75.own.refs_0_, bf16[256,1024]{1,0:T(8,128)(2,1)S(1)} %collective-permute-done.4.other.refs_1_, bf16[2048,1024]{1,0:T(8,128)(2,1)} %get-tuple-element.24.scaled, f32[1,2048]{1,0:T(1,128)S(1)} %bitcast.36), custom_call_target="tpu_custom_call" | custom-call | flops 2147483648 | bytes 9437184 | tf_op jit(solution)/shard_map/pallas_call | solution.py:112
  29.6 4.7 %all-to-all-start = ((f32[32,4,128]{2,1,0:T(4,128)}), f32[32,4,128]{2,1,0:T(4,128)S(1)}, u32[]{:S(2)}, u32[]{:S(2)}) async-start(f32[32,4,128]{2,1,0:T(4,128)} %get-tuple-element.14), calls=%async_computation | async-start | bytes 131072 | tf_op jit(solution)/shard_map/all_to_all | solution.py:296
  34.9 6.9 %all-to-all-done.refs_0_ = f32[32,4,128]{2,1,0:T(4,128)S(1)} async-done(((f32[32,4,128]{2,1,0:T(4,128)}), f32[32,4,128]{2,1,0:T(4,128)S(1)}, u32[]{:S(2)}, u32[]{:S(2)}) %all-to-all-start) | async-done | bytes 65568 | tf_op jit(solution)/shard_map/all_to_all | solution.py:296
  42.7 1.8 %collective-permute-done.12.refs_7_ = bf16[256,1024]{1,0:T(8,128)(2,1)S(1)} collective-permute-done((bf16[256,1024]{1,0:T(8,128)(2,1)S(1)}, bf16[256,1024]{1,0:T(8,128)(2,1)S(1)}, u32[]{:S(2)}, u32[]{:S(2)}) %collective-permute-start.12) | collective-permute-done | bytes 524320 | tf_op jit(solution)/shard_map/ppermute | solution.py:21
  44.5 11.3 %shard_map.78.first = bf16[32,40,512]{2,1,0:T(8,128)(2,1)} custom-call(s32[3]{0:T(128)S(1)} %pad_add_fusion.at, f32[4,8,4,128]{3,2,1,0:T(4,128)S(1)} %bitcast.30, bf16[2048,1024]{1,0:T(8,128)(2,1)} %get-tuple-element.24.scaled, f32[2048,1]{1,0:T(8,128)S(1)} %copy.15.refs_1_.bias, bf16[256,1024]{1,0:T(8,128)(2,1)S(1)} %shard_map.75.own.refs_0_, ...), custom_call_target="tpu_custom_call" | custom-call | flops 4294967296 | bytes 8388608 | tf_op jit(solution)/shard_map/pallas_call | solution.py:186
  55.9 9.6 %all-to-all-start.1 = ((bf16[32,40,512]{2,1,0:T(8,128)(2,1)}), bf16[32,40,512]{2,1,0:T(8,128)(2,1)}, u32[]{:S(2)}, u32[]{:S(2)}) async-start(bf16[32,40,512]{2,1,0:T(8,128)(2,1)} %shard_map.78.first), calls=%async_computation.1 | async-start | bytes 2621440 | tf_op jit(solution)/shard_map/all_to_all | solution.py:304
  65.5 2.0 %constant_dynamic-slice_fusion.1 = bf16[2048,32]{1,0:T(8,128)(2,1)} fusion(bf16[2048,1024]{1,0:T(8,128)(2,1)} %param.5, s32[]{:T(128)S(6)} %select_n.11), kind=kLoop, calls=%fused_computation.20 | loop fusion | bytes 262148 | tf_op jit(solution)/shard_map/dynamic_slice | solution.py:315
  67.5 3.6 %shard_map.79 = (bf16[64,2048]{1,0:T(8,128)(2,1)S(1)}, bf16[64,2048]{1,0:T(8,128)(2,1)}, bf16[64,2048]{1,0:T(8,128)(2,1)}, bf16[64,2048]{1,0:T(8,128)(2,1)S(1)},...) custom-call(s32[3]{0:T(128)S(1)} %pad_add_fusion.at, ...), custom_call_target="tpu_custom_call" | custom-call | flops 2097152 | bytes 6291456 | tf_op jit(solution)/shard_map/pallas_call | solution.py:237
  73.5 1.2 %copy.19 = bf16[2048,32]{0,1:T(8,128)(2,1)S(1)} copy(bf16[2048,32]{1,0:T(8,128)(2,1)} %constant_dynamic-slice_fusion.1) | data formatting | bytes 262144
  75.6 2.2 %collective-permute-start.21 = (bf16[64,2048]{1,0:T(8,128)(2,1)S(1)}, bf16[64,2048]{1,0:T(8,128)(2,1)S(1)}, u32[]{:S(2)}, u32[]{:S(2)}) collective-permute-start(bf16[64,2048]{1,0:T(8,128)(2,1)S(1)} %get-tuple-element.22), channel_id=1, source_target_pairs={{0,4},{2,6},{4,0},{6,2},{1,5},{3,7},{5,1},{7,3},{8,12},{10,14},{12... | collective-permute-start | bytes 786440 | tf_op jit(solution)/shard_map/ppermute | solution.py:21
  79.9 1.5 %collective-permute-start.17 = (bf16[64,2048]{1,0:T(8,128)(2,1)}, bf16[64,2048]{1,0:T(8,128)(2,1)S(1)}, u32[]{:S(2)}, u32[]{:S(2)}) collective-permute-start(bf16[64,2048]{1,0:T(8,128)(2,1)} %collective-permute-done.16), channel_id=1, source_target_pairs={{0,4},{2,6},{4,0},{6,2},{1,5},{3,7},{5,1},{7,3},{8,12},{10,14},{12... | collective-permute-start | bytes 786440 | tf_op jit(solution)/shard_map/ppermute | solution.py:21
  81.4 6.4 %collective-permute-done.20.refs_5_ = bf16[64,2048]{1,0:T(8,128)(2,1)S(1)} collective-permute-done((bf16[64,2048]{1,0:T(8,128)(2,1)S(1)}, bf16[64,2048]{1,0:T(8,128)(2,1)S(1)}, u32[]{:S(2)}, u32[]{:S(2)}) %collective-permute-start.20) | collective-permute-done | bytes 262176 | tf_op jit(solution)/shard_map/ppermute | solution.py:21
  88.4 3.6 %collective-permute-done.22.refs_7_ = bf16[64,2048]{1,0:T(8,128)(2,1)S(1)} collective-permute-done((bf16[64,2048]{1,0:T(8,128)(2,1)S(1)}, bf16[64,2048]{1,0:T(8,128)(2,1)S(1)}, u32[]{:S(2)}, u32[]{:S(2)}) %collective-permute-start.22) | collective-permute-done | bytes 262176 | tf_op jit(solution)/shard_map/ppermute | solution.py:21
  92.0 6.6 %collective-permute-done.15.refs_1_ = bf16[64,2048]{1,0:T(8,128)(2,1)S(1)} collective-permute-done((bf16[64,2048]{1,0:T(8,128)(2,1)}, bf16[64,2048]{1,0:T(8,128)(2,1)S(1)}, u32[]{:S(2)}, u32[]{:S(2)}) %collective-permute-start.15) | collective-permute-done | bytes 262176 | tf_op jit(solution)/shard_map/ppermute | solution.py:21
  98.6 3.6 %collective-permute-done.19.refs_3_ = bf16[64,2048]{1,0:T(8,128)(2,1)S(1)} collective-permute-done((bf16[64,2048]{1,0:T(8,128)(2,1)}, bf16[64,2048]{1,0:T(8,128)(2,1)S(1)}, u32[]{:S(2)}, u32[]{:S(2)}) %collective-permute-start.19) | collective-permute-done | bytes 262176 | tf_op jit(solution)/shard_map/ppermute | solution.py:21
  102.2 1.9 %shard_map.80 = bf16[64,16384]{1,0:T(8,128)(2,1)} custom-call(s32[3]{0:T(128)S(1)} %pad_add_fusion.at, bf16[64,2048]{1,0:T(8,128)(2,1)S(1)} %collective-permute-done.13.refs_0_, bf16[64,2048]{1,0:T(8,128)(2,1)S(1)} %collective-permute-done.15.refs_1_, bf16[64,2048]{1,0:T(8,128)(2,1)S(1)} %collective-permute-done.17.refs_2_, ...), custom_call_target="tpu_custom_call" | custom-call | tf_op jit(solution)/shard_map/pallas_call | solution.py:268
  104.1 1.5 %convert_reduce_fusion = f32[4,40,512]{2,1,0:T(8,128)S(1)} fusion(bf16[32,40,512]{2,1,0:T(8,128)(2,1)} %all-to-all-done.1), kind=kLoop, calls=%fused_computation.5 | loop fusion | flops 1228800 | bytes 1638400 | tf_op jit(solution)/shard_map/reduce_sum | solution.py:312
  (61 shorter events, 11.2 us)
Async XLA Ops:
  0.7 14.4 %collective-permute-start.3 = (bf16[64,1024]{1,0:T(8,128)(2,1)}, bf16[64,1024]{1,0:T(8,128)(2,1)S(1)}, u32[]{:S(2)}, u32[]{:S(2)}) collective-permute-start(bf16[64,1024]{1,0:T(8,128)(2,1)} %own.1), channel_id=1, source_target_pairs={{0,128},{64,192},{128,0},{192,64},{1,129},{65,193},{129,1},{193,65... | collective-permute-start | bytes 393224 | tf_op jit(solution)/shard_map/ppermute | solution.py:21
  3.9 11.2 %collective-permute-start = (bf16[64,1024]{1,0:T(8,128)(2,1)}, bf16[64,1024]{1,0:T(8,128)(2,1)S(1)}, u32[]{:S(2)}, u32[]{:S(2)}) collective-permute-start(bf16[64,1024]{1,0:T(8,128)(2,1)} %own.1), channel_id=1, source_target_pairs={{0,2},{2,4},{4,6},{6,0},{1,3},{3,5},{5,7},{7,1},{8,10},{10,12},{12... | collective-permute-start | bytes 393224 | tf_op jit(solution)/shard_map/ppermute | solution.py:21
  5.4 9.7 %collective-permute-start.1 = (bf16[64,1024]{1,0:T(8,128)(2,1)}, bf16[64,1024]{1,0:T(8,128)(2,1)S(1)}, u32[]{:S(2)}, u32[]{:S(2)}) collective-permute-start(bf16[64,1024]{1,0:T(8,128)(2,1)} %own.1), channel_id=1, source_target_pairs={{0,6},{2,0},{4,2},{6,4},{1,7},{3,1},{5,3},{7,5},{8,14},{10,8},{12,... | collective-permute-start | bytes 393224 | tf_op jit(solution)/shard_map/ppermute | solution.py:21
  7.2 7.9 %collective-permute-start.2 = (bf16[64,1024]{1,0:T(8,128)(2,1)}, bf16[64,1024]{1,0:T(8,128)(2,1)S(1)}, u32[]{:S(2)}, u32[]{:S(2)}) collective-permute-start(bf16[64,1024]{1,0:T(8,128)(2,1)} %own.1), channel_id=1, source_target_pairs={{0,4},{2,6},{4,0},{6,2},{1,5},{3,7},{5,1},{7,3},{8,12},{10,14},{12... | collective-permute-start | bytes 393224 | tf_op jit(solution)/shard_map/ppermute | solution.py:21
  15.7 6.1 %collective-permute-start.4 = (bf16[256,1024]{1,0:T(8,128)(2,1)S(1)}, bf16[256,1024]{1,0:T(8,128)(2,1)S(1)}, u32[]{:S(2)}, u32[]{:S(2)}) collective-permute-start(bf16[256,1024]{1,0:T(8,128)(2,1)S(1)} %shard_map.75.own.refs_0_), channel_id=1, source_target_pairs={{0,1},{1,0},{2,3},{3,2},{4,5},{5,4},{6,7},{7,6},{8,9},{9,8},{10,11... | collective-permute-start | bytes 1572872 | tf_op jit(solution)/shard_map/ppermute | solution.py:21
  15.8 18.4 %collective-permute-start.5 = (bf16[256,1024]{1,0:T(8,128)(2,1)S(1)}, bf16[256,1024]{1,0:T(8,128)(2,1)S(1)}, u32[]{:S(2)}, u32[]{:S(2)}) collective-permute-start(bf16[256,1024]{1,0:T(8,128)(2,1)S(1)} %shard_map.75.own.refs_0_), channel_id=1, source_target_pairs={{0,64},{64,128},{128,192},{192,0},{1,65},{65,129},{129,193},{193,1... | collective-permute-start | bytes 1572872 | tf_op jit(solution)/shard_map/ppermute | solution.py:21
  16.6 18.1 %collective-permute-start.7 = (bf16[256,1024]{1,0:T(8,128)(2,1)S(1)}, bf16[256,1024]{1,0:T(8,128)(2,1)}, u32[]{:S(2)}, u32[]{:S(2)}) collective-permute-start(bf16[256,1024]{1,0:T(8,128)(2,1)S(1)} %shard_map.75.own.refs_0_), channel_id=1, source_target_pairs={{0,192},{64,0},{128,64},{192,128},{1,193},{65,1},{129,65},{193,129... | collective-permute-start | bytes 1572872 | tf_op jit(solution)/shard_map/ppermute | solution.py:21
  19.1 15.7 %collective-permute-start.10 = (bf16[64,1024]{1,0:T(8,128)(2,1)S(1)}, bf16[64,1024]{1,0:T(8,128)(2,1)S(1)}, u32[]{:S(2)}, u32[]{:S(2)}) collective-permute-start(bf16[64,1024]{1,0:T(8,128)(2,1)S(1)} %collective-permute-done.3.refs_2_.own), channel_id=1, source_target_pairs={{0,6},{2,0},{4,2},{6,4},{1,7},{3,1},{5,3},{7,5},{8,14},{10,8},{12,... | collective-permute-start | bytes 393224 | tf_op jit(solution)/shard_map/ppermute | solution.py:21
  20.3 14.6 %collective-permute-start.11 = (bf16[64,1024]{1,0:T(8,128)(2,1)S(1)}, bf16[64,1024]{1,0:T(8,128)(2,1)S(1)}, u32[]{:S(2)}, u32[]{:S(2)}) collective-permute-start(bf16[64,1024]{1,0:T(8,128)(2,1)S(1)} %collective-permute-done.3.refs_2_.own), channel_id=1, source_target_pairs={{0,4},{2,6},{4,0},{6,2},{1,5},{3,7},{5,1},{7,3},{8,12},{10,14},{12... | collective-permute-start | bytes 393224 | tf_op jit(solution)/shard_map/ppermute | solution.py:21
  21.8 13.1 %collective-permute-start.9 = (bf16[64,1024]{1,0:T(8,128)(2,1)S(1)}, bf16[64,1024]{1,0:T(8,128)(2,1)S(1)}, u32[]{:S(2)}, u32[]{:S(2)}) collective-permute-start(bf16[64,1024]{1,0:T(8,128)(2,1)S(1)} %collective-permute-done.3.refs_2_.own), channel_id=1, source_target_pairs={{0,2},{2,4},{4,6},{6,0},{1,3},{3,5},{5,7},{7,1},{8,10},{10,12},{12... | collective-permute-start | bytes 393224 | tf_op jit(solution)/shard_map/ppermute | solution.py:21
  29.6 12.2 %all-to-all-start = ((f32[32,4,128]{2,1,0:T(4,128)}), f32[32,4,128]{2,1,0:T(4,128)S(1)}, u32[]{:S(2)}, u32[]{:S(2)}) async-start(f32[32,4,128]{2,1,0:T(4,128)} %get-tuple-element.14), calls=%async_computation | async-start | bytes 131072 | tf_op jit(solution)/shard_map/all_to_all | solution.py:296
  34.3 8.4 %collective-permute-start.6 = (bf16[256,1024]{1,0:T(8,128)(2,1)S(1)}, bf16[256,1024]{1,0:T(8,128)(2,1)}, u32[]{:S(2)}, u32[]{:S(2)}) collective-permute-start(bf16[256,1024]{1,0:T(8,128)(2,1)S(1)} %collective-permute-done.5.refs_2_), channel_id=1, source_target_pairs={{0,1},{1,0},{2,3},{3,2},{4,5},{5,4},{6,7},{7,6},{8,9},{9,8},{10,11... | collective-permute-start | bytes 1572872 | tf_op jit(solution)/shard_map/ppermute | solution.py:21
  34.6 8.1 %collective-permute-start.8 = (bf16[256,1024]{1,0:T(8,128)(2,1)}, bf16[256,1024]{1,0:T(8,128)(2,1)}, u32[]{:S(2)}, u32[]{:S(2)}) collective-permute-start(bf16[256,1024]{1,0:T(8,128)(2,1)} %collective-permute-done.7.refs_4_), channel_id=1, source_target_pairs={{0,1},{1,0},{2,3},{3,2},{4,5},{5,4},{6,7},{7,6},{8,9},{9,8},{10,11... | collective-permute-start | bytes 1572872 | tf_op jit(solution)/shard_map/ppermute | solution.py:21
  55.9 48.2 %all-to-all-start.1 = ((bf16[32,40,512]{2,1,0:T(8,128)(2,1)}), bf16[32,40,512]{2,1,0:T(8,128)(2,1)}, u32[]{:S(2)}, u32[]{:S(2)}) async-start(bf16[32,40,512]{2,1,0:T(8,128)(2,1)} %shard_map.78.first), calls=%async_computation.1 | async-start | bytes 2621440 | tf_op jit(solution)/shard_map/all_to_all | solution.py:304
  71.1 4.5 %collective-permute-start.14 = (bf16[64,2048]{1,0:T(8,128)(2,1)}, bf16[64,2048]{1,0:T(8,128)(2,1)}, u32[]{:S(2)}, u32[]{:S(2)}) collective-permute-start(bf16[64,2048]{1,0:T(8,128)(2,1)} %get-tuple-element.17), channel_id=1, source_target_pairs={{0,1},{1,0},{2,3},{3,2},{4,5},{5,4},{6,7},{7,6},{8,9},{9,8},{10,11... | collective-permute-start | bytes 786440 | tf_op jit(solution)/shard_map/ppermute | solution.py:26
  71.2 6.6 %collective-permute-start.16 = (bf16[64,2048]{1,0:T(8,128)(2,1)}, bf16[64,2048]{1,0:T(8,128)(2,1)}, u32[]{:S(2)}, u32[]{:S(2)}) collective-permute-start(bf16[64,2048]{1,0:T(8,128)(2,1)} %get-tuple-element.18), channel_id=1, source_target_pairs={{0,1},{1,0},{2,3},{3,2},{4,5},{5,4},{6,7},{7,6},{8,9},{9,8},{10,11... | collective-permute-start | bytes 786440 | tf_op jit(solution)/shard_map/ppermute | solution.py:26
  71.7 7.2 %collective-permute-start.18 = (bf16[64,2048]{1,0:T(8,128)(2,1)S(1)}, bf16[64,2048]{1,0:T(8,128)(2,1)}, u32[]{:S(2)}, u32[]{:S(2)}) collective-permute-start(bf16[64,2048]{1,0:T(8,128)(2,1)S(1)} %get-tuple-element.19), channel_id=1, source_target_pairs={{0,1},{1,0},{2,3},{3,2},{4,5},{5,4},{6,7},{7,6},{8,9},{9,8},{10,11... | collective-permute-start | bytes 786440 | tf_op jit(solution)/shard_map/ppermute | solution.py:26
  71.8 8.0 %collective-permute-start.13 = (bf16[64,2048]{1,0:T(8,128)(2,1)S(1)}, bf16[64,2048]{1,0:T(8,128)(2,1)S(1)}, u32[]{:S(2)}, u32[]{:S(2)}) collective-permute-start(bf16[64,2048]{1,0:T(8,128)(2,1)S(1)} %get-tuple-element.16), channel_id=1, source_target_pairs={{0,1},{1,0},{2,3},{3,2},{4,5},{5,4},{6,7},{7,6},{8,9},{9,8},{10,11... | collective-permute-start | bytes 786440 | tf_op jit(solution)/shard_map/ppermute | solution.py:26
  72.2 15.5 %collective-permute-start.20 = (bf16[64,2048]{1,0:T(8,128)(2,1)S(1)}, bf16[64,2048]{1,0:T(8,128)(2,1)S(1)}, u32[]{:S(2)}, u32[]{:S(2)}) collective-permute-start(bf16[64,2048]{1,0:T(8,128)(2,1)S(1)} %get-tuple-element.21), channel_id=1, source_target_pairs={{0,2},{2,4},{4,6},{6,0},{1,3},{3,5},{5,7},{7,1},{8,10},{10,12},{12... | collective-permute-start | bytes 786440 | tf_op jit(solution)/shard_map/ppermute | solution.py:21
  75.6 12.7 %collective-permute-start.21 = (bf16[64,2048]{1,0:T(8,128)(2,1)S(1)}, bf16[64,2048]{1,0:T(8,128)(2,1)S(1)}, u32[]{:S(2)}, u32[]{:S(2)}) collective-permute-start(bf16[64,2048]{1,0:T(8,128)(2,1)S(1)} %get-tuple-element.22), channel_id=1, source_target_pairs={{0,4},{2,6},{4,0},{6,2},{1,5},{3,7},{5,1},{7,3},{8,12},{10,14},{12... | collective-permute-start | bytes 786440 | tf_op jit(solution)/shard_map/ppermute | solution.py:21
  77.8 14.2 %collective-permute-start.22 = (bf16[64,2048]{1,0:T(8,128)(2,1)S(1)}, bf16[64,2048]{1,0:T(8,128)(2,1)S(1)}, u32[]{:S(2)}, u32[]{:S(2)}) collective-permute-start(bf16[64,2048]{1,0:T(8,128)(2,1)S(1)} %get-tuple-element.23), channel_id=1, source_target_pairs={{0,6},{2,0},{4,2},{6,4},{1,7},{3,1},{5,3},{7,5},{8,14},{10,8},{12,... | collective-permute-start | bytes 786440 | tf_op jit(solution)/shard_map/ppermute | solution.py:21
  78.9 19.7 %collective-permute-start.15 = (bf16[64,2048]{1,0:T(8,128)(2,1)}, bf16[64,2048]{1,0:T(8,128)(2,1)S(1)}, u32[]{:S(2)}, u32[]{:S(2)}) collective-permute-start(bf16[64,2048]{1,0:T(8,128)(2,1)} %collective-permute-done.14), channel_id=1, source_target_pairs={{0,2},{2,4},{4,6},{6,0},{1,3},{3,5},{5,7},{7,1},{8,10},{10,12},{12... | collective-permute-start | bytes 786440 | tf_op jit(solution)/shard_map/ppermute | solution.py:21
  79.9 18.7 %collective-permute-start.17 = (bf16[64,2048]{1,0:T(8,128)(2,1)}, bf16[64,2048]{1,0:T(8,128)(2,1)S(1)}, u32[]{:S(2)}, u32[]{:S(2)}) collective-permute-start(bf16[64,2048]{1,0:T(8,128)(2,1)} %collective-permute-done.16), channel_id=1, source_target_pairs={{0,4},{2,6},{4,0},{6,2},{1,5},{3,7},{5,1},{7,3},{8,12},{10,14},{12... | collective-permute-start | bytes 786440 | tf_op jit(solution)/shard_map/ppermute | solution.py:21
  87.7 14.4 %collective-permute-start.19 = (bf16[64,2048]{1,0:T(8,128)(2,1)}, bf16[64,2048]{1,0:T(8,128)(2,1)S(1)}, u32[]{:S(2)}, u32[]{:S(2)}) collective-permute-start(bf16[64,2048]{1,0:T(8,128)(2,1)} %collective-permute-done.18), channel_id=1, source_target_pairs={{0,6},{2,0},{4,2},{6,4},{1,7},{3,1},{5,3},{7,5},{8,14},{10,8},{12,... | collective-permute-start | bytes 786440 | tf_op jit(solution)/shard_map/ppermute | solution.py:21
  (6 other events, 60.1 us)

commit v4 on v3

--- a/solution.py
+++ b/solution.py
@@ -21,9 +21,8 @@
     return lax.ppermute(value, axis, [(i, (i + step) % n) for i in range(n)])
 
 
-def swap(value, axis, bit):
-    n = SIZES[axis]
-    return lax.ppermute(value, axis, [(i, i ^ bit) for i in range(n)])
+def still(value):
+    return pltpu.with_memory_space_constraint(value, pltpu.HBM)
 
 
 def params():
@@ -44,6 +43,43 @@
 
 def hbm(n=1):
     return [pl.BlockSpec(memory_space=pltpu.HBM)] * n
+
+
+def prepare_kernel(means, inv_var, weights, scaled, row, col):
+    values = means[...].astype(F32)
+    product = values * inv_var[...]
+    scaled[...] = product.astype(BF)
+    square = values * product
+    norm = functools.reduce(jnp.add, [square[:, i : i + 128] for i in range(0, 1024, 128)])
+    norm = 0.5 * jnp.sum(norm, axis=1, keepdims=True)
+    for i in range(0, 256, 128):
+        part = weights[:, i : i + 128] - line(norm[i : i + 128])
+        row[:, i : i + 128] = part
+        col[i : i + 128, :] = column(part)
+
+
+def prepare(means, inv_var, log_weights):
+    return pl.pallas_call(
+        prepare_kernel,
+        grid=(8,),
+        in_specs=[
+            pl.BlockSpec((256, 1024), lambda i: (i, 0)),
+            pl.BlockSpec((1, 1024), lambda i: (0, 0)),
+            pl.BlockSpec((1, 256), lambda i: (0, i)),
+        ],
+        out_specs=(
+            pl.BlockSpec((256, 1024), lambda i: (i, 0)),
+            pl.BlockSpec((1, 256), lambda i: (0, i)),
+            pl.BlockSpec((256, 1), lambda i: (i, 0)),
+        ),
+        out_shape=(
+            pltpu.HBM((2048, 1024), BF),
+            jax.ShapeDtypeStruct((1, 2048), F32),
+            jax.ShapeDtypeStruct((2048, 1), F32),
+        ),
+        compiler_params=params(),
+        cost_estimate=pl.CostEstimate(flops=6 << 21, bytes_accessed=8 << 20, transcendentals=0),
+    )(still(means), inv_var.reshape(1, 1024), log_weights.reshape(1, 2048))
 
 
 def place_kernel(at, own, before, after, far, *refs):
@@ -54,15 +90,15 @@
         out[pl.ds(pl.multiple_of(slot * 64, 64), 64), :] = piece[...]
 
 
-def gather_x(at, own, ahead):
+def gather_x(at, own, ahead, there=()):
     parts = (own, shift(own, "x", 1), shift(own, "x", -1), shift(own, "x", 2))
     return pl.pallas_call(
         place_kernel,
         out_shape=jax.ShapeDtypeStruct((256, 1024), BF),
-        in_specs=[scalar()] + [whole()] * 4 + anywhere(len(ahead)),
+        in_specs=[scalar()] + [whole()] * 4 + hbm(len(ahead)) + anywhere(len(there)),
         out_specs=whole(),
         compiler_params=params(),
-    )(at, *parts, *ahead)
+    )(at, *parts, *(still(a) for a in ahead), *there)
 
 
 def column(row):
@@ -132,7 +168,7 @@
         cost_estimate=pl.CostEstimate(
             flops=2 * 512 * 2048 * 1024, bytes_accessed=9 << 20, transcendentals=1 << 20
         ),
-    )(at, own, other, scaled, bias_row)
+    )(at, own, other, still(scaled), bias_row)
 
 
 def joined(shares):
@@ -207,12 +243,12 @@
         cost_estimate=pl.CostEstimate(
             flops=4 * 512 * 2048 * 1024, bytes_accessed=8 << 20, transcendentals=1 << 20
         ),
-    )(at, shares, scaled, bias_col, *pieces)
-
-
-def resp_kernel(at, shares, score, first, *refs):
-    del first
-    outs, norm, held, sems = refs[:8], refs[8], refs[9], refs[10]
+    )(at, shares, still(scaled), bias_col, *pieces)
+
+
+def resp_kernel(at, shares, score, sums, *refs):
+    del sums
+    outs, norm, held, sems = refs[:5], refs[6], refs[7], refs[8]
     x, c, y = at[0], at[1], at[2]
     copies = []
     for j in range(8):
@@ -230,23 +266,52 @@
         )
     for j, (start, copy) in enumerate(copies):
         copy.wait()
-        outs[j][...] = jnp.exp(held[j] - norm[pl.ds(start, 64), 0:1]).astype(BF)
-
-
-def responsibilities(at, shares, score, first):
+        block = jnp.exp(held[j] - norm[pl.ds(start, 64), 0:1]).astype(BF)
+        if j % 4 == 0:
+            outs[j // 4][...] = block
+        else:
+            outs[1 + j % 4][j // 4 * 64 : j // 4 * 64 + 64, :] = block
+
+
+def responsibilities(at, shares, score, sums):
     return pl.pallas_call(
         resp_kernel,
         in_specs=[scalar(), whole()] + hbm(2),
-        out_specs=[whole()] * 8,
+        out_specs=[whole()] * 5 + hbm(),
+        input_output_aliases={3: 5},
         scratch_shapes=[
             VMEM((512, 128), F32),
             VMEM((8, 64, 2048), F32),
             pltpu.SemaphoreType.DMA((8,)),
         ],
-        out_shape=[jax.ShapeDtypeStruct((64, 2048), BF)] * 8,
+        out_shape=[jax.ShapeDtypeStruct((64, 2048), BF)] * 2
+        + [jax.ShapeDtypeStruct((128, 2048), BF)] * 3
+        + [pltpu.HBM((32, 40, 512), BF)],
         compiler_params=params(),
         cost_estimate=pl.CostEstimate(flops=1 << 21, bytes_accessed=6 << 20, transcendentals=1 << 20),
-    )(at, shares, pltpu.with_memory_space_constraint(score, pltpu.HBM), first)
+    )(at, shares, still(score), sums)
+
+
+def cut_kernel(at, means, ahead, out, turned):
+    del ahead
+    for i in range(0, 2048, 128):
+        turned[:, i : i + 128] = jnp.transpose(means[i : i + 128, :].astype(F32))
+    out[...] = turned[pl.ds(pl.multiple_of(lax.rem(at[3], 4) * 32, 32), 32), :]
+
+
+def mean_columns(at, means, ahead):
+    return pl.pallas_call(
+        cut_kernel,
+        grid_spec=pltpu.PrefetchScalarGridSpec(
+            num_scalar_prefetch=1,
+            grid=(1,),
+            in_specs=[pl.BlockSpec((2048, 128), lambda i, at: (0, at[3] // 4))] + anywhere(),
+            out_specs=pl.BlockSpec((32, 2048), lambda i, at: (0, 0)),
+            scratch_shapes=[VMEM((128, 2048), F32)],
+        ),
+        out_shape=pltpu.HBM((32, 2048), F32),
+        compiler_params=params(),
+    )(at, still(means), ahead)
 
 
 def lay_kernel(at, *refs):
@@ -257,7 +322,8 @@
         core = 1 - c if j < 4 else c
         comp = lax.rem(x + 4 - j % 4, 4) * 2 + core
         spot = out.at[:, pl.ds(pl.multiple_of(comp * 2048, 2048), 2048)]
-        copies.append(pltpu.make_async_copy(pieces[j], spot, sems.at[j]))
+        piece = pieces[j].at[pl.ds(64, 64)] if j > 4 else pieces[j]
+        copies.append(pltpu.make_async_copy(piece, spot, sems.at[j]))
     for copy in copies:
         copy.start()
     for copy in copies:
@@ -277,42 +343,36 @@
 
 def body(points, means, log_weights, inv_var):
     x, c, y, z = (lax.axis_index(a) for a in "xcyz")
-    at = jnp.stack([x, c, y]).astype(jnp.int32)
+    at = jnp.stack([x, c, y, y * 8 + z]).astype(jnp.int32)
 
     far = shift(points, "y", 2)
-    means_f = means.astype(F32)
-    scaled = (means_f * inv_var[None, :]).astype(BF)
-    scaled = pltpu.with_memory_space_constraint(scaled, pltpu.HBM)
-    half_norm = 0.5 * jnp.sum(means_f * means_f * inv_var[None, :], axis=1)
-    bias = log_weights - half_norm
-    bias_row, bias_col = bias.reshape(1, 2048), bias[:, None]
-
-    own = gather_x(at, points, (bias_row, bias_col, far))
+    scaled, bias_row, bias_col = prepare(means, inv_var, log_weights)
+
+    own = gather_x(at, points, (scaled,), (far,))
     other = shift(own, "c", 1)
     before = shift(own, "y", 1)
     after = shift(own, "y", -1)
     score, share = scores(at, own, other, scaled, bias_row)
 
     shares = lax.all_to_all(share, ("y", "x", "c"), split_axis=0, concat_axis=0, tiled=True)
-    far = gather_x(at, far, (shares,))
+    mean_cols = mean_columns(at, means, share)
+    far = gather_x(at, far, (mean_cols,), (shares,))
     shares = shares.reshape(4, 8, 4, 128)
     pieces = [own, other]
     for mine in (before, after, far):
         pieces += [mine, shift(mine, "c", 1)]
 
     sums = partial_sums(at, shares, scaled, bias_col, pieces)
+    *blocks, sums = responsibilities(at, shares, score, sums)
+    pairs = [shift(b, "x", j + 1) for j, b in enumerate(blocks[2:])]
+    theirs = [shift(b, "c", 1) for b in [blocks[0]] + [pair[:64] for pair in pairs]]
+    held = theirs + [blocks[1]] + pairs
     sent = lax.all_to_all(sums, ("y", "z"), split_axis=0, concat_axis=0, tiled=True)
-
-    blocks = responsibilities(at, shares, score, sums)
-    theirs = [swap(b, "c", 1) for b in blocks[:4]]
-    held = theirs + list(blocks[4:])
-    held = [shift(b, "x", j % 4) if j % 4 else b for j, b in enumerate(held)]
     resp_rows = lay_out(at, held)
 
     sums = jnp.sum(sent.reshape(4, 8, 40, 512).astype(F32), axis=1)
     counts = (sums[:, 32, :] + sums[:, 33, :]).reshape(2048)
     sums = sums[:, :32, :].transpose(1, 0, 2).reshape(32, 2048)
-    mean_cols = lax.dynamic_slice_in_dim(means, (y * 8 + z) * 32, 32, 1).T.astype(F32)
     new_means_t = (sums + mean_cols) / (counts[None, :] + 1.0)
 
     lse = joined(lax.dynamic_index_in_dim(shares, y, 0, keepdims=False)).reshape(8, 64)

time: 107 us -> 109 us (1.019)
  Pallas kernels: 25.3 us -> 34.9 us
  other arithmetic: 9.4 us -> 3.69 us
  starting transfers between devices: 37.6 us -> 35.2 us
    pallas_call x0 -> x2, Pallas kernels: none -> 9.51 us  [the longest x1 7 us: prepare(): pl.pallas_call(prepare_kernel, grid=(8,), in_specs=[pl.BlockSpec((256, 10...]
    convert_element_type x1 -> x0, other arithmetic: 5.65 us -> none  [body(): scaled = (means_f * inv_var[None, :]).astype(BF)]
    ppermute x19 -> x20, starting transfers between devices: 22.2 us -> 19.1 us  [shift(): return lax.ppermute(value, axis, [(i, (i + step) % n) for i in range(n)])]
    all_to_all x1, waiting for transfers between devices: 6.86 us -> 4.44 us  [body(): lax.all_to_all(share, ('y', 'x', 'c'), split_axis=0, concat_axis=0, tiled...]
    slice x0 -> x3, local copies, waits for them, and re-layouts: none -> 2.15 us  [body(): pair[:64]]
    dynamic_slice x1 -> x0, local copies, waits for them, and re-layouts: 2.05 us -> none  [body(): lax.dynamic_slice_in_dim(means, (y * 8 + z) * 32, 32, 1).T.astype(F32)]
    all_to_all x1, starting transfers between devices: 4.69 us -> 6.59 us  [body(): lax.all_to_all(share, ('y', 'x', 'c'), split_axis=0, concat_axis=0, tiled...]
    ppermute x19 -> x20, waiting for transfers between devices: 22 us -> 23.7 us  [shift(): return lax.ppermute(value, axis, [(i, (i + step) % n) for i in range(n)])]
  transfers between devices with their start and end apart: 25 -> 22, of which waited for: 6 -> 5; matrix products, arithmetic and copies ran while one was open for 10% -> 3% of each run, Pallas kernels for 13% -> 18%
where the time goes in v4:
time: 109 us
  starting transfers between devices  35.2 us (32%)
  Pallas kernels  34.9 us (32%)
  waiting for transfers between devices  29.6 us (27%)
  other arithmetic  3.69 us (3%)
  local copies, waits for them, and re-layouts  3.67 us (3%)
  between operations  1.47 us (1%)
    ppermute x20, waiting for transfers between devices, shift(): return lax.ppermute(value, axis, [(i, (i + step) % n) for i in range(n)])  23.7 us
    ppermute x20, starting transfers between devices, shift(): return lax.ppermute(value, axis, [(i, (i + step) % n) for i in range(n)])  19.1 us
    pallas_call x1, Pallas kernels, partial_sums(): pl.pallas_call(sums_kernel, grid_spec=pltpu.PrefetchScalarGridSpec(num_sc...  11.3 us
    all_to_all x1, starting transfers between devices, body(): lax.all_to_all(sums, ('y', 'z'), split_axis=0, concat_axis=0, tiled=True)  9.47 us
    pallas_call x1, Pallas kernels, scores(): pl.pallas_call(score_kernel, grid=(2048 // width,), out_shape=(pltpu.HBM(...  7.21 us
    pallas_call x1, Pallas kernels, prepare(): pl.pallas_call(prepare_kernel, grid=(8,), in_specs=[pl.BlockSpec((256, 10...  7 us
    all_to_all x1, starting transfers between devices, body(): lax.all_to_all(share, ('y', 'x', 'c'), split_axis=0, concat_axis=0, tiled...  6.59 us
    all_to_all x1, waiting for transfers between devices, body(): lax.all_to_all(share, ('y', 'x', 'c'), split_axis=0, concat_axis=0, tiled...  4.44 us
  transfers between devices with their start and end apart: 22, of which 5 were waited for; matrix products, arithmetic and copies ran while one was open for 3% of the time, Pallas kernels for 18%

profile of v4, /device:TPU:32, one launch (start us, length us, event | category | flops | bytes accessed | tf_op | source)
XLA Modules:
  0.0 108.5 jit_solution(8152836789049911300)
XLA Ops:
  0.6 3.3 %collective-permute-start.3 = (bf16[64,1024]{1,0:T(8,128)(2,1)}, bf16[64,1024]{1,0:T(8,128)(2,1)S(1)}, u32[]{:S(2)}, u32[]{:S(2)}) collective-permute-start(bf16[64,1024]{1,0:T(8,128)(2,1)} %own.1), channel_id=1, source_target_pairs={{0,128},{64,192},{128,0},{192,64},{1,129},{65,193},{129,1},{193,65... | collective-permute-start | bytes 393224 | tf_op jit(solution)/shard_map/ppermute | solution.py:21
  3.9 3.0 %collective-permute-start.2 = (bf16[64,1024]{1,0:T(8,128)(2,1)}, bf16[64,1024]{1,0:T(8,128)(2,1)S(1)}, u32[]{:S(2)}, u32[]{:S(2)}) collective-permute-start(bf16[64,1024]{1,0:T(8,128)(2,1)} %own.1), channel_id=1, source_target_pairs={{0,4},{2,6},{4,0},{6,2},{1,5},{3,7},{5,1},{7,3},{8,12},{10,14},{12... | collective-permute-start | bytes 393224 | tf_op jit(solution)/shard_map/ppermute | solution.py:21
  6.9 1.1 %collective-permute-start.1 = (bf16[64,1024]{1,0:T(8,128)(2,1)}, bf16[64,1024]{1,0:T(8,128)(2,1)S(1)}, u32[]{:S(2)}, u32[]{:S(2)}) collective-permute-start(bf16[64,1024]{1,0:T(8,128)(2,1)} %own.1), channel_id=1, source_target_pairs={{0,6},{2,0},{4,2},{6,4},{1,7},{3,1},{5,3},{7,5},{8,14},{10,8},{12,... | collective-permute-start | bytes 393224 | tf_op jit(solution)/shard_map/ppermute | solution.py:21
  8.1 0.9 collective-permute-start
  10.3 7.0 %shard_map.75 = (bf16[2048,1024]{1,0:T(8,128)(2,1)}, f32[1,2048]{1,0:T(1,128)S(1)}, f32[2048,1]{1,0:T(8,128)S(1)}) custom-call(bf16[2048,1024]{1,0:T(8,128)(2,1)} %means.3, f32[1,1024]{1,0:T(1,128)S(1)} %bitcast.29, f32[1,2048]{1,0:T(1,128)S(1)} %bitcast.30), custom_call_target="tpu_custom_call" | custom-call | flops 12582912 | bytes 8388608 | tf_op jit(solution)/shard_map/pallas_call | solution.py:62
  18.2 1.1 %collective-permute-start.7 = (bf16[256,1024]{1,0:T(8,128)(2,1)S(1)}, bf16[256,1024]{1,0:T(8,128)(2,1)}, u32[]{:S(2)}, u32[]{:S(2)}) collective-permute-start(bf16[256,1024]{1,0:T(8,128)(2,1)S(1)} %shard_map.76.own.refs_0_), channel_id=1, source_target_pairs={{0,192},{64,0},{128,64},{192,128},{1,193},{65,1},{129,65},{193,129... | collective-permute-start | bytes 1572872 | tf_op jit(solution)/shard_map/ppermute | solution.py:21
  19.3 1.0 collective-permute-start.5
  20.9 2.6 %collective-permute-start.10 = (bf16[64,1024]{1,0:T(8,128)(2,1)S(1)}, bf16[64,1024]{1,0:T(8,128)(2,1)S(1)}, u32[]{:S(2)}, u32[]{:S(2)}) collective-permute-start(bf16[64,1024]{1,0:T(8,128)(2,1)S(1)} %collective-permute-done.3.refs_1_.own), channel_id=1, source_target_pairs={{0,6},{2,0},{4,2},{6,4},{1,7},{3,1},{5,3},{7,5},{8,14},{10,8},{12,... | collective-permute-start | bytes 393224 | tf_op jit(solution)/shard_map/ppermute | solution.py:21
  23.5 7.2 %shard_map.77 = (f32[512,2048]{1,0:T(8,128)}, f32[32,4,128]{2,1,0:T(4,128)}) custom-call(s32[4]{0:T(128)S(1)} %pad_add_fusion.at, bf16[256,1024]{1,0:T(8,128)(2,1)S(1)} %shard_map.76.own.refs_0_, bf16[256,1024]{1,0:T(8,128)(2,1)S(1)} %collective-permute-done.4.other.refs_1_, bf16[2048,1024]{1,0:T(8,128)(2,1)} %get-tuple-element.15.refs_0_.scaled, ...), custom_call_target="tpu_custom_call" | custom-call | flops 2147483648 | bytes 9437184 | tf_op jit(solution)/shard_map/pallas_call | solution.py:148
  30.7 6.6 %all-to-all-start = ((f32[32,4,128]{2,1,0:T(4,128)}), f32[32,4,128]{2,1,0:T(4,128)S(1)}, u32[]{:S(2)}, u32[]{:S(2)}) async-start(f32[32,4,128]{2,1,0:T(4,128)} %get-tuple-element.17.ahead), calls=%async_computation | async-start | bytes 131072 | tf_op jit(solution)/shard_map/all_to_all | solution.py:357
  37.3 2.5 %shard_map.78.refs_0_ = f32[32,2048]{1,0:T(8,128)} custom-call(s32[4]{0:T(128)S(1)} %pad_add_fusion.at, bf16[2048,1024]{1,0:T(8,128)(2,1)} %means.3, f32[32,4,128]{2,1,0:T(4,128)} %get-tuple-element.17.ahead), custom_call_target="tpu_custom_call" | custom-call | tf_op jit(solution)/shard_map/pallas_call | solution.py:303
  40.4 4.4 %all-to-all-done.refs_1_ = f32[32,4,128]{2,1,0:T(4,128)S(1)} async-done(((f32[32,4,128]{2,1,0:T(4,128)}), f32[32,4,128]{2,1,0:T(4,128)S(1)}, u32[]{:S(2)}, u32[]{:S(2)}) %all-to-all-start) | async-done | bytes 65568 | tf_op jit(solution)/shard_map/all_to_all | solution.py:357
  45.8 1.8 %collective-permute-done.12.refs_7_ = bf16[256,1024]{1,0:T(8,128)(2,1)S(1)} collective-permute-done((bf16[256,1024]{1,0:T(8,128)(2,1)S(1)}, bf16[256,1024]{1,0:T(8,128)(2,1)S(1)}, u32[]{:S(2)}, u32[]{:S(2)}) %collective-permute-start.12) | collective-permute-done | bytes 524320 | tf_op jit(solution)/shard_map/ppermute | solution.py:21
  47.6 11.3 %shard_map.80.sums = bf16[32,40,512]{2,1,0:T(8,128)(2,1)} custom-call(s32[4]{0:T(128)S(1)} %pad_add_fusion.at, f32[4,8,4,128]{3,2,1,0:T(4,128)S(1)} %bitcast.25, bf16[2048,1024]{1,0:T(8,128)(2,1)} %get-tuple-element.15.refs_0_.scaled, f32[2048,1]{1,0:T(8,128)S(1)} %get-tuple-element.19.bias, bf16[256,1024]{1,0:T(8,128)(2,1)S(1)} %shard_map.76.own.refs_0_, ...), custom_call_target="tpu_custom_call" | custom-call | flops 4294967296 | bytes 8388608 | tf_op jit(solution)/shard_map/pallas_call | solution.py:222
  58.9 3.7 %shard_map.81 = (bf16[64,2048]{1,0:T(8,128)(2,1)S(1)}, bf16[64,2048]{1,0:T(8,128)(2,1)S(1)}, bf16[128,2048]{1,0:T(8,128)(2,1)}, bf16[128,2048]{1,0:T(8,128)(2,1)...) custom-call(s32[4]{0:T(128)S(1)} %pad_add_fusion.at, ...), custom_call_target="tpu_custom_call", output_to_operand_aliasing={{5}: (3, {})} | custom-call | flops 2097152 | bytes 6291456 | tf_op jit(solution)/shard_map/pallas_call | solution.py:277
  62.7 9.5 %all-to-all-start.1 = ((bf16[32,40,512]{2,1,0:T(8,128)(2,1)}), bf16[32,40,512]{2,1,0:T(8,128)(2,1)}, u32[]{:S(2)}, u32[]{:S(2)}) async-start(bf16[32,40,512]{2,1,0:T(8,128)(2,1)} %get-tuple-element.25), calls=%async_computation.1 | async-start | bytes 2621440 | tf_op jit(solution)/shard_map/all_to_all | solution.py:370
  72.8 2.1 %collective-permute-start.16 = (bf16[128,2048]{1,0:T(8,128)(2,1)S(1)}, bf16[128,2048]{1,0:T(8,128)(2,1)S(1)}, u32[]{:S(2)}, u32[]{:S(2)}) collective-permute-start(bf16[128,2048]{1,0:T(8,128)(2,1)S(1)} %get-tuple-element.22), channel_id=1, source_target_pairs={{0,4},{2,6},{4,0},{6,2},{1,5},{3,7},{5,1},{7,3},{8,12},{10,14},{12... | collective-permute-start | bytes 1572872 | tf_op jit(solution)/shard_map/ppermute | solution.py:21
  74.9 1.0 collective-permute-start.18
  77.5 20.8 %collective-permute-done.14.refs_5_ = bf16[128,2048]{1,0:T(8,128)(2,1)S(1)} collective-permute-done((bf16[128,2048]{1,0:T(8,128)(2,1)}, bf16[128,2048]{1,0:T(8,128)(2,1)S(1)}, u32[]{:S(2)}, u32[]{:S(2)}) %collective-permute-start.14) | collective-permute-done | bytes 524320 | tf_op jit(solution)/shard_map/ppermute | solution.py:21
  101.6 1.1 %collective-permute-done.19.refs_3_ = bf16[64,2048]{1,0:T(8,128)(2,1)S(1)} collective-permute-done((bf16[64,2048]{1,0:T(8,128)(2,1)}, bf16[64,2048]{1,0:T(8,128)(2,1)S(1)}, u32[]{:S(2)}, u32[]{:S(2)}) %collective-permute-start.19) | collective-permute-done | bytes 262176 | tf_op jit(solution)/shard_map/ppermute | solution.py:21
  102.7 1.9 %shard_map.82 = bf16[64,16384]{1,0:T(8,128)(2,1)} custom-call(s32[4]{0:T(128)S(1)} %pad_add_fusion.at, bf16[64,2048]{1,0:T(8,128)(2,1)S(1)} %collective-permute-done.13.refs_0_, bf16[64,2048]{1,0:T(8,128)(2,1)S(1)} %collective-permute-done.15.refs_1_, bf16[64,2048]{1,0:T(8,128)(2,1)S(1)} %collective-permute-done.17.refs_2_, ...), custom_call_target="tpu_custom_call" | custom-call | tf_op jit(solution)/shard_map/pallas_call | solution.py:334
  104.6 1.5 %all-to-all-done.1 = bf16[32,40,512]{2,1,0:T(8,128)(2,1)} async-done(((bf16[32,40,512]{2,1,0:T(8,128)(2,1)}), bf16[32,40,512]{2,1,0:T(8,128)(2,1)}, u32[]{:S(2)}, u32[]{:S(2)}) %all-to-all-start.1) | async-done | bytes 1310752 | tf_op jit(solution)/shard_map/all_to_all | solution.py:370
  106.1 1.5 %convert_reduce_fusion = f32[4,40,512]{2,1,0:T(8,128)S(1)} fusion(bf16[32,40,512]{2,1,0:T(8,128)(2,1)} %all-to-all-done.1), kind=kLoop, calls=%fused_computation | loop fusion | flops 1228800 | bytes 1638400 | tf_op jit(solution)/shard_map/reduce_sum | solution.py:373
  107.7 0.8 add_divide_fusion
  (57 shorter events, 9.3 us)
Async XLA Ops:
  0.6 16.8 %collective-permute-start.3 = (bf16[64,1024]{1,0:T(8,128)(2,1)}, bf16[64,1024]{1,0:T(8,128)(2,1)S(1)}, u32[]{:S(2)}, u32[]{:S(2)}) collective-permute-start(bf16[64,1024]{1,0:T(8,128)(2,1)} %own.1), channel_id=1, source_target_pairs={{0,128},{64,192},{128,0},{192,64},{1,129},{65,193},{129,1},{193,65... | collective-permute-start | bytes 393224 | tf_op jit(solution)/shard_map/ppermute | solution.py:21
  3.9 13.5 %collective-permute-start.2 = (bf16[64,1024]{1,0:T(8,128)(2,1)}, bf16[64,1024]{1,0:T(8,128)(2,1)S(1)}, u32[]{:S(2)}, u32[]{:S(2)}) collective-permute-start(bf16[64,1024]{1,0:T(8,128)(2,1)} %own.1), channel_id=1, source_target_pairs={{0,4},{2,6},{4,0},{6,2},{1,5},{3,7},{5,1},{7,3},{8,12},{10,14},{12... | collective-permute-start | bytes 393224 | tf_op jit(solution)/shard_map/ppermute | solution.py:21
  6.9 10.5 %collective-permute-start.1 = (bf16[64,1024]{1,0:T(8,128)(2,1)}, bf16[64,1024]{1,0:T(8,128)(2,1)S(1)}, u32[]{:S(2)}, u32[]{:S(2)}) collective-permute-start(bf16[64,1024]{1,0:T(8,128)(2,1)} %own.1), channel_id=1, source_target_pairs={{0,6},{2,0},{4,2},{6,4},{1,7},{3,1},{5,3},{7,5},{8,14},{10,8},{12,... | collective-permute-start | bytes 393224 | tf_op jit(solution)/shard_map/ppermute | solution.py:21
  8.1 9.4 %collective-permute-start = (bf16[64,1024]{1,0:T(8,128)(2,1)}, bf16[64,1024]{1,0:T(8,128)(2,1)S(1)}, u32[]{:S(2)}, u32[]{:S(2)}) collective-permute-start(bf16[64,1024]{1,0:T(8,128)(2,1)} %own.1), channel_id=1, source_target_pairs={{0,2},{2,4},{4,6},{6,0},{1,3},{3,5},{5,7},{7,1},{8,10},{10,12},{12... | collective-permute-start | bytes 393224 | tf_op jit(solution)/shard_map/ppermute | solution.py:21
  10.3 7.1 %copy-start = (bf16[64,1024]{1,0:T(8,128)(2,1)S(1)}, bf16[64,1024]{1,0:T(8,128)(2,1)}, u32[]{:S(2)}) copy-start(bf16[64,1024]{1,0:T(8,128)(2,1)} %own.1) | copy-start | bytes 393220
  18.1 5.5 %collective-permute-start.4 = (bf16[256,1024]{1,0:T(8,128)(2,1)S(1)}, bf16[256,1024]{1,0:T(8,128)(2,1)S(1)}, u32[]{:S(2)}, u32[]{:S(2)}) collective-permute-start(bf16[256,1024]{1,0:T(8,128)(2,1)S(1)} %shard_map.76.own.refs_0_), channel_id=1, source_target_pairs={{0,1},{1,0},{2,3},{3,2},{4,5},{5,4},{6,7},{7,6},{8,9},{9,8},{10,11... | collective-permute-start | bytes 1572872 | tf_op jit(solution)/shard_map/ppermute | solution.py:21
  18.2 21.7 %collective-permute-start.7 = (bf16[256,1024]{1,0:T(8,128)(2,1)S(1)}, bf16[256,1024]{1,0:T(8,128)(2,1)}, u32[]{:S(2)}, u32[]{:S(2)}) collective-permute-start(bf16[256,1024]{1,0:T(8,128)(2,1)S(1)} %shard_map.76.own.refs_0_), channel_id=1, source_target_pairs={{0,192},{64,0},{128,64},{192,128},{1,193},{65,1},{129,65},{193,129... | collective-permute-start | bytes 1572872 | tf_op jit(solution)/shard_map/ppermute | solution.py:21
  19.3 20.8 %collective-permute-start.5 = (bf16[256,1024]{1,0:T(8,128)(2,1)S(1)}, bf16[256,1024]{1,0:T(8,128)(2,1)}, u32[]{:S(2)}, u32[]{:S(2)}) collective-permute-start(bf16[256,1024]{1,0:T(8,128)(2,1)S(1)} %shard_map.76.own.refs_0_), channel_id=1, source_target_pairs={{0,64},{64,128},{128,192},{192,0},{1,65},{65,129},{129,193},{193,1... | collective-permute-start | bytes 1572872 | tf_op jit(solution)/shard_map/ppermute | solution.py:21
  20.3 20.1 %collective-permute-start.11 = (bf16[64,1024]{1,0:T(8,128)(2,1)S(1)}, bf16[64,1024]{1,0:T(8,128)(2,1)S(1)}, u32[]{:S(2)}, u32[]{:S(2)}) collective-permute-start(bf16[64,1024]{1,0:T(8,128)(2,1)S(1)} %collective-permute-done.3.refs_1_.own), channel_id=1, source_target_pairs={{0,4},{2,6},{4,0},{6,2},{1,5},{3,7},{5,1},{7,3},{8,12},{10,14},{12... | collective-permute-start | bytes 393224 | tf_op jit(solution)/shard_map/ppermute | solution.py:21
  20.9 19.5 %collective-permute-start.10 = (bf16[64,1024]{1,0:T(8,128)(2,1)S(1)}, bf16[64,1024]{1,0:T(8,128)(2,1)S(1)}, u32[]{:S(2)}, u32[]{:S(2)}) collective-permute-start(bf16[64,1024]{1,0:T(8,128)(2,1)S(1)} %collective-permute-done.3.refs_1_.own), channel_id=1, source_target_pairs={{0,6},{2,0},{4,2},{6,4},{1,7},{3,1},{5,3},{7,5},{8,14},{10,8},{12,... | collective-permute-start | bytes 393224 | tf_op jit(solution)/shard_map/ppermute | solution.py:21
  23.5 16.9 %collective-permute-start.9 = (bf16[64,1024]{1,0:T(8,128)(2,1)S(1)}, bf16[64,1024]{1,0:T(8,128)(2,1)S(1)}, u32[]{:S(2)}, u32[]{:S(2)}) collective-permute-start(bf16[64,1024]{1,0:T(8,128)(2,1)S(1)} %collective-permute-done.3.refs_1_.own), channel_id=1, source_target_pairs={{0,2},{2,4},{4,6},{6,0},{1,3},{3,5},{5,7},{7,1},{8,10},{10,12},{12... | collective-permute-start | bytes 393224 | tf_op jit(solution)/shard_map/ppermute | solution.py:21
  30.7 14.1 %all-to-all-start = ((f32[32,4,128]{2,1,0:T(4,128)}), f32[32,4,128]{2,1,0:T(4,128)S(1)}, u32[]{:S(2)}, u32[]{:S(2)}) async-start(f32[32,4,128]{2,1,0:T(4,128)} %get-tuple-element.17.ahead), calls=%async_computation | async-start | bytes 131072 | tf_op jit(solution)/shard_map/all_to_all | solution.py:357
  39.9 5.9 %collective-permute-start.8 = (bf16[256,1024]{1,0:T(8,128)(2,1)}, bf16[256,1024]{1,0:T(8,128)(2,1)}, u32[]{:S(2)}, u32[]{:S(2)}) collective-permute-start(bf16[256,1024]{1,0:T(8,128)(2,1)} %collective-permute-done.7.refs_4_), channel_id=1, source_target_pairs={{0,1},{1,0},{2,3},{3,2},{4,5},{5,4},{6,7},{7,6},{8,9},{9,8},{10,11... | collective-permute-start | bytes 1572872 | tf_op jit(solution)/shard_map/ppermute | solution.py:21
  40.1 5.7 %collective-permute-start.6 = (bf16[256,1024]{1,0:T(8,128)(2,1)}, bf16[256,1024]{1,0:T(8,128)(2,1)}, u32[]{:S(2)}, u32[]{:S(2)}) collective-permute-start(bf16[256,1024]{1,0:T(8,128)(2,1)} %collective-permute-done.5.refs_2_), channel_id=1, source_target_pairs={{0,1},{1,0},{2,3},{3,2},{4,5},{5,4},{6,7},{7,6},{8,9},{9,8},{10,11... | collective-permute-start | bytes 1572872 | tf_op jit(solution)/shard_map/ppermute | solution.py:21
  45.4 2.2 %collective-permute-start.12 = (bf16[256,1024]{1,0:T(8,128)(2,1)S(1)}, bf16[256,1024]{1,0:T(8,128)(2,1)S(1)}, u32[]{:S(2)}, u32[]{:S(2)}) collective-permute-start(bf16[256,1024]{1,0:T(8,128)(2,1)S(1)} %shard_map.79.refs_6_), channel_id=1, source_target_pairs={{0,1},{1,0},{2,3},{3,2},{4,5},{5,4},{6,7},{7,6},{8,9},{9,8},{10,11... | collective-permute-start | bytes 1572872 | tf_op jit(solution)/shard_map/ppermute | solution.py:21
  62.7 13.3 %copy-start.2 = (f32[1024]{0:T(1024)S(1)}, f32[1024]{0:T(1024)}, u32[]{:S(2)}) copy-start(f32[1024]{0:T(1024)} %param.7) | copy-start | bytes 12292
  62.7 43.4 %all-to-all-start.1 = ((bf16[32,40,512]{2,1,0:T(8,128)(2,1)}), bf16[32,40,512]{2,1,0:T(8,128)(2,1)}, u32[]{:S(2)}, u32[]{:S(2)}) async-start(bf16[32,40,512]{2,1,0:T(8,128)(2,1)} %get-tuple-element.25), calls=%async_computation.1 | async-start | bytes 2621440 | tf_op jit(solution)/shard_map/all_to_all | solution.py:370
  72.1 26.1 %collective-permute-start.14 = (bf16[128,2048]{1,0:T(8,128)(2,1)}, bf16[128,2048]{1,0:T(8,128)(2,1)S(1)}, u32[]{:S(2)}, u32[]{:S(2)}) collective-permute-start(bf16[128,2048]{1,0:T(8,128)(2,1)} %get-tuple-element.21), channel_id=1, source_target_pairs={{0,2},{2,4},{4,6},{6,0},{1,3},{3,5},{5,7},{7,1},{8,10},{10,12},{12... | collective-permute-start | bytes 1572872 | tf_op jit(solution)/shard_map/ppermute | solution.py:21
  72.8 26.2 %collective-permute-start.16 = (bf16[128,2048]{1,0:T(8,128)(2,1)S(1)}, bf16[128,2048]{1,0:T(8,128)(2,1)S(1)}, u32[]{:S(2)}, u32[]{:S(2)}) collective-permute-start(bf16[128,2048]{1,0:T(8,128)(2,1)S(1)} %get-tuple-element.22), channel_id=1, source_target_pairs={{0,4},{2,6},{4,0},{6,2},{1,5},{3,7},{5,1},{7,3},{8,12},{10,14},{12... | collective-permute-start | bytes 1572872 | tf_op jit(solution)/shard_map/ppermute | solution.py:21
  74.9 25.3 %collective-permute-start.18 = (bf16[128,2048]{1,0:T(8,128)(2,1)}, bf16[128,2048]{1,0:T(8,128)(2,1)S(1)}, u32[]{:S(2)}, u32[]{:S(2)}) collective-permute-start(bf16[128,2048]{1,0:T(8,128)(2,1)} %get-tuple-element.23), channel_id=1, source_target_pairs={{0,6},{2,0},{4,2},{6,4},{1,7},{3,1},{5,3},{7,5},{8,14},{10,8},{12,... | collective-permute-start | bytes 1572872 | tf_op jit(solution)/shard_map/ppermute | solution.py:21
  77.4 24.2 %collective-permute-start.13 = (bf16[64,2048]{1,0:T(8,128)(2,1)S(1)}, bf16[64,2048]{1,0:T(8,128)(2,1)S(1)}, u32[]{:S(2)}, u32[]{:S(2)}) collective-permute-start(bf16[64,2048]{1,0:T(8,128)(2,1)S(1)} %get-tuple-element.20), channel_id=1, source_target_pairs={{0,1},{1,0},{2,3},{3,2},{4,5},{5,4},{6,7},{7,6},{8,9},{9,8},{10,11... | collective-permute-start | bytes 786440 | tf_op jit(solution)/shard_map/ppermute | solution.py:21
  99.0 2.6 %collective-permute-start.15 = (bf16[64,2048]{1,0:T(8,128)(2,1)}, bf16[64,2048]{1,0:T(8,128)(2,1)S(1)}, u32[]{:S(2)}, u32[]{:S(2)}) collective-permute-start(bf16[64,2048]{1,0:T(8,128)(2,1)} %slice.24), channel_id=1, source_target_pairs={{0,1},{1,0},{2,3},{3,2},{4,5},{5,4},{6,7},{7,6},{8,9},{9,8},{10,11... | collective-permute-start | bytes 786440 | tf_op jit(solution)/shard_map/ppermute | solution.py:21
  99.7 1.9 %collective-permute-start.17 = (bf16[64,2048]{1,0:T(8,128)(2,1)}, bf16[64,2048]{1,0:T(8,128)(2,1)S(1)}, u32[]{:S(2)}, u32[]{:S(2)}) collective-permute-start(bf16[64,2048]{1,0:T(8,128)(2,1)} %slice.25), channel_id=1, source_target_pairs={{0,1},{1,0},{2,3},{3,2},{4,5},{5,4},{6,7},{7,6},{8,9},{9,8},{10,11... | collective-permute-start | bytes 786440 | tf_op jit(solution)/shard_map/ppermute | solution.py:21
  101.0 1.7 %collective-permute-start.19 = (bf16[64,2048]{1,0:T(8,128)(2,1)}, bf16[64,2048]{1,0:T(8,128)(2,1)S(1)}, u32[]{:S(2)}, u32[]{:S(2)}) collective-permute-start(bf16[64,2048]{1,0:T(8,128)(2,1)} %slice.26), channel_id=1, source_target_pairs={{0,1},{1,0},{2,3},{3,2},{4,5},{5,4},{6,7},{7,6},{8,9},{9,8},{10,11... | collective-permute-start | bytes 786440 | tf_op jit(solution)/shard_map/ppermute | solution.py:21
  (4 other events, 5.3 us)

commit v5 on v4

--- a/solution.py
+++ b/solution.py
@@ -13,7 +13,7 @@
 F32 = jnp.float32
 VMEM_LIMIT = 24 * 1024 * 1024
 VMEM = pltpu.VMEM
-SIZES = {"y": 4, "z": 8, "x": 4, "c": 2}
+SIZES = {"y": 4, "x": 4, "c": 2}
 
 
 def shift(value, axis, step):
@@ -45,37 +45,33 @@
     return [pl.BlockSpec(memory_space=pltpu.HBM)] * n
 
 
-def prepare_kernel(means, inv_var, weights, scaled, row, col):
+def prepare_kernel(means, inv_var, weights, scaled, row):
     values = means[...].astype(F32)
     product = values * inv_var[...]
     scaled[...] = product.astype(BF)
     square = values * product
     norm = functools.reduce(jnp.add, [square[:, i : i + 128] for i in range(0, 1024, 128)])
     norm = 0.5 * jnp.sum(norm, axis=1, keepdims=True)
-    for i in range(0, 256, 128):
-        part = weights[:, i : i + 128] - line(norm[i : i + 128])
-        row[:, i : i + 128] = part
-        col[i : i + 128, :] = column(part)
+    for i in range(0, 512, 128):
+        row[:, i : i + 128] = weights[:, i : i + 128] - line(norm[i : i + 128])
 
 
 def prepare(means, inv_var, log_weights):
     return pl.pallas_call(
         prepare_kernel,
-        grid=(8,),
+        grid=(4,),
         in_specs=[
-            pl.BlockSpec((256, 1024), lambda i: (i, 0)),
+            pl.BlockSpec((512, 1024), lambda i: (i, 0)),
             pl.BlockSpec((1, 1024), lambda i: (0, 0)),
-            pl.BlockSpec((1, 256), lambda i: (0, i)),
+            pl.BlockSpec((1, 512), lambda i: (0, i)),
         ],
         out_specs=(
-            pl.BlockSpec((256, 1024), lambda i: (i, 0)),
-            pl.BlockSpec((1, 256), lambda i: (0, i)),
-            pl.BlockSpec((256, 1), lambda i: (i, 0)),
+            pl.BlockSpec((512, 1024), lambda i: (i, 0)),
+            pl.BlockSpec((1, 512), lambda i: (0, i)),
         ),
         out_shape=(
             pltpu.HBM((2048, 1024), BF),
             jax.ShapeDtypeStruct((1, 2048), F32),
-            jax.ShapeDtypeStruct((2048, 1), F32),
         ),
         compiler_params=params(),
         cost_estimate=pl.CostEstimate(flops=6 << 21, bytes_accessed=8 << 20, transcendentals=0),
@@ -176,10 +172,41 @@
     return top + jnp.log(jnp.sum(jnp.exp(shares - top[None]), axis=0))
 
 
+def split_count(count):
+    high = count.astype(BF).astype(F32)
+    return jnp.concatenate([high, count - high, jnp.zeros((6, 512), F32)], axis=0).astype(BF)
+
+
+def add_kernel(kept, got_a, got_b, *refs):
+    out = refs[-1]
+    other = jnp.concatenate([got_a[...], got_b[...]], axis=2).astype(F32)
+    mine = kept[...].astype(F32)
+    out[:, 0:32, :] = (mine[:, 0:32, :] + other[:, 0:32, :]).astype(BF)
+    tails = mine[0, 32:34, :] + other[0, 32:34, :]
+    count = tails[0:1, :] + tails[1:2, :]
+    out[:, 32:40, :] = jnp.broadcast_to(split_count(count)[None], (4, 8, 512))
+
+
+def added(kept, got_a, got_b, *first):
+    return pl.pallas_call(
+        add_kernel,
+        grid=(4,),
+        in_specs=[
+            pl.BlockSpec((4, 40, 512), lambda i: (i, 0, 0)),
+            pl.BlockSpec((4, 40, 256), lambda i: (i, 0, 0)),
+            pl.BlockSpec((4, 40, 256), lambda i: (i, 0, 0)),
+        ]
+        + anywhere(len(first)),
+        out_specs=pl.BlockSpec((4, 40, 512), lambda i: (i, 0, 0)),
+        out_shape=pltpu.HBM((16, 40, 512), BF),
+        compiler_params=params(),
+    )(still(kept), got_a, got_b, *first)
+
+
 def sums_kernel(at, shares, scaled, bias, *refs):
     pieces = refs[:8]
-    sums = refs[8]
-    rows, weights, lse, sems = refs[9:]
+    kept, away_a, away_b = refs[9:12]
+    rows, weights, lse, wide, sems = refs[12:]
     copies = [
         pltpu.make_async_copy(piece, rows.at[pl.ds(i * 256, 256)], sems.at[i])
         for i, piece in enumerate(pieces)
@@ -189,6 +216,9 @@
     y, c = at[2], at[1]
     for yy in range(4):
         lse[pl.ds(yy * 4, 4), :] = joined(shares[yy])
+    for b in range(0, 512, 128):
+        wide[b : b + 128, :] = jnp.transpose(jnp.broadcast_to(bias[:, b : b + 128], (128, 128)))
+    shift_up = jnp.concatenate([wide[...], wide[...]], axis=1)
     count = jnp.zeros((512, 128), F32)
     for i in range(8):
         there = lax.rem(y + (0, 3, 1, 2)[i // 2], 4)
@@ -200,14 +230,16 @@
         score = lax.dot_general(
             scaled[...], rows[cut, :], (((1,), (1,)), ((), ())), preferred_element_type=F32
         )
-        weight = jnp.exp(score + bias[...] - norm).astype(BF)
+        weight = jnp.exp(score + shift_up - norm).astype(BF)
         weights[:, cut] = weight
         count = count + weight[:, :128].astype(F32) + weight[:, 128:].astype(F32)
     count = jnp.sum(count, axis=1, keepdims=True)
     count = jnp.concatenate([line(count[b : b + 128]) for b in range(0, 512, 128)], axis=1)
-    high = count.astype(BF).astype(F32)
-    tail = jnp.concatenate([high, count - high, jnp.zeros((6, 512), F32)], axis=0).astype(BF)
-    sums[:, 32:40, :] = jnp.broadcast_to(tail[None], (32, 8, 512))
+    tail = jnp.broadcast_to(split_count(count)[None], (16, 8, 512))
+    kept[:, 32:40, :] = tail
+    away_a[:, 32:40, :] = tail[:, :, :256]
+    away_b[:, 32:40, :] = tail[:, :, 256:]
+    even = at[4] == 0
     for j in range(4):
         block = lax.dot_general(
             weights[...],
@@ -215,10 +247,17 @@
             (((1,), (0,)), ((), ())),
             preferred_element_type=F32,
         )
-        sums[j * 8 : j * 8 + 8, 0:32, :] = jnp.transpose(block.astype(BF)).reshape(8, 32, 512)
-
-
-def partial_sums(at, shares, scaled, bias_col, pieces):
+        block = jnp.transpose(block.astype(BF))
+        for h in range(4):
+            first = block[h * 64 : h * 64 + 32, :]
+            second = block[h * 64 + 32 : h * 64 + 64, :]
+            kept[j * 4 + h, 0:32, :] = jnp.where(even, first, second)
+            other = jnp.where(even, second, first)
+            away_a[j * 4 + h, 0:32, :] = other[:, :256]
+            away_b[j * 4 + h, 0:32, :] = other[:, 256:]
+
+
+def partial_sums(at, shares, scaled, bias_row, pieces, first):
     return pl.pallas_call(
         sums_kernel,
         grid_spec=pltpu.PrefetchScalarGridSpec(
@@ -227,28 +266,30 @@
             in_specs=[
                 pl.BlockSpec((4, 8, 4, 128), lambda i, at: (0, 0, 0, 0)),
                 pl.BlockSpec((512, 1024), lambda i, at: (at[2], 0)),
-                pl.BlockSpec((512, 1), lambda i, at: (at[2], 0)),
+                pl.BlockSpec((1, 512), lambda i, at: (0, at[2])),
             ]
-            + anywhere(8),
-            out_specs=pl.BlockSpec((32, 40, 512), lambda i, at: (0, 0, 0)),
+            + anywhere(9),
+            out_specs=[
+                pl.BlockSpec((16, 40, width), lambda i, at: (0, 0, 0)) for width in (512, 256, 256)
+            ],
             scratch_shapes=[
                 VMEM((2048, 1024), BF),
                 VMEM((512, 2048), BF),
                 VMEM((16, 128), F32),
+                VMEM((512, 128), F32),
                 pltpu.SemaphoreType.DMA((8,)),
             ],
         ),
-        out_shape=pltpu.HBM((32, 40, 512), BF),
+        out_shape=[pltpu.HBM((16, 40, width), BF) for width in (512, 256, 256)],
         compiler_params=params(),
         cost_estimate=pl.CostEstimate(
             flops=4 * 512 * 2048 * 1024, bytes_accessed=8 << 20, transcendentals=1 << 20
         ),
-    )(at, shares, still(scaled), bias_col, *pieces)
-
-
-def resp_kernel(at, shares, score, sums, *refs):
-    del sums
-    outs, norm, held, sems = refs[:5], refs[6], refs[7], refs[8]
+    )(at, shares, still(scaled), bias_row, *pieces, first)
+
+
+def resp_kernel(at, shares, score, *refs):
+    outs, norm, held, sems = refs[:5], refs[5], refs[6], refs[7]
     x, c, y = at[0], at[1], at[2]
     copies = []
     for j in range(8):
@@ -273,23 +314,21 @@
             outs[1 + j % 4][j // 4 * 64 : j // 4 * 64 + 64, :] = block
 
 
-def responsibilities(at, shares, score, sums):
+def responsibilities(at, shares, score):
     return pl.pallas_call(
         resp_kernel,
-        in_specs=[scalar(), whole()] + hbm(2),
-        out_specs=[whole()] * 5 + hbm(),
-        input_output_aliases={3: 5},
+        in_specs=[scalar(), whole()] + hbm(),
+        out_specs=[whole()] * 5,
         scratch_shapes=[
             VMEM((512, 128), F32),
             VMEM((8, 64, 2048), F32),
             pltpu.SemaphoreType.DMA((8,)),
         ],
         out_shape=[jax.ShapeDtypeStruct((64, 2048), BF)] * 2
-        + [jax.ShapeDtypeStruct((128, 2048), BF)] * 3
-        + [pltpu.HBM((32, 40, 512), BF)],
+        + [jax.ShapeDtypeStruct((128, 2048), BF)] * 3,
         compiler_params=params(),
         cost_estimate=pl.CostEstimate(flops=1 << 21, bytes_accessed=6 << 20, transcendentals=1 << 20),
-    )(at, shares, still(score), sums)
+    )(at, shares, still(score))
 
 
 def cut_kernel(at, means, ahead, out, turned):
@@ -338,15 +377,16 @@
         scratch_shapes=[pltpu.SemaphoreType.DMA((8,))],
         out_shape=jax.ShapeDtypeStruct((64, 16384), BF),
         compiler_params=params(),
+        cost_estimate=pl.CostEstimate(flops=0, bytes_accessed=4 << 20, transcendentals=0),
     )(at, *pieces)
 
 
 def body(points, means, log_weights, inv_var):
-    x, c, y, z = (lax.axis_index(a) for a in "xcyz")
-    at = jnp.stack([x, c, y, y * 8 + z]).astype(jnp.int32)
+    x, c, y, h, l = (lax.axis_index(a) for a in "xcyhl")
+    at = jnp.stack([x, c, y, y * 8 + h * 2 + l, l]).astype(jnp.int32)
 
     far = shift(points, "y", 2)
-    scaled, bias_row, bias_col = prepare(means, inv_var, log_weights)
+    scaled, bias_row = prepare(means, inv_var, log_weights)
 
     own = gather_x(at, points, (scaled,), (far,))
     other = shift(own, "c", 1)
@@ -362,15 +402,20 @@
     for mine in (before, after, far):
         pieces += [mine, shift(mine, "c", 1)]
 
-    sums = partial_sums(at, shares, scaled, bias_col, pieces)
-    *blocks, sums = responsibilities(at, shares, score, sums)
+    blocks = responsibilities(at, shares, score)
     pairs = [shift(b, "x", j + 1) for j, b in enumerate(blocks[2:])]
+    kept, away_a, away_b = partial_sums(at, shares, scaled, bias_row, pieces, blocks[0])
+    near = [(z, z ^ 1) for z in range(8)]
+    got_a = lax.ppermute(away_a, ("h", "l"), near)
+    near = [(z, (z + (1 if z % 2 else 7)) % 8) for z in range(8)]
+    got_b = lax.ppermute(away_b, ("h", "l"), near)
+    sums = added(kept, got_a, got_b, *pairs)
+    sent = lax.all_to_all(sums, ("y", "h"), split_axis=0, concat_axis=0, tiled=True)
     theirs = [shift(b, "c", 1) for b in [blocks[0]] + [pair[:64] for pair in pairs]]
     held = theirs + [blocks[1]] + pairs
-    sent = lax.all_to_all(sums, ("y", "z"), split_axis=0, concat_axis=0, tiled=True)
     resp_rows = lay_out(at, held)
 
-    sums = jnp.sum(sent.reshape(4, 8, 40, 512).astype(F32), axis=1)
+    sums = jnp.sum(sent.reshape(4, 4, 40, 512).astype(F32), axis=1)
     counts = (sums[:, 32, :] + sums[:, 33, :]).reshape(2048)
     sums = sums[:, :32, :].transpose(1, 0, 2).reshape(32, 2048)
     new_means_t = (sums + mean_cols) / (counts[None, :] + 1.0)
@@ -384,9 +429,9 @@
 
 
 def solution(mesh):
-    axes = ("y", "z", "x", "c")
-    mesh = Mesh(mesh.devices.reshape(4, 8, 4, 2), axes)
-    comp, pt = ("x", "c"), ("y", "z")
+    axes = ("y", "h", "l", "x", "c")
+    mesh = Mesh(mesh.devices.reshape(4, 4, 2, 4, 2), axes)
+    comp, pt = ("x", "c"), ("y", "h", "l")
     return jax.shard_map(
         body,
         mesh=mesh,

time: 109 us -> 111 us (1.018)
  waiting for transfers between devices: 29.6 us -> 26.2 us
  starting transfers between devices: 35.2 us -> 37.7 us
  local copies, waits for them, and re-layouts: 3.67 us -> 4.79 us
    ppermute x20, waiting for transfers between devices: 23.7 us -> 8.96 us  [shift(): return lax.ppermute(value, axis, [(i, (i + step) % n) for i in range(n)])]
    all_to_all x1, waiting for transfers between devices: 1.46 us -> 12.8 us  [body(): lax.all_to_all(sums, ('y', 'h'), split_axis=0, concat_axis=0, tiled=True)]
    ppermute x0 -> x2, starting transfers between devices: none -> 3.92 us  [the longest x1 3.72 us: body(): got_b = lax.ppermute(away_b, ('h', 'l'), near)]
    all_to_all x1, starting transfers between devices: 6.59 us -> 4.69 us  [body(): lax.all_to_all(share, ('y', 'x', 'c'), split_axis=0, concat_axis=0, tiled...]
    ppermute x20, starting transfers between devices: 19.1 us -> 20.7 us  [shift(): return lax.ppermute(value, axis, [(i, (i + step) % n) for i in range(n)])]
    unnamed x13 -> x15, local copies, waits for them, and re-layouts: 1.42 us -> 2.46 us
    pallas_call x2 -> x3, Pallas kernels: 10.7 us -> 11.4 us  [the longest x1 5.21 us: prepare(): pl.pallas_call(prepare_kernel, grid=(4,), in_specs=[pl.BlockSpec((512, 10...]
  transfers between devices with their start and end apart: 22 -> 24, of which waited for: 5 -> 4; matrix products, arithmetic and copies ran while one was open for 3% -> 3% of each run, Pallas kernels for 18% -> 29%
where the time goes in v5:
time: 111 us; the launch traced here: 110 us
  starting transfers between devices  37.7 us (34%)
  Pallas kernels  35.5 us (32%)
  waiting for transfers between devices  26.2 us (24%)
  local copies, waits for them, and re-layouts  4.79 us (4%)
  other arithmetic  4.26 us (4%)
  between operations  1.49 us (1%)
    ppermute x20, starting transfers between devices, shift(): return lax.ppermute(value, axis, [(i, (i + step) % n) for i in range(n)])  20.7 us
    all_to_all x1, waiting for transfers between devices, body(): lax.all_to_all(sums, ('y', 'h'), split_axis=0, concat_axis=0, tiled=True)  12.8 us
    pallas_call x1, Pallas kernels, partial_sums(): pl.pallas_call(sums_kernel, grid_spec=pltpu.PrefetchScalarGridSpec(num_sc...  11.3 us
    ppermute x20, waiting for transfers between devices, shift(): return lax.ppermute(value, axis, [(i, (i + step) % n) for i in range(n)])  8.96 us
    all_to_all x1, starting transfers between devices, body(): lax.all_to_all(sums, ('y', 'h'), split_axis=0, concat_axis=0, tiled=True)  8.41 us
    pallas_call x1, Pallas kernels, scores(): pl.pallas_call(score_kernel, grid=(2048 // width,), out_shape=(pltpu.HBM(...  7.25 us
    pallas_call x1, Pallas kernels, prepare(): pl.pallas_call(prepare_kernel, grid=(4,), in_specs=[pl.BlockSpec((512, 10...  5.21 us
    all_to_all x1, starting transfers between devices, body(): lax.all_to_all(share, ('y', 'x', 'c'), split_axis=0, concat_axis=0, tiled...  4.69 us
  transfers between devices with their start and end apart: 24, of which 4 were waited for; matrix products, arithmetic and copies ran while one was open for 3% of the time, Pallas kernels for 29%

profile of v5, /device:TPU:32, one launch (start us, length us, event | category | flops | bytes accessed | tf_op | source)
XLA Modules:
  0.0 110.0 jit_solution(14163177270864113698)
XLA Ops:
  0.6 3.3 %collective-permute-start.3 = (bf16[64,1024]{1,0:T(8,128)(2,1)}, bf16[64,1024]{1,0:T(8,128)(2,1)S(1)}, u32[]{:S(2)}, u32[]{:S(2)}) collective-permute-start(bf16[64,1024]{1,0:T(8,128)(2,1)} %own.1), channel_id=1, source_target_pairs={{0,128},{64,192},{128,0},{192,64},{1,129},{65,193},{129,1},{193,65... | collective-permute-start | bytes 393224 | tf_op jit(solution)/shard_map/ppermute | solution.py:21
  3.9 1.5 %collective-permute-start = (bf16[64,1024]{1,0:T(8,128)(2,1)}, bf16[64,1024]{1,0:T(8,128)(2,1)S(1)}, u32[]{:S(2)}, u32[]{:S(2)}) collective-permute-start(bf16[64,1024]{1,0:T(8,128)(2,1)} %own.1), channel_id=1, source_target_pairs={{0,2},{2,4},{4,6},{6,0},{1,3},{3,5},{5,7},{7,1},{8,10},{10,12},{12... | collective-permute-start | bytes 393224 | tf_op jit(solution)/shard_map/ppermute | solution.py:21
  5.4 1.7 %collective-permute-start.1 = (bf16[64,1024]{1,0:T(8,128)(2,1)}, bf16[64,1024]{1,0:T(8,128)(2,1)S(1)}, u32[]{:S(2)}, u32[]{:S(2)}) collective-permute-start(bf16[64,1024]{1,0:T(8,128)(2,1)} %own.1), channel_id=1, source_target_pairs={{0,6},{2,0},{4,2},{6,4},{1,7},{3,1},{5,3},{7,5},{8,14},{10,8},{12,... | collective-permute-start | bytes 393224 | tf_op jit(solution)/shard_map/ppermute | solution.py:21
  7.2 1.8 %collective-permute-start.2 = (bf16[64,1024]{1,0:T(8,128)(2,1)}, bf16[64,1024]{1,0:T(8,128)(2,1)S(1)}, u32[]{:S(2)}, u32[]{:S(2)}) collective-permute-start(bf16[64,1024]{1,0:T(8,128)(2,1)} %own.1), channel_id=1, source_target_pairs={{0,4},{2,6},{4,0},{6,2},{1,5},{3,7},{5,1},{7,3},{8,12},{10,14},{12... | collective-permute-start | bytes 393224 | tf_op jit(solution)/shard_map/ppermute | solution.py:21
  10.4 5.2 %shard_map.75 = (bf16[2048,1024]{1,0:T(8,128)(2,1)}, f32[1,2048]{1,0:T(1,128)S(1)}) custom-call(bf16[2048,1024]{1,0:T(8,128)(2,1)} %means.3, f32[1,1024]{1,0:T(1,128)S(1)} %bitcast.30, f32[1,2048]{1,0:T(1,128)S(1)} %bitcast.31), custom_call_target="tpu_custom_call" | custom-call | flops 12582912 | bytes 8388608 | tf_op jit(solution)/shard_map/pallas_call | solution.py:60
  17.1 2.6 %collective-permute-start.14 = (bf16[256,1024]{1,0:T(8,128)(2,1)S(1)}, bf16[256,1024]{1,0:T(8,128)(2,1)}, u32[]{:S(2)}, u32[]{:S(2)}) collective-permute-start(bf16[256,1024]{1,0:T(8,128)(2,1)S(1)} %shard_map.76.own.refs_0_), channel_id=1, source_target_pairs={{0,192},{64,0},{128,64},{192,128},{1,193},{65,1},{129,65},{193,129... | collective-permute-start | bytes 1572872 | tf_op jit(solution)/shard_map/ppermute | solution.py:21
  20.3 2.6 %collective-permute-start.17 = (bf16[64,1024]{1,0:T(8,128)(2,1)S(1)}, bf16[64,1024]{1,0:T(8,128)(2,1)S(1)}, u32[]{:S(2)}, u32[]{:S(2)}) collective-permute-start(bf16[64,1024]{1,0:T(8,128)(2,1)S(1)} %collective-permute-done.3.refs_1_.own), channel_id=1, source_target_pairs={{0,6},{2,0},{4,2},{6,4},{1,7},{3,1},{5,3},{7,5},{8,14},{10,8},{12,... | collective-permute-start | bytes 393224 | tf_op jit(solution)/shard_map/ppermute | solution.py:21
  23.4 7.3 %shard_map.77 = (f32[512,2048]{1,0:T(8,128)}, f32[32,4,128]{2,1,0:T(4,128)}) custom-call(s32[5]{0:T(128)S(1)} %stack.23.at, bf16[256,1024]{1,0:T(8,128)(2,1)S(1)} %shard_map.76.own.refs_0_, bf16[256,1024]{1,0:T(8,128)(2,1)S(1)} %collective-permute-done.4.other.refs_1_, bf16[2048,1024]{1,0:T(8,128)(2,1)} %get-tuple-element.16.refs_0_.scaled, ...), custom_call_target="tpu_custom_call" | custom-call | flops 2147483648 | bytes 9437184 | tf_op jit(solution)/shard_map/pallas_call | solution.py:144
  30.7 4.7 %all-to-all-start = ((f32[32,4,128]{2,1,0:T(4,128)}), f32[32,4,128]{2,1,0:T(4,128)S(1)}, u32[]{:S(2)}, u32[]{:S(2)}) async-start(f32[32,4,128]{2,1,0:T(4,128)} %get-tuple-element.18.ahead), calls=%async_computation | async-start | bytes 131072 | tf_op jit(solution)/shard_map/all_to_all | solution.py:397
  35.4 2.5 %shard_map.80.refs_0_ = f32[32,2048]{1,0:T(8,128)} custom-call(s32[5]{0:T(128)S(1)} %stack.23.at, bf16[2048,1024]{1,0:T(8,128)(2,1)} %means.3, f32[32,4,128]{2,1,0:T(4,128)} %get-tuple-element.18.ahead), custom_call_target="tpu_custom_call" | custom-call | tf_op jit(solution)/shard_map/pallas_call | solution.py:342
  38.4 4.4 %all-to-all-done.refs_1_ = f32[32,4,128]{2,1,0:T(4,128)S(1)} async-done(((f32[32,4,128]{2,1,0:T(4,128)}), f32[32,4,128]{2,1,0:T(4,128)S(1)}, u32[]{:S(2)}, u32[]{:S(2)}) %all-to-all-start) | async-done | bytes 65568 | tf_op jit(solution)/shard_map/all_to_all | solution.py:397
  43.7 2.9 %shard_map.78 = (bf16[64,2048]{1,0:T(8,128)(2,1)S(1)}, bf16[64,2048]{1,0:T(8,128)(2,1)S(1)}, bf16[128,2048]{1,0:T(8,128)(2,1)S(1)}, bf16[128,2048]{1,0:T(8,128)(2,1)S(1)}, bf16[128,2048]{1,0:T(8,128)(2,1)S(1)}) custom-call(s32[5]{0:T(128)S(1)} %stack.23.at, f32[4,8,4,128]{3,2,1,0:T(4,128)S(1)} %bitcast.26, f32[512,2048]{1,0:T(8,128)} %get-tuple-element.19.score), custom_call_target="tpu_custom_call" | custom-call | flops 2097152 | bytes 6291456 | tf_op jit(solution)/shard_map/pallas_call | solution.py:318
  46.6 1.5 %collective-permute-start.10 = (bf16[128,2048]{1,0:T(8,128)(2,1)S(1)}, bf16[128,2048]{1,0:T(8,128)(2,1)S(1)}, u32[]{:S(2)}, u32[]{:S(2)}) collective-permute-start(bf16[128,2048]{1,0:T(8,128)(2,1)S(1)} %get-tuple-element.23), channel_id=1, source_target_pairs={{0,6},{2,0},{4,2},{6,4},{1,7},{3,1},{5,3},{7,5},{8,14},{10,8},{12,... | collective-permute-start | bytes 1572872 | tf_op jit(solution)/shard_map/ppermute | solution.py:21
  48.9 1.1 %collective-permute-start.8 = (bf16[128,2048]{1,0:T(8,128)(2,1)S(1)}, bf16[128,2048]{1,0:T(8,128)(2,1)S(1)}, u32[]{:S(2)}, u32[]{:S(2)}) collective-permute-start(bf16[128,2048]{1,0:T(8,128)(2,1)S(1)} %get-tuple-element.22), channel_id=1, source_target_pairs={{0,4},{2,6},{4,0},{6,2},{1,5},{3,7},{5,1},{7,3},{8,12},{10,14},{12... | collective-permute-start | bytes 1572872 | tf_op jit(solution)/shard_map/ppermute | solution.py:21
  50.0 1.0 copy-done.5
  51.1 11.3 %shard_map.82 = (bf16[16,40,512]{2,1,0:T(8,128)(2,1)}, bf16[16,40,256]{2,1,0:T(8,128)(2,1)}, bf16[16,40,256]{2,1,0:T(8,128)(2,1)}) custom-call(s32[5]{0:T(128)S(1)} %stack.23.at, f32[4,8,4,128]{3,2,1,0:T(4,128)S(1)} %bitcast.27, bf16[2048,1024]{1,0:T(8,128)(2,1)} %get-tuple-element.16.refs_0_.scaled, f32[1,2048]{1,0:T(1,128)S(1)} %get-tuple-element.17.bias, ...), custom_call_target="tpu_custom_call" | custom-call | flops 4294967296 | bytes 8388608 | tf_op jit(solution)/shard_map/pallas_call | solution.py:261
  62.6 3.7 %collective-permute-start.21 = (bf16[16,40,256]{2,1,0:T(8,128)(2,1)}, bf16[16,40,256]{2,1,0:T(8,128)(2,1)S(1)}, u32[]{:S(2)}, u32[]{:S(2)}) collective-permute-start(bf16[16,40,256]{2,1,0:T(8,128)(2,1)} %get-tuple-element.27), channel_id=1, source_target_pairs={{0,56},{8,16},{16,8},{24,32},{32,24},{40,48},{48,40},{56,0},{1,57}... | collective-permute-start | bytes 983048 | tf_op jit(solution)/shard_map/ppermute | solution.py:411
  66.3 8.2 %collective-permute-done.6.refs_5_.refs_0_ = bf16[128,2048]{1,0:T(8,128)(2,1)S(1)} collective-permute-done((bf16[128,2048]{1,0:T(8,128)(2,1)S(1)}, bf16[128,2048]{1,0:T(8,128)(2,1)S(1)}, u32[]{:S(2)}, u32[]{:S(2)}) %collective-permute-start.6) | collective-permute-done | bytes 524320 | tf_op jit(solution)/shard_map/ppermute | solution.py:21
  74.5 3.3 %shard_map.83 = bf16[16,40,512]{2,1,0:T(8,128)(2,1)} custom-call(bf16[16,40,512]{2,1,0:T(8,128)(2,1)} %get-tuple-element.25.kept, bf16[16,40,256]{2,1,0:T(8,128)(2,1)S(1)} %collective-permute-done.20.got_a, bf16[16,40,256]{2,1,0:T(8,128)(2,1)S(1)} %collective-permute-done.21.got_b, bf16[128,2048]{1,0:T(8,128)(2,1)S(1)} %collective-permute-done.6.refs_5_.refs_0_, ...), custom_call_target="tpu_custom_call" | custom-call | tf_op jit(solution)/shard_map/pallas_call | solution.py:191
  77.7 8.4 %all-to-all-start.1 = ((bf16[16,40,512]{2,1,0:T(8,128)(2,1)}), bf16[16,40,512]{2,1,0:T(8,128)(2,1)}, u32[]{:S(2)}, u32[]{:S(2)}) async-start(bf16[16,40,512]{2,1,0:T(8,128)(2,1)} %shard_map.83), calls=%async_computation.1 | async-start | bytes 1310720 | tf_op jit(solution)/shard_map/all_to_all | solution.py:413
  92.3 1.9 %shard_map.79 = bf16[64,16384]{1,0:T(8,128)(2,1)} custom-call(s32[5]{0:T(128)S(1)} %stack.23.at, bf16[64,2048]{1,0:T(8,128)(2,1)S(1)} %collective-permute-done.5.refs_0_, bf16[64,2048]{1,0:T(8,128)(2,1)S(1)} %collective-permute-done.7.refs_1_, bf16[64,2048]{1,0:T(8,128)(2,1)S(1)} %collective-permute-done.9.refs_2_, ...), custom_call_target="tpu_custom_call" | custom-call | bytes 4194304 | tf_op jit(solution)/shard_map/pallas_call | solution.py:373
  94.2 12.8 %all-to-all-done.1 = bf16[16,40,512]{2,1,0:T(8,128)(2,1)} async-done(((bf16[16,40,512]{2,1,0:T(8,128)(2,1)}), bf16[16,40,512]{2,1,0:T(8,128)(2,1)}, u32[]{:S(2)}, u32[]{:S(2)}) %all-to-all-start.1) | async-done | bytes 655392 | tf_op jit(solution)/shard_map/all_to_all | solution.py:413
  107.0 1.2 %convert_reduce_fusion = f32[4,40,512]{2,1,0:T(8,128)S(1)} fusion(bf16[16,40,512]{2,1,0:T(8,128)(2,1)} %all-to-all-done.1), kind=kLoop, calls=%fused_computation | loop fusion | flops 573440 | bytes 983040 | tf_op jit(solution)/shard_map/reduce_sum | solution.py:418
  108.3 1.7 %add_divide_fusion = f32[32,2048]{1,0:T(8,128)} fusion(f32[32,2048]{1,0:T(8,128)S(1)} %bitcast.32, f32[32,2048]{1,0:T(8,128)} %shard_map.80.refs_0_, f32[2048]{0:T(1024)S(1)} %broadcast_add_fusion), kind=kLoop, calls=%fused_computation.3 | loop fusion | flops 131072 | bytes 794624 | tf_op jit(solution)/shard_map/div | solution.py:421
  (64 shorter events, 11.8 us)
Async XLA Ops:
  0.6 15.0 %collective-permute-start.3 = (bf16[64,1024]{1,0:T(8,128)(2,1)}, bf16[64,1024]{1,0:T(8,128)(2,1)S(1)}, u32[]{:S(2)}, u32[]{:S(2)}) collective-permute-start(bf16[64,1024]{1,0:T(8,128)(2,1)} %own.1), channel_id=1, source_target_pairs={{0,128},{64,192},{128,0},{192,64},{1,129},{65,193},{129,1},{193,65... | collective-permute-start | bytes 393224 | tf_op jit(solution)/shard_map/ppermute | solution.py:21
  3.9 11.7 %collective-permute-start = (bf16[64,1024]{1,0:T(8,128)(2,1)}, bf16[64,1024]{1,0:T(8,128)(2,1)S(1)}, u32[]{:S(2)}, u32[]{:S(2)}) collective-permute-start(bf16[64,1024]{1,0:T(8,128)(2,1)} %own.1), channel_id=1, source_target_pairs={{0,2},{2,4},{4,6},{6,0},{1,3},{3,5},{5,7},{7,1},{8,10},{10,12},{12... | collective-permute-start | bytes 393224 | tf_op jit(solution)/shard_map/ppermute | solution.py:21
  5.4 10.2 %collective-permute-start.1 = (bf16[64,1024]{1,0:T(8,128)(2,1)}, bf16[64,1024]{1,0:T(8,128)(2,1)S(1)}, u32[]{:S(2)}, u32[]{:S(2)}) collective-permute-start(bf16[64,1024]{1,0:T(8,128)(2,1)} %own.1), channel_id=1, source_target_pairs={{0,6},{2,0},{4,2},{6,4},{1,7},{3,1},{5,3},{7,5},{8,14},{10,8},{12,... | collective-permute-start | bytes 393224 | tf_op jit(solution)/shard_map/ppermute | solution.py:21
  7.2 8.5 %collective-permute-start.2 = (bf16[64,1024]{1,0:T(8,128)(2,1)}, bf16[64,1024]{1,0:T(8,128)(2,1)S(1)}, u32[]{:S(2)}, u32[]{:S(2)}) collective-permute-start(bf16[64,1024]{1,0:T(8,128)(2,1)} %own.1), channel_id=1, source_target_pairs={{0,4},{2,6},{4,0},{6,2},{1,5},{3,7},{5,1},{7,3},{8,12},{10,14},{12... | collective-permute-start | bytes 393224 | tf_op jit(solution)/shard_map/ppermute | solution.py:21
  16.3 6.7 %collective-permute-start.4 = (bf16[256,1024]{1,0:T(8,128)(2,1)S(1)}, bf16[256,1024]{1,0:T(8,128)(2,1)S(1)}, u32[]{:S(2)}, u32[]{:S(2)}) collective-permute-start(bf16[256,1024]{1,0:T(8,128)(2,1)S(1)} %shard_map.76.own.refs_0_), channel_id=1, source_target_pairs={{0,1},{1,0},{2,3},{3,2},{4,5},{5,4},{6,7},{7,6},{8,9},{9,8},{10,11... | collective-permute-start | bytes 1572872 | tf_op jit(solution)/shard_map/ppermute | solution.py:21
  16.4 21.5 %collective-permute-start.12 = (bf16[256,1024]{1,0:T(8,128)(2,1)S(1)}, bf16[256,1024]{1,0:T(8,128)(2,1)S(1)}, u32[]{:S(2)}, u32[]{:S(2)}) collective-permute-start(bf16[256,1024]{1,0:T(8,128)(2,1)S(1)} %shard_map.76.own.refs_0_), channel_id=1, source_target_pairs={{0,64},{64,128},{128,192},{192,0},{1,65},{65,129},{129,193},{193,1... | collective-permute-start | bytes 1572872 | tf_op jit(solution)/shard_map/ppermute | solution.py:21
  17.1 21.1 %collective-permute-start.14 = (bf16[256,1024]{1,0:T(8,128)(2,1)S(1)}, bf16[256,1024]{1,0:T(8,128)(2,1)}, u32[]{:S(2)}, u32[]{:S(2)}) collective-permute-start(bf16[256,1024]{1,0:T(8,128)(2,1)S(1)} %shard_map.76.own.refs_0_), channel_id=1, source_target_pairs={{0,192},{64,0},{128,64},{192,128},{1,193},{65,1},{129,65},{193,129... | collective-permute-start | bytes 1572872 | tf_op jit(solution)/shard_map/ppermute | solution.py:21
  19.7 18.7 %collective-permute-start.16 = (bf16[64,1024]{1,0:T(8,128)(2,1)S(1)}, bf16[64,1024]{1,0:T(8,128)(2,1)S(1)}, u32[]{:S(2)}, u32[]{:S(2)}) collective-permute-start(bf16[64,1024]{1,0:T(8,128)(2,1)S(1)} %collective-permute-done.3.refs_1_.own), channel_id=1, source_target_pairs={{0,2},{2,4},{4,6},{6,0},{1,3},{3,5},{5,7},{7,1},{8,10},{10,12},{12... | collective-permute-start | bytes 393224 | tf_op jit(solution)/shard_map/ppermute | solution.py:21
  20.3 18.1 %collective-permute-start.17 = (bf16[64,1024]{1,0:T(8,128)(2,1)S(1)}, bf16[64,1024]{1,0:T(8,128)(2,1)S(1)}, u32[]{:S(2)}, u32[]{:S(2)}) collective-permute-start(bf16[64,1024]{1,0:T(8,128)(2,1)S(1)} %collective-permute-done.3.refs_1_.own), channel_id=1, source_target_pairs={{0,6},{2,0},{4,2},{6,4},{1,7},{3,1},{5,3},{7,5},{8,14},{10,8},{12,... | collective-permute-start | bytes 393224 | tf_op jit(solution)/shard_map/ppermute | solution.py:21
  22.9 15.5 %collective-permute-start.18 = (bf16[64,1024]{1,0:T(8,128)(2,1)S(1)}, bf16[64,1024]{1,0:T(8,128)(2,1)S(1)}, u32[]{:S(2)}, u32[]{:S(2)}) collective-permute-start(bf16[64,1024]{1,0:T(8,128)(2,1)S(1)} %collective-permute-done.3.refs_1_.own), channel_id=1, source_target_pairs={{0,4},{2,6},{4,0},{6,2},{1,5},{3,7},{5,1},{7,3},{8,12},{10,14},{12... | collective-permute-start | bytes 393224 | tf_op jit(solution)/shard_map/ppermute | solution.py:21
  30.7 12.2 %all-to-all-start = ((f32[32,4,128]{2,1,0:T(4,128)}), f32[32,4,128]{2,1,0:T(4,128)S(1)}, u32[]{:S(2)}, u32[]{:S(2)}) async-start(f32[32,4,128]{2,1,0:T(4,128)} %get-tuple-element.18.ahead), calls=%async_computation | async-start | bytes 131072 | tf_op jit(solution)/shard_map/all_to_all | solution.py:397
  37.9 11.0 %collective-permute-start.13 = (bf16[256,1024]{1,0:T(8,128)(2,1)S(1)}, bf16[256,1024]{1,0:T(8,128)(2,1)}, u32[]{:S(2)}, u32[]{:S(2)}) collective-permute-start(bf16[256,1024]{1,0:T(8,128)(2,1)S(1)} %collective-permute-done.12.refs_2_), channel_id=1, source_target_pairs={{0,1},{1,0},{2,3},{3,2},{4,5},{5,4},{6,7},{7,6},{8,9},{9,8},{10,11... | collective-permute-start | bytes 1572872 | tf_op jit(solution)/shard_map/ppermute | solution.py:21
  38.2 11.8 %collective-permute-start.15 = (bf16[256,1024]{1,0:T(8,128)(2,1)}, bf16[256,1024]{1,0:T(8,128)(2,1)}, u32[]{:S(2)}, u32[]{:S(2)}) collective-permute-start(bf16[256,1024]{1,0:T(8,128)(2,1)} %collective-permute-done.14.refs_4_), channel_id=1, source_target_pairs={{0,1},{1,0},{2,3},{3,2},{4,5},{5,4},{6,7},{7,6},{8,9},{9,8},{10,11... | collective-permute-start | bytes 1572872 | tf_op jit(solution)/shard_map/ppermute | solution.py:21
  43.5 6.6 %collective-permute-start.19 = (bf16[256,1024]{1,0:T(8,128)(2,1)S(1)}, bf16[256,1024]{1,0:T(8,128)(2,1)S(1)}, u32[]{:S(2)}, u32[]{:S(2)}) collective-permute-start(bf16[256,1024]{1,0:T(8,128)(2,1)S(1)} %shard_map.81.refs_6_), channel_id=1, source_target_pairs={{0,1},{1,0},{2,3},{3,2},{4,5},{5,4},{6,7},{7,6},{8,9},{9,8},{10,11... | collective-permute-start | bytes 1572872 | tf_op jit(solution)/shard_map/ppermute | solution.py:21
  46.6 19.7 %collective-permute-start.10 = (bf16[128,2048]{1,0:T(8,128)(2,1)S(1)}, bf16[128,2048]{1,0:T(8,128)(2,1)S(1)}, u32[]{:S(2)}, u32[]{:S(2)}) collective-permute-start(bf16[128,2048]{1,0:T(8,128)(2,1)S(1)} %get-tuple-element.23), channel_id=1, source_target_pairs={{0,6},{2,0},{4,2},{6,4},{1,7},{3,1},{5,3},{7,5},{8,14},{10,8},{12,... | collective-permute-start | bytes 1572872 | tf_op jit(solution)/shard_map/ppermute | solution.py:21
  48.1 26.4 %collective-permute-start.6 = (bf16[128,2048]{1,0:T(8,128)(2,1)S(1)}, bf16[128,2048]{1,0:T(8,128)(2,1)S(1)}, u32[]{:S(2)}, u32[]{:S(2)}) collective-permute-start(bf16[128,2048]{1,0:T(8,128)(2,1)S(1)} %get-tuple-element.21), channel_id=1, source_target_pairs={{0,2},{2,4},{4,6},{6,0},{1,3},{3,5},{5,7},{7,1},{8,10},{10,12},{12... | collective-permute-start | bytes 1572872 | tf_op jit(solution)/shard_map/ppermute | solution.py:21
  48.9 25.6 %collective-permute-start.8 = (bf16[128,2048]{1,0:T(8,128)(2,1)S(1)}, bf16[128,2048]{1,0:T(8,128)(2,1)S(1)}, u32[]{:S(2)}, u32[]{:S(2)}) collective-permute-start(bf16[128,2048]{1,0:T(8,128)(2,1)S(1)} %get-tuple-element.22), channel_id=1, source_target_pairs={{0,4},{2,6},{4,0},{6,2},{1,5},{3,7},{5,1},{7,3},{8,12},{10,14},{12... | collective-permute-start | bytes 1572872 | tf_op jit(solution)/shard_map/ppermute | solution.py:21
  62.4 12.1 %collective-permute-start.20 = (bf16[16,40,256]{2,1,0:T(8,128)(2,1)}, bf16[16,40,256]{2,1,0:T(8,128)(2,1)S(1)}, u32[]{:S(2)}, u32[]{:S(2)}) collective-permute-start(bf16[16,40,256]{2,1,0:T(8,128)(2,1)} %get-tuple-element.26), channel_id=1, source_target_pairs={{0,8},{8,0},{16,24},{24,16},{32,40},{40,32},{48,56},{56,48},{1,9},... | collective-permute-start | bytes 983048 | tf_op jit(solution)/shard_map/ppermute | solution.py:409
  62.6 11.9 %collective-permute-start.21 = (bf16[16,40,256]{2,1,0:T(8,128)(2,1)}, bf16[16,40,256]{2,1,0:T(8,128)(2,1)S(1)}, u32[]{:S(2)}, u32[]{:S(2)}) collective-permute-start(bf16[16,40,256]{2,1,0:T(8,128)(2,1)} %get-tuple-element.27), channel_id=1, source_target_pairs={{0,56},{8,16},{16,8},{24,32},{32,24},{40,48},{48,40},{56,0},{1,57}... | collective-permute-start | bytes 983048 | tf_op jit(solution)/shard_map/ppermute | solution.py:411
  77.7 29.3 %all-to-all-start.1 = ((bf16[16,40,512]{2,1,0:T(8,128)(2,1)}), bf16[16,40,512]{2,1,0:T(8,128)(2,1)}, u32[]{:S(2)}, u32[]{:S(2)}) async-start(bf16[16,40,512]{2,1,0:T(8,128)(2,1)} %shard_map.83), calls=%async_computation.1 | async-start | bytes 1310720 | tf_op jit(solution)/shard_map/all_to_all | solution.py:413
  87.6 3.9 %collective-permute-start.5 = (bf16[64,2048]{1,0:T(8,128)(2,1)S(1)}, bf16[64,2048]{1,0:T(8,128)(2,1)S(1)}, u32[]{:S(2)}, u32[]{:S(2)}) collective-permute-start(bf16[64,2048]{1,0:T(8,128)(2,1)S(1)} %get-tuple-element.20.refs_8_), channel_id=1, source_target_pairs={{0,1},{1,0},{2,3},{3,2},{4,5},{5,4},{6,7},{7,6},{8,9},{9,8},{10,11... | collective-permute-start | bytes 786440 | tf_op jit(solution)/shard_map/ppermute | solution.py:21
  88.4 3.1 %collective-permute-start.11 = (bf16[64,2048]{1,0:T(8,128)(2,1)}, bf16[64,2048]{1,0:T(8,128)(2,1)S(1)}, u32[]{:S(2)}, u32[]{:S(2)}) collective-permute-start(bf16[64,2048]{1,0:T(8,128)(2,1)} %slice.26), channel_id=1, source_target_pairs={{0,1},{1,0},{2,3},{3,2},{4,5},{5,4},{6,7},{7,6},{8,9},{9,8},{10,11... | collective-permute-start | bytes 786440 | tf_op jit(solution)/shard_map/ppermute | solution.py:21
  89.6 1.8 %collective-permute-start.7 = (bf16[64,2048]{1,0:T(8,128)(2,1)}, bf16[64,2048]{1,0:T(8,128)(2,1)S(1)}, u32[]{:S(2)}, u32[]{:S(2)}) collective-permute-start(bf16[64,2048]{1,0:T(8,128)(2,1)} %slice.24), channel_id=1, source_target_pairs={{0,1},{1,0},{2,3},{3,2},{4,5},{5,4},{6,7},{7,6},{8,9},{9,8},{10,11... | collective-permute-start | bytes 786440 | tf_op jit(solution)/shard_map/ppermute | solution.py:21
  90.4 1.9 %collective-permute-start.9 = (bf16[64,2048]{1,0:T(8,128)(2,1)}, bf16[64,2048]{1,0:T(8,128)(2,1)S(1)}, u32[]{:S(2)}, u32[]{:S(2)}) collective-permute-start(bf16[64,2048]{1,0:T(8,128)(2,1)} %slice.25), channel_id=1, source_target_pairs={{0,1},{1,0},{2,3},{3,2},{4,5},{5,4},{6,7},{7,6},{8,9},{9,8},{10,11... | collective-permute-start | bytes 786440 | tf_op jit(solution)/shard_map/ppermute | solution.py:21
  (7 other events, 54.0 us)

commit v6 on v4

--- a/solution.py
+++ b/solution.py
@@ -45,41 +45,37 @@
     return [pl.BlockSpec(memory_space=pltpu.HBM)] * n
 
 
-def prepare_kernel(means, inv_var, weights, scaled, row, col):
+def prepare_kernel(means, inv_var, weights, scaled, row):
     values = means[...].astype(F32)
     product = values * inv_var[...]
     scaled[...] = product.astype(BF)
     square = values * product
     norm = functools.reduce(jnp.add, [square[:, i : i + 128] for i in range(0, 1024, 128)])
     norm = 0.5 * jnp.sum(norm, axis=1, keepdims=True)
-    for i in range(0, 256, 128):
-        part = weights[:, i : i + 128] - line(norm[i : i + 128])
-        row[:, i : i + 128] = part
-        col[i : i + 128, :] = column(part)
+    for i in range(0, 512, 128):
+        row[:, i : i + 128] = weights[:, i : i + 128] - line(norm[i : i + 128])
 
 
 def prepare(means, inv_var, log_weights):
     return pl.pallas_call(
         prepare_kernel,
-        grid=(8,),
+        grid=(4,),
         in_specs=[
-            pl.BlockSpec((256, 1024), lambda i: (i, 0)),
+            pl.BlockSpec((512, 1024), lambda i: (i, 0)),
             pl.BlockSpec((1, 1024), lambda i: (0, 0)),
-            pl.BlockSpec((1, 256), lambda i: (0, i)),
+            pl.BlockSpec((1, 512), lambda i: (0, i)),
         ],
         out_specs=(
-            pl.BlockSpec((256, 1024), lambda i: (i, 0)),
-            pl.BlockSpec((1, 256), lambda i: (0, i)),
-            pl.BlockSpec((256, 1), lambda i: (i, 0)),
+            pl.BlockSpec((512, 1024), lambda i: (i, 0)),
+            pl.BlockSpec((1, 512), lambda i: (0, i)),
         ),
         out_shape=(
             pltpu.HBM((2048, 1024), BF),
             jax.ShapeDtypeStruct((1, 2048), F32),
-            jax.ShapeDtypeStruct((2048, 1), F32),
         ),
         compiler_params=params(),
         cost_estimate=pl.CostEstimate(flops=6 << 21, bytes_accessed=8 << 20, transcendentals=0),
-    )(still(means), inv_var.reshape(1, 1024), log_weights.reshape(1, 2048))
+    )(still(means), still(inv_var.reshape(1, 1024)), still(log_weights.reshape(1, 2048)))
 
 
 def place_kernel(at, own, before, after, far, *refs):
@@ -179,7 +175,7 @@
 def sums_kernel(at, shares, scaled, bias, *refs):
     pieces = refs[:8]
     sums = refs[8]
-    rows, weights, lse, sems = refs[9:]
+    rows, weights, lse, wide, sems = refs[9:]
     copies = [
         pltpu.make_async_copy(piece, rows.at[pl.ds(i * 256, 256)], sems.at[i])
         for i, piece in enumerate(pieces)
@@ -189,6 +185,9 @@
     y, c = at[2], at[1]
     for yy in range(4):
         lse[pl.ds(yy * 4, 4), :] = joined(shares[yy])
+    for b in range(0, 512, 128):
+        wide[b : b + 128, :] = jnp.transpose(jnp.broadcast_to(bias[:, b : b + 128], (128, 128)))
+    shift_up = jnp.concatenate([wide[...], wide[...]], axis=1)
     count = jnp.zeros((512, 128), F32)
     for i in range(8):
         there = lax.rem(y + (0, 3, 1, 2)[i // 2], 4)
@@ -200,14 +199,18 @@
         score = lax.dot_general(
             scaled[...], rows[cut, :], (((1,), (1,)), ((), ())), preferred_element_type=F32
         )
-        weight = jnp.exp(score + bias[...] - norm).astype(BF)
+        weight = jnp.exp(score + shift_up - norm).astype(BF)
         weights[:, cut] = weight
         count = count + weight[:, :128].astype(F32) + weight[:, 128:].astype(F32)
     count = jnp.sum(count, axis=1, keepdims=True)
     count = jnp.concatenate([line(count[b : b + 128]) for b in range(0, 512, 128)], axis=1)
-    high = count.astype(BF).astype(F32)
-    tail = jnp.concatenate([high, count - high, jnp.zeros((6, 512), F32)], axis=0).astype(BF)
-    sums[:, 32:40, :] = jnp.broadcast_to(tail[None], (32, 8, 512))
+    digits = []
+    for _ in range(8):
+        digit = jnp.floor(count * (1.0 / 1024.0))
+        digits.append(digit)
+        count = (count - digit * 1024.0) * 32.0
+    tail = jnp.concatenate(digits, axis=0).astype(BF)
+    sums[:, :, 32:40, :] = jnp.broadcast_to(tail[None, None], (8, 4, 8, 512))
     for j in range(4):
         block = lax.dot_general(
             weights[...],
@@ -215,10 +218,11 @@
             (((1,), (0,)), ((), ())),
             preferred_element_type=F32,
         )
-        sums[j * 8 : j * 8 + 8, 0:32, :] = jnp.transpose(block.astype(BF)).reshape(8, 32, 512)
-
-
-def partial_sums(at, shares, scaled, bias_col, pieces):
+        block = jnp.transpose(block.astype(BF))
+        sums[:, j, 0:32, :] = block.reshape(8, 32, 512)
+
+
+def partial_sums(at, shares, scaled, bias_row, pieces):
     return pl.pallas_call(
         sums_kernel,
         grid_spec=pltpu.PrefetchScalarGridSpec(
@@ -227,28 +231,29 @@
             in_specs=[
                 pl.BlockSpec((4, 8, 4, 128), lambda i, at: (0, 0, 0, 0)),
                 pl.BlockSpec((512, 1024), lambda i, at: (at[2], 0)),
-                pl.BlockSpec((512, 1), lambda i, at: (at[2], 0)),
+                pl.BlockSpec((1, 512), lambda i, at: (0, at[2])),
             ]
             + anywhere(8),
-            out_specs=pl.BlockSpec((32, 40, 512), lambda i, at: (0, 0, 0)),
+            out_specs=pl.BlockSpec((8, 4, 40, 512), lambda i, at: (0, 0, 0, 0)),
             scratch_shapes=[
                 VMEM((2048, 1024), BF),
                 VMEM((512, 2048), BF),
                 VMEM((16, 128), F32),
+                VMEM((512, 128), F32),
                 pltpu.SemaphoreType.DMA((8,)),
             ],
         ),
-        out_shape=pltpu.HBM((32, 40, 512), BF),
+        out_shape=pltpu.HBM((8, 4, 40, 512), BF),
         compiler_params=params(),
         cost_estimate=pl.CostEstimate(
             flops=4 * 512 * 2048 * 1024, bytes_accessed=8 << 20, transcendentals=1 << 20
         ),
-    )(at, shares, still(scaled), bias_col, *pieces)
-
-
-def resp_kernel(at, shares, score, sums, *refs):
-    del sums
-    outs, norm, held, sems = refs[:5], refs[6], refs[7], refs[8]
+    )(at, shares, still(scaled), bias_row, *pieces)
+
+
+def resp_kernel(at, shares, score, first, *refs):
+    del first
+    outs, norm, held, sems = refs[:5], refs[5], refs[6], refs[7]
     x, c, y = at[0], at[1], at[2]
     copies = []
     for j in range(8):
@@ -273,23 +278,21 @@
             outs[1 + j % 4][j // 4 * 64 : j // 4 * 64 + 64, :] = block
 
 
-def responsibilities(at, shares, score, sums):
+def responsibilities(at, shares, score, first):
     return pl.pallas_call(
         resp_kernel,
         in_specs=[scalar(), whole()] + hbm(2),
-        out_specs=[whole()] * 5 + hbm(),
-        input_output_aliases={3: 5},
+        out_specs=[whole()] * 5,
         scratch_shapes=[
             VMEM((512, 128), F32),
             VMEM((8, 64, 2048), F32),
             pltpu.SemaphoreType.DMA((8,)),
         ],
         out_shape=[jax.ShapeDtypeStruct((64, 2048), BF)] * 2
-        + [jax.ShapeDtypeStruct((128, 2048), BF)] * 3
-        + [pltpu.HBM((32, 40, 512), BF)],
+        + [jax.ShapeDtypeStruct((128, 2048), BF)] * 3,
         compiler_params=params(),
         cost_estimate=pl.CostEstimate(flops=1 << 21, bytes_accessed=6 << 20, transcendentals=1 << 20),
-    )(at, shares, still(score), sums)
+    )(at, shares, still(score), still(first))
 
 
 def cut_kernel(at, means, ahead, out, turned):
@@ -346,7 +349,7 @@
     at = jnp.stack([x, c, y, y * 8 + z]).astype(jnp.int32)
 
     far = shift(points, "y", 2)
-    scaled, bias_row, bias_col = prepare(means, inv_var, log_weights)
+    scaled, bias_row = prepare(means, inv_var, log_weights)
 
     own = gather_x(at, points, (scaled,), (far,))
     other = shift(own, "c", 1)
@@ -362,17 +365,18 @@
     for mine in (before, after, far):
         pieces += [mine, shift(mine, "c", 1)]
 
-    sums = partial_sums(at, shares, scaled, bias_col, pieces)
-    *blocks, sums = responsibilities(at, shares, score, sums)
+    sums = partial_sums(at, shares, scaled, bias_row, pieces)
+    blocks = responsibilities(at, shares, score, sums)
     pairs = [shift(b, "x", j + 1) for j, b in enumerate(blocks[2:])]
     theirs = [shift(b, "c", 1) for b in [blocks[0]] + [pair[:64] for pair in pairs]]
     held = theirs + [blocks[1]] + pairs
-    sent = lax.all_to_all(sums, ("y", "z"), split_axis=0, concat_axis=0, tiled=True)
+    sums = lax.psum_scatter(sums.reshape(1280, 512), "z", scatter_dimension=0, tiled=True)
+    sent = lax.all_to_all(sums, "y", split_axis=0, concat_axis=0, tiled=True)
     resp_rows = lay_out(at, held)
 
-    sums = jnp.sum(sent.reshape(4, 8, 40, 512).astype(F32), axis=1)
-    counts = (sums[:, 32, :] + sums[:, 33, :]).reshape(2048)
-    sums = sums[:, :32, :].transpose(1, 0, 2).reshape(32, 2048)
+    sent = sent.reshape(4, 40, 512).astype(F32)
+    counts = sum(sent[:, 32 + i, :] * (32.0 ** (2 - i)) for i in range(8)).reshape(2048)
+    sums = sent[:, :32, :].transpose(1, 0, 2).reshape(32, 2048)
     new_means_t = (sums + mean_cols) / (counts[None, :] + 1.0)
 
     lse = joined(lax.dynamic_index_in_dim(shares, y, 0, keepdims=False)).reshape(8, 64)

time: 109 us -> 121 us (1.11)
  between operations: 1.47 us -> 14.9 us
  waiting for transfers between devices: 29.6 us -> 35.9 us
  starting transfers between devices: 35.2 us -> 30 us
  Pallas kernels: 34.9 us -> 33.2 us
  local copies, waits for them, and re-layouts: 3.67 us -> 2.29 us
    all_to_all x1, starting transfers between devices: 9.47 us -> 4.3 us  [body(): sent = lax.all_to_all(sums, 'y', split_axis=0, concat_axis=0, tiled=True)]
    reduce_scatter x0 -> x1, waiting for transfers between devices: none -> 4.51 us  [body(): lax.psum_scatter(sums.reshape(1280, 512), 'z', scatter_dimension=0, tiled...]
    all_to_all x1, waiting for transfers between devices: 1.46 us -> 3.68 us  [body(): sent = lax.all_to_all(sums, 'y', split_axis=0, concat_axis=0, tiled=True)]
    pallas_call x1, Pallas kernels: 7 us -> 5.28 us  [prepare(): pl.pallas_call(prepare_kernel, grid=(4,), in_specs=[pl.BlockSpec((512, 10...]
    reduce_sum x1 -> x0, other arithmetic: 1.53 us -> none  [body(): sums = jnp.sum(sent.reshape(4, 8, 40, 512).astype(F32), axis=1)]
    unnamed x13 -> x7, local copies, waits for them, and re-layouts: 1.42 us -> 0.04 us
  transfers between devices with their start and end apart: 22 -> 23, of which waited for: 5 -> 6; matrix products, arithmetic and copies ran while one was open for 3% -> 3% of each run, Pallas kernels for 18% -> 18%
where the time goes in v6:
time: 121 us; the launch traced here: 119 us
  waiting for transfers between devices  35.9 us (30%)
  Pallas kernels  33.2 us (27%)
  starting transfers between devices  30 us (25%)
  between operations  14.9 us (12%)
  other arithmetic  3.19 us (3%)
  local copies, waits for them, and re-layouts  2.29 us (2%)
    ppermute x20, waiting for transfers between devices, shift(): return lax.ppermute(value, axis, [(i, (i + step) % n) for i in range(n)])  23.3 us
    ppermute x20, starting transfers between devices, shift(): return lax.ppermute(value, axis, [(i, (i + step) % n) for i in range(n)])  19.8 us
    pallas_call x1, Pallas kernels, partial_sums(): pl.pallas_call(sums_kernel, grid_spec=pltpu.PrefetchScalarGridSpec(num_sc...  11.4 us
    pallas_call x1, Pallas kernels, scores(): pl.pallas_call(score_kernel, grid=(2048 // width,), out_shape=(pltpu.HBM(...  7.2 us
    all_to_all x1, starting transfers between devices, body(): lax.all_to_all(share, ('y', 'x', 'c'), split_axis=0, concat_axis=0, tiled...  5.78 us
    pallas_call x1, Pallas kernels, prepare(): pl.pallas_call(prepare_kernel, grid=(4,), in_specs=[pl.BlockSpec((512, 10...  5.28 us
    reduce_scatter x1, waiting for transfers between devices, body(): lax.psum_scatter(sums.reshape(1280, 512), 'z', scatter_dimension=0, tiled...  4.51 us
    all_to_all x1, waiting for transfers between devices, body(): lax.all_to_all(share, ('y', 'x', 'c'), split_axis=0, concat_axis=0, tiled...  4.39 us
  transfers between devices with their start and end apart: 23, of which 6 were waited for; matrix products, arithmetic and copies ran while one was open for 3% of the time, Pallas kernels for 18%

profile of v6, /device:TPU:32, one launch (start us, length us, event | category | flops | bytes accessed | tf_op | source)
XLA Modules:
  0.0 119.3 jit_solution(7239468882288358380)
XLA Ops:
  7.2 3.3 %collective-permute-start.3 = (bf16[64,1024]{1,0:T(8,128)(2,1)}, bf16[64,1024]{1,0:T(8,128)(2,1)S(1)}, u32[]{:S(2)}, u32[]{:S(2)}) collective-permute-start(bf16[64,1024]{1,0:T(8,128)(2,1)} %own.1), channel_id=1, source_target_pairs={{0,128},{64,192},{128,0},{192,64},{1,129},{65,193},{129,1},{193,65... | collective-permute-start | bytes 393224 | tf_op jit(solution)/shard_map/ppermute | solution.py:21
  10.5 3.0 %collective-permute-start.2 = (bf16[64,1024]{1,0:T(8,128)(2,1)}, bf16[64,1024]{1,0:T(8,128)(2,1)S(1)}, u32[]{:S(2)}, u32[]{:S(2)}) collective-permute-start(bf16[64,1024]{1,0:T(8,128)(2,1)} %own.1), channel_id=1, source_target_pairs={{0,4},{2,6},{4,0},{6,2},{1,5},{3,7},{5,1},{7,3},{8,12},{10,14},{12... | collective-permute-start | bytes 393224 | tf_op jit(solution)/shard_map/ppermute | solution.py:21
  13.5 1.1 collective-permute-start.1
  14.6 0.9 collective-permute-start
  15.5 5.3 %shard_map.75 = (bf16[2048,1024]{1,0:T(8,128)(2,1)}, f32[1,2048]{1,0:T(1,128)S(1)}) custom-call(bf16[2048,1024]{1,0:T(8,128)(2,1)} %means.3, f32[1,1024]{1,0:T(1,128)} %bitcast.31, f32[1,2048]{1,0:T(1,128)} %bitcast.34), custom_call_target="tpu_custom_call" | custom-call | flops 12582912 | bytes 8388608 | tf_op jit(solution)/shard_map/pallas_call | solution.py:60
  21.7 1.1 collective-permute-start.7
  22.8 1.0 collective-permute-start.5
  23.8 2.0 %collective-permute-start.11 = (bf16[64,1024]{1,0:T(8,128)(2,1)S(1)}, bf16[64,1024]{1,0:T(8,128)(2,1)S(1)}, u32[]{:S(2)}, u32[]{:S(2)}) collective-permute-start(bf16[64,1024]{1,0:T(8,128)(2,1)S(1)} %collective-permute-done.3.refs_1_.own), channel_id=1, source_target_pairs={{0,4},{2,6},{4,0},{6,2},{1,5},{3,7},{5,1},{7,3},{8,12},{10,14},{12... | collective-permute-start | bytes 393224 | tf_op jit(solution)/shard_map/ppermute | solution.py:21
  25.8 1.2 %collective-permute-start.10 = (bf16[64,1024]{1,0:T(8,128)(2,1)S(1)}, bf16[64,1024]{1,0:T(8,128)(2,1)S(1)}, u32[]{:S(2)}, u32[]{:S(2)}) collective-permute-start(bf16[64,1024]{1,0:T(8,128)(2,1)S(1)} %collective-permute-done.3.refs_1_.own), channel_id=1, source_target_pairs={{0,6},{2,0},{4,2},{6,4},{1,7},{3,1},{5,3},{7,5},{8,14},{10,8},{12,... | collective-permute-start | bytes 393224 | tf_op jit(solution)/shard_map/ppermute | solution.py:21
  27.8 7.2 %shard_map.77 = (f32[512,2048]{1,0:T(8,128)}, f32[32,4,128]{2,1,0:T(4,128)}) custom-call(s32[4]{0:T(128)S(1)} %pad_add_fusion.at, bf16[256,1024]{1,0:T(8,128)(2,1)S(1)} %shard_map.76.own.refs_0_, bf16[256,1024]{1,0:T(8,128)(2,1)S(1)} %collective-permute-done.4.other.refs_1_, bf16[2048,1024]{1,0:T(8,128)(2,1)} %get-tuple-element.13.refs_0_.scaled, ...), custom_call_target="tpu_custom_call" | custom-call | flops 2147483648 | bytes 9437184 | tf_op jit(solution)/shard_map/pallas_call | solution.py:144
  35.0 5.8 %all-to-all-start = ((f32[32,4,128]{2,1,0:T(4,128)}), f32[32,4,128]{2,1,0:T(4,128)S(1)}, u32[]{:S(2)}, u32[]{:S(2)}) async-start(f32[32,4,128]{2,1,0:T(4,128)} %get-tuple-element.15.ahead), calls=%async_computation | async-start | bytes 131072 | tf_op jit(solution)/shard_map/all_to_all | solution.py:360
  40.8 2.5 %shard_map.78.refs_0_ = f32[32,2048]{1,0:T(8,128)} custom-call(s32[4]{0:T(128)S(1)} %pad_add_fusion.at, bf16[2048,1024]{1,0:T(8,128)(2,1)} %means.3, f32[32,4,128]{2,1,0:T(4,128)} %get-tuple-element.15.ahead), custom_call_target="tpu_custom_call" | custom-call | tf_op jit(solution)/shard_map/pallas_call | solution.py:306
  43.9 4.4 %all-to-all-done.refs_1_ = f32[32,4,128]{2,1,0:T(4,128)S(1)} async-done(((f32[32,4,128]{2,1,0:T(4,128)}), f32[32,4,128]{2,1,0:T(4,128)S(1)}, u32[]{:S(2)}, u32[]{:S(2)}) %all-to-all-start) | async-done | bytes 65568 | tf_op jit(solution)/shard_map/all_to_all | solution.py:360
  49.2 1.8 %collective-permute-done.12.refs_7_ = bf16[256,1024]{1,0:T(8,128)(2,1)S(1)} collective-permute-done((bf16[256,1024]{1,0:T(8,128)(2,1)S(1)}, bf16[256,1024]{1,0:T(8,128)(2,1)S(1)}, u32[]{:S(2)}, u32[]{:S(2)}) %collective-permute-start.12) | collective-permute-done | bytes 524320 | tf_op jit(solution)/shard_map/ppermute | solution.py:21
  51.0 11.4 %shard_map.80.first = bf16[8,4,40,512]{3,2,1,0:T(8,128)(2,1)} custom-call(s32[4]{0:T(128)S(1)} %pad_add_fusion.at, f32[4,8,4,128]{3,2,1,0:T(4,128)S(1)} %bitcast.24, bf16[2048,1024]{1,0:T(8,128)(2,1)} %get-tuple-element.13.refs_0_.scaled, f32[1,2048]{1,0:T(1,128)S(1)} %get-tuple-element.14.bias, bf16[256,1024]{1,0:T(8,128)(2,1)S(1)} %shard_map.76.own.refs_0_, ...), custom_call_target="tpu_custom_call" | custom-call | flops 4294967296 | bytes 8388608 | tf_op jit(solution)/shard_map/pallas_call | solution.py:226
  62.4 3.7 %shard_map.81 = (bf16[64,2048]{1,0:T(8,128)(2,1)S(1)}, bf16[64,2048]{1,0:T(8,128)(2,1)S(1)}, bf16[128,2048]{1,0:T(8,128)(2,1)}, bf16[128,2048]{1,0:T(8,128)(2,1)S(1)}, bf16[128,2048]{1,0:T(8,128)(2,1)}) custom-call(s32[4]{0:T(128)S(1)} %pad_add_fusion.at, f32[4,8,4,128]{3,2,1,0:T(4,128)S(1)} %bitcast.25, f32[512,2048]{1,0:T(8,128)} %get-tuple-element.16.score, ...), custom_call_target="tpu_custom_call" | custom-call | flops 2097152 | bytes 6291456 | tf_op jit(solution)/shard_map/pallas_call | solution.py:282
  66.9 2.1 %collective-permute-start.16 = (bf16[128,2048]{1,0:T(8,128)(2,1)S(1)}, bf16[128,2048]{1,0:T(8,128)(2,1)S(1)}, u32[]{:S(2)}, u32[]{:S(2)}) collective-permute-start(bf16[128,2048]{1,0:T(8,128)(2,1)S(1)} %get-tuple-element.19), channel_id=1, source_target_pairs={{0,4},{2,6},{4,0},{6,2},{1,5},{3,7},{5,1},{7,3},{8,12},{10,14},{12... | collective-permute-start | bytes 1572872 | tf_op jit(solution)/shard_map/ppermute | solution.py:21
  68.9 1.1 collective-permute-start.18
  71.6 21.3 %collective-permute-done.14.refs_5_ = bf16[128,2048]{1,0:T(8,128)(2,1)S(1)} collective-permute-done((bf16[128,2048]{1,0:T(8,128)(2,1)}, bf16[128,2048]{1,0:T(8,128)(2,1)S(1)}, u32[]{:S(2)}, u32[]{:S(2)}) %collective-permute-start.14) | collective-permute-done | bytes 524320 | tf_op jit(solution)/shard_map/ppermute | solution.py:21
  95.6 4.5 %reduce-scatter.2.cloned.1.call-done = bf16[160,512]{1,0:T(8,128)(2,1)} async-done(((bf16[1280,512]{1,0:T(8,128)(2,1)}), bf16[160,512]{1,0:T(8,128)(2,1)}) %reduce-scatter.2.cloned.1.call-update) | async-done | bytes 163856 | tf_op jit(solution)/shard_map/reduce_scatter | solution.py:373
  100.1 4.3 %all-to-all-start.1 = ((bf16[4,40,512]{2,1,0:T(8,128)(2,1)}), bf16[4,40,512]{2,1,0:T(8,128)(2,1)S(1)}, u32[]{:S(2)}, u32[]{:S(2)}) async-start(bf16[4,40,512]{2,1,0:T(8,128)(2,1)} %bitcast.30), calls=%async_computation.2 | async-start | bytes 327680 | tf_op jit(solution)/shard_map/all_to_all | solution.py:374
  105.0 1.9 %shard_map.82 = bf16[64,16384]{1,0:T(8,128)(2,1)} custom-call(s32[4]{0:T(128)S(1)} %pad_add_fusion.at, bf16[64,2048]{1,0:T(8,128)(2,1)S(1)} %collective-permute-done.13.refs_0_, bf16[64,2048]{1,0:T(8,128)(2,1)S(1)} %collective-permute-done.15.refs_1_, bf16[64,2048]{1,0:T(8,128)(2,1)S(1)} %collective-permute-done.17.refs_2_, ...), custom_call_target="tpu_custom_call" | custom-call | tf_op jit(solution)/shard_map/pallas_call | solution.py:337
  106.9 3.7 %all-to-all-done.1 = bf16[4,40,512]{2,1,0:T(8,128)(2,1)S(1)} async-done(((bf16[4,40,512]{2,1,0:T(8,128)(2,1)}), bf16[4,40,512]{2,1,0:T(8,128)(2,1)S(1)}, u32[]{:S(2)}, u32[]{:S(2)}) %all-to-all-start.1) | async-done | bytes 163872 | tf_op jit(solution)/shard_map/all_to_all | solution.py:374
  110.8 1.7 %add_divide_fusion = f32[32,2048]{1,0:T(8,128)} fusion(f32[32,2048]{1,0:T(8,128)S(1)} %bitcast.29, f32[32,2048]{1,0:T(8,128)} %shard_map.78.refs_0_, f32[2048]{0:T(1024)S(1)} %broadcast_add_fusion), kind=kLoop, calls=%fused_computation.2 | loop fusion | flops 131072 | bytes 794624 | tf_op jit(solution)/shard_map/div | solution.py:380
  (54 shorter events, 8.3 us)
Async XLA Ops:
  7.2 13.8 %copy-start = (bf16[64,1024]{1,0:T(8,128)(2,1)S(1)}, bf16[64,1024]{1,0:T(8,128)(2,1)}, u32[]{:S(2)}) copy-start(bf16[64,1024]{1,0:T(8,128)(2,1)} %own.1) | copy-start | bytes 393220
  7.2 13.7 %collective-permute-start.3 = (bf16[64,1024]{1,0:T(8,128)(2,1)}, bf16[64,1024]{1,0:T(8,128)(2,1)S(1)}, u32[]{:S(2)}, u32[]{:S(2)}) collective-permute-start(bf16[64,1024]{1,0:T(8,128)(2,1)} %own.1), channel_id=1, source_target_pairs={{0,128},{64,192},{128,0},{192,64},{1,129},{65,193},{129,1},{193,65... | collective-permute-start | bytes 393224 | tf_op jit(solution)/shard_map/ppermute | solution.py:21
  10.5 10.4 %collective-permute-start.2 = (bf16[64,1024]{1,0:T(8,128)(2,1)}, bf16[64,1024]{1,0:T(8,128)(2,1)S(1)}, u32[]{:S(2)}, u32[]{:S(2)}) collective-permute-start(bf16[64,1024]{1,0:T(8,128)(2,1)} %own.1), channel_id=1, source_target_pairs={{0,4},{2,6},{4,0},{6,2},{1,5},{3,7},{5,1},{7,3},{8,12},{10,14},{12... | collective-permute-start | bytes 393224 | tf_op jit(solution)/shard_map/ppermute | solution.py:21
  13.5 7.4 %collective-permute-start.1 = (bf16[64,1024]{1,0:T(8,128)(2,1)}, bf16[64,1024]{1,0:T(8,128)(2,1)S(1)}, u32[]{:S(2)}, u32[]{:S(2)}) collective-permute-start(bf16[64,1024]{1,0:T(8,128)(2,1)} %own.1), channel_id=1, source_target_pairs={{0,6},{2,0},{4,2},{6,4},{1,7},{3,1},{5,3},{7,5},{8,14},{10,8},{12,... | collective-permute-start | bytes 393224 | tf_op jit(solution)/shard_map/ppermute | solution.py:21
  14.6 6.4 %collective-permute-start = (bf16[64,1024]{1,0:T(8,128)(2,1)}, bf16[64,1024]{1,0:T(8,128)(2,1)S(1)}, u32[]{:S(2)}, u32[]{:S(2)}) collective-permute-start(bf16[64,1024]{1,0:T(8,128)(2,1)} %own.1), channel_id=1, source_target_pairs={{0,2},{2,4},{4,6},{6,0},{1,3},{3,5},{5,7},{7,1},{8,10},{10,12},{12... | collective-permute-start | bytes 393224 | tf_op jit(solution)/shard_map/ppermute | solution.py:21
  21.6 5.4 %collective-permute-start.4 = (bf16[256,1024]{1,0:T(8,128)(2,1)S(1)}, bf16[256,1024]{1,0:T(8,128)(2,1)S(1)}, u32[]{:S(2)}, u32[]{:S(2)}) collective-permute-start(bf16[256,1024]{1,0:T(8,128)(2,1)S(1)} %shard_map.76.own.refs_0_), channel_id=1, source_target_pairs={{0,1},{1,0},{2,3},{3,2},{4,5},{5,4},{6,7},{7,6},{8,9},{9,8},{10,11... | collective-permute-start | bytes 1572872 | tf_op jit(solution)/shard_map/ppermute | solution.py:21
  21.7 21.6 %collective-permute-start.7 = (bf16[256,1024]{1,0:T(8,128)(2,1)S(1)}, bf16[256,1024]{1,0:T(8,128)(2,1)S(1)}, u32[]{:S(2)}, u32[]{:S(2)}) collective-permute-start(bf16[256,1024]{1,0:T(8,128)(2,1)S(1)} %shard_map.76.own.refs_0_), channel_id=1, source_target_pairs={{0,192},{64,0},{128,64},{192,128},{1,193},{65,1},{129,65},{193,129... | collective-permute-start | bytes 1572872 | tf_op jit(solution)/shard_map/ppermute | solution.py:21
  22.8 20.8 %collective-permute-start.5 = (bf16[256,1024]{1,0:T(8,128)(2,1)S(1)}, bf16[256,1024]{1,0:T(8,128)(2,1)S(1)}, u32[]{:S(2)}, u32[]{:S(2)}) collective-permute-start(bf16[256,1024]{1,0:T(8,128)(2,1)S(1)} %shard_map.76.own.refs_0_), channel_id=1, source_target_pairs={{0,64},{64,128},{128,192},{192,0},{1,65},{65,129},{129,193},{193,1... | collective-permute-start | bytes 1572872 | tf_op jit(solution)/shard_map/ppermute | solution.py:21
  23.8 20.1 %collective-permute-start.11 = (bf16[64,1024]{1,0:T(8,128)(2,1)S(1)}, bf16[64,1024]{1,0:T(8,128)(2,1)S(1)}, u32[]{:S(2)}, u32[]{:S(2)}) collective-permute-start(bf16[64,1024]{1,0:T(8,128)(2,1)S(1)} %collective-permute-done.3.refs_1_.own), channel_id=1, source_target_pairs={{0,4},{2,6},{4,0},{6,2},{1,5},{3,7},{5,1},{7,3},{8,12},{10,14},{12... | collective-permute-start | bytes 393224 | tf_op jit(solution)/shard_map/ppermute | solution.py:21
  25.8 18.1 %collective-permute-start.10 = (bf16[64,1024]{1,0:T(8,128)(2,1)S(1)}, bf16[64,1024]{1,0:T(8,128)(2,1)S(1)}, u32[]{:S(2)}, u32[]{:S(2)}) collective-permute-start(bf16[64,1024]{1,0:T(8,128)(2,1)S(1)} %collective-permute-done.3.refs_1_.own), channel_id=1, source_target_pairs={{0,6},{2,0},{4,2},{6,4},{1,7},{3,1},{5,3},{7,5},{8,14},{10,8},{12,... | collective-permute-start | bytes 393224 | tf_op jit(solution)/shard_map/ppermute | solution.py:21
  27.0 16.9 %collective-permute-start.9 = (bf16[64,1024]{1,0:T(8,128)(2,1)S(1)}, bf16[64,1024]{1,0:T(8,128)(2,1)S(1)}, u32[]{:S(2)}, u32[]{:S(2)}) collective-permute-start(bf16[64,1024]{1,0:T(8,128)(2,1)S(1)} %collective-permute-done.3.refs_1_.own), channel_id=1, source_target_pairs={{0,2},{2,4},{4,6},{6,0},{1,3},{3,5},{5,7},{7,1},{8,10},{10,12},{12... | collective-permute-start | bytes 393224 | tf_op jit(solution)/shard_map/ppermute | solution.py:21
  35.0 13.3 %all-to-all-start = ((f32[32,4,128]{2,1,0:T(4,128)}), f32[32,4,128]{2,1,0:T(4,128)S(1)}, u32[]{:S(2)}, u32[]{:S(2)}) async-start(f32[32,4,128]{2,1,0:T(4,128)} %get-tuple-element.15.ahead), calls=%async_computation | async-start | bytes 131072 | tf_op jit(solution)/shard_map/all_to_all | solution.py:360
  40.8 59.4 %reduce-scatter.2.cloned.1.call-start = ((), (), s32[]{:S(2)}) async-start(), calls=%async_computation.3 | async-start | bytes 1474560 | tf_op jit(solution)/shard_map/reduce_scatter | solution.py:373
  43.3 5.9 %collective-permute-start.8 = (bf16[256,1024]{1,0:T(8,128)(2,1)S(1)}, bf16[256,1024]{1,0:T(8,128)(2,1)}, u32[]{:S(2)}, u32[]{:S(2)}) collective-permute-start(bf16[256,1024]{1,0:T(8,128)(2,1)S(1)} %collective-permute-done.7.refs_4_), channel_id=1, source_target_pairs={{0,1},{1,0},{2,3},{3,2},{4,5},{5,4},{6,7},{7,6},{8,9},{9,8},{10,11... | collective-permute-start | bytes 1572872 | tf_op jit(solution)/shard_map/ppermute | solution.py:21
  43.6 5.6 %collective-permute-start.6 = (bf16[256,1024]{1,0:T(8,128)(2,1)S(1)}, bf16[256,1024]{1,0:T(8,128)(2,1)}, u32[]{:S(2)}, u32[]{:S(2)}) collective-permute-start(bf16[256,1024]{1,0:T(8,128)(2,1)S(1)} %collective-permute-done.5.refs_2_), channel_id=1, source_target_pairs={{0,1},{1,0},{2,3},{3,2},{4,5},{5,4},{6,7},{7,6},{8,9},{9,8},{10,11... | collective-permute-start | bytes 1572872 | tf_op jit(solution)/shard_map/ppermute | solution.py:21
  48.8 2.2 %collective-permute-start.12 = (bf16[256,1024]{1,0:T(8,128)(2,1)S(1)}, bf16[256,1024]{1,0:T(8,128)(2,1)S(1)}, u32[]{:S(2)}, u32[]{:S(2)}) collective-permute-start(bf16[256,1024]{1,0:T(8,128)(2,1)S(1)} %shard_map.79.refs_6_), channel_id=1, source_target_pairs={{0,1},{1,0},{2,3},{3,2},{4,5},{5,4},{6,7},{7,6},{8,9},{9,8},{10,11... | collective-permute-start | bytes 1572872 | tf_op jit(solution)/shard_map/ppermute | solution.py:21
  66.2 26.7 %collective-permute-start.14 = (bf16[128,2048]{1,0:T(8,128)(2,1)}, bf16[128,2048]{1,0:T(8,128)(2,1)S(1)}, u32[]{:S(2)}, u32[]{:S(2)}) collective-permute-start(bf16[128,2048]{1,0:T(8,128)(2,1)} %get-tuple-element.18), channel_id=1, source_target_pairs={{0,2},{2,4},{4,6},{6,0},{1,3},{3,5},{5,7},{7,1},{8,10},{10,12},{12... | collective-permute-start | bytes 1572872 | tf_op jit(solution)/shard_map/ppermute | solution.py:21
  66.9 26.8 %collective-permute-start.16 = (bf16[128,2048]{1,0:T(8,128)(2,1)S(1)}, bf16[128,2048]{1,0:T(8,128)(2,1)S(1)}, u32[]{:S(2)}, u32[]{:S(2)}) collective-permute-start(bf16[128,2048]{1,0:T(8,128)(2,1)S(1)} %get-tuple-element.19), channel_id=1, source_target_pairs={{0,4},{2,6},{4,0},{6,2},{1,5},{3,7},{5,1},{7,3},{8,12},{10,14},{12... | collective-permute-start | bytes 1572872 | tf_op jit(solution)/shard_map/ppermute | solution.py:21
  68.9 25.9 %collective-permute-start.18 = (bf16[128,2048]{1,0:T(8,128)(2,1)}, bf16[128,2048]{1,0:T(8,128)(2,1)S(1)}, u32[]{:S(2)}, u32[]{:S(2)}) collective-permute-start(bf16[128,2048]{1,0:T(8,128)(2,1)} %get-tuple-element.20), channel_id=1, source_target_pairs={{0,6},{2,0},{4,2},{6,4},{1,7},{3,1},{5,3},{7,5},{8,14},{10,8},{12,... | collective-permute-start | bytes 1572872 | tf_op jit(solution)/shard_map/ppermute | solution.py:21
  71.5 33.5 %collective-permute-start.13 = (bf16[64,2048]{1,0:T(8,128)(2,1)S(1)}, bf16[64,2048]{1,0:T(8,128)(2,1)S(1)}, u32[]{:S(2)}, u32[]{:S(2)}) collective-permute-start(bf16[64,2048]{1,0:T(8,128)(2,1)S(1)} %get-tuple-element.17), channel_id=1, source_target_pairs={{0,1},{1,0},{2,3},{3,2},{4,5},{5,4},{6,7},{7,6},{8,9},{9,8},{10,11... | collective-permute-start | bytes 786440 | tf_op jit(solution)/shard_map/ppermute | solution.py:21
  93.6 11.4 %collective-permute-start.15 = (bf16[64,2048]{1,0:T(8,128)(2,1)}, bf16[64,2048]{1,0:T(8,128)(2,1)S(1)}, u32[]{:S(2)}, u32[]{:S(2)}) collective-permute-start(bf16[64,2048]{1,0:T(8,128)(2,1)} %slice.48), channel_id=1, source_target_pairs={{0,1},{1,0},{2,3},{3,2},{4,5},{5,4},{6,7},{7,6},{8,9},{9,8},{10,11... | collective-permute-start | bytes 786440 | tf_op jit(solution)/shard_map/ppermute | solution.py:21
  94.3 10.7 %collective-permute-start.17 = (bf16[64,2048]{1,0:T(8,128)(2,1)}, bf16[64,2048]{1,0:T(8,128)(2,1)S(1)}, u32[]{:S(2)}, u32[]{:S(2)}) collective-permute-start(bf16[64,2048]{1,0:T(8,128)(2,1)} %slice.49), channel_id=1, source_target_pairs={{0,1},{1,0},{2,3},{3,2},{4,5},{5,4},{6,7},{7,6},{8,9},{9,8},{10,11... | collective-permute-start | bytes 786440 | tf_op jit(solution)/shard_map/ppermute | solution.py:21
  95.6 9.4 %collective-permute-start.19 = (bf16[64,2048]{1,0:T(8,128)(2,1)}, bf16[64,2048]{1,0:T(8,128)(2,1)S(1)}, u32[]{:S(2)}, u32[]{:S(2)}) collective-permute-start(bf16[64,2048]{1,0:T(8,128)(2,1)} %slice.50), channel_id=1, source_target_pairs={{0,1},{1,0},{2,3},{3,2},{4,5},{5,4},{6,7},{7,6},{8,9},{9,8},{10,11... | collective-permute-start | bytes 786440 | tf_op jit(solution)/shard_map/ppermute | solution.py:21
  100.1 10.5 %all-to-all-start.1 = ((bf16[4,40,512]{2,1,0:T(8,128)(2,1)}), bf16[4,40,512]{2,1,0:T(8,128)(2,1)S(1)}, u32[]{:S(2)}, u32[]{:S(2)}) async-start(bf16[4,40,512]{2,1,0:T(8,128)(2,1)} %bitcast.30), calls=%async_computation.2 | async-start | bytes 327680 | tf_op jit(solution)/shard_map/all_to_all | solution.py:374
  (2 other events, 9.4 us)
Sparse Core Ops, SparseCore 0:
  62.6 37.5 reduce-scatter.1

commit v7 on v6

--- a/solution.py
+++ b/solution.py
@@ -13,12 +13,16 @@
 F32 = jnp.float32
 VMEM_LIMIT = 24 * 1024 * 1024
 VMEM = pltpu.VMEM
-SIZES = {"y": 4, "z": 8, "x": 4, "c": 2}
+SIZES = {"y": 4, "x": 4, "c": 2}
 
 
 def shift(value, axis, step):
     n = SIZES[axis]
     return lax.ppermute(value, axis, [(i, (i + step) % n) for i in range(n)])
+
+
+def swap(value, bit):
+    return lax.ppermute(value, ("h", "l"), [(z, z ^ bit) for z in range(8)])
 
 
 def still(value):
@@ -172,10 +176,25 @@
     return top + jnp.log(jnp.sum(jnp.exp(shares - top[None]), axis=0))
 
 
+def hold_kernel(*refs):
+    del refs
+
+
+def hold(value, *first):
+    return pl.pallas_call(
+        hold_kernel,
+        out_shape=pltpu.HBM(value.shape, value.dtype),
+        in_specs=hbm() + anywhere(len(first)),
+        out_specs=pl.BlockSpec(memory_space=pltpu.HBM),
+        input_output_aliases={0: 0},
+        compiler_params=params(),
+    )(value, *first)
+
+
 def sums_kernel(at, shares, scaled, bias, *refs):
     pieces = refs[:8]
-    sums = refs[8]
-    rows, weights, lse, wide, sems = refs[9:]
+    sums, counts = refs[9:11]
+    rows, weights, lse, wide, sems = refs[11:]
     copies = [
         pltpu.make_async_copy(piece, rows.at[pl.ds(i * 256, 256)], sems.at[i])
         for i, piece in enumerate(pieces)
@@ -203,14 +222,9 @@
         weights[:, cut] = weight
         count = count + weight[:, :128].astype(F32) + weight[:, 128:].astype(F32)
     count = jnp.sum(count, axis=1, keepdims=True)
-    count = jnp.concatenate([line(count[b : b + 128]) for b in range(0, 512, 128)], axis=1)
-    digits = []
-    for _ in range(8):
-        digit = jnp.floor(count * (1.0 / 1024.0))
-        digits.append(digit)
-        count = (count - digit * 1024.0) * 32.0
-    tail = jnp.concatenate(digits, axis=0).astype(BF)
-    sums[:, :, 32:40, :] = jnp.broadcast_to(tail[None, None], (8, 4, 8, 512))
+    counts[...] = jnp.zeros_like(counts)
+    for b in range(4):
+        counts[pl.ds(y * 4 + b, 1), :] = line(count[b * 128 : b * 128 + 128])
     for j in range(4):
         block = lax.dot_general(
             weights[...],
@@ -218,11 +232,10 @@
             (((1,), (0,)), ((), ())),
             preferred_element_type=F32,
         )
-        block = jnp.transpose(block.astype(BF))
-        sums[:, j, 0:32, :] = block.reshape(8, 32, 512)
-
-
-def partial_sums(at, shares, scaled, bias_row, pieces):
+        sums[j * 256 : j * 256 + 256, :] = jnp.transpose(block.astype(BF))
+
+
+def partial_sums(at, shares, scaled, bias_row, pieces, first):
     return pl.pallas_call(
         sums_kernel,
         grid_spec=pltpu.PrefetchScalarGridSpec(
@@ -233,8 +246,11 @@
                 pl.BlockSpec((512, 1024), lambda i, at: (at[2], 0)),
                 pl.BlockSpec((1, 512), lambda i, at: (0, at[2])),
             ]
-            + anywhere(8),
-            out_specs=pl.BlockSpec((8, 4, 40, 512), lambda i, at: (0, 0, 0, 0)),
+            + anywhere(9),
+            out_specs=(
+                pl.BlockSpec((1024, 512), lambda i, at: (0, 0)),
+                pl.BlockSpec((16, 128), lambda i, at: (0, 0)),
+            ),
             scratch_shapes=[
                 VMEM((2048, 1024), BF),
                 VMEM((512, 2048), BF),
@@ -243,17 +259,17 @@
                 pltpu.SemaphoreType.DMA((8,)),
             ],
         ),
-        out_shape=pltpu.HBM((8, 4, 40, 512), BF),
+        out_shape=(pltpu.HBM((1024, 512), BF), jax.ShapeDtypeStruct((16, 128), F32)),
         compiler_params=params(),
         cost_estimate=pl.CostEstimate(
             flops=4 * 512 * 2048 * 1024, bytes_accessed=8 << 20, transcendentals=1 << 20
         ),
-    )(at, shares, still(scaled), bias_row, *pieces)
-
-
-def resp_kernel(at, shares, score, first, *refs):
-    del first
-    outs, norm, held, sems = refs[:5], refs[5], refs[6], refs[7]
+    )(at, shares, still(scaled), bias_row, *pieces, first)
+
+
+def resp_kernel(at, shares, score, *refs):
+    outs, norm, held, sems, across = refs[:5], refs[5], refs[6], refs[7], refs[8]
+    outs, out_across = (*outs[:3], across, outs[4]), outs[3]
     x, c, y = at[0], at[1], at[2]
     copies = []
     for j in range(8):
@@ -276,23 +292,27 @@
             outs[j // 4][...] = block
         else:
             outs[1 + j % 4][j // 4 * 64 : j // 4 * 64 + 64, :] = block
-
-
-def responsibilities(at, shares, score, first):
+    copy = pltpu.make_async_copy(across, out_across, sems.at[0])
+    copy.start()
+    copy.wait()
+
+
+def responsibilities(at, shares, score):
     return pl.pallas_call(
         resp_kernel,
-        in_specs=[scalar(), whole()] + hbm(2),
-        out_specs=[whole()] * 5,
+        in_specs=[scalar(), whole()] + hbm(),
+        out_specs=[whole()] * 3 + hbm() + [whole()],
         scratch_shapes=[
             VMEM((512, 128), F32),
             VMEM((8, 64, 2048), F32),
             pltpu.SemaphoreType.DMA((8,)),
+            VMEM((128, 2048), BF),
         ],
         out_shape=[jax.ShapeDtypeStruct((64, 2048), BF)] * 2
-        + [jax.ShapeDtypeStruct((128, 2048), BF)] * 3,
+        + [jax.ShapeDtypeStruct((128, 2048), BF), pltpu.HBM((128, 2048), BF), jax.ShapeDtypeStruct((128, 2048), BF)],
         compiler_params=params(),
         cost_estimate=pl.CostEstimate(flops=1 << 21, bytes_accessed=6 << 20, transcendentals=1 << 20),
-    )(at, shares, still(score), still(first))
+    )(at, shares, still(score))
 
 
 def cut_kernel(at, means, ahead, out, turned):
@@ -341,12 +361,13 @@
         scratch_shapes=[pltpu.SemaphoreType.DMA((8,))],
         out_shape=jax.ShapeDtypeStruct((64, 16384), BF),
         compiler_params=params(),
+        cost_estimate=pl.CostEstimate(flops=0, bytes_accessed=4 << 20, transcendentals=0),
     )(at, *pieces)
 
 
 def body(points, means, log_weights, inv_var):
-    x, c, y, z = (lax.axis_index(a) for a in "xcyz")
-    at = jnp.stack([x, c, y, y * 8 + z]).astype(jnp.int32)
+    x, c, y, h, l = (lax.axis_index(a) for a in "xcyhl")
+    at = jnp.stack([x, c, y, y * 8 + h * 2 + l, l]).astype(jnp.int32)
 
     far = shift(points, "y", 2)
     scaled, bias_row = prepare(means, inv_var, log_weights)
@@ -365,18 +386,22 @@
     for mine in (before, after, far):
         pieces += [mine, shift(mine, "c", 1)]
 
-    sums = partial_sums(at, shares, scaled, bias_row, pieces)
-    blocks = responsibilities(at, shares, score, sums)
-    pairs = [shift(b, "x", j + 1) for j, b in enumerate(blocks[2:])]
+    blocks = responsibilities(at, shares, score)
+    ahead, behind = shift(blocks[2], "x", 1), shift(blocks[4], "x", 3)
+    sums, counts = partial_sums(at, shares, scaled, bias_row, pieces, blocks[0])
+    pairs = [ahead, shift(hold(blocks[3], counts), "x", 2), behind]
+    sums = hold(sums, ahead, behind)
+    sent = lax.all_to_all(sums, ("y", "h", "l"), split_axis=0, concat_axis=0, tiled=True)
     theirs = [shift(b, "c", 1) for b in [blocks[0]] + [pair[:64] for pair in pairs]]
     held = theirs + [blocks[1]] + pairs
-    sums = lax.psum_scatter(sums.reshape(1280, 512), "z", scatter_dimension=0, tiled=True)
-    sent = lax.all_to_all(sums, "y", split_axis=0, concat_axis=0, tiled=True)
     resp_rows = lay_out(at, held)
 
-    sent = sent.reshape(4, 40, 512).astype(F32)
-    counts = sum(sent[:, 32 + i, :] * (32.0 ** (2 - i)) for i in range(8)).reshape(2048)
-    sums = sent[:, :32, :].transpose(1, 0, 2).reshape(32, 2048)
+    counts = counts + swap(counts, 1)
+    counts = counts + swap(counts, 2)
+    counts = counts + swap(counts, 4)
+    counts = sum([shift(counts, "y", i) for i in range(1, 4)], counts).reshape(2048)
+    sums = jnp.sum(sent.reshape(4, 8, 32, 512).astype(F32), axis=1)
+    sums = sums.transpose(1, 0, 2).reshape(32, 2048)
     new_means_t = (sums + mean_cols) / (counts[None, :] + 1.0)
 
     lse = joined(lax.dynamic_index_in_dim(shares, y, 0, keepdims=False)).reshape(8, 64)
@@ -388,9 +413,9 @@
 
 
 def solution(mesh):
-    axes = ("y", "z", "x", "c")
-    mesh = Mesh(mesh.devices.reshape(4, 8, 4, 2), axes)
-    comp, pt = ("x", "c"), ("y", "z")
+    axes = ("y", "h", "l", "x", "c")
+    mesh = Mesh(mesh.devices.reshape(4, 4, 2, 4, 2), axes)
+    comp, pt = ("x", "c"), ("y", "h", "l")
     return jax.shard_map(
         body,
         mesh=mesh,

time: 121 us -> 123 us (1.017)
  the two profiles are of different devices: /device:TPU:32 before, /device:TPU:1 now
where the time goes in v7:
time: 123 us; the launch traced here: 122 us
  starting transfers between devices  57.2 us (47%)
  Pallas kernels  32.9 us (27%)
  waiting for transfers between devices  26.5 us (22%)
  other arithmetic  4.09 us (3%)
  between operations  1.48 us (1%)
    ppermute x23, starting transfers between devices, shift(): return lax.ppermute(value, axis, [(i, (i + step) % n) for i in range(n)])  33.3 us
    ppermute x3, waiting for transfers between devices, swap(): return lax.ppermute(value, ('h', 'l'), [(z, z ^ bit) for z in range(8)])  21.4 us
    pallas_call x1, Pallas kernels, partial_sums(): pl.pallas_call(sums_kernel, grid_spec=pltpu.PrefetchScalarGridSpec(num_sc...  11.2 us
    all_to_all x1, starting transfers between devices, body(): lax.all_to_all(sums, ('y', 'h', 'l'), split_axis=0, concat_axis=0, tiled=...  9.39 us
    ppermute x3, starting transfers between devices, swap(): return lax.ppermute(value, ('h', 'l'), [(z, z ^ bit) for z in range(8)])  8.55 us
    pallas_call x1, Pallas kernels, scores(): pl.pallas_call(score_kernel, grid=(2048 // width,), out_shape=(pltpu.HBM(...  7.3 us
    all_to_all x1, starting transfers between devices, body(): lax.all_to_all(share, ('y', 'x', 'c'), split_axis=0, concat_axis=0, tiled...  5.94 us
    pallas_call x1, Pallas kernels, prepare(): pl.pallas_call(prepare_kernel, grid=(4,), in_specs=[pl.BlockSpec((512, 10...  5.21 us
  transfers between devices with their start and end apart: 28, of which 4 were waited for; matrix products, arithmetic and copies ran while one was open for 2% of the time, Pallas kernels for 26%

profile of v7, /device:TPU:1, one launch (start us, length us, event | category | flops | bytes accessed | tf_op | source)
XLA Modules:
  0.0 122.4 jit_solution(4365610070682569123)
XLA Ops:
  0.6 2.1 %collective-permute-start = (bf16[64,1024]{1,0:T(8,128)(2,1)}, bf16[64,1024]{1,0:T(8,128)(2,1)S(1)}, u32[]{:S(2)}, u32[]{:S(2)}) collective-permute-start(bf16[64,1024]{1,0:T(8,128)(2,1)} %own.1), channel_id=1, source_target_pairs={{0,2},{2,4},{4,6},{6,0},{1,3},{3,5},{5,7},{7,1},{8,10},{10,12},{12... | collective-permute-start | bytes 393224 | tf_op jit(solution)/shard_map/ppermute | solution.py:21
  2.8 1.4 %collective-permute-start.1 = (bf16[64,1024]{1,0:T(8,128)(2,1)}, bf16[64,1024]{1,0:T(8,128)(2,1)S(1)}, u32[]{:S(2)}, u32[]{:S(2)}) collective-permute-start(bf16[64,1024]{1,0:T(8,128)(2,1)} %own.1), channel_id=1, source_target_pairs={{0,6},{2,0},{4,2},{6,4},{1,7},{3,1},{5,3},{7,5},{8,14},{10,8},{12,... | collective-permute-start | bytes 393224 | tf_op jit(solution)/shard_map/ppermute | solution.py:21
  4.1 1.6 %collective-permute-start.2 = (bf16[64,1024]{1,0:T(8,128)(2,1)}, bf16[64,1024]{1,0:T(8,128)(2,1)S(1)}, u32[]{:S(2)}, u32[]{:S(2)}) collective-permute-start(bf16[64,1024]{1,0:T(8,128)(2,1)} %own.1), channel_id=1, source_target_pairs={{0,4},{2,6},{4,0},{6,2},{1,5},{3,7},{5,1},{7,3},{8,12},{10,14},{12... | collective-permute-start | bytes 393224 | tf_op jit(solution)/shard_map/ppermute | solution.py:21
  5.8 2.9 %collective-permute-start.3 = (bf16[64,1024]{1,0:T(8,128)(2,1)}, bf16[64,1024]{1,0:T(8,128)(2,1)S(1)}, u32[]{:S(2)}, u32[]{:S(2)}) collective-permute-start(bf16[64,1024]{1,0:T(8,128)(2,1)} %own.1), channel_id=1, source_target_pairs={{0,128},{64,192},{128,0},{192,64},{1,129},{65,193},{129,1},{193,65... | collective-permute-start | bytes 393224 | tf_op jit(solution)/shard_map/ppermute | solution.py:21
  8.8 5.2 %shard_map.75 = (bf16[2048,1024]{1,0:T(8,128)(2,1)}, f32[1,2048]{1,0:T(1,128)S(1)}) custom-call(bf16[2048,1024]{1,0:T(8,128)(2,1)} %means.3, f32[1,1024]{1,0:T(1,128)} %bitcast.35, f32[1,2048]{1,0:T(1,128)} %bitcast.36), custom_call_target="tpu_custom_call" | custom-call | flops 12582912 | bytes 8388608 | tf_op jit(solution)/shard_map/pallas_call | solution.py:64
  14.6 1.9 %collective-permute-start.4 = (bf16[256,1024]{1,0:T(8,128)(2,1)S(1)}, bf16[256,1024]{1,0:T(8,128)(2,1)S(1)}, u32[]{:S(2)}, u32[]{:S(2)}) collective-permute-start(bf16[256,1024]{1,0:T(8,128)(2,1)S(1)} %shard_map.76.own.refs_0_), channel_id=1, source_target_pairs={{0,1},{1,0},{2,3},{3,2},{4,5},{5,4},{6,7},{7,6},{8,9},{9,8},{10,11... | collective-permute-start | bytes 1572872 | tf_op jit(solution)/shard_map/ppermute | solution.py:21
  16.9 2.3 %collective-permute-start.10 = (bf16[256,1024]{1,0:T(8,128)(2,1)S(1)}, bf16[256,1024]{1,0:T(8,128)(2,1)}, u32[]{:S(2)}, u32[]{:S(2)}) collective-permute-start(bf16[256,1024]{1,0:T(8,128)(2,1)S(1)} %shard_map.76.own.refs_0_), channel_id=1, source_target_pairs={{0,192},{64,0},{128,64},{192,128},{1,193},{65,1},{129,65},{193,129... | collective-permute-start | bytes 1572872 | tf_op jit(solution)/shard_map/ppermute | solution.py:21
  19.5 2.4 %collective-permute-start.13 = (bf16[64,1024]{1,0:T(8,128)(2,1)S(1)}, bf16[64,1024]{1,0:T(8,128)(2,1)S(1)}, u32[]{:S(2)}, u32[]{:S(2)}) collective-permute-start(bf16[64,1024]{1,0:T(8,128)(2,1)S(1)} %collective-permute-done.3.refs_1_.own), channel_id=1, source_target_pairs={{0,6},{2,0},{4,2},{6,4},{1,7},{3,1},{5,3},{7,5},{8,14},{10,8},{12,... | collective-permute-start | bytes 393224 | tf_op jit(solution)/shard_map/ppermute | solution.py:21
  22.1 7.3 %shard_map.77 = (f32[512,2048]{1,0:T(8,128)}, f32[32,4,128]{2,1,0:T(4,128)}) custom-call(s32[5]{0:T(128)S(1)} %stack.23.at, bf16[256,1024]{1,0:T(8,128)(2,1)S(1)} %shard_map.76.own.refs_0_, bf16[256,1024]{1,0:T(8,128)(2,1)S(1)} %collective-permute-done.4.other.refs_1_, bf16[2048,1024]{1,0:T(8,128)(2,1)} %get-tuple-element.15.refs_0_.scaled, ...), custom_call_target="tpu_custom_call" | custom-call | flops 2147483648 | bytes 9437184 | tf_op jit(solution)/shard_map/pallas_call | solution.py:148
  29.4 5.9 %all-to-all-start = ((f32[32,4,128]{2,1,0:T(4,128)}), f32[32,4,128]{2,1,0:T(4,128)S(1)}, u32[]{:S(2)}, u32[]{:S(2)}) async-start(f32[32,4,128]{2,1,0:T(4,128)} %get-tuple-element.17.ahead), calls=%async_computation | async-start | bytes 131072 | tf_op jit(solution)/shard_map/all_to_all | solution.py:381
  35.3 2.5 %shard_map.79.refs_0_ = f32[32,2048]{1,0:T(8,128)} custom-call(s32[5]{0:T(128)S(1)} %stack.23.at, bf16[2048,1024]{1,0:T(8,128)(2,1)} %means.3, f32[32,4,128]{2,1,0:T(4,128)} %get-tuple-element.17.ahead), custom_call_target="tpu_custom_call" | custom-call | tf_op jit(solution)/shard_map/pallas_call | solution.py:326
  38.4 4.3 %all-to-all-done.refs_1_ = f32[32,4,128]{2,1,0:T(4,128)S(1)} async-done(((f32[32,4,128]{2,1,0:T(4,128)}), f32[32,4,128]{2,1,0:T(4,128)S(1)}, u32[]{:S(2)}, u32[]{:S(2)}) %all-to-all-start) | async-done | bytes 65568 | tf_op jit(solution)/shard_map/all_to_all | solution.py:381
  43.7 3.6 %shard_map.78 = (bf16[64,2048]{1,0:T(8,128)(2,1)S(1)}, bf16[64,2048]{1,0:T(8,128)(2,1)S(1)}, bf16[128,2048]{1,0:T(8,128)(2,1)S(1)}, bf16[128,2048]{1,0:T(8,128)(2,1)}, bf16[128,2048]{1,0:T(8,128)(2,1)S(1)}) custom-call(s32[5]{0:T(128)S(1)} %stack.23.at, f32[4,8,4,128]{3,2,1,0:T(4,128)S(1)} %bitcast.28, f32[512,2048]{1,0:T(8,128)} %get-tuple-element.18.score), custom_call_target="tpu_custom_call" | custom-call | flops 2097152 | bytes 6291456 | tf_op jit(solution)/shard_map/pallas_call | solution.py:301
  47.9 2.4 %collective-permute-start.18 = (bf16[128,2048]{1,0:T(8,128)(2,1)S(1)}, bf16[128,2048]{1,0:T(8,128)(2,1)S(1)}, u32[]{:S(2)}, u32[]{:S(2)}) collective-permute-start(bf16[128,2048]{1,0:T(8,128)(2,1)S(1)} %get-tuple-element.23), channel_id=1, source_target_pairs={{0,6},{2,0},{4,2},{6,4},{1,7},{3,1},{5,3},{7,5},{8,14},{10,8},{12,... | collective-permute-start | bytes 1572872 | tf_op jit(solution)/shard_map/ppermute | solution.py:21
  50.2 11.2 %shard_map.81 = (bf16[1024,512]{1,0:T(8,128)(2,1)}, f32[16,128]{1,0:T(8,128)S(1)}) custom-call(s32[5]{0:T(128)S(1)} %stack.23.at, f32[4,8,4,128]{3,2,1,0:T(4,128)S(1)} %bitcast.29, bf16[2048,1024]{1,0:T(8,128)(2,1)} %get-tuple-element.15.refs_0_.scaled, f32[1,2048]{1,0:T(1,128)S(1)} %get-tuple-element.16.bias, bf16[256,1024]{1,0:T(8,128)(2,1)S(1)} %shard_map.76.own.refs_0_, ...), custom_call_target="tpu_custom_call" | custom-call | flops 4294967296 | bytes 8388608 | tf_op jit(solution)/shard_map/pallas_call | solution.py:239
  62.1 9.4 %all-to-all-start.1 = ((bf16[32,32,512]{2,1,0:T(8,128)(2,1)}), bf16[32,32,512]{2,1,0:T(8,128)(2,1)}, u32[]{:S(2)}, u32[]{:S(2)}) async-start(bf16[32,32,512]{2,1,0:T(8,128)(2,1)} %bitcast.32), calls=%async_computation.1 | async-start | bytes 2097152 | tf_op jit(solution)/shard_map/all_to_all | solution.py:394
  74.1 20.4 %collective-permute-done.20 = f32[16,128]{1,0:T(8,128)S(1)} collective-permute-done((f32[16,128]{1,0:T(8,128)S(1)}, f32[16,128]{1,0:T(8,128)S(1)}, u32[]{:S(2)}, u32[]{:S(2)}) %collective-permute-start.20) | collective-permute-done | bytes 8224 | tf_op jit(solution)/shard_map/ppermute | solution.py:25
  94.5 1.9 %collective-permute-start.21 = (f32[16,128]{1,0:T(8,128)S(1)}, f32[16,128]{1,0:T(8,128)S(1)}, u32[]{:S(2)}, u32[]{:S(2)}) collective-permute-start(f32[16,128]{1,0:T(8,128)S(1)} %add.65), channel_id=1, source_target_pairs={{0,16},{8,24},{16,0},{24,8},{32,48},{40,56},{48,32},{56,40},{1,17}... | collective-permute-start | bytes 24584 | tf_op jit(solution)/shard_map/ppermute | solution.py:25
  98.8 5.4 %collective-permute-start.22 = (f32[16,128]{1,0:T(8,128)S(1)}, f32[16,128]{1,0:T(8,128)S(1)}, u32[]{:S(2)}, u32[]{:S(2)}) collective-permute-start(f32[16,128]{1,0:T(8,128)S(1)} %add.66), channel_id=1, source_target_pairs={{0,32},{8,40},{16,48},{24,56},{32,0},{40,8},{48,16},{56,24},{1,33}... | collective-permute-start | bytes 24584 | tf_op jit(solution)/shard_map/ppermute | solution.py:25
  105.3 2.7 %collective-permute-start.25 = (f32[16,128]{1,0:T(8,128)S(1)}, f32[16,128]{1,0:T(8,128)S(1)}, u32[]{:S(2)}, u32[]{:S(2)}) collective-permute-start(f32[16,128]{1,0:T(8,128)S(1)} %add.67), channel_id=1, source_target_pairs={{0,192},{64,0},{128,64},{192,128},{1,193},{65,1},{129,65},{193,129... | collective-permute-start | bytes 24584 | tf_op jit(solution)/shard_map/ppermute | solution.py:21
  108.5 4.4 %collective-permute-start.7 = (bf16[64,2048]{1,0:T(8,128)(2,1)S(1)}, bf16[64,2048]{1,0:T(8,128)(2,1)S(1)}, u32[]{:S(2)}, u32[]{:S(2)}) collective-permute-start(bf16[64,2048]{1,0:T(8,128)(2,1)S(1)} %slice.12), channel_id=1, source_target_pairs={{0,1},{1,0},{2,3},{3,2},{4,5},{5,4},{6,7},{7,6},{8,9},{9,8},{10,11... | collective-permute-start | bytes 786440 | tf_op jit(solution)/shard_map/ppermute | solution.py:21
  113.8 3.3 %collective-permute-start.17 = (bf16[64,2048]{1,0:T(8,128)(2,1)S(1)}, bf16[64,2048]{1,0:T(8,128)(2,1)S(1)}, u32[]{:S(2)}, u32[]{:S(2)}) collective-permute-start(bf16[64,2048]{1,0:T(8,128)(2,1)S(1)} %slice.13), channel_id=1, source_target_pairs={{0,1},{1,0},{2,3},{3,2},{4,5},{5,4},{6,7},{7,6},{8,9},{9,8},{10,11... | collective-permute-start | bytes 786440 | tf_op jit(solution)/shard_map/ppermute | solution.py:21
  118.2 1.9 %shard_map.83 = bf16[64,16384]{1,0:T(8,128)(2,1)} custom-call(s32[5]{0:T(128)S(1)} %stack.23.at, bf16[64,2048]{1,0:T(8,128)(2,1)S(1)} %collective-permute-done.5.refs_0_, bf16[64,2048]{1,0:T(8,128)(2,1)S(1)} %collective-permute-done.7.refs_1_, bf16[64,2048]{1,0:T(8,128)(2,1)S(1)} %collective-permute-done.17.refs_2_, ...), custom_call_target="tpu_custom_call" | custom-call | bytes 4194304 | tf_op jit(solution)/shard_map/pallas_call | solution.py:357
  120.2 1.4 %convert_reduce_fusion = f32[4,32,512]{2,1,0:T(8,128)S(1)} fusion(bf16[32,32,512]{2,1,0:T(8,128)(2,1)} %all-to-all-done.1), kind=kLoop, calls=%fused_computation | loop fusion | flops 983040 | bytes 1310720 | tf_op jit(solution)/shard_map/reduce_sum | solution.py:403
  (66 shorter events, 13.1 us)
Async XLA Ops:
  0.6 13.3 %collective-permute-start = (bf16[64,1024]{1,0:T(8,128)(2,1)}, bf16[64,1024]{1,0:T(8,128)(2,1)S(1)}, u32[]{:S(2)}, u32[]{:S(2)}) collective-permute-start(bf16[64,1024]{1,0:T(8,128)(2,1)} %own.1), channel_id=1, source_target_pairs={{0,2},{2,4},{4,6},{6,0},{1,3},{3,5},{5,7},{7,1},{8,10},{10,12},{12... | collective-permute-start | bytes 393224 | tf_op jit(solution)/shard_map/ppermute | solution.py:21
  2.8 11.2 %collective-permute-start.1 = (bf16[64,1024]{1,0:T(8,128)(2,1)}, bf16[64,1024]{1,0:T(8,128)(2,1)S(1)}, u32[]{:S(2)}, u32[]{:S(2)}) collective-permute-start(bf16[64,1024]{1,0:T(8,128)(2,1)} %own.1), channel_id=1, source_target_pairs={{0,6},{2,0},{4,2},{6,4},{1,7},{3,1},{5,3},{7,5},{8,14},{10,8},{12,... | collective-permute-start | bytes 393224 | tf_op jit(solution)/shard_map/ppermute | solution.py:21
  4.1 9.9 %collective-permute-start.2 = (bf16[64,1024]{1,0:T(8,128)(2,1)}, bf16[64,1024]{1,0:T(8,128)(2,1)S(1)}, u32[]{:S(2)}, u32[]{:S(2)}) collective-permute-start(bf16[64,1024]{1,0:T(8,128)(2,1)} %own.1), channel_id=1, source_target_pairs={{0,4},{2,6},{4,0},{6,2},{1,5},{3,7},{5,1},{7,3},{8,12},{10,14},{12... | collective-permute-start | bytes 393224 | tf_op jit(solution)/shard_map/ppermute | solution.py:21
  5.8 8.2 %collective-permute-start.3 = (bf16[64,1024]{1,0:T(8,128)(2,1)}, bf16[64,1024]{1,0:T(8,128)(2,1)S(1)}, u32[]{:S(2)}, u32[]{:S(2)}) collective-permute-start(bf16[64,1024]{1,0:T(8,128)(2,1)} %own.1), channel_id=1, source_target_pairs={{0,128},{64,192},{128,0},{192,64},{1,129},{65,193},{129,1},{193,65... | collective-permute-start | bytes 393224 | tf_op jit(solution)/shard_map/ppermute | solution.py:21
  14.6 7.3 %collective-permute-start.4 = (bf16[256,1024]{1,0:T(8,128)(2,1)S(1)}, bf16[256,1024]{1,0:T(8,128)(2,1)S(1)}, u32[]{:S(2)}, u32[]{:S(2)}) collective-permute-start(bf16[256,1024]{1,0:T(8,128)(2,1)S(1)} %shard_map.76.own.refs_0_), channel_id=1, source_target_pairs={{0,1},{1,0},{2,3},{3,2},{4,5},{5,4},{6,7},{7,6},{8,9},{9,8},{10,11... | collective-permute-start | bytes 1572872 | tf_op jit(solution)/shard_map/ppermute | solution.py:21
  16.5 21.4 %collective-permute-start.8 = (bf16[256,1024]{1,0:T(8,128)(2,1)S(1)}, bf16[256,1024]{1,0:T(8,128)(2,1)}, u32[]{:S(2)}, u32[]{:S(2)}) collective-permute-start(bf16[256,1024]{1,0:T(8,128)(2,1)S(1)} %shard_map.76.own.refs_0_), channel_id=1, source_target_pairs={{0,64},{64,128},{128,192},{192,0},{1,65},{65,129},{129,193},{193,1... | collective-permute-start | bytes 1572872 | tf_op jit(solution)/shard_map/ppermute | solution.py:21
  16.9 21.2 %collective-permute-start.10 = (bf16[256,1024]{1,0:T(8,128)(2,1)S(1)}, bf16[256,1024]{1,0:T(8,128)(2,1)}, u32[]{:S(2)}, u32[]{:S(2)}) collective-permute-start(bf16[256,1024]{1,0:T(8,128)(2,1)S(1)} %shard_map.76.own.refs_0_), channel_id=1, source_target_pairs={{0,192},{64,0},{128,64},{192,128},{1,193},{65,1},{129,65},{193,129... | collective-permute-start | bytes 1572872 | tf_op jit(solution)/shard_map/ppermute | solution.py:21
  19.2 19.2 %collective-permute-start.12 = (bf16[64,1024]{1,0:T(8,128)(2,1)S(1)}, bf16[64,1024]{1,0:T(8,128)(2,1)S(1)}, u32[]{:S(2)}, u32[]{:S(2)}) collective-permute-start(bf16[64,1024]{1,0:T(8,128)(2,1)S(1)} %collective-permute-done.3.refs_1_.own), channel_id=1, source_target_pairs={{0,2},{2,4},{4,6},{6,0},{1,3},{3,5},{5,7},{7,1},{8,10},{10,12},{12... | collective-permute-start | bytes 393224 | tf_op jit(solution)/shard_map/ppermute | solution.py:21
  19.5 18.9 %collective-permute-start.13 = (bf16[64,1024]{1,0:T(8,128)(2,1)S(1)}, bf16[64,1024]{1,0:T(8,128)(2,1)S(1)}, u32[]{:S(2)}, u32[]{:S(2)}) collective-permute-start(bf16[64,1024]{1,0:T(8,128)(2,1)S(1)} %collective-permute-done.3.refs_1_.own), channel_id=1, source_target_pairs={{0,6},{2,0},{4,2},{6,4},{1,7},{3,1},{5,3},{7,5},{8,14},{10,8},{12,... | collective-permute-start | bytes 393224 | tf_op jit(solution)/shard_map/ppermute | solution.py:21
  21.9 16.5 %collective-permute-start.14 = (bf16[64,1024]{1,0:T(8,128)(2,1)S(1)}, bf16[64,1024]{1,0:T(8,128)(2,1)S(1)}, u32[]{:S(2)}, u32[]{:S(2)}) collective-permute-start(bf16[64,1024]{1,0:T(8,128)(2,1)S(1)} %collective-permute-done.3.refs_1_.own), channel_id=1, source_target_pairs={{0,4},{2,6},{4,0},{6,2},{1,5},{3,7},{5,1},{7,3},{8,12},{10,14},{12... | collective-permute-start | bytes 393224 | tf_op jit(solution)/shard_map/ppermute | solution.py:21
  29.4 13.3 %all-to-all-start = ((f32[32,4,128]{2,1,0:T(4,128)}), f32[32,4,128]{2,1,0:T(4,128)S(1)}, u32[]{:S(2)}, u32[]{:S(2)}) async-start(f32[32,4,128]{2,1,0:T(4,128)} %get-tuple-element.17.ahead), calls=%async_computation | async-start | bytes 131072 | tf_op jit(solution)/shard_map/all_to_all | solution.py:381
  37.8 12.4 %collective-permute-start.9 = (bf16[256,1024]{1,0:T(8,128)(2,1)}, bf16[256,1024]{1,0:T(8,128)(2,1)}, u32[]{:S(2)}, u32[]{:S(2)}) collective-permute-start(bf16[256,1024]{1,0:T(8,128)(2,1)} %collective-permute-done.8.refs_2_), channel_id=1, source_target_pairs={{0,1},{1,0},{2,3},{3,2},{4,5},{5,4},{6,7},{7,6},{8,9},{9,8},{10,11... | collective-permute-start | bytes 1572872 | tf_op jit(solution)/shard_map/ppermute | solution.py:21
  38.1 12.1 %collective-permute-start.11 = (bf16[256,1024]{1,0:T(8,128)(2,1)}, bf16[256,1024]{1,0:T(8,128)(2,1)}, u32[]{:S(2)}, u32[]{:S(2)}) collective-permute-start(bf16[256,1024]{1,0:T(8,128)(2,1)} %collective-permute-done.10.refs_4_), channel_id=1, source_target_pairs={{0,1},{1,0},{2,3},{3,2},{4,5},{5,4},{6,7},{7,6},{8,9},{9,8},{10,11... | collective-permute-start | bytes 1572872 | tf_op jit(solution)/shard_map/ppermute | solution.py:21
  43.2 7.0 %collective-permute-start.15 = (bf16[256,1024]{1,0:T(8,128)(2,1)S(1)}, bf16[256,1024]{1,0:T(8,128)(2,1)S(1)}, u32[]{:S(2)}, u32[]{:S(2)}) collective-permute-start(bf16[256,1024]{1,0:T(8,128)(2,1)S(1)} %shard_map.80.refs_6_), channel_id=1, source_target_pairs={{0,1},{1,0},{2,3},{3,2},{4,5},{5,4},{6,7},{7,6},{8,9},{9,8},{10,11... | collective-permute-start | bytes 1572872 | tf_op jit(solution)/shard_map/ppermute | solution.py:21
  47.3 14.9 %collective-permute-start.6 = (bf16[128,2048]{1,0:T(8,128)(2,1)S(1)}, bf16[128,2048]{1,0:T(8,128)(2,1)S(1)}, u32[]{:S(2)}, u32[]{:S(2)}) collective-permute-start(bf16[128,2048]{1,0:T(8,128)(2,1)S(1)} %get-tuple-element.20), channel_id=1, source_target_pairs={{0,2},{2,4},{4,6},{6,0},{1,3},{3,5},{5,7},{7,1},{8,10},{10,12},{12... | collective-permute-start | bytes 1572872 | tf_op jit(solution)/shard_map/ppermute | solution.py:21
  47.9 14.3 %collective-permute-start.18 = (bf16[128,2048]{1,0:T(8,128)(2,1)S(1)}, bf16[128,2048]{1,0:T(8,128)(2,1)S(1)}, u32[]{:S(2)}, u32[]{:S(2)}) collective-permute-start(bf16[128,2048]{1,0:T(8,128)(2,1)S(1)} %get-tuple-element.23), channel_id=1, source_target_pairs={{0,6},{2,0},{4,2},{6,4},{1,7},{3,1},{5,3},{7,5},{8,14},{10,8},{12,... | collective-permute-start | bytes 1572872 | tf_op jit(solution)/shard_map/ppermute | solution.py:21
  62.1 58.0 %all-to-all-start.1 = ((bf16[32,32,512]{2,1,0:T(8,128)(2,1)}), bf16[32,32,512]{2,1,0:T(8,128)(2,1)}, u32[]{:S(2)}, u32[]{:S(2)}) async-start(bf16[32,32,512]{2,1,0:T(8,128)(2,1)} %bitcast.32), calls=%async_computation.1 | async-start | bytes 2097152 | tf_op jit(solution)/shard_map/all_to_all | solution.py:394
  71.5 22.9 %collective-permute-start.20 = (f32[16,128]{1,0:T(8,128)S(1)}, f32[16,128]{1,0:T(8,128)S(1)}, u32[]{:S(2)}, u32[]{:S(2)}) collective-permute-start(f32[16,128]{1,0:T(8,128)S(1)} %get-tuple-element.22.refs_1_), channel_id=1, source_target_pairs={{0,8},{8,0},{16,24},{24,16},{32,40},{40,32},{48,56},{56,48},{1,9},... | collective-permute-start | bytes 24584 | tf_op jit(solution)/shard_map/ppermute | solution.py:25
  72.8 40.2 %collective-permute-start.16 = (bf16[128,2048]{1,0:T(8,128)(2,1)}, bf16[128,2048]{1,0:T(8,128)(2,1)S(1)}, u32[]{:S(2)}, u32[]{:S(2)}) collective-permute-start(bf16[128,2048]{1,0:T(8,128)(2,1)} %shard_map.82), channel_id=1, source_target_pairs={{0,4},{2,6},{4,0},{6,2},{1,5},{3,7},{5,1},{7,3},{8,12},{10,14},{12... | collective-permute-start | bytes 1572872 | tf_op jit(solution)/shard_map/ppermute | solution.py:21
  97.7 20.5 %collective-permute-start.5 = (bf16[64,2048]{1,0:T(8,128)(2,1)S(1)}, bf16[64,2048]{1,0:T(8,128)(2,1)S(1)}, u32[]{:S(2)}, u32[]{:S(2)}) collective-permute-start(bf16[64,2048]{1,0:T(8,128)(2,1)S(1)} %get-tuple-element.19.refs_8_), channel_id=1, source_target_pairs={{0,1},{1,0},{2,3},{3,2},{4,5},{5,4},{6,7},{7,6},{8,9},{9,8},{10,11... | collective-permute-start | bytes 786440 | tf_op jit(solution)/shard_map/ppermute | solution.py:21
  98.8 6.5 %collective-permute-start.22 = (f32[16,128]{1,0:T(8,128)S(1)}, f32[16,128]{1,0:T(8,128)S(1)}, u32[]{:S(2)}, u32[]{:S(2)}) collective-permute-start(f32[16,128]{1,0:T(8,128)S(1)} %add.66), channel_id=1, source_target_pairs={{0,32},{8,40},{16,48},{24,56},{32,0},{40,8},{48,16},{56,24},{1,33}... | collective-permute-start | bytes 24584 | tf_op jit(solution)/shard_map/ppermute | solution.py:25
  105.3 7.8 %collective-permute-start.25 = (f32[16,128]{1,0:T(8,128)S(1)}, f32[16,128]{1,0:T(8,128)S(1)}, u32[]{:S(2)}, u32[]{:S(2)}) collective-permute-start(f32[16,128]{1,0:T(8,128)S(1)} %add.67), channel_id=1, source_target_pairs={{0,192},{64,0},{128,64},{192,128},{1,193},{65,1},{129,65},{193,129... | collective-permute-start | bytes 24584 | tf_op jit(solution)/shard_map/ppermute | solution.py:21
  107.9 5.8 %collective-permute-start.24 = (f32[16,128]{1,0:T(8,128)S(1)}, f32[16,128]{1,0:T(8,128)S(1)}, u32[]{:S(2)}, u32[]{:S(2)}) collective-permute-start(f32[16,128]{1,0:T(8,128)S(1)} %add.67), channel_id=1, source_target_pairs={{0,128},{64,192},{128,0},{192,64},{1,129},{65,193},{129,1},{193,65... | collective-permute-start | bytes 24584 | tf_op jit(solution)/shard_map/ppermute | solution.py:21
  108.5 9.7 %collective-permute-start.7 = (bf16[64,2048]{1,0:T(8,128)(2,1)S(1)}, bf16[64,2048]{1,0:T(8,128)(2,1)S(1)}, u32[]{:S(2)}, u32[]{:S(2)}) collective-permute-start(bf16[64,2048]{1,0:T(8,128)(2,1)S(1)} %slice.12), channel_id=1, source_target_pairs={{0,1},{1,0},{2,3},{3,2},{4,5},{5,4},{6,7},{7,6},{8,9},{9,8},{10,11... | collective-permute-start | bytes 786440 | tf_op jit(solution)/shard_map/ppermute | solution.py:21
  (7 other events, 57.5 us)

commit v8 on v7

--- a/solution.py
+++ b/solution.py
@@ -19,10 +19,6 @@
 def shift(value, axis, step):
     n = SIZES[axis]
     return lax.ppermute(value, axis, [(i, (i + step) % n) for i in range(n)])
-
-
-def swap(value, bit):
-    return lax.ppermute(value, ("h", "l"), [(z, z ^ bit) for z in range(8)])
 
 
 def still(value):
@@ -193,8 +189,8 @@
 
 def sums_kernel(at, shares, scaled, bias, *refs):
     pieces = refs[:8]
-    sums, counts = refs[9:11]
-    rows, weights, lse, wide, sems = refs[11:]
+    sums = refs[9]
+    rows, weights, lse, wide, sems = refs[10:]
     copies = [
         pltpu.make_async_copy(piece, rows.at[pl.ds(i * 256, 256)], sems.at[i])
         for i, piece in enumerate(pieces)
@@ -222,9 +218,10 @@
         weights[:, cut] = weight
         count = count + weight[:, :128].astype(F32) + weight[:, 128:].astype(F32)
     count = jnp.sum(count, axis=1, keepdims=True)
-    counts[...] = jnp.zeros_like(counts)
-    for b in range(4):
-        counts[pl.ds(y * 4 + b, 1), :] = line(count[b * 128 : b * 128 + 128])
+    lines = jnp.concatenate([line(count[b : b + 128]) for b in range(0, 512, 128)], axis=0)
+    high = lines.astype(BF).astype(F32)
+    tail = jnp.concatenate([high, lines - high], axis=0).astype(BF)
+    sums[:, 128:136, :] = jnp.broadcast_to(tail[None], (32, 8, 128))
     for j in range(4):
         block = lax.dot_general(
             weights[...],
@@ -232,7 +229,10 @@
             (((1,), (0,)), ((), ())),
             preferred_element_type=F32,
         )
-        sums[j * 256 : j * 256 + 256, :] = jnp.transpose(block.astype(BF))
+        block = jnp.transpose(block.astype(BF))
+        for q in range(4):
+            part = block[:, q * 128 : q * 128 + 128].reshape(8, 32, 128)
+            sums[j * 8 : j * 8 + 8, q * 32 : q * 32 + 32, :] = part
 
 
 def partial_sums(at, shares, scaled, bias_row, pieces, first):
@@ -247,10 +247,7 @@
                 pl.BlockSpec((1, 512), lambda i, at: (0, at[2])),
             ]
             + anywhere(9),
-            out_specs=(
-                pl.BlockSpec((1024, 512), lambda i, at: (0, 0)),
-                pl.BlockSpec((16, 128), lambda i, at: (0, 0)),
-            ),
+            out_specs=pl.BlockSpec((32, 136, 128), lambda i, at: (0, 0, 0)),
             scratch_shapes=[
                 VMEM((2048, 1024), BF),
                 VMEM((512, 2048), BF),
@@ -259,7 +256,7 @@
                 pltpu.SemaphoreType.DMA((8,)),
             ],
         ),
-        out_shape=(pltpu.HBM((1024, 512), BF), jax.ShapeDtypeStruct((16, 128), F32)),
+        out_shape=pltpu.HBM((32, 136, 128), BF),
         compiler_params=params(),
         cost_estimate=pl.CostEstimate(
             flops=4 * 512 * 2048 * 1024, bytes_accessed=8 << 20, transcendentals=1 << 20
@@ -337,6 +334,39 @@
     )(at, still(means), ahead)
 
 
+def finish_kernel(sent, means, new, counts):
+    for y in range(4):
+        total = sent[y * 8, :, :].astype(F32)
+        for z in range(1, 8):
+            total = total + sent[y * 8 + z, :, :].astype(F32)
+        count = total[128:132, :] + total[132:136, :]
+        counts[y * 4 : y * 4 + 4, :] = count
+        for q in range(4):
+            cut = slice(y * 512 + q * 128, y * 512 + q * 128 + 128)
+            part = total[q * 32 : q * 32 + 32, :] + means[:, cut]
+            new[:, cut] = part / (count[q : q + 1, :] + 1.0)
+
+
+def finish(sent, mean_cols):
+    return pl.pallas_call(
+        finish_kernel,
+        grid=(1,),
+        in_specs=[
+            pl.BlockSpec((32, 136, 128), lambda i: (0, 0, 0)),
+            pl.BlockSpec((32, 2048), lambda i: (0, 0)),
+        ],
+        out_specs=[
+            pl.BlockSpec((32, 2048), lambda i: (0, 0)),
+            pl.BlockSpec((16, 128), lambda i: (0, 0)),
+        ],
+        out_shape=[
+            jax.ShapeDtypeStruct((32, 2048), F32),
+            jax.ShapeDtypeStruct((16, 128), F32),
+        ],
+        compiler_params=params(),
+    )(sent, still(mean_cols))
+
+
 def lay_kernel(at, *refs):
     pieces, out, sems = refs[:8], refs[8], refs[9]
     x, c = at[0], at[1]
@@ -388,21 +418,16 @@
 
     blocks = responsibilities(at, shares, score)
     ahead, behind = shift(blocks[2], "x", 1), shift(blocks[4], "x", 3)
-    sums, counts = partial_sums(at, shares, scaled, bias_row, pieces, blocks[0])
-    pairs = [ahead, shift(hold(blocks[3], counts), "x", 2), behind]
+    sums = partial_sums(at, shares, scaled, bias_row, pieces, blocks[0])
     sums = hold(sums, ahead, behind)
+    pairs = [ahead, shift(hold(blocks[3], still(sums)), "x", 2), behind]
     sent = lax.all_to_all(sums, ("y", "h", "l"), split_axis=0, concat_axis=0, tiled=True)
     theirs = [shift(b, "c", 1) for b in [blocks[0]] + [pair[:64] for pair in pairs]]
     held = theirs + [blocks[1]] + pairs
     resp_rows = lay_out(at, held)
 
-    counts = counts + swap(counts, 1)
-    counts = counts + swap(counts, 2)
-    counts = counts + swap(counts, 4)
-    counts = sum([shift(counts, "y", i) for i in range(1, 4)], counts).reshape(2048)
-    sums = jnp.sum(sent.reshape(4, 8, 32, 512).astype(F32), axis=1)
-    sums = sums.transpose(1, 0, 2).reshape(32, 2048)
-    new_means_t = (sums + mean_cols) / (counts[None, :] + 1.0)
+    new_means_t, counts = finish(sent, mean_cols)
+    counts = counts.reshape(2048)
 
     lse = joined(lax.dynamic_index_in_dim(shares, y, 0, keepdims=False)).reshape(8, 64)
     own_lse = lax.dynamic_index_in_dim(lse, c * 4 + x, 0, keepdims=False)

time: 123 us -> 118 us (0.959)
  the two profiles are of different devices: /device:TPU:1 before, /device:TPU:32 now
where the time goes in v8:
time: 118 us; the launch traced here: 116 us
  Pallas kernels  58.4 us (49%)
  starting transfers between devices  36.1 us (31%)
  waiting for transfers between devices  16.2 us (14%)
  local copies, waits for them, and re-layouts  2.33 us (2%)
  between operations  1.46 us (1%)
  other arithmetic  1.32 us (1%)
    pallas_call x1, Pallas kernels, lay_out(): pl.pallas_call(lay_kernel, in_specs=[scalar()] + anywhere(8), out_specs=p...  25.6 us
    ppermute x20, starting transfers between devices, shift(): return lax.ppermute(value, axis, [(i, (i + step) % n) for i in range(n)])  21.9 us
    ppermute x20, waiting for transfers between devices, shift(): return lax.ppermute(value, axis, [(i, (i + step) % n) for i in range(n)])  11.8 us
    pallas_call x1, Pallas kernels, partial_sums(): pl.pallas_call(sums_kernel, grid_spec=pltpu.PrefetchScalarGridSpec(num_sc...  11.3 us
    all_to_all x1, starting transfers between devices, body(): lax.all_to_all(sums, ('y', 'h', 'l'), split_axis=0, concat_axis=0, tiled=...  9.54 us
    pallas_call x1, Pallas kernels, scores(): pl.pallas_call(score_kernel, grid=(2048 // width,), out_shape=(pltpu.HBM(...  7.24 us
    pallas_call x1, Pallas kernels, prepare(): pl.pallas_call(prepare_kernel, grid=(4,), in_specs=[pl.BlockSpec((512, 10...  5.26 us
    all_to_all x1, starting transfers between devices, body(): lax.all_to_all(share, ('y', 'x', 'c'), split_axis=0, concat_axis=0, tiled...  4.69 us
  transfers between devices with their start and end apart: 22, of which 4 were waited for; matrix products, arithmetic and copies ran while one was open for 3% of the time, Pallas kernels for 48%

profile of v8, /device:TPU:32, one launch (start us, length us, event | category | flops | bytes accessed | tf_op | source)
XLA Modules:
  0.0 115.8 jit_solution(12791149586669810195)
XLA Ops:
  0.6 1.6 %collective-permute-start = (bf16[64,1024]{1,0:T(8,128)(2,1)}, bf16[64,1024]{1,0:T(8,128)(2,1)S(1)}, u32[]{:S(2)}, u32[]{:S(2)}) collective-permute-start(bf16[64,1024]{1,0:T(8,128)(2,1)} %own.1), channel_id=1, source_target_pairs={{0,2},{2,4},{4,6},{6,0},{1,3},{3,5},{5,7},{7,1},{8,10},{10,12},{12... | collective-permute-start | bytes 393224 | tf_op jit(solution)/shard_map/ppermute | solution.py:21
  2.2 1.7 %collective-permute-start.1 = (bf16[64,1024]{1,0:T(8,128)(2,1)}, bf16[64,1024]{1,0:T(8,128)(2,1)S(1)}, u32[]{:S(2)}, u32[]{:S(2)}) collective-permute-start(bf16[64,1024]{1,0:T(8,128)(2,1)} %own.1), channel_id=1, source_target_pairs={{0,6},{2,0},{4,2},{6,4},{1,7},{3,1},{5,3},{7,5},{8,14},{10,8},{12,... | collective-permute-start | bytes 393224 | tf_op jit(solution)/shard_map/ppermute | solution.py:21
  3.9 1.8 %collective-permute-start.2 = (bf16[64,1024]{1,0:T(8,128)(2,1)}, bf16[64,1024]{1,0:T(8,128)(2,1)S(1)}, u32[]{:S(2)}, u32[]{:S(2)}) collective-permute-start(bf16[64,1024]{1,0:T(8,128)(2,1)} %own.1), channel_id=1, source_target_pairs={{0,4},{2,6},{4,0},{6,2},{1,5},{3,7},{5,1},{7,3},{8,12},{10,14},{12... | collective-permute-start | bytes 393224 | tf_op jit(solution)/shard_map/ppermute | solution.py:21
  5.8 3.2 %collective-permute-start.3 = (bf16[64,1024]{1,0:T(8,128)(2,1)}, bf16[64,1024]{1,0:T(8,128)(2,1)S(1)}, u32[]{:S(2)}, u32[]{:S(2)}) collective-permute-start(bf16[64,1024]{1,0:T(8,128)(2,1)} %own.1), channel_id=1, source_target_pairs={{0,128},{64,192},{128,0},{192,64},{1,129},{65,193},{129,1},{193,65... | collective-permute-start | bytes 393224 | tf_op jit(solution)/shard_map/ppermute | solution.py:21
  9.0 5.3 %shard_map.75 = (bf16[2048,1024]{1,0:T(8,128)(2,1)}, f32[1,2048]{1,0:T(1,128)S(1)}) custom-call(bf16[2048,1024]{1,0:T(8,128)(2,1)} %means.3, f32[1,1024]{1,0:T(1,128)} %bitcast.23, f32[1,2048]{1,0:T(1,128)} %bitcast.24), custom_call_target="tpu_custom_call" | custom-call | flops 12582912 | bytes 8388608 | tf_op jit(solution)/shard_map/pallas_call | solution.py:60
  15.0 0.8 collective-permute-start.8
  15.8 2.6 %collective-permute-start.10 = (bf16[256,1024]{1,0:T(8,128)(2,1)S(1)}, bf16[256,1024]{1,0:T(8,128)(2,1)}, u32[]{:S(2)}, u32[]{:S(2)}) collective-permute-start(bf16[256,1024]{1,0:T(8,128)(2,1)S(1)} %shard_map.76.own.refs_0_), channel_id=1, source_target_pairs={{0,192},{64,0},{128,64},{192,128},{1,193},{65,1},{129,65},{193,129... | collective-permute-start | bytes 1572872 | tf_op jit(solution)/shard_map/ppermute | solution.py:21
  18.9 2.6 %collective-permute-start.13 = (bf16[64,1024]{1,0:T(8,128)(2,1)S(1)}, bf16[64,1024]{1,0:T(8,128)(2,1)S(1)}, u32[]{:S(2)}, u32[]{:S(2)}) collective-permute-start(bf16[64,1024]{1,0:T(8,128)(2,1)S(1)} %collective-permute-done.3.refs_1_.own), channel_id=1, source_target_pairs={{0,6},{2,0},{4,2},{6,4},{1,7},{3,1},{5,3},{7,5},{8,14},{10,8},{12,... | collective-permute-start | bytes 393224 | tf_op jit(solution)/shard_map/ppermute | solution.py:21
  22.1 7.2 %shard_map.77 = (f32[512,2048]{1,0:T(8,128)}, f32[32,4,128]{2,1,0:T(4,128)}) custom-call(s32[5]{0:T(128)S(1)} %stack.23.at, bf16[256,1024]{1,0:T(8,128)(2,1)S(1)} %shard_map.76.own.refs_0_, bf16[256,1024]{1,0:T(8,128)(2,1)S(1)} %collective-permute-done.4.other.refs_1_, bf16[2048,1024]{1,0:T(8,128)(2,1)} %get-tuple-element.15.refs_0_.scaled, ...), custom_call_target="tpu_custom_call" | custom-call | flops 2147483648 | bytes 9437184 | tf_op jit(solution)/shard_map/pallas_call | solution.py:144
  29.3 4.7 %all-to-all-start = ((f32[32,4,128]{2,1,0:T(4,128)}), f32[32,4,128]{2,1,0:T(4,128)S(1)}, u32[]{:S(2)}, u32[]{:S(2)}) async-start(f32[32,4,128]{2,1,0:T(4,128)} %get-tuple-element.17.ahead), calls=%async_computation | async-start | bytes 131072 | tf_op jit(solution)/shard_map/all_to_all | solution.py:411
  34.0 2.5 %shard_map.79.refs_0_.means = f32[32,2048]{1,0:T(8,128)} custom-call(s32[5]{0:T(128)S(1)} %stack.23.at, bf16[2048,1024]{1,0:T(8,128)(2,1)} %means.3, f32[32,4,128]{2,1,0:T(4,128)} %get-tuple-element.17.ahead), custom_call_target="tpu_custom_call" | custom-call | tf_op jit(solution)/shard_map/pallas_call | solution.py:323
  37.1 4.4 %all-to-all-done.refs_1_ = f32[32,4,128]{2,1,0:T(4,128)S(1)} async-done(((f32[32,4,128]{2,1,0:T(4,128)}), f32[32,4,128]{2,1,0:T(4,128)S(1)}, u32[]{:S(2)}, u32[]{:S(2)}) %all-to-all-start) | async-done | bytes 65568 | tf_op jit(solution)/shard_map/all_to_all | solution.py:411
  42.3 3.6 %shard_map.78 = (bf16[64,2048]{1,0:T(8,128)(2,1)S(1)}, bf16[64,2048]{1,0:T(8,128)(2,1)S(1)}, bf16[128,2048]{1,0:T(8,128)(2,1)S(1)}, bf16[128,2048]{1,0:T(8,128)(2,1)}, bf16[128,2048]{1,0:T(8,128)(2,1)S(1)}) custom-call(s32[5]{0:T(128)S(1)} %stack.23.at, f32[4,8,4,128]{3,2,1,0:T(4,128)S(1)} %bitcast.19, f32[512,2048]{1,0:T(8,128)} %get-tuple-element.18.score), custom_call_target="tpu_custom_call" | custom-call | flops 2097152 | bytes 6291456 | tf_op jit(solution)/shard_map/pallas_call | solution.py:298
  45.9 0.9 collective-permute-start.6
  46.8 2.6 %collective-permute-start.16 = (bf16[128,2048]{1,0:T(8,128)(2,1)S(1)}, bf16[128,2048]{1,0:T(8,128)(2,1)S(1)}, u32[]{:S(2)}, u32[]{:S(2)}) collective-permute-start(bf16[128,2048]{1,0:T(8,128)(2,1)S(1)} %get-tuple-element.22), channel_id=1, source_target_pairs={{0,6},{2,0},{4,2},{6,4},{1,7},{3,1},{5,3},{7,5},{8,14},{10,8},{12,... | collective-permute-start | bytes 1572872 | tf_op jit(solution)/shard_map/ppermute | solution.py:21
  49.4 11.3 %shard_map.81.refs_0_ = bf16[32,136,128]{2,1,0:T(8,128)(2,1)} custom-call(s32[5]{0:T(128)S(1)} %stack.23.at, f32[4,8,4,128]{3,2,1,0:T(4,128)S(1)} %bitcast.20, bf16[2048,1024]{1,0:T(8,128)(2,1)} %get-tuple-element.15.refs_0_.scaled, f32[1,2048]{1,0:T(1,128)S(1)} %get-tuple-element.16.bias, bf16[256,1024]{1,0:T(8,128)(2,1)S(1)} %shard_map.76.own.refs_0_, ...), custom_call_target="tpu_custom_call" | custom-call | flops 4294967296 | bytes 8388608 | tf_op jit(solution)/shard_map/pallas_call | solution.py:239
  60.7 0.9 collective-permute-done.6.refs_1_.refs_5_
  61.6 9.5 %all-to-all-start.1 = ((bf16[32,136,128]{2,1,0:T(8,128)(2,1)}), bf16[32,136,128]{2,1,0:T(8,128)(2,1)S(1)}, u32[]{:S(2)}, u32[]{:S(2)}) async-start(bf16[32,136,128]{2,1,0:T(8,128)(2,1)} %shard_map.82.refs_1_), calls=%async_computation.1 | async-start | bytes 2228224 | tf_op jit(solution)/shard_map/all_to_all | solution.py:424
  71.2 1.5 %collective-permute-start.17 = (bf16[128,2048]{1,0:T(8,128)(2,1)}, bf16[128,2048]{1,0:T(8,128)(2,1)S(1)}, u32[]{:S(2)}, u32[]{:S(2)}) collective-permute-start(bf16[128,2048]{1,0:T(8,128)(2,1)} %shard_map.83), channel_id=1, source_target_pairs={{0,4},{2,6},{4,0},{6,2},{1,5},{3,7},{5,1},{7,3},{8,12},{10,14},{12... | collective-permute-start | bytes 1572872 | tf_op jit(solution)/shard_map/ppermute | solution.py:21
  76.2 9.6 %collective-permute-done.17.refs_6_ = bf16[128,2048]{1,0:T(8,128)(2,1)S(1)} collective-permute-done((bf16[128,2048]{1,0:T(8,128)(2,1)}, bf16[128,2048]{1,0:T(8,128)(2,1)S(1)}, u32[]{:S(2)}, u32[]{:S(2)}) %collective-permute-start.17) | collective-permute-done | bytes 524320 | tf_op jit(solution)/shard_map/ppermute | solution.py:21
  85.8 0.7 slice.13
  87.1 1.3 %collective-permute-done.18.refs_2_ = bf16[64,2048]{1,0:T(8,128)(2,1)} collective-permute-done((bf16[64,2048]{1,0:T(8,128)(2,1)}, bf16[64,2048]{1,0:T(8,128)(2,1)}, u32[]{:S(2)}, u32[]{:S(2)}) %collective-permute-start.18) | collective-permute-done | bytes 262176 | tf_op jit(solution)/shard_map/ppermute | solution.py:21
  88.4 25.6 %shard_map.84 = bf16[64,16384]{1,0:T(8,128)(2,1)} custom-call(s32[5]{0:T(128)S(1)} %stack.23.at, bf16[64,2048]{1,0:T(8,128)(2,1)S(1)} %collective-permute-done.5.refs_0_, bf16[64,2048]{1,0:T(8,128)(2,1)} %collective-permute-done.7.refs_1_, bf16[64,2048]{1,0:T(8,128)(2,1)} %collective-permute-done.18.refs_2_, ...), custom_call_target="tpu_custom_call" | custom-call | bytes 4194304 | tf_op jit(solution)/shard_map/pallas_call | solution.py:387
  114.0 1.8 %shard_map.85 = (f32[32,2048]{1,0:T(8,128)}, f32[16,128]{1,0:T(8,128)}) custom-call(bf16[32,136,128]{2,1,0:T(8,128)(2,1)S(1)} %all-to-all-done.1.sent, f32[32,2048]{1,0:T(8,128)} %shard_map.79.refs_0_.means), custom_call_target="tpu_custom_call" | custom-call | tf_op jit(solution)/shard_map/pallas_call | solution.py:351
  (52 shorter events, 6.7 us)
Async XLA Ops:
  0.6 13.7 %collective-permute-start = (bf16[64,1024]{1,0:T(8,128)(2,1)}, bf16[64,1024]{1,0:T(8,128)(2,1)S(1)}, u32[]{:S(2)}, u32[]{:S(2)}) collective-permute-start(bf16[64,1024]{1,0:T(8,128)(2,1)} %own.1), channel_id=1, source_target_pairs={{0,2},{2,4},{4,6},{6,0},{1,3},{3,5},{5,7},{7,1},{8,10},{10,12},{12... | collective-permute-start | bytes 393224 | tf_op jit(solution)/shard_map/ppermute | solution.py:21
  2.2 12.1 %collective-permute-start.1 = (bf16[64,1024]{1,0:T(8,128)(2,1)}, bf16[64,1024]{1,0:T(8,128)(2,1)S(1)}, u32[]{:S(2)}, u32[]{:S(2)}) collective-permute-start(bf16[64,1024]{1,0:T(8,128)(2,1)} %own.1), channel_id=1, source_target_pairs={{0,6},{2,0},{4,2},{6,4},{1,7},{3,1},{5,3},{7,5},{8,14},{10,8},{12,... | collective-permute-start | bytes 393224 | tf_op jit(solution)/shard_map/ppermute | solution.py:21
  3.9 10.4 %collective-permute-start.2 = (bf16[64,1024]{1,0:T(8,128)(2,1)}, bf16[64,1024]{1,0:T(8,128)(2,1)S(1)}, u32[]{:S(2)}, u32[]{:S(2)}) collective-permute-start(bf16[64,1024]{1,0:T(8,128)(2,1)} %own.1), channel_id=1, source_target_pairs={{0,4},{2,6},{4,0},{6,2},{1,5},{3,7},{5,1},{7,3},{8,12},{10,14},{12... | collective-permute-start | bytes 393224 | tf_op jit(solution)/shard_map/ppermute | solution.py:21
  5.8 8.6 %collective-permute-start.3 = (bf16[64,1024]{1,0:T(8,128)(2,1)}, bf16[64,1024]{1,0:T(8,128)(2,1)S(1)}, u32[]{:S(2)}, u32[]{:S(2)}) collective-permute-start(bf16[64,1024]{1,0:T(8,128)(2,1)} %own.1), channel_id=1, source_target_pairs={{0,128},{64,192},{128,0},{192,64},{1,129},{65,193},{129,1},{193,65... | collective-permute-start | bytes 393224 | tf_op jit(solution)/shard_map/ppermute | solution.py:21
  14.9 6.7 %collective-permute-start.4 = (bf16[256,1024]{1,0:T(8,128)(2,1)S(1)}, bf16[256,1024]{1,0:T(8,128)(2,1)S(1)}, u32[]{:S(2)}, u32[]{:S(2)}) collective-permute-start(bf16[256,1024]{1,0:T(8,128)(2,1)S(1)} %shard_map.76.own.refs_0_), channel_id=1, source_target_pairs={{0,1},{1,0},{2,3},{3,2},{4,5},{5,4},{6,7},{7,6},{8,9},{9,8},{10,11... | collective-permute-start | bytes 1572872 | tf_op jit(solution)/shard_map/ppermute | solution.py:21
  15.0 21.5 %collective-permute-start.8 = (bf16[256,1024]{1,0:T(8,128)(2,1)S(1)}, bf16[256,1024]{1,0:T(8,128)(2,1)}, u32[]{:S(2)}, u32[]{:S(2)}) collective-permute-start(bf16[256,1024]{1,0:T(8,128)(2,1)S(1)} %shard_map.76.own.refs_0_), channel_id=1, source_target_pairs={{0,64},{64,128},{128,192},{192,0},{1,65},{65,129},{129,193},{193,1... | collective-permute-start | bytes 1572872 | tf_op jit(solution)/shard_map/ppermute | solution.py:21
  15.8 21.0 %collective-permute-start.10 = (bf16[256,1024]{1,0:T(8,128)(2,1)S(1)}, bf16[256,1024]{1,0:T(8,128)(2,1)}, u32[]{:S(2)}, u32[]{:S(2)}) collective-permute-start(bf16[256,1024]{1,0:T(8,128)(2,1)S(1)} %shard_map.76.own.refs_0_), channel_id=1, source_target_pairs={{0,192},{64,0},{128,64},{192,128},{1,193},{65,1},{129,65},{193,129... | collective-permute-start | bytes 1572872 | tf_op jit(solution)/shard_map/ppermute | solution.py:21
  18.3 18.7 %collective-permute-start.12 = (bf16[64,1024]{1,0:T(8,128)(2,1)S(1)}, bf16[64,1024]{1,0:T(8,128)(2,1)S(1)}, u32[]{:S(2)}, u32[]{:S(2)}) collective-permute-start(bf16[64,1024]{1,0:T(8,128)(2,1)S(1)} %collective-permute-done.3.refs_1_.own), channel_id=1, source_target_pairs={{0,2},{2,4},{4,6},{6,0},{1,3},{3,5},{5,7},{7,1},{8,10},{10,12},{12... | collective-permute-start | bytes 393224 | tf_op jit(solution)/shard_map/ppermute | solution.py:21
  18.9 18.1 %collective-permute-start.13 = (bf16[64,1024]{1,0:T(8,128)(2,1)S(1)}, bf16[64,1024]{1,0:T(8,128)(2,1)S(1)}, u32[]{:S(2)}, u32[]{:S(2)}) collective-permute-start(bf16[64,1024]{1,0:T(8,128)(2,1)S(1)} %collective-permute-done.3.refs_1_.own), channel_id=1, source_target_pairs={{0,6},{2,0},{4,2},{6,4},{1,7},{3,1},{5,3},{7,5},{8,14},{10,8},{12,... | collective-permute-start | bytes 393224 | tf_op jit(solution)/shard_map/ppermute | solution.py:21
  21.6 15.5 %collective-permute-start.14 = (bf16[64,1024]{1,0:T(8,128)(2,1)S(1)}, bf16[64,1024]{1,0:T(8,128)(2,1)S(1)}, u32[]{:S(2)}, u32[]{:S(2)}) collective-permute-start(bf16[64,1024]{1,0:T(8,128)(2,1)S(1)} %collective-permute-done.3.refs_1_.own), channel_id=1, source_target_pairs={{0,4},{2,6},{4,0},{6,2},{1,5},{3,7},{5,1},{7,3},{8,12},{10,14},{12... | collective-permute-start | bytes 393224 | tf_op jit(solution)/shard_map/ppermute | solution.py:21
  29.3 12.2 %all-to-all-start = ((f32[32,4,128]{2,1,0:T(4,128)}), f32[32,4,128]{2,1,0:T(4,128)S(1)}, u32[]{:S(2)}, u32[]{:S(2)}) async-start(f32[32,4,128]{2,1,0:T(4,128)} %get-tuple-element.17.ahead), calls=%async_computation | async-start | bytes 131072 | tf_op jit(solution)/shard_map/all_to_all | solution.py:411
  36.6 12.9 %collective-permute-start.9 = (bf16[256,1024]{1,0:T(8,128)(2,1)}, bf16[256,1024]{1,0:T(8,128)(2,1)}, u32[]{:S(2)}, u32[]{:S(2)}) collective-permute-start(bf16[256,1024]{1,0:T(8,128)(2,1)} %collective-permute-done.8.refs_2_), channel_id=1, source_target_pairs={{0,1},{1,0},{2,3},{3,2},{4,5},{5,4},{6,7},{7,6},{8,9},{9,8},{10,11... | collective-permute-start | bytes 1572872 | tf_op jit(solution)/shard_map/ppermute | solution.py:21
  36.8 12.6 %collective-permute-start.11 = (bf16[256,1024]{1,0:T(8,128)(2,1)}, bf16[256,1024]{1,0:T(8,128)(2,1)}, u32[]{:S(2)}, u32[]{:S(2)}) collective-permute-start(bf16[256,1024]{1,0:T(8,128)(2,1)} %collective-permute-done.10.refs_4_), channel_id=1, source_target_pairs={{0,1},{1,0},{2,3},{3,2},{4,5},{5,4},{6,7},{7,6},{8,9},{9,8},{10,11... | collective-permute-start | bytes 1572872 | tf_op jit(solution)/shard_map/ppermute | solution.py:21
  42.1 7.3 %collective-permute-start.15 = (bf16[256,1024]{1,0:T(8,128)(2,1)S(1)}, bf16[256,1024]{1,0:T(8,128)(2,1)S(1)}, u32[]{:S(2)}, u32[]{:S(2)}) collective-permute-start(bf16[256,1024]{1,0:T(8,128)(2,1)S(1)} %shard_map.80.refs_6_), channel_id=1, source_target_pairs={{0,1},{1,0},{2,3},{3,2},{4,5},{5,4},{6,7},{7,6},{8,9},{9,8},{10,11... | collective-permute-start | bytes 1572872 | tf_op jit(solution)/shard_map/ppermute | solution.py:21
  45.9 14.8 %copy-start.3 = (bf16[64,2048]{1,0:T(8,128)(2,1)}, bf16[64,2048]{1,0:T(8,128)(2,1)S(1)}, u32[]{:S(2)}) copy-start(bf16[64,2048]{1,0:T(8,128)(2,1)S(1)} %get-tuple-element.19.refs_8_) | copy-start | bytes 786436
  45.9 15.7 %collective-permute-start.6 = (bf16[128,2048]{1,0:T(8,128)(2,1)S(1)}, bf16[128,2048]{1,0:T(8,128)(2,1)S(1)}, u32[]{:S(2)}, u32[]{:S(2)}) collective-permute-start(bf16[128,2048]{1,0:T(8,128)(2,1)S(1)} %get-tuple-element.20), channel_id=1, source_target_pairs={{0,2},{2,4},{4,6},{6,0},{1,3},{3,5},{5,7},{7,1},{8,10},{10,12},{12... | collective-permute-start | bytes 1572872 | tf_op jit(solution)/shard_map/ppermute | solution.py:21
  46.8 14.8 %collective-permute-start.16 = (bf16[128,2048]{1,0:T(8,128)(2,1)S(1)}, bf16[128,2048]{1,0:T(8,128)(2,1)S(1)}, u32[]{:S(2)}, u32[]{:S(2)}) collective-permute-start(bf16[128,2048]{1,0:T(8,128)(2,1)S(1)} %get-tuple-element.22), channel_id=1, source_target_pairs={{0,6},{2,0},{4,2},{6,4},{1,7},{3,1},{5,3},{7,5},{8,14},{10,8},{12,... | collective-permute-start | bytes 1572872 | tf_op jit(solution)/shard_map/ppermute | solution.py:21
  61.6 11.1 %copy-start.4 = (f32[1024]{0:T(1024)S(1)}, f32[1024]{0:T(1024)}, u32[]{:S(2)}) copy-start(f32[1024]{0:T(1024)} %param.7) | copy-start | bytes 12292
  61.6 52.4 %all-to-all-start.1 = ((bf16[32,136,128]{2,1,0:T(8,128)(2,1)}), bf16[32,136,128]{2,1,0:T(8,128)(2,1)S(1)}, u32[]{:S(2)}, u32[]{:S(2)}) async-start(bf16[32,136,128]{2,1,0:T(8,128)(2,1)} %shard_map.82.refs_1_), calls=%async_computation.1 | async-start | bytes 2228224 | tf_op jit(solution)/shard_map/all_to_all | solution.py:424
  71.2 14.6 %collective-permute-start.17 = (bf16[128,2048]{1,0:T(8,128)(2,1)}, bf16[128,2048]{1,0:T(8,128)(2,1)S(1)}, u32[]{:S(2)}, u32[]{:S(2)}) collective-permute-start(bf16[128,2048]{1,0:T(8,128)(2,1)} %shard_map.83), channel_id=1, source_target_pairs={{0,4},{2,6},{4,0},{6,2},{1,5},{3,7},{5,1},{7,3},{8,12},{10,14},{12... | collective-permute-start | bytes 1572872 | tf_op jit(solution)/shard_map/ppermute | solution.py:21
  74.1 13.0 %collective-permute-start.5 = (bf16[64,2048]{1,0:T(8,128)(2,1)}, bf16[64,2048]{1,0:T(8,128)(2,1)S(1)}, u32[]{:S(2)}, u32[]{:S(2)}) collective-permute-start(bf16[64,2048]{1,0:T(8,128)(2,1)} %copy-done.3), channel_id=1, source_target_pairs={{0,1},{1,0},{2,3},{3,2},{4,5},{5,4},{6,7},{7,6},{8,9},{9,8},{10,11... | collective-permute-start | bytes 786440 | tf_op jit(solution)/shard_map/ppermute | solution.py:21
  75.0 12.2 %collective-permute-start.7 = (bf16[64,2048]{1,0:T(8,128)(2,1)}, bf16[64,2048]{1,0:T(8,128)(2,1)}, u32[]{:S(2)}, u32[]{:S(2)}) collective-permute-start(bf16[64,2048]{1,0:T(8,128)(2,1)} %slice.12), channel_id=1, source_target_pairs={{0,1},{1,0},{2,3},{3,2},{4,5},{5,4},{6,7},{7,6},{8,9},{9,8},{10,11... | collective-permute-start | bytes 786440 | tf_op jit(solution)/shard_map/ppermute | solution.py:21
  76.2 11.0 %collective-permute-start.19 = (bf16[64,2048]{1,0:T(8,128)(2,1)}, bf16[64,2048]{1,0:T(8,128)(2,1)}, u32[]{:S(2)}, u32[]{:S(2)}) collective-permute-start(bf16[64,2048]{1,0:T(8,128)(2,1)} %slice.14), channel_id=1, source_target_pairs={{0,1},{1,0},{2,3},{3,2},{4,5},{5,4},{6,7},{7,6},{8,9},{9,8},{10,11... | collective-permute-start | bytes 786440 | tf_op jit(solution)/shard_map/ppermute | solution.py:21
  86.5 1.9 %collective-permute-start.18 = (bf16[64,2048]{1,0:T(8,128)(2,1)}, bf16[64,2048]{1,0:T(8,128)(2,1)}, u32[]{:S(2)}, u32[]{:S(2)}) collective-permute-start(bf16[64,2048]{1,0:T(8,128)(2,1)} %slice.13), channel_id=1, source_target_pairs={{0,1},{1,0},{2,3},{3,2},{4,5},{5,4},{6,7},{7,6},{8,9},{9,8},{10,11... | collective-permute-start | bytes 786440 | tf_op jit(solution)/shard_map/ppermute | solution.py:21
  (3 other events, 20.2 us)

commit v9 on v8

--- a/solution.py
+++ b/solution.py
@@ -386,7 +386,7 @@
 def lay_out(at, pieces):
     return pl.pallas_call(
         lay_kernel,
-        in_specs=[scalar()] + anywhere(8),
+        in_specs=[scalar()] + [whole()] * 8,
         out_specs=pl.BlockSpec(memory_space=pl.ANY),
         scratch_shapes=[pltpu.SemaphoreType.DMA((8,))],
         out_shape=jax.ShapeDtypeStruct((64, 16384), BF),

time: 118 us -> 103 us (0.87); the launches traced: 116 us -> 103 us
  Pallas kernels: 58.4 us -> 35.3 us
  waiting for transfers between devices: 16.2 us -> 26 us
    pallas_call x1, Pallas kernels: 25.6 us -> 2.5 us  [lay_out(): pl.pallas_call(lay_kernel, in_specs=[scalar()] + [whole()] * 8, out_specs...]
    all_to_all x1, waiting for transfers between devices: 0.01 us -> 9.84 us  [body(): lax.all_to_all(sums, ('y', 'h', 'l'), split_axis=0, concat_axis=0, tiled=...]
  transfers between devices with their start and end apart: 22 -> 22, of which waited for: 4 -> 5; matrix products, arithmetic and copies ran while one was open for 3% -> 4% of each run, Pallas kernels for 48% -> 32%
where the time goes in v9:
time: 103 us
  starting transfers between devices  36.1 us (35%)
  Pallas kernels  35.3 us (34%)
  waiting for transfers between devices  26 us (25%)
  local copies, waits for them, and re-layouts  2.33 us (2%)
  between operations  1.45 us (1%)
  other arithmetic  1.32 us (1%)
    ppermute x20, starting transfers between devices, shift(): return lax.ppermute(value, axis, [(i, (i + step) % n) for i in range(n)])  21.9 us
    ppermute x20, waiting for transfers between devices, shift(): return lax.ppermute(value, axis, [(i, (i + step) % n) for i in range(n)])  11.8 us
    pallas_call x1, Pallas kernels, partial_sums(): pl.pallas_call(sums_kernel, grid_spec=pltpu.PrefetchScalarGridSpec(num_sc...  11.3 us
    all_to_all x1, waiting for transfers between devices, body(): lax.all_to_all(sums, ('y', 'h', 'l'), split_axis=0, concat_axis=0, tiled=...  9.84 us
    all_to_all x1, starting transfers between devices, body(): lax.all_to_all(sums, ('y', 'h', 'l'), split_axis=0, concat_axis=0, tiled=...  9.54 us
    pallas_call x1, Pallas kernels, scores(): pl.pallas_call(score_kernel, grid=(2048 // width,), out_shape=(pltpu.HBM(...  7.24 us
    pallas_call x1, Pallas kernels, prepare(): pl.pallas_call(prepare_kernel, grid=(4,), in_specs=[pl.BlockSpec((512, 10...  5.26 us
    all_to_all x1, starting transfers between devices, body(): lax.all_to_all(share, ('y', 'x', 'c'), split_axis=0, concat_axis=0, tiled...  4.69 us
  transfers between devices with their start and end apart: 22, of which 5 were waited for; matrix products, arithmetic and copies ran while one was open for 4% of the time, Pallas kernels for 32%

profile of v9, /device:TPU:32, one launch (start us, length us, event | category | flops | bytes accessed | tf_op | source)
XLA Modules:
  0.0 102.6 jit_solution(11959340261344505240)
XLA Ops:
  0.6 1.6 %collective-permute-start = (bf16[64,1024]{1,0:T(8,128)(2,1)}, bf16[64,1024]{1,0:T(8,128)(2,1)S(1)}, u32[]{:S(2)}, u32[]{:S(2)}) collective-permute-start(bf16[64,1024]{1,0:T(8,128)(2,1)} %own.1), channel_id=1, source_target_pairs={{0,2},{2,4},{4,6},{6,0},{1,3},{3,5},{5,7},{7,1},{8,10},{10,12},{12... | collective-permute-start | bytes 393224 | tf_op jit(solution)/shard_map/ppermute | solution.py:21
  2.2 1.7 %collective-permute-start.1 = (bf16[64,1024]{1,0:T(8,128)(2,1)}, bf16[64,1024]{1,0:T(8,128)(2,1)S(1)}, u32[]{:S(2)}, u32[]{:S(2)}) collective-permute-start(bf16[64,1024]{1,0:T(8,128)(2,1)} %own.1), channel_id=1, source_target_pairs={{0,6},{2,0},{4,2},{6,4},{1,7},{3,1},{5,3},{7,5},{8,14},{10,8},{12,... | collective-permute-start | bytes 393224 | tf_op jit(solution)/shard_map/ppermute | solution.py:21
  3.9 1.8 %collective-permute-start.2 = (bf16[64,1024]{1,0:T(8,128)(2,1)}, bf16[64,1024]{1,0:T(8,128)(2,1)S(1)}, u32[]{:S(2)}, u32[]{:S(2)}) collective-permute-start(bf16[64,1024]{1,0:T(8,128)(2,1)} %own.1), channel_id=1, source_target_pairs={{0,4},{2,6},{4,0},{6,2},{1,5},{3,7},{5,1},{7,3},{8,12},{10,14},{12... | collective-permute-start | bytes 393224 | tf_op jit(solution)/shard_map/ppermute | solution.py:21
  5.8 3.2 %collective-permute-start.3 = (bf16[64,1024]{1,0:T(8,128)(2,1)}, bf16[64,1024]{1,0:T(8,128)(2,1)S(1)}, u32[]{:S(2)}, u32[]{:S(2)}) collective-permute-start(bf16[64,1024]{1,0:T(8,128)(2,1)} %own.1), channel_id=1, source_target_pairs={{0,128},{64,192},{128,0},{192,64},{1,129},{65,193},{129,1},{193,65... | collective-permute-start | bytes 393224 | tf_op jit(solution)/shard_map/ppermute | solution.py:21
  9.0 5.3 %shard_map.75 = (bf16[2048,1024]{1,0:T(8,128)(2,1)}, f32[1,2048]{1,0:T(1,128)S(1)}) custom-call(bf16[2048,1024]{1,0:T(8,128)(2,1)} %means.3, f32[1,1024]{1,0:T(1,128)} %bitcast.23, f32[1,2048]{1,0:T(1,128)} %bitcast.24), custom_call_target="tpu_custom_call" | custom-call | flops 12582912 | bytes 8388608 | tf_op jit(solution)/shard_map/pallas_call | solution.py:60
  15.0 0.8 collective-permute-start.8
  15.8 2.6 %collective-permute-start.10 = (bf16[256,1024]{1,0:T(8,128)(2,1)S(1)}, bf16[256,1024]{1,0:T(8,128)(2,1)}, u32[]{:S(2)}, u32[]{:S(2)}) collective-permute-start(bf16[256,1024]{1,0:T(8,128)(2,1)S(1)} %shard_map.76.own.refs_0_), channel_id=1, source_target_pairs={{0,192},{64,0},{128,64},{192,128},{1,193},{65,1},{129,65},{193,129... | collective-permute-start | bytes 1572872 | tf_op jit(solution)/shard_map/ppermute | solution.py:21
  18.9 2.6 %collective-permute-start.13 = (bf16[64,1024]{1,0:T(8,128)(2,1)S(1)}, bf16[64,1024]{1,0:T(8,128)(2,1)S(1)}, u32[]{:S(2)}, u32[]{:S(2)}) collective-permute-start(bf16[64,1024]{1,0:T(8,128)(2,1)S(1)} %collective-permute-done.3.refs_1_.own), channel_id=1, source_target_pairs={{0,6},{2,0},{4,2},{6,4},{1,7},{3,1},{5,3},{7,5},{8,14},{10,8},{12,... | collective-permute-start | bytes 393224 | tf_op jit(solution)/shard_map/ppermute | solution.py:21
  22.1 7.2 %shard_map.77 = (f32[512,2048]{1,0:T(8,128)}, f32[32,4,128]{2,1,0:T(4,128)}) custom-call(s32[5]{0:T(128)S(1)} %stack.23.at, bf16[256,1024]{1,0:T(8,128)(2,1)S(1)} %shard_map.76.own.refs_0_, bf16[256,1024]{1,0:T(8,128)(2,1)S(1)} %collective-permute-done.4.other.refs_1_, bf16[2048,1024]{1,0:T(8,128)(2,1)} %get-tuple-element.15.refs_0_.scaled, ...), custom_call_target="tpu_custom_call" | custom-call | flops 2147483648 | bytes 9437184 | tf_op jit(solution)/shard_map/pallas_call | solution.py:144
  29.3 4.7 %all-to-all-start = ((f32[32,4,128]{2,1,0:T(4,128)}), f32[32,4,128]{2,1,0:T(4,128)S(1)}, u32[]{:S(2)}, u32[]{:S(2)}) async-start(f32[32,4,128]{2,1,0:T(4,128)} %get-tuple-element.17.ahead), calls=%async_computation | async-start | bytes 131072 | tf_op jit(solution)/shard_map/all_to_all | solution.py:411
  34.0 2.5 %shard_map.79.refs_0_.means = f32[32,2048]{1,0:T(8,128)} custom-call(s32[5]{0:T(128)S(1)} %stack.23.at, bf16[2048,1024]{1,0:T(8,128)(2,1)} %means.3, f32[32,4,128]{2,1,0:T(4,128)} %get-tuple-element.17.ahead), custom_call_target="tpu_custom_call" | custom-call | tf_op jit(solution)/shard_map/pallas_call | solution.py:323
  37.1 4.4 %all-to-all-done.refs_1_ = f32[32,4,128]{2,1,0:T(4,128)S(1)} async-done(((f32[32,4,128]{2,1,0:T(4,128)}), f32[32,4,128]{2,1,0:T(4,128)S(1)}, u32[]{:S(2)}, u32[]{:S(2)}) %all-to-all-start) | async-done | bytes 65568 | tf_op jit(solution)/shard_map/all_to_all | solution.py:411
  42.3 3.6 %shard_map.78 = (bf16[64,2048]{1,0:T(8,128)(2,1)S(1)}, bf16[64,2048]{1,0:T(8,128)(2,1)S(1)}, bf16[128,2048]{1,0:T(8,128)(2,1)S(1)}, bf16[128,2048]{1,0:T(8,128)(2,1)}, bf16[128,2048]{1,0:T(8,128)(2,1)S(1)}) custom-call(s32[5]{0:T(128)S(1)} %stack.23.at, f32[4,8,4,128]{3,2,1,0:T(4,128)S(1)} %bitcast.19, f32[512,2048]{1,0:T(8,128)} %get-tuple-element.18.score), custom_call_target="tpu_custom_call" | custom-call | flops 2097152 | bytes 6291456 | tf_op jit(solution)/shard_map/pallas_call | solution.py:298
  45.9 0.9 collective-permute-start.6
  46.8 2.6 %collective-permute-start.16 = (bf16[128,2048]{1,0:T(8,128)(2,1)S(1)}, bf16[128,2048]{1,0:T(8,128)(2,1)S(1)}, u32[]{:S(2)}, u32[]{:S(2)}) collective-permute-start(bf16[128,2048]{1,0:T(8,128)(2,1)S(1)} %get-tuple-element.22), channel_id=1, source_target_pairs={{0,6},{2,0},{4,2},{6,4},{1,7},{3,1},{5,3},{7,5},{8,14},{10,8},{12,... | collective-permute-start | bytes 1572872 | tf_op jit(solution)/shard_map/ppermute | solution.py:21
  49.4 11.3 %shard_map.81.refs_0_ = bf16[32,136,128]{2,1,0:T(8,128)(2,1)} custom-call(s32[5]{0:T(128)S(1)} %stack.23.at, f32[4,8,4,128]{3,2,1,0:T(4,128)S(1)} %bitcast.20, bf16[2048,1024]{1,0:T(8,128)(2,1)} %get-tuple-element.15.refs_0_.scaled, f32[1,2048]{1,0:T(1,128)S(1)} %get-tuple-element.16.bias, bf16[256,1024]{1,0:T(8,128)(2,1)S(1)} %shard_map.76.own.refs_0_, ...), custom_call_target="tpu_custom_call" | custom-call | flops 4294967296 | bytes 8388608 | tf_op jit(solution)/shard_map/pallas_call | solution.py:239
  60.7 0.9 collective-permute-done.6.refs_1_.refs_5_
  61.6 9.5 %all-to-all-start.1 = ((bf16[32,136,128]{2,1,0:T(8,128)(2,1)}), bf16[32,136,128]{2,1,0:T(8,128)(2,1)S(1)}, u32[]{:S(2)}, u32[]{:S(2)}) async-start(bf16[32,136,128]{2,1,0:T(8,128)(2,1)} %shard_map.82.refs_1_), calls=%async_computation.1 | async-start | bytes 2228224 | tf_op jit(solution)/shard_map/all_to_all | solution.py:424
  71.2 1.5 %collective-permute-start.17 = (bf16[128,2048]{1,0:T(8,128)(2,1)}, bf16[128,2048]{1,0:T(8,128)(2,1)S(1)}, u32[]{:S(2)}, u32[]{:S(2)}) collective-permute-start(bf16[128,2048]{1,0:T(8,128)(2,1)} %shard_map.83), channel_id=1, source_target_pairs={{0,4},{2,6},{4,0},{6,2},{1,5},{3,7},{5,1},{7,3},{8,12},{10,14},{12... | collective-permute-start | bytes 1572872 | tf_op jit(solution)/shard_map/ppermute | solution.py:21
  76.2 9.6 %collective-permute-done.17.refs_6_ = bf16[128,2048]{1,0:T(8,128)(2,1)S(1)} collective-permute-done((bf16[128,2048]{1,0:T(8,128)(2,1)}, bf16[128,2048]{1,0:T(8,128)(2,1)S(1)}, u32[]{:S(2)}, u32[]{:S(2)}) %collective-permute-start.17) | collective-permute-done | bytes 524320 | tf_op jit(solution)/shard_map/ppermute | solution.py:21
  87.1 1.3 %collective-permute-done.18.refs_2_ = bf16[64,2048]{1,0:T(8,128)(2,1)} collective-permute-done((bf16[64,2048]{1,0:T(8,128)(2,1)}, bf16[64,2048]{1,0:T(8,128)(2,1)}, u32[]{:S(2)}, u32[]{:S(2)}) %collective-permute-start.18) | collective-permute-done | bytes 262176 | tf_op jit(solution)/shard_map/ppermute | solution.py:21
  88.4 2.5 %shard_map.84 = bf16[64,16384]{1,0:T(8,128)(2,1)} custom-call(s32[5]{0:T(128)S(1)} %stack.23.at, bf16[64,2048]{1,0:T(8,128)(2,1)S(1)} %collective-permute-done.5.refs_0_, bf16[64,2048]{1,0:T(8,128)(2,1)} %collective-permute-done.7.refs_1_, bf16[64,2048]{1,0:T(8,128)(2,1)} %collective-permute-done.18.refs_2_, ...), custom_call_target="tpu_custom_call" | custom-call | bytes 4194304 | tf_op jit(solution)/shard_map/pallas_call | solution.py:387
  90.9 9.8 %all-to-all-done.1.sent = bf16[32,136,128]{2,1,0:T(8,128)(2,1)S(1)} async-done(((bf16[32,136,128]{2,1,0:T(8,128)(2,1)}), bf16[32,136,128]{2,1,0:T(8,128)(2,1)S(1)}, u32[]{:S(2)}, u32[]{:S(2)}) %all-to-all-start.1) | async-done | bytes 1114144 | tf_op jit(solution)/shard_map/all_to_all | solution.py:424
  100.7 1.8 %shard_map.85 = (f32[32,2048]{1,0:T(8,128)}, f32[16,128]{1,0:T(8,128)}) custom-call(bf16[32,136,128]{2,1,0:T(8,128)(2,1)S(1)} %all-to-all-done.1.sent, f32[32,2048]{1,0:T(8,128)} %shard_map.79.refs_0_.means), custom_call_target="tpu_custom_call" | custom-call | tf_op jit(solution)/shard_map/pallas_call | solution.py:351
  (52 shorter events, 7.4 us)
Async XLA Ops:
  0.6 13.7 %collective-permute-start = (bf16[64,1024]{1,0:T(8,128)(2,1)}, bf16[64,1024]{1,0:T(8,128)(2,1)S(1)}, u32[]{:S(2)}, u32[]{:S(2)}) collective-permute-start(bf16[64,1024]{1,0:T(8,128)(2,1)} %own.1), channel_id=1, source_target_pairs={{0,2},{2,4},{4,6},{6,0},{1,3},{3,5},{5,7},{7,1},{8,10},{10,12},{12... | collective-permute-start | bytes 393224 | tf_op jit(solution)/shard_map/ppermute | solution.py:21
  2.2 12.1 %collective-permute-start.1 = (bf16[64,1024]{1,0:T(8,128)(2,1)}, bf16[64,1024]{1,0:T(8,128)(2,1)S(1)}, u32[]{:S(2)}, u32[]{:S(2)}) collective-permute-start(bf16[64,1024]{1,0:T(8,128)(2,1)} %own.1), channel_id=1, source_target_pairs={{0,6},{2,0},{4,2},{6,4},{1,7},{3,1},{5,3},{7,5},{8,14},{10,8},{12,... | collective-permute-start | bytes 393224 | tf_op jit(solution)/shard_map/ppermute | solution.py:21
  3.9 10.4 %collective-permute-start.2 = (bf16[64,1024]{1,0:T(8,128)(2,1)}, bf16[64,1024]{1,0:T(8,128)(2,1)S(1)}, u32[]{:S(2)}, u32[]{:S(2)}) collective-permute-start(bf16[64,1024]{1,0:T(8,128)(2,1)} %own.1), channel_id=1, source_target_pairs={{0,4},{2,6},{4,0},{6,2},{1,5},{3,7},{5,1},{7,3},{8,12},{10,14},{12... | collective-permute-start | bytes 393224 | tf_op jit(solution)/shard_map/ppermute | solution.py:21
  5.8 8.6 %collective-permute-start.3 = (bf16[64,1024]{1,0:T(8,128)(2,1)}, bf16[64,1024]{1,0:T(8,128)(2,1)S(1)}, u32[]{:S(2)}, u32[]{:S(2)}) collective-permute-start(bf16[64,1024]{1,0:T(8,128)(2,1)} %own.1), channel_id=1, source_target_pairs={{0,128},{64,192},{128,0},{192,64},{1,129},{65,193},{129,1},{193,65... | collective-permute-start | bytes 393224 | tf_op jit(solution)/shard_map/ppermute | solution.py:21
  14.9 6.7 %collective-permute-start.4 = (bf16[256,1024]{1,0:T(8,128)(2,1)S(1)}, bf16[256,1024]{1,0:T(8,128)(2,1)S(1)}, u32[]{:S(2)}, u32[]{:S(2)}) collective-permute-start(bf16[256,1024]{1,0:T(8,128)(2,1)S(1)} %shard_map.76.own.refs_0_), channel_id=1, source_target_pairs={{0,1},{1,0},{2,3},{3,2},{4,5},{5,4},{6,7},{7,6},{8,9},{9,8},{10,11... | collective-permute-start | bytes 1572872 | tf_op jit(solution)/shard_map/ppermute | solution.py:21
  15.0 21.5 %collective-permute-start.8 = (bf16[256,1024]{1,0:T(8,128)(2,1)S(1)}, bf16[256,1024]{1,0:T(8,128)(2,1)}, u32[]{:S(2)}, u32[]{:S(2)}) collective-permute-start(bf16[256,1024]{1,0:T(8,128)(2,1)S(1)} %shard_map.76.own.refs_0_), channel_id=1, source_target_pairs={{0,64},{64,128},{128,192},{192,0},{1,65},{65,129},{129,193},{193,1... | collective-permute-start | bytes 1572872 | tf_op jit(solution)/shard_map/ppermute | solution.py:21
  15.8 21.0 %collective-permute-start.10 = (bf16[256,1024]{1,0:T(8,128)(2,1)S(1)}, bf16[256,1024]{1,0:T(8,128)(2,1)}, u32[]{:S(2)}, u32[]{:S(2)}) collective-permute-start(bf16[256,1024]{1,0:T(8,128)(2,1)S(1)} %shard_map.76.own.refs_0_), channel_id=1, source_target_pairs={{0,192},{64,0},{128,64},{192,128},{1,193},{65,1},{129,65},{193,129... | collective-permute-start | bytes 1572872 | tf_op jit(solution)/shard_map/ppermute | solution.py:21
  18.3 18.7 %collective-permute-start.12 = (bf16[64,1024]{1,0:T(8,128)(2,1)S(1)}, bf16[64,1024]{1,0:T(8,128)(2,1)S(1)}, u32[]{:S(2)}, u32[]{:S(2)}) collective-permute-start(bf16[64,1024]{1,0:T(8,128)(2,1)S(1)} %collective-permute-done.3.refs_1_.own), channel_id=1, source_target_pairs={{0,2},{2,4},{4,6},{6,0},{1,3},{3,5},{5,7},{7,1},{8,10},{10,12},{12... | collective-permute-start | bytes 393224 | tf_op jit(solution)/shard_map/ppermute | solution.py:21
  18.9 18.1 %collective-permute-start.13 = (bf16[64,1024]{1,0:T(8,128)(2,1)S(1)}, bf16[64,1024]{1,0:T(8,128)(2,1)S(1)}, u32[]{:S(2)}, u32[]{:S(2)}) collective-permute-start(bf16[64,1024]{1,0:T(8,128)(2,1)S(1)} %collective-permute-done.3.refs_1_.own), channel_id=1, source_target_pairs={{0,6},{2,0},{4,2},{6,4},{1,7},{3,1},{5,3},{7,5},{8,14},{10,8},{12,... | collective-permute-start | bytes 393224 | tf_op jit(solution)/shard_map/ppermute | solution.py:21
  21.6 15.5 %collective-permute-start.14 = (bf16[64,1024]{1,0:T(8,128)(2,1)S(1)}, bf16[64,1024]{1,0:T(8,128)(2,1)S(1)}, u32[]{:S(2)}, u32[]{:S(2)}) collective-permute-start(bf16[64,1024]{1,0:T(8,128)(2,1)S(1)} %collective-permute-done.3.refs_1_.own), channel_id=1, source_target_pairs={{0,4},{2,6},{4,0},{6,2},{1,5},{3,7},{5,1},{7,3},{8,12},{10,14},{12... | collective-permute-start | bytes 393224 | tf_op jit(solution)/shard_map/ppermute | solution.py:21
  29.3 12.2 %all-to-all-start = ((f32[32,4,128]{2,1,0:T(4,128)}), f32[32,4,128]{2,1,0:T(4,128)S(1)}, u32[]{:S(2)}, u32[]{:S(2)}) async-start(f32[32,4,128]{2,1,0:T(4,128)} %get-tuple-element.17.ahead), calls=%async_computation | async-start | bytes 131072 | tf_op jit(solution)/shard_map/all_to_all | solution.py:411
  36.6 12.9 %collective-permute-start.9 = (bf16[256,1024]{1,0:T(8,128)(2,1)}, bf16[256,1024]{1,0:T(8,128)(2,1)}, u32[]{:S(2)}, u32[]{:S(2)}) collective-permute-start(bf16[256,1024]{1,0:T(8,128)(2,1)} %collective-permute-done.8.refs_2_), channel_id=1, source_target_pairs={{0,1},{1,0},{2,3},{3,2},{4,5},{5,4},{6,7},{7,6},{8,9},{9,8},{10,11... | collective-permute-start | bytes 1572872 | tf_op jit(solution)/shard_map/ppermute | solution.py:21
  36.8 12.6 %collective-permute-start.11 = (bf16[256,1024]{1,0:T(8,128)(2,1)}, bf16[256,1024]{1,0:T(8,128)(2,1)}, u32[]{:S(2)}, u32[]{:S(2)}) collective-permute-start(bf16[256,1024]{1,0:T(8,128)(2,1)} %collective-permute-done.10.refs_4_), channel_id=1, source_target_pairs={{0,1},{1,0},{2,3},{3,2},{4,5},{5,4},{6,7},{7,6},{8,9},{9,8},{10,11... | collective-permute-start | bytes 1572872 | tf_op jit(solution)/shard_map/ppermute | solution.py:21
  42.1 7.3 %collective-permute-start.15 = (bf16[256,1024]{1,0:T(8,128)(2,1)S(1)}, bf16[256,1024]{1,0:T(8,128)(2,1)S(1)}, u32[]{:S(2)}, u32[]{:S(2)}) collective-permute-start(bf16[256,1024]{1,0:T(8,128)(2,1)S(1)} %shard_map.80.refs_6_), channel_id=1, source_target_pairs={{0,1},{1,0},{2,3},{3,2},{4,5},{5,4},{6,7},{7,6},{8,9},{9,8},{10,11... | collective-permute-start | bytes 1572872 | tf_op jit(solution)/shard_map/ppermute | solution.py:21
  45.9 14.8 %copy-start.3 = (bf16[64,2048]{1,0:T(8,128)(2,1)}, bf16[64,2048]{1,0:T(8,128)(2,1)S(1)}, u32[]{:S(2)}) copy-start(bf16[64,2048]{1,0:T(8,128)(2,1)S(1)} %get-tuple-element.19.refs_8_) | copy-start | bytes 786436
  45.9 15.7 %collective-permute-start.6 = (bf16[128,2048]{1,0:T(8,128)(2,1)S(1)}, bf16[128,2048]{1,0:T(8,128)(2,1)S(1)}, u32[]{:S(2)}, u32[]{:S(2)}) collective-permute-start(bf16[128,2048]{1,0:T(8,128)(2,1)S(1)} %get-tuple-element.20), channel_id=1, source_target_pairs={{0,2},{2,4},{4,6},{6,0},{1,3},{3,5},{5,7},{7,1},{8,10},{10,12},{12... | collective-permute-start | bytes 1572872 | tf_op jit(solution)/shard_map/ppermute | solution.py:21
  46.8 14.8 %collective-permute-start.16 = (bf16[128,2048]{1,0:T(8,128)(2,1)S(1)}, bf16[128,2048]{1,0:T(8,128)(2,1)S(1)}, u32[]{:S(2)}, u32[]{:S(2)}) collective-permute-start(bf16[128,2048]{1,0:T(8,128)(2,1)S(1)} %get-tuple-element.22), channel_id=1, source_target_pairs={{0,6},{2,0},{4,2},{6,4},{1,7},{3,1},{5,3},{7,5},{8,14},{10,8},{12,... | collective-permute-start | bytes 1572872 | tf_op jit(solution)/shard_map/ppermute | solution.py:21
  61.6 11.1 %copy-start.4 = (f32[1024]{0:T(1024)S(1)}, f32[1024]{0:T(1024)}, u32[]{:S(2)}) copy-start(f32[1024]{0:T(1024)} %param.7) | copy-start | bytes 12292
  61.6 39.1 %all-to-all-start.1 = ((bf16[32,136,128]{2,1,0:T(8,128)(2,1)}), bf16[32,136,128]{2,1,0:T(8,128)(2,1)S(1)}, u32[]{:S(2)}, u32[]{:S(2)}) async-start(bf16[32,136,128]{2,1,0:T(8,128)(2,1)} %shard_map.82.refs_1_), calls=%async_computation.1 | async-start | bytes 2228224 | tf_op jit(solution)/shard_map/all_to_all | solution.py:424
  71.2 14.6 %collective-permute-start.17 = (bf16[128,2048]{1,0:T(8,128)(2,1)}, bf16[128,2048]{1,0:T(8,128)(2,1)S(1)}, u32[]{:S(2)}, u32[]{:S(2)}) collective-permute-start(bf16[128,2048]{1,0:T(8,128)(2,1)} %shard_map.83), channel_id=1, source_target_pairs={{0,4},{2,6},{4,0},{6,2},{1,5},{3,7},{5,1},{7,3},{8,12},{10,14},{12... | collective-permute-start | bytes 1572872 | tf_op jit(solution)/shard_map/ppermute | solution.py:21
  74.1 13.0 %collective-permute-start.5 = (bf16[64,2048]{1,0:T(8,128)(2,1)}, bf16[64,2048]{1,0:T(8,128)(2,1)S(1)}, u32[]{:S(2)}, u32[]{:S(2)}) collective-permute-start(bf16[64,2048]{1,0:T(8,128)(2,1)} %copy-done.3), channel_id=1, source_target_pairs={{0,1},{1,0},{2,3},{3,2},{4,5},{5,4},{6,7},{7,6},{8,9},{9,8},{10,11... | collective-permute-start | bytes 786440 | tf_op jit(solution)/shard_map/ppermute | solution.py:21
  75.0 12.2 %collective-permute-start.7 = (bf16[64,2048]{1,0:T(8,128)(2,1)}, bf16[64,2048]{1,0:T(8,128)(2,1)}, u32[]{:S(2)}, u32[]{:S(2)}) collective-permute-start(bf16[64,2048]{1,0:T(8,128)(2,1)} %slice.12), channel_id=1, source_target_pairs={{0,1},{1,0},{2,3},{3,2},{4,5},{5,4},{6,7},{7,6},{8,9},{9,8},{10,11... | collective-permute-start | bytes 786440 | tf_op jit(solution)/shard_map/ppermute | solution.py:21
  76.2 11.0 %collective-permute-start.19 = (bf16[64,2048]{1,0:T(8,128)(2,1)}, bf16[64,2048]{1,0:T(8,128)(2,1)}, u32[]{:S(2)}, u32[]{:S(2)}) collective-permute-start(bf16[64,2048]{1,0:T(8,128)(2,1)} %slice.14), channel_id=1, source_target_pairs={{0,1},{1,0},{2,3},{3,2},{4,5},{5,4},{6,7},{7,6},{8,9},{9,8},{10,11... | collective-permute-start | bytes 786440 | tf_op jit(solution)/shard_map/ppermute | solution.py:21
  86.5 1.9 %collective-permute-start.18 = (bf16[64,2048]{1,0:T(8,128)(2,1)}, bf16[64,2048]{1,0:T(8,128)(2,1)}, u32[]{:S(2)}, u32[]{:S(2)}) collective-permute-start(bf16[64,2048]{1,0:T(8,128)(2,1)} %slice.13), channel_id=1, source_target_pairs={{0,1},{1,0},{2,3},{3,2},{4,5},{5,4},{6,7},{7,6},{8,9},{9,8},{10,11... | collective-permute-start | bytes 786440 | tf_op jit(solution)/shard_map/ppermute | solution.py:21
  (3 other events, 20.2 us)

commit v10 on v9

--- a/solution.py
+++ b/solution.py
@@ -190,7 +190,7 @@
 def sums_kernel(at, shares, scaled, bias, *refs):
     pieces = refs[:8]
     sums = refs[9]
-    rows, weights, lse, wide, sems = refs[10:]
+    rows, weights, lse, norms, sems = refs[10:]
     copies = [
         pltpu.make_async_copy(piece, rows.at[pl.ds(i * 256, 256)], sems.at[i])
         for i, piece in enumerate(pieces)
@@ -200,39 +200,43 @@
     y, c = at[2], at[1]
     for yy in range(4):
         lse[pl.ds(yy * 4, 4), :] = joined(shares[yy])
-    for b in range(0, 512, 128):
-        wide[b : b + 128, :] = jnp.transpose(jnp.broadcast_to(bias[:, b : b + 128], (128, 128)))
-    shift_up = jnp.concatenate([wide[...], wide[...]], axis=1)
-    count = jnp.zeros((512, 128), F32)
+    parts = []
     for i in range(8):
         there = lax.rem(y + (0, 3, 1, 2)[i // 2], 4)
         core = c if i % 2 == 0 else 1 - c
-        at_row = there * 4 + core * 2
-        norm = jnp.concatenate([lse[pl.ds(at_row, 1), :], lse[pl.ds(at_row + 1, 1), :]], axis=1)
-        cut = slice(i * 256, i * 256 + 256)
-        copies[i].wait()
+        line_at = there * 4 + core * 2
+        parts += [lse[pl.ds(line_at, 1), :], lse[pl.ds(line_at + 1, 1), :]]
+    norms[...] = jnp.transpose(jnp.concatenate(parts + [jnp.zeros((112, 128), F32)], axis=0))
+    count = jnp.zeros((8, 512), F32)
+    for g in range(2):
+        for copy in copies[g * 4 : g * 4 + 4]:
+            copy.wait()
         score = lax.dot_general(
-            scaled[...], rows[cut, :], (((1,), (1,)), ((), ())), preferred_element_type=F32
+            rows[g * 1024 : g * 1024 + 1024, :],
+            scaled[...],
+            (((1,), (1,)), ((), ())),
+            preferred_element_type=F32,
         )
-        weight = jnp.exp(score + shift_up - norm).astype(BF)
-        weights[:, cut] = weight
-        count = count + weight[:, :128].astype(F32) + weight[:, 128:].astype(F32)
-    count = jnp.sum(count, axis=1, keepdims=True)
-    lines = jnp.concatenate([line(count[b : b + 128]) for b in range(0, 512, 128)], axis=0)
+        for q in range(8):
+            j = g * 8 + q
+            shifted = score[q * 128 : q * 128 + 128, :] + (bias[...] - norms[:, j : j + 1])
+            weight = jnp.exp(shifted).astype(BF)
+            weights[j * 128 : j * 128 + 128, :] = weight
+            weight = weight.astype(F32)
+            count = count + functools.reduce(
+                jnp.add, [weight[t : t + 8, :] for t in range(0, 128, 8)]
+            )
+    count = jnp.sum(count, axis=0, keepdims=True)
+    lines = jnp.concatenate([count[:, b : b + 128] for b in range(0, 512, 128)], axis=0)
     high = lines.astype(BF).astype(F32)
     tail = jnp.concatenate([high, lines - high], axis=0).astype(BF)
     sums[:, 128:136, :] = jnp.broadcast_to(tail[None], (32, 8, 128))
-    for j in range(4):
-        block = lax.dot_general(
-            weights[...],
-            rows[:, j * 256 : j * 256 + 256],
-            (((1,), (0,)), ((), ())),
-            preferred_element_type=F32,
-        )
-        block = jnp.transpose(block.astype(BF))
-        for q in range(4):
-            part = block[:, q * 128 : q * 128 + 128].reshape(8, 32, 128)
-            sums[j * 8 : j * 8 + 8, q * 32 : q * 32 + 32, :] = part
+    block = lax.dot_general(
+        rows[...], weights[...], (((0,), (0,)), ((), ())), preferred_element_type=F32
+    ).astype(BF)
+    for q in range(4):
+        part = block[:, q * 128 : q * 128 + 128].reshape(32, 32, 128)
+        sums[:, q * 32 : q * 32 + 32, :] = part
 
 
 def partial_sums(at, shares, scaled, bias_row, pieces, first):
@@ -250,9 +254,9 @@
             out_specs=pl.BlockSpec((32, 136, 128), lambda i, at: (0, 0, 0)),
             scratch_shapes=[
                 VMEM((2048, 1024), BF),
-                VMEM((512, 2048), BF),
+                VMEM((2048, 512), BF),
                 VMEM((16, 128), F32),
-                VMEM((512, 128), F32),
+                VMEM((128, 128), F32),
                 pltpu.SemaphoreType.DMA((8,)),
             ],
         ),
@@ -419,7 +423,7 @@
     blocks = responsibilities(at, shares, score)
     ahead, behind = shift(blocks[2], "x", 1), shift(blocks[4], "x", 3)
     sums = partial_sums(at, shares, scaled, bias_row, pieces, blocks[0])
-    sums = hold(sums, ahead, behind)
+    sums = hold(sums, ahead)
     pairs = [ahead, shift(hold(blocks[3], still(sums)), "x", 2), behind]
     sent = lax.all_to_all(sums, ("y", "h", "l"), split_axis=0, concat_axis=0, tiled=True)
     theirs = [shift(b, "c", 1) for b in [blocks[0]] + [pair[:64] for pair in pairs]]

time: 103 us -> 105 us (1.019); the launches traced: 103 us -> 103 us
  waiting for transfers between devices: 26 us -> 30.3 us
  starting transfers between devices: 36.1 us -> 33.9 us
  Pallas kernels: 35.3 us -> 34.1 us
    ppermute x20, waiting for transfers between devices: 11.8 us -> 17.4 us  [shift(): return lax.ppermute(value, axis, [(i, (i + step) % n) for i in range(n)])]
    ppermute x20, starting transfers between devices: 21.9 us -> 19.7 us  [shift(): return lax.ppermute(value, axis, [(i, (i + step) % n) for i in range(n)])]
    pallas_call x1, Pallas kernels: 11.3 us -> 9.17 us  [partial_sums(): pl.pallas_call(sums_kernel, grid_spec=pltpu.PrefetchScalarGridSpec(num_sc...]
    all_to_all x1, waiting for transfers between devices: 9.84 us -> 8.48 us  [body(): lax.all_to_all(sums, ('y', 'h', 'l'), split_axis=0, concat_axis=0, tiled=...]
  transfers between devices with their start and end apart: 22 -> 22, of which waited for: 5 -> 5; matrix products, arithmetic and copies ran while one was open for 4% -> 4% of each run, Pallas kernels for 32% -> 31%
where the time goes in v10:
time: 105 us; the launch traced here: 103 us
  Pallas kernels  34.1 us (32%)
  starting transfers between devices  33.9 us (32%)
  waiting for transfers between devices  30.3 us (29%)
  local copies, waits for them, and re-layouts  2.32 us (2%)
  between operations  1.43 us (1%)
  other arithmetic  1.32 us (1%)
    ppermute x20, starting transfers between devices, shift(): return lax.ppermute(value, axis, [(i, (i + step) % n) for i in range(n)])  19.7 us
    ppermute x20, waiting for transfers between devices, shift(): return lax.ppermute(value, axis, [(i, (i + step) % n) for i in range(n)])  17.4 us
    all_to_all x1, starting transfers between devices, body(): lax.all_to_all(sums, ('y', 'h', 'l'), split_axis=0, concat_axis=0, tiled=...  9.54 us
    pallas_call x1, Pallas kernels, partial_sums(): pl.pallas_call(sums_kernel, grid_spec=pltpu.PrefetchScalarGridSpec(num_sc...  9.17 us
    all_to_all x1, waiting for transfers between devices, body(): lax.all_to_all(sums, ('y', 'h', 'l'), split_axis=0, concat_axis=0, tiled=...  8.48 us
    pallas_call x1, Pallas kernels, scores(): pl.pallas_call(score_kernel, grid=(2048 // width,), out_shape=(pltpu.HBM(...  7.3 us
    pallas_call x1, Pallas kernels, prepare(): pl.pallas_call(prepare_kernel, grid=(4,), in_specs=[pl.BlockSpec((512, 10...  5.28 us
    all_to_all x1, starting transfers between devices, body(): lax.all_to_all(share, ('y', 'x', 'c'), split_axis=0, concat_axis=0, tiled...  4.68 us
  transfers between devices with their start and end apart: 22, of which 5 were waited for; matrix products, arithmetic and copies ran while one was open for 4% of the time, Pallas kernels for 31%

profile of v10, /device:TPU:32, one launch (start us, length us, event | category | flops | bytes accessed | tf_op | source)
XLA Modules:
  0.0 103.5 jit_solution(7888211699888380337)
XLA Ops:
  0.6 1.6 %collective-permute-start = (bf16[64,1024]{1,0:T(8,128)(2,1)}, bf16[64,1024]{1,0:T(8,128)(2,1)S(1)}, u32[]{:S(2)}, u32[]{:S(2)}) collective-permute-start(bf16[64,1024]{1,0:T(8,128)(2,1)} %own.1), channel_id=1, source_target_pairs={{0,2},{2,4},{4,6},{6,0},{1,3},{3,5},{5,7},{7,1},{8,10},{10,12},{12... | collective-permute-start | bytes 393224 | tf_op jit(solution)/shard_map/ppermute | solution.py:21
  2.2 1.7 %collective-permute-start.1 = (bf16[64,1024]{1,0:T(8,128)(2,1)}, bf16[64,1024]{1,0:T(8,128)(2,1)S(1)}, u32[]{:S(2)}, u32[]{:S(2)}) collective-permute-start(bf16[64,1024]{1,0:T(8,128)(2,1)} %own.1), channel_id=1, source_target_pairs={{0,6},{2,0},{4,2},{6,4},{1,7},{3,1},{5,3},{7,5},{8,14},{10,8},{12,... | collective-permute-start | bytes 393224 | tf_op jit(solution)/shard_map/ppermute | solution.py:21
  3.9 1.8 %collective-permute-start.2 = (bf16[64,1024]{1,0:T(8,128)(2,1)}, bf16[64,1024]{1,0:T(8,128)(2,1)S(1)}, u32[]{:S(2)}, u32[]{:S(2)}) collective-permute-start(bf16[64,1024]{1,0:T(8,128)(2,1)} %own.1), channel_id=1, source_target_pairs={{0,4},{2,6},{4,0},{6,2},{1,5},{3,7},{5,1},{7,3},{8,12},{10,14},{12... | collective-permute-start | bytes 393224 | tf_op jit(solution)/shard_map/ppermute | solution.py:21
  5.8 3.2 %collective-permute-start.3 = (bf16[64,1024]{1,0:T(8,128)(2,1)}, bf16[64,1024]{1,0:T(8,128)(2,1)S(1)}, u32[]{:S(2)}, u32[]{:S(2)}) collective-permute-start(bf16[64,1024]{1,0:T(8,128)(2,1)} %own.1), channel_id=1, source_target_pairs={{0,128},{64,192},{128,0},{192,64},{1,129},{65,193},{129,1},{193,65... | collective-permute-start | bytes 393224 | tf_op jit(solution)/shard_map/ppermute | solution.py:21
  9.0 5.3 %shard_map.75 = (bf16[2048,1024]{1,0:T(8,128)(2,1)}, f32[1,2048]{1,0:T(1,128)S(1)}) custom-call(bf16[2048,1024]{1,0:T(8,128)(2,1)} %means.3, f32[1,1024]{1,0:T(1,128)} %bitcast.23, f32[1,2048]{1,0:T(1,128)} %bitcast.24), custom_call_target="tpu_custom_call" | custom-call | flops 12582912 | bytes 8388608 | tf_op jit(solution)/shard_map/pallas_call | solution.py:60
  15.1 0.8 collective-permute-start.8
  15.8 2.6 %collective-permute-start.10 = (bf16[256,1024]{1,0:T(8,128)(2,1)S(1)}, bf16[256,1024]{1,0:T(8,128)(2,1)}, u32[]{:S(2)}, u32[]{:S(2)}) collective-permute-start(bf16[256,1024]{1,0:T(8,128)(2,1)S(1)} %shard_map.76.own.refs_0_), channel_id=1, source_target_pairs={{0,192},{64,0},{128,64},{192,128},{1,193},{65,1},{129,65},{193,129... | collective-permute-start | bytes 1572872 | tf_op jit(solution)/shard_map/ppermute | solution.py:21
  19.0 2.6 %collective-permute-start.13 = (bf16[64,1024]{1,0:T(8,128)(2,1)S(1)}, bf16[64,1024]{1,0:T(8,128)(2,1)S(1)}, u32[]{:S(2)}, u32[]{:S(2)}) collective-permute-start(bf16[64,1024]{1,0:T(8,128)(2,1)S(1)} %collective-permute-done.3.refs_1_.own), channel_id=1, source_target_pairs={{0,6},{2,0},{4,2},{6,4},{1,7},{3,1},{5,3},{7,5},{8,14},{10,8},{12,... | collective-permute-start | bytes 393224 | tf_op jit(solution)/shard_map/ppermute | solution.py:21
  22.1 7.3 %shard_map.77 = (f32[512,2048]{1,0:T(8,128)}, f32[32,4,128]{2,1,0:T(4,128)}) custom-call(s32[5]{0:T(128)S(1)} %stack.23.at, bf16[256,1024]{1,0:T(8,128)(2,1)S(1)} %shard_map.76.own.refs_0_, bf16[256,1024]{1,0:T(8,128)(2,1)S(1)} %collective-permute-done.4.other.refs_1_, bf16[2048,1024]{1,0:T(8,128)(2,1)} %get-tuple-element.15.refs_0_.scaled, ...), custom_call_target="tpu_custom_call" | custom-call | flops 2147483648 | bytes 9437184 | tf_op jit(solution)/shard_map/pallas_call | solution.py:144
  29.4 4.7 %all-to-all-start = ((f32[32,4,128]{2,1,0:T(4,128)}), f32[32,4,128]{2,1,0:T(4,128)S(1)}, u32[]{:S(2)}, u32[]{:S(2)}) async-start(f32[32,4,128]{2,1,0:T(4,128)} %get-tuple-element.17.ahead), calls=%async_computation | async-start | bytes 131072 | tf_op jit(solution)/shard_map/all_to_all | solution.py:415
  34.1 2.5 %shard_map.79.refs_0_.means = f32[32,2048]{1,0:T(8,128)} custom-call(s32[5]{0:T(128)S(1)} %stack.23.at, bf16[2048,1024]{1,0:T(8,128)(2,1)} %means.3, f32[32,4,128]{2,1,0:T(4,128)} %get-tuple-element.17.ahead), custom_call_target="tpu_custom_call" | custom-call | tf_op jit(solution)/shard_map/pallas_call | solution.py:327
  37.1 4.4 %all-to-all-done.refs_1_ = f32[32,4,128]{2,1,0:T(4,128)S(1)} async-done(((f32[32,4,128]{2,1,0:T(4,128)}), f32[32,4,128]{2,1,0:T(4,128)S(1)}, u32[]{:S(2)}, u32[]{:S(2)}) %all-to-all-start) | async-done | bytes 65568 | tf_op jit(solution)/shard_map/all_to_all | solution.py:415
  42.4 4.4 %shard_map.78 = (bf16[64,2048]{1,0:T(8,128)(2,1)S(1)}, bf16[64,2048]{1,0:T(8,128)(2,1)S(1)}, bf16[128,2048]{1,0:T(8,128)(2,1)S(1)}, bf16[128,2048]{1,0:T(8,128)(2,1)}, bf16[128,2048]{1,0:T(8,128)(2,1)}) custom-call(s32[5]{0:T(128)S(1)} %stack.23.at, f32[4,8,4,128]{3,2,1,0:T(4,128)S(1)} %bitcast.19, f32[512,2048]{1,0:T(8,128)} %get-tuple-element.18.score), custom_call_target="tpu_custom_call" | custom-call | flops 2097152 | bytes 6291456 | tf_op jit(solution)/shard_map/pallas_call | solution.py:302
  46.8 0.9 collective-permute-start.6
  47.7 9.2 %shard_map.81.refs_0_ = bf16[32,136,128]{2,1,0:T(8,128)(2,1)} custom-call(s32[5]{0:T(128)S(1)} %stack.23.at, f32[4,8,4,128]{3,2,1,0:T(4,128)S(1)} %bitcast.20, bf16[2048,1024]{1,0:T(8,128)(2,1)} %get-tuple-element.15.refs_0_.scaled, f32[1,2048]{1,0:T(1,128)S(1)} %get-tuple-element.16.bias, bf16[256,1024]{1,0:T(8,128)(2,1)S(1)} %shard_map.76.own.refs_0_, ...), custom_call_target="tpu_custom_call" | custom-call | flops 4294967296 | bytes 8388608 | tf_op jit(solution)/shard_map/pallas_call | solution.py:243
  56.9 5.6 %collective-permute-done.6.refs_1_.refs_5_ = bf16[128,2048]{1,0:T(8,128)(2,1)S(1)} collective-permute-done((bf16[128,2048]{1,0:T(8,128)(2,1)S(1)}, bf16[128,2048]{1,0:T(8,128)(2,1)S(1)}, u32[]{:S(2)}, u32[]{:S(2)}) %collective-permute-start.6) | collective-permute-done | bytes 524320 | tf_op jit(solution)/shard_map/ppermute | solution.py:21
  62.5 9.5 %all-to-all-start.1 = ((bf16[32,136,128]{2,1,0:T(8,128)(2,1)}), bf16[32,136,128]{2,1,0:T(8,128)(2,1)S(1)}, u32[]{:S(2)}, u32[]{:S(2)}) async-start(bf16[32,136,128]{2,1,0:T(8,128)(2,1)} %shard_map.82.refs_1_), calls=%async_computation.1 | async-start | bytes 2228224 | tf_op jit(solution)/shard_map/all_to_all | solution.py:428
  72.2 1.4 %collective-permute-start.16 = (bf16[128,2048]{1,0:T(8,128)(2,1)}, bf16[128,2048]{1,0:T(8,128)(2,1)S(1)}, u32[]{:S(2)}, u32[]{:S(2)}) collective-permute-start(bf16[128,2048]{1,0:T(8,128)(2,1)} %shard_map.83), channel_id=1, source_target_pairs={{0,4},{2,6},{4,0},{6,2},{1,5},{3,7},{5,1},{7,3},{8,12},{10,14},{12... | collective-permute-start | bytes 1572872 | tf_op jit(solution)/shard_map/ppermute | solution.py:21
  76.3 10.8 %collective-permute-done.18.refs_7_ = bf16[128,2048]{1,0:T(8,128)(2,1)S(1)} collective-permute-done((bf16[128,2048]{1,0:T(8,128)(2,1)}, bf16[128,2048]{1,0:T(8,128)(2,1)S(1)}, u32[]{:S(2)}, u32[]{:S(2)}) %collective-permute-start.18) | collective-permute-done | bytes 524320 | tf_op jit(solution)/shard_map/ppermute | solution.py:21
  87.9 0.7 slice.13
  89.8 0.9 collective-permute-done.17.refs_2_
  90.6 2.5 %shard_map.84 = bf16[64,16384]{1,0:T(8,128)(2,1)} custom-call(s32[5]{0:T(128)S(1)} %stack.23.at, bf16[64,2048]{1,0:T(8,128)(2,1)S(1)} %collective-permute-done.5.refs_0_, bf16[64,2048]{1,0:T(8,128)(2,1)} %collective-permute-done.7.refs_1_, bf16[64,2048]{1,0:T(8,128)(2,1)} %collective-permute-done.17.refs_2_, ...), custom_call_target="tpu_custom_call" | custom-call | bytes 4194304 | tf_op jit(solution)/shard_map/pallas_call | solution.py:391
  93.2 8.5 %all-to-all-done.1.sent = bf16[32,136,128]{2,1,0:T(8,128)(2,1)S(1)} async-done(((bf16[32,136,128]{2,1,0:T(8,128)(2,1)}), bf16[32,136,128]{2,1,0:T(8,128)(2,1)S(1)}, u32[]{:S(2)}, u32[]{:S(2)}) %all-to-all-start.1) | async-done | bytes 1114144 | tf_op jit(solution)/shard_map/all_to_all | solution.py:428
  101.6 1.8 %shard_map.85 = (f32[32,2048]{1,0:T(8,128)}, f32[16,128]{1,0:T(8,128)}) custom-call(bf16[32,136,128]{2,1,0:T(8,128)(2,1)S(1)} %all-to-all-done.1.sent, f32[32,2048]{1,0:T(8,128)} %shard_map.79.refs_0_.means), custom_call_target="tpu_custom_call" | custom-call | tf_op jit(solution)/shard_map/pallas_call | solution.py:355
  (48 shorter events, 7.3 us)
Async XLA Ops:
  0.6 13.7 %collective-permute-start = (bf16[64,1024]{1,0:T(8,128)(2,1)}, bf16[64,1024]{1,0:T(8,128)(2,1)S(1)}, u32[]{:S(2)}, u32[]{:S(2)}) collective-permute-start(bf16[64,1024]{1,0:T(8,128)(2,1)} %own.1), channel_id=1, source_target_pairs={{0,2},{2,4},{4,6},{6,0},{1,3},{3,5},{5,7},{7,1},{8,10},{10,12},{12... | collective-permute-start | bytes 393224 | tf_op jit(solution)/shard_map/ppermute | solution.py:21
  2.2 12.1 %collective-permute-start.1 = (bf16[64,1024]{1,0:T(8,128)(2,1)}, bf16[64,1024]{1,0:T(8,128)(2,1)S(1)}, u32[]{:S(2)}, u32[]{:S(2)}) collective-permute-start(bf16[64,1024]{1,0:T(8,128)(2,1)} %own.1), channel_id=1, source_target_pairs={{0,6},{2,0},{4,2},{6,4},{1,7},{3,1},{5,3},{7,5},{8,14},{10,8},{12,... | collective-permute-start | bytes 393224 | tf_op jit(solution)/shard_map/ppermute | solution.py:21
  3.9 10.4 %collective-permute-start.2 = (bf16[64,1024]{1,0:T(8,128)(2,1)}, bf16[64,1024]{1,0:T(8,128)(2,1)S(1)}, u32[]{:S(2)}, u32[]{:S(2)}) collective-permute-start(bf16[64,1024]{1,0:T(8,128)(2,1)} %own.1), channel_id=1, source_target_pairs={{0,4},{2,6},{4,0},{6,2},{1,5},{3,7},{5,1},{7,3},{8,12},{10,14},{12... | collective-permute-start | bytes 393224 | tf_op jit(solution)/shard_map/ppermute | solution.py:21
  5.8 8.6 %collective-permute-start.3 = (bf16[64,1024]{1,0:T(8,128)(2,1)}, bf16[64,1024]{1,0:T(8,128)(2,1)S(1)}, u32[]{:S(2)}, u32[]{:S(2)}) collective-permute-start(bf16[64,1024]{1,0:T(8,128)(2,1)} %own.1), channel_id=1, source_target_pairs={{0,128},{64,192},{128,0},{192,64},{1,129},{65,193},{129,1},{193,65... | collective-permute-start | bytes 393224 | tf_op jit(solution)/shard_map/ppermute | solution.py:21
  15.0 6.7 %collective-permute-start.4 = (bf16[256,1024]{1,0:T(8,128)(2,1)S(1)}, bf16[256,1024]{1,0:T(8,128)(2,1)S(1)}, u32[]{:S(2)}, u32[]{:S(2)}) collective-permute-start(bf16[256,1024]{1,0:T(8,128)(2,1)S(1)} %shard_map.76.own.refs_0_), channel_id=1, source_target_pairs={{0,1},{1,0},{2,3},{3,2},{4,5},{5,4},{6,7},{7,6},{8,9},{9,8},{10,11... | collective-permute-start | bytes 1572872 | tf_op jit(solution)/shard_map/ppermute | solution.py:21
  15.1 21.6 %collective-permute-start.8 = (bf16[256,1024]{1,0:T(8,128)(2,1)S(1)}, bf16[256,1024]{1,0:T(8,128)(2,1)}, u32[]{:S(2)}, u32[]{:S(2)}) collective-permute-start(bf16[256,1024]{1,0:T(8,128)(2,1)S(1)} %shard_map.76.own.refs_0_), channel_id=1, source_target_pairs={{0,64},{64,128},{128,192},{192,0},{1,65},{65,129},{129,193},{193,1... | collective-permute-start | bytes 1572872 | tf_op jit(solution)/shard_map/ppermute | solution.py:21
  15.8 21.1 %collective-permute-start.10 = (bf16[256,1024]{1,0:T(8,128)(2,1)S(1)}, bf16[256,1024]{1,0:T(8,128)(2,1)}, u32[]{:S(2)}, u32[]{:S(2)}) collective-permute-start(bf16[256,1024]{1,0:T(8,128)(2,1)S(1)} %shard_map.76.own.refs_0_), channel_id=1, source_target_pairs={{0,192},{64,0},{128,64},{192,128},{1,193},{65,1},{129,65},{193,129... | collective-permute-start | bytes 1572872 | tf_op jit(solution)/shard_map/ppermute | solution.py:21
  18.4 18.8 %collective-permute-start.12 = (bf16[64,1024]{1,0:T(8,128)(2,1)S(1)}, bf16[64,1024]{1,0:T(8,128)(2,1)S(1)}, u32[]{:S(2)}, u32[]{:S(2)}) collective-permute-start(bf16[64,1024]{1,0:T(8,128)(2,1)S(1)} %collective-permute-done.3.refs_1_.own), channel_id=1, source_target_pairs={{0,2},{2,4},{4,6},{6,0},{1,3},{3,5},{5,7},{7,1},{8,10},{10,12},{12... | collective-permute-start | bytes 393224 | tf_op jit(solution)/shard_map/ppermute | solution.py:21
  19.0 18.2 %collective-permute-start.13 = (bf16[64,1024]{1,0:T(8,128)(2,1)S(1)}, bf16[64,1024]{1,0:T(8,128)(2,1)S(1)}, u32[]{:S(2)}, u32[]{:S(2)}) collective-permute-start(bf16[64,1024]{1,0:T(8,128)(2,1)S(1)} %collective-permute-done.3.refs_1_.own), channel_id=1, source_target_pairs={{0,6},{2,0},{4,2},{6,4},{1,7},{3,1},{5,3},{7,5},{8,14},{10,8},{12,... | collective-permute-start | bytes 393224 | tf_op jit(solution)/shard_map/ppermute | solution.py:21
  21.6 15.5 %collective-permute-start.14 = (bf16[64,1024]{1,0:T(8,128)(2,1)S(1)}, bf16[64,1024]{1,0:T(8,128)(2,1)S(1)}, u32[]{:S(2)}, u32[]{:S(2)}) collective-permute-start(bf16[64,1024]{1,0:T(8,128)(2,1)S(1)} %collective-permute-done.3.refs_1_.own), channel_id=1, source_target_pairs={{0,4},{2,6},{4,0},{6,2},{1,5},{3,7},{5,1},{7,3},{8,12},{10,14},{12... | collective-permute-start | bytes 393224 | tf_op jit(solution)/shard_map/ppermute | solution.py:21
  29.4 12.2 %all-to-all-start = ((f32[32,4,128]{2,1,0:T(4,128)}), f32[32,4,128]{2,1,0:T(4,128)S(1)}, u32[]{:S(2)}, u32[]{:S(2)}) async-start(f32[32,4,128]{2,1,0:T(4,128)} %get-tuple-element.17.ahead), calls=%async_computation | async-start | bytes 131072 | tf_op jit(solution)/shard_map/all_to_all | solution.py:415
  36.6 11.1 %collective-permute-start.9 = (bf16[256,1024]{1,0:T(8,128)(2,1)}, bf16[256,1024]{1,0:T(8,128)(2,1)}, u32[]{:S(2)}, u32[]{:S(2)}) collective-permute-start(bf16[256,1024]{1,0:T(8,128)(2,1)} %collective-permute-done.8.refs_2_), channel_id=1, source_target_pairs={{0,1},{1,0},{2,3},{3,2},{4,5},{5,4},{6,7},{7,6},{8,9},{9,8},{10,11... | collective-permute-start | bytes 1572872 | tf_op jit(solution)/shard_map/ppermute | solution.py:21
  36.9 10.8 %collective-permute-start.11 = (bf16[256,1024]{1,0:T(8,128)(2,1)}, bf16[256,1024]{1,0:T(8,128)(2,1)}, u32[]{:S(2)}, u32[]{:S(2)}) collective-permute-start(bf16[256,1024]{1,0:T(8,128)(2,1)} %collective-permute-done.10.refs_4_), channel_id=1, source_target_pairs={{0,1},{1,0},{2,3},{3,2},{4,5},{5,4},{6,7},{7,6},{8,9},{9,8},{10,11... | collective-permute-start | bytes 1572872 | tf_op jit(solution)/shard_map/ppermute | solution.py:21
  42.2 5.5 %collective-permute-start.15 = (bf16[256,1024]{1,0:T(8,128)(2,1)S(1)}, bf16[256,1024]{1,0:T(8,128)(2,1)S(1)}, u32[]{:S(2)}, u32[]{:S(2)}) collective-permute-start(bf16[256,1024]{1,0:T(8,128)(2,1)S(1)} %shard_map.80.refs_6_), channel_id=1, source_target_pairs={{0,1},{1,0},{2,3},{3,2},{4,5},{5,4},{6,7},{7,6},{8,9},{9,8},{10,11... | collective-permute-start | bytes 1572872 | tf_op jit(solution)/shard_map/ppermute | solution.py:21
  46.8 10.1 %copy-start.1 = (bf16[64,2048]{1,0:T(8,128)(2,1)}, bf16[64,2048]{1,0:T(8,128)(2,1)S(1)}, u32[]{:S(2)}) copy-start(bf16[64,2048]{1,0:T(8,128)(2,1)S(1)} %get-tuple-element.19.refs_8_) | copy-start | bytes 786436
  46.8 15.7 %collective-permute-start.6 = (bf16[128,2048]{1,0:T(8,128)(2,1)S(1)}, bf16[128,2048]{1,0:T(8,128)(2,1)S(1)}, u32[]{:S(2)}, u32[]{:S(2)}) collective-permute-start(bf16[128,2048]{1,0:T(8,128)(2,1)S(1)} %get-tuple-element.20), channel_id=1, source_target_pairs={{0,2},{2,4},{4,6},{6,0},{1,3},{3,5},{5,7},{7,1},{8,10},{10,12},{12... | collective-permute-start | bytes 1572872 | tf_op jit(solution)/shard_map/ppermute | solution.py:21
  62.5 11.1 %copy-start.2 = (f32[1024]{0:T(1024)S(1)}, f32[1024]{0:T(1024)}, u32[]{:S(2)}) copy-start(f32[1024]{0:T(1024)} %param.7) | copy-start | bytes 12292
  62.5 39.1 %all-to-all-start.1 = ((bf16[32,136,128]{2,1,0:T(8,128)(2,1)}), bf16[32,136,128]{2,1,0:T(8,128)(2,1)S(1)}, u32[]{:S(2)}, u32[]{:S(2)}) async-start(bf16[32,136,128]{2,1,0:T(8,128)(2,1)} %shard_map.82.refs_1_), calls=%async_computation.1 | async-start | bytes 2228224 | tf_op jit(solution)/shard_map/all_to_all | solution.py:428
  72.0 15.1 %collective-permute-start.18 = (bf16[128,2048]{1,0:T(8,128)(2,1)}, bf16[128,2048]{1,0:T(8,128)(2,1)S(1)}, u32[]{:S(2)}, u32[]{:S(2)}) collective-permute-start(bf16[128,2048]{1,0:T(8,128)(2,1)} %get-tuple-element.22), channel_id=1, source_target_pairs={{0,6},{2,0},{4,2},{6,4},{1,7},{3,1},{5,3},{7,5},{8,14},{10,8},{12,... | collective-permute-start | bytes 1572872 | tf_op jit(solution)/shard_map/ppermute | solution.py:21
  72.2 15.8 %collective-permute-start.16 = (bf16[128,2048]{1,0:T(8,128)(2,1)}, bf16[128,2048]{1,0:T(8,128)(2,1)S(1)}, u32[]{:S(2)}, u32[]{:S(2)}) collective-permute-start(bf16[128,2048]{1,0:T(8,128)(2,1)} %shard_map.83), channel_id=1, source_target_pairs={{0,4},{2,6},{4,0},{6,2},{1,5},{3,7},{5,1},{7,3},{8,12},{10,14},{12... | collective-permute-start | bytes 1572872 | tf_op jit(solution)/shard_map/ppermute | solution.py:21
  75.0 14.8 %collective-permute-start.5 = (bf16[64,2048]{1,0:T(8,128)(2,1)}, bf16[64,2048]{1,0:T(8,128)(2,1)S(1)}, u32[]{:S(2)}, u32[]{:S(2)}) collective-permute-start(bf16[64,2048]{1,0:T(8,128)(2,1)} %copy-done.1), channel_id=1, source_target_pairs={{0,1},{1,0},{2,3},{3,2},{4,5},{5,4},{6,7},{7,6},{8,9},{9,8},{10,11... | collective-permute-start | bytes 786440 | tf_op jit(solution)/shard_map/ppermute | solution.py:21
  75.9 13.9 %collective-permute-start.7 = (bf16[64,2048]{1,0:T(8,128)(2,1)}, bf16[64,2048]{1,0:T(8,128)(2,1)}, u32[]{:S(2)}, u32[]{:S(2)}) collective-permute-start(bf16[64,2048]{1,0:T(8,128)(2,1)} %slice.12), channel_id=1, source_target_pairs={{0,1},{1,0},{2,3},{3,2},{4,5},{5,4},{6,7},{7,6},{8,9},{9,8},{10,11... | collective-permute-start | bytes 786440 | tf_op jit(solution)/shard_map/ppermute | solution.py:21
  87.9 1.9 %collective-permute-start.19 = (bf16[64,2048]{1,0:T(8,128)(2,1)}, bf16[64,2048]{1,0:T(8,128)(2,1)}, u32[]{:S(2)}, u32[]{:S(2)}) collective-permute-start(bf16[64,2048]{1,0:T(8,128)(2,1)} %slice.14), channel_id=1, source_target_pairs={{0,1},{1,0},{2,3},{3,2},{4,5},{5,4},{6,7},{7,6},{8,9},{9,8},{10,11... | collective-permute-start | bytes 786440 | tf_op jit(solution)/shard_map/ppermute | solution.py:21
  88.6 2.0 %collective-permute-start.17 = (bf16[64,2048]{1,0:T(8,128)(2,1)}, bf16[64,2048]{1,0:T(8,128)(2,1)}, u32[]{:S(2)}, u32[]{:S(2)}) collective-permute-start(bf16[64,2048]{1,0:T(8,128)(2,1)} %slice.13), channel_id=1, source_target_pairs={{0,1},{1,0},{2,3},{3,2},{4,5},{5,4},{6,7},{7,6},{8,9},{9,8},{10,11... | collective-permute-start | bytes 786440 | tf_op jit(solution)/shard_map/ppermute | solution.py:21
  (1 other events, 5.3 us)

commit v11 on v10

--- a/solution.py
+++ b/solution.py
@@ -269,8 +269,8 @@
 
 
 def resp_kernel(at, shares, score, *refs):
-    outs, norm, held, sems, across = refs[:5], refs[5], refs[6], refs[7], refs[8]
-    outs, out_across = (*outs[:3], across, outs[4]), outs[3]
+    outs, out_across = refs[:6], refs[6]
+    norm, held, sems, across = refs[7:]
     x, c, y = at[0], at[1], at[2]
     copies = []
     for j in range(8):
@@ -289,10 +289,10 @@
     for j, (start, copy) in enumerate(copies):
         copy.wait()
         block = jnp.exp(held[j] - norm[pl.ds(start, 64), 0:1]).astype(BF)
-        if j % 4 == 0:
-            outs[j // 4][...] = block
+        if j % 4 == 2:
+            across[j // 4 * 64 : j // 4 * 64 + 64, :] = block
         else:
-            outs[1 + j % 4][j // 4 * 64 : j // 4 * 64 + 64, :] = block
+            outs[(0, 2, None, 4, 1, 3, None, 5)[j]][...] = block
     copy = pltpu.make_async_copy(across, out_across, sems.at[0])
     copy.start()
     copy.wait()
@@ -302,15 +302,14 @@
     return pl.pallas_call(
         resp_kernel,
         in_specs=[scalar(), whole()] + hbm(),
-        out_specs=[whole()] * 3 + hbm() + [whole()],
+        out_specs=[whole()] * 6 + hbm(),
         scratch_shapes=[
             VMEM((512, 128), F32),
             VMEM((8, 64, 2048), F32),
             pltpu.SemaphoreType.DMA((8,)),
             VMEM((128, 2048), BF),
         ],
-        out_shape=[jax.ShapeDtypeStruct((64, 2048), BF)] * 2
-        + [jax.ShapeDtypeStruct((128, 2048), BF), pltpu.HBM((128, 2048), BF), jax.ShapeDtypeStruct((128, 2048), BF)],
+        out_shape=[jax.ShapeDtypeStruct((64, 2048), BF)] * 6 + [pltpu.HBM((128, 2048), BF)],
         compiler_params=params(),
         cost_estimate=pl.CostEstimate(flops=1 << 21, bytes_accessed=6 << 20, transcendentals=1 << 20),
     )(at, shares, still(score))
@@ -379,7 +378,7 @@
         core = 1 - c if j < 4 else c
         comp = lax.rem(x + 4 - j % 4, 4) * 2 + core
         spot = out.at[:, pl.ds(pl.multiple_of(comp * 2048, 2048), 2048)]
-        piece = pieces[j].at[pl.ds(64, 64)] if j > 4 else pieces[j]
+        piece = pieces[j].at[pl.ds(64, 64)] if j == 6 else pieces[j]
         copies.append(pltpu.make_async_copy(piece, spot, sems.at[j]))
     for copy in copies:
         copy.start()
@@ -421,13 +420,14 @@
         pieces += [mine, shift(mine, "c", 1)]
 
     blocks = responsibilities(at, shares, score)
-    ahead, behind = shift(blocks[2], "x", 1), shift(blocks[4], "x", 3)
+    near = [shift(blocks[2], "x", 1), shift(blocks[4], "x", 3)]
     sums = partial_sums(at, shares, scaled, bias_row, pieces, blocks[0])
-    sums = hold(sums, ahead)
-    pairs = [ahead, shift(hold(blocks[3], still(sums)), "x", 2), behind]
+    sums = hold(sums, *near)
+    across = shift(hold(blocks[6], still(sums)), "x", 2)
+    mine = [blocks[1], shift(blocks[3], "x", 1), across, shift(blocks[5], "x", 3)]
     sent = lax.all_to_all(sums, ("y", "h", "l"), split_axis=0, concat_axis=0, tiled=True)
-    theirs = [shift(b, "c", 1) for b in [blocks[0]] + [pair[:64] for pair in pairs]]
-    held = theirs + [blocks[1]] + pairs
+    theirs = [shift(b, "c", 1) for b in (blocks[0], near[0], across[:64], near[1])]
+    held = theirs + mine
     resp_rows = lay_out(at, held)
 
     new_means_t, counts = finish(sent, mean_cols)

time: 105 us -> 102 us (0.971)
  waiting for transfers between devices: 30.3 us -> 25.2 us
  starting transfers between devices: 33.9 us -> 38 us
    ppermute x20 -> x22, starting transfers between devices: 19.7 us -> 23.8 us  [shift(): return lax.ppermute(value, axis, [(i, (i + step) % n) for i in range(n)])]
    ppermute x20 -> x22, waiting for transfers between devices: 17.4 us -> 13.8 us  [shift(): return lax.ppermute(value, axis, [(i, (i + step) % n) for i in range(n)])]
    all_to_all x1, waiting for transfers between devices: 8.48 us -> 6.95 us  [body(): lax.all_to_all(sums, ('y', 'h', 'l'), split_axis=0, concat_axis=0, tiled=...]
    slice x3 -> x1, local copies, waits for them, and re-layouts: 2.15 us -> 0.72 us  [body(): across[:64]]
  transfers between devices with their start and end apart: 22 -> 24, of which waited for: 5 -> 4; matrix products, arithmetic and copies ran while one was open for 4% -> 2% of each run, Pallas kernels for 31% -> 31%
where the time goes in v11:
time: 102 us; the launch traced here: 101 us
  starting transfers between devices  38 us (37%)
  Pallas kernels  33.8 us (33%)
  waiting for transfers between devices  25.2 us (25%)
  local copies, waits for them, and re-layouts  1.58 us (2%)
  between operations  1.39 us (1%)
  other arithmetic  1.28 us (1%)
    ppermute x22, starting transfers between devices, shift(): return lax.ppermute(value, axis, [(i, (i + step) % n) for i in range(n)])  23.8 us
    ppermute x22, waiting for transfers between devices, shift(): return lax.ppermute(value, axis, [(i, (i + step) % n) for i in range(n)])  13.8 us
    all_to_all x1, starting transfers between devices, body(): lax.all_to_all(sums, ('y', 'h', 'l'), split_axis=0, concat_axis=0, tiled=...  9.54 us
    pallas_call x1, Pallas kernels, partial_sums(): pl.pallas_call(sums_kernel, grid_spec=pltpu.PrefetchScalarGridSpec(num_sc...  9.06 us
    pallas_call x1, Pallas kernels, scores(): pl.pallas_call(score_kernel, grid=(2048 // width,), out_shape=(pltpu.HBM(...  7.24 us
    all_to_all x1, waiting for transfers between devices, body(): lax.all_to_all(sums, ('y', 'h', 'l'), split_axis=0, concat_axis=0, tiled=...  6.95 us
    pallas_call x1, Pallas kernels, prepare(): pl.pallas_call(prepare_kernel, grid=(4,), in_specs=[pl.BlockSpec((512, 10...  5.26 us
    all_to_all x1, starting transfers between devices, body(): lax.all_to_all(share, ('y', 'x', 'c'), split_axis=0, concat_axis=0, tiled...  4.69 us
  transfers between devices with their start and end apart: 24, of which 4 were waited for; matrix products, arithmetic and copies ran while one was open for 2% of the time, Pallas kernels for 31%

profile of v11, /device:TPU:32, one launch (start us, length us, event | category | flops | bytes accessed | tf_op | source)
XLA Modules:
  0.0 101.3 jit_solution(12735124933445893300)
XLA Ops:
  0.6 1.6 %collective-permute-start = (bf16[64,1024]{1,0:T(8,128)(2,1)}, bf16[64,1024]{1,0:T(8,128)(2,1)S(1)}, u32[]{:S(2)}, u32[]{:S(2)}) collective-permute-start(bf16[64,1024]{1,0:T(8,128)(2,1)} %own.1), channel_id=1, source_target_pairs={{0,2},{2,4},{4,6},{6,0},{1,3},{3,5},{5,7},{7,1},{8,10},{10,12},{12... | collective-permute-start | bytes 393224 | tf_op jit(solution)/shard_map/ppermute | solution.py:21
  2.2 1.7 %collective-permute-start.1 = (bf16[64,1024]{1,0:T(8,128)(2,1)}, bf16[64,1024]{1,0:T(8,128)(2,1)S(1)}, u32[]{:S(2)}, u32[]{:S(2)}) collective-permute-start(bf16[64,1024]{1,0:T(8,128)(2,1)} %own.1), channel_id=1, source_target_pairs={{0,6},{2,0},{4,2},{6,4},{1,7},{3,1},{5,3},{7,5},{8,14},{10,8},{12,... | collective-permute-start | bytes 393224 | tf_op jit(solution)/shard_map/ppermute | solution.py:21
  3.9 1.8 %collective-permute-start.2 = (bf16[64,1024]{1,0:T(8,128)(2,1)}, bf16[64,1024]{1,0:T(8,128)(2,1)S(1)}, u32[]{:S(2)}, u32[]{:S(2)}) collective-permute-start(bf16[64,1024]{1,0:T(8,128)(2,1)} %own.1), channel_id=1, source_target_pairs={{0,4},{2,6},{4,0},{6,2},{1,5},{3,7},{5,1},{7,3},{8,12},{10,14},{12... | collective-permute-start | bytes 393224 | tf_op jit(solution)/shard_map/ppermute | solution.py:21
  5.8 3.2 %collective-permute-start.3 = (bf16[64,1024]{1,0:T(8,128)(2,1)}, bf16[64,1024]{1,0:T(8,128)(2,1)S(1)}, u32[]{:S(2)}, u32[]{:S(2)}) collective-permute-start(bf16[64,1024]{1,0:T(8,128)(2,1)} %own.1), channel_id=1, source_target_pairs={{0,128},{64,192},{128,0},{192,64},{1,129},{65,193},{129,1},{193,65... | collective-permute-start | bytes 393224 | tf_op jit(solution)/shard_map/ppermute | solution.py:21
  9.0 5.3 %shard_map.75 = (bf16[2048,1024]{1,0:T(8,128)(2,1)}, f32[1,2048]{1,0:T(1,128)S(1)}) custom-call(bf16[2048,1024]{1,0:T(8,128)(2,1)} %means.3, f32[1,1024]{1,0:T(1,128)} %bitcast.23, f32[1,2048]{1,0:T(1,128)} %bitcast.24), custom_call_target="tpu_custom_call" | custom-call | flops 12582912 | bytes 8388608 | tf_op jit(solution)/shard_map/pallas_call | solution.py:60
  15.0 0.8 collective-permute-start.8
  15.8 2.6 %collective-permute-start.10 = (bf16[256,1024]{1,0:T(8,128)(2,1)S(1)}, bf16[256,1024]{1,0:T(8,128)(2,1)S(1)}, u32[]{:S(2)}, u32[]{:S(2)}) collective-permute-start(bf16[256,1024]{1,0:T(8,128)(2,1)S(1)} %shard_map.76.own.refs_0_), channel_id=1, source_target_pairs={{0,192},{64,0},{128,64},{192,128},{1,193},{65,1},{129,65},{193,129... | collective-permute-start | bytes 1572872 | tf_op jit(solution)/shard_map/ppermute | solution.py:21
  18.9 2.6 %collective-permute-start.13 = (bf16[64,1024]{1,0:T(8,128)(2,1)S(1)}, bf16[64,1024]{1,0:T(8,128)(2,1)S(1)}, u32[]{:S(2)}, u32[]{:S(2)}) collective-permute-start(bf16[64,1024]{1,0:T(8,128)(2,1)S(1)} %collective-permute-done.3.refs_1_.own), channel_id=1, source_target_pairs={{0,6},{2,0},{4,2},{6,4},{1,7},{3,1},{5,3},{7,5},{8,14},{10,8},{12,... | collective-permute-start | bytes 393224 | tf_op jit(solution)/shard_map/ppermute | solution.py:21
  22.1 7.2 %shard_map.77 = (f32[512,2048]{1,0:T(8,128)}, f32[32,4,128]{2,1,0:T(4,128)}) custom-call(s32[5]{0:T(128)S(1)} %stack.23.at, bf16[256,1024]{1,0:T(8,128)(2,1)S(1)} %shard_map.76.own.refs_0_, bf16[256,1024]{1,0:T(8,128)(2,1)S(1)} %collective-permute-done.4.other.refs_1_, bf16[2048,1024]{1,0:T(8,128)(2,1)} %get-tuple-element.17.refs_0_.scaled, ...), custom_call_target="tpu_custom_call" | custom-call | flops 2147483648 | bytes 9437184 | tf_op jit(solution)/shard_map/pallas_call | solution.py:144
  29.3 4.7 %all-to-all-start = ((f32[32,4,128]{2,1,0:T(4,128)}), f32[32,4,128]{2,1,0:T(4,128)S(1)}, u32[]{:S(2)}, u32[]{:S(2)}) async-start(f32[32,4,128]{2,1,0:T(4,128)} %get-tuple-element.19.ahead), calls=%async_computation | async-start | bytes 131072 | tf_op jit(solution)/shard_map/all_to_all | solution.py:414
  34.0 2.5 %shard_map.79.refs_0_.means = f32[32,2048]{1,0:T(8,128)} custom-call(s32[5]{0:T(128)S(1)} %stack.23.at, bf16[2048,1024]{1,0:T(8,128)(2,1)} %means.3, f32[32,4,128]{2,1,0:T(4,128)} %get-tuple-element.19.ahead), custom_call_target="tpu_custom_call" | custom-call | tf_op jit(solution)/shard_map/pallas_call | solution.py:326
  37.1 4.4 %all-to-all-done.refs_1_ = f32[32,4,128]{2,1,0:T(4,128)S(1)} async-done(((f32[32,4,128]{2,1,0:T(4,128)}), f32[32,4,128]{2,1,0:T(4,128)S(1)}, u32[]{:S(2)}, u32[]{:S(2)}) %all-to-all-start) | async-done | bytes 65568 | tf_op jit(solution)/shard_map/all_to_all | solution.py:414
  42.3 4.4 %shard_map.78 = (bf16[64,2048]{1,0:T(8,128)(2,1)}, bf16[64,2048]{1,0:T(8,128)(2,1)S(1)}, bf16[64,2048]{1,0:T(8,128)(2,1)S(1)}, bf16[64,2048]{1,0:T(8,128)(2,1)},...) custom-call(s32[5]{0:T(128)S(1)} %stack.23.at, f32[4,8,4,128]{3,2,1,0:T(4,128)S(1)} %bitcast.19, ...), custom_call_target="tpu_custom_call" | custom-call | flops 2097152 | bytes 6291456 | tf_op jit(solution)/shard_map/pallas_call | solution.py:302
  46.7 0.9 collective-permute-start.6
  47.6 2.6 %collective-permute-start.16 = (bf16[64,2048]{1,0:T(8,128)(2,1)S(1)}, bf16[64,2048]{1,0:T(8,128)(2,1)S(1)}, u32[]{:S(2)}, u32[]{:S(2)}) collective-permute-start(bf16[64,2048]{1,0:T(8,128)(2,1)S(1)} %get-tuple-element.24), channel_id=1, source_target_pairs={{0,6},{2,0},{4,2},{6,4},{1,7},{3,1},{5,3},{7,5},{8,14},{10,8},{12,... | collective-permute-start | bytes 786440 | tf_op jit(solution)/shard_map/ppermute | solution.py:21
  50.3 9.1 %shard_map.81.refs_0_ = bf16[32,136,128]{2,1,0:T(8,128)(2,1)} custom-call(s32[5]{0:T(128)S(1)} %stack.23.at, f32[4,8,4,128]{3,2,1,0:T(4,128)S(1)} %bitcast.20, bf16[2048,1024]{1,0:T(8,128)(2,1)} %get-tuple-element.17.refs_0_.scaled, f32[1,2048]{1,0:T(1,128)S(1)} %get-tuple-element.18.bias, bf16[256,1024]{1,0:T(8,128)(2,1)S(1)} %shard_map.76.own.refs_0_, ...), custom_call_target="tpu_custom_call" | custom-call | flops 4294967296 | bytes 8388608 | tf_op jit(solution)/shard_map/pallas_call | solution.py:243
  60.1 9.5 %all-to-all-start.1 = ((bf16[32,136,128]{2,1,0:T(8,128)(2,1)}), bf16[32,136,128]{2,1,0:T(8,128)(2,1)S(1)}, u32[]{:S(2)}, u32[]{:S(2)}) async-start(bf16[32,136,128]{2,1,0:T(8,128)(2,1)} %shard_map.82.refs_1_), calls=%async_computation.1 | async-start | bytes 2228224 | tf_op jit(solution)/shard_map/all_to_all | solution.py:428
  71.1 1.2 %collective-permute-start.20 = (bf16[64,2048]{1,0:T(8,128)(2,1)}, bf16[64,2048]{1,0:T(8,128)(2,1)S(1)}, u32[]{:S(2)}, u32[]{:S(2)}) collective-permute-start(bf16[64,2048]{1,0:T(8,128)(2,1)} %get-tuple-element.26), channel_id=1, source_target_pairs={{0,2},{2,4},{4,6},{6,0},{1,3},{3,5},{5,7},{7,1},{8,10},{10,12},{12... | collective-permute-start | bytes 786440 | tf_op jit(solution)/shard_map/ppermute | solution.py:21
  72.3 2.1 %collective-permute-start.21 = (bf16[64,2048]{1,0:T(8,128)(2,1)}, bf16[64,2048]{1,0:T(8,128)(2,1)S(1)}, u32[]{:S(2)}, u32[]{:S(2)}) collective-permute-start(bf16[64,2048]{1,0:T(8,128)(2,1)} %get-tuple-element.27), channel_id=1, source_target_pairs={{0,6},{2,0},{4,2},{6,4},{1,7},{3,1},{5,3},{7,5},{8,14},{10,8},{12,... | collective-permute-start | bytes 786440 | tf_op jit(solution)/shard_map/ppermute | solution.py:21
  74.6 11.8 %collective-permute-done.17.refs_6_ = bf16[128,2048]{1,0:T(8,128)(2,1)S(1)} collective-permute-done((bf16[128,2048]{1,0:T(8,128)(2,1)}, bf16[128,2048]{1,0:T(8,128)(2,1)S(1)}, u32[]{:S(2)}, u32[]{:S(2)}) %collective-permute-start.17) | collective-permute-done | bytes 524320 | tf_op jit(solution)/shard_map/ppermute | solution.py:21
  88.2 1.9 %collective-permute-done.20.refs_5_ = bf16[64,2048]{1,0:T(8,128)(2,1)S(1)} collective-permute-done((bf16[64,2048]{1,0:T(8,128)(2,1)}, bf16[64,2048]{1,0:T(8,128)(2,1)S(1)}, u32[]{:S(2)}, u32[]{:S(2)}) %collective-permute-start.20) | collective-permute-done | bytes 262176 | tf_op jit(solution)/shard_map/ppermute | solution.py:21
  90.2 2.3 %shard_map.84 = bf16[64,16384]{1,0:T(8,128)(2,1)} custom-call(s32[5]{0:T(128)S(1)} %stack.23.at, bf16[64,2048]{1,0:T(8,128)(2,1)S(1)} %collective-permute-done.5.refs_0_, bf16[64,2048]{1,0:T(8,128)(2,1)S(1)} %collective-permute-done.7.refs_1_, bf16[64,2048]{1,0:T(8,128)(2,1)} %collective-permute-done.18.refs_2_, ...), custom_call_target="tpu_custom_call" | custom-call | bytes 4194304 | tf_op jit(solution)/shard_map/pallas_call | solution.py:390
  92.5 7.0 %all-to-all-done.1.sent = bf16[32,136,128]{2,1,0:T(8,128)(2,1)S(1)} async-done(((bf16[32,136,128]{2,1,0:T(8,128)(2,1)}), bf16[32,136,128]{2,1,0:T(8,128)(2,1)S(1)}, u32[]{:S(2)}, u32[]{:S(2)}) %all-to-all-start.1) | async-done | bytes 1114144 | tf_op jit(solution)/shard_map/all_to_all | solution.py:428
  99.5 1.8 %shard_map.85 = (f32[32,2048]{1,0:T(8,128)}, f32[16,128]{1,0:T(8,128)}) custom-call(bf16[32,136,128]{2,1,0:T(8,128)(2,1)S(1)} %all-to-all-done.1.sent, f32[32,2048]{1,0:T(8,128)} %shard_map.79.refs_0_.means), custom_call_target="tpu_custom_call" | custom-call | tf_op jit(solution)/shard_map/pallas_call | solution.py:354
  (50 shorter events, 6.8 us)
Async XLA Ops:
  0.6 13.7 %collective-permute-start = (bf16[64,1024]{1,0:T(8,128)(2,1)}, bf16[64,1024]{1,0:T(8,128)(2,1)S(1)}, u32[]{:S(2)}, u32[]{:S(2)}) collective-permute-start(bf16[64,1024]{1,0:T(8,128)(2,1)} %own.1), channel_id=1, source_target_pairs={{0,2},{2,4},{4,6},{6,0},{1,3},{3,5},{5,7},{7,1},{8,10},{10,12},{12... | collective-permute-start | bytes 393224 | tf_op jit(solution)/shard_map/ppermute | solution.py:21
  2.2 12.1 %collective-permute-start.1 = (bf16[64,1024]{1,0:T(8,128)(2,1)}, bf16[64,1024]{1,0:T(8,128)(2,1)S(1)}, u32[]{:S(2)}, u32[]{:S(2)}) collective-permute-start(bf16[64,1024]{1,0:T(8,128)(2,1)} %own.1), channel_id=1, source_target_pairs={{0,6},{2,0},{4,2},{6,4},{1,7},{3,1},{5,3},{7,5},{8,14},{10,8},{12,... | collective-permute-start | bytes 393224 | tf_op jit(solution)/shard_map/ppermute | solution.py:21
  3.9 10.4 %collective-permute-start.2 = (bf16[64,1024]{1,0:T(8,128)(2,1)}, bf16[64,1024]{1,0:T(8,128)(2,1)S(1)}, u32[]{:S(2)}, u32[]{:S(2)}) collective-permute-start(bf16[64,1024]{1,0:T(8,128)(2,1)} %own.1), channel_id=1, source_target_pairs={{0,4},{2,6},{4,0},{6,2},{1,5},{3,7},{5,1},{7,3},{8,12},{10,14},{12... | collective-permute-start | bytes 393224 | tf_op jit(solution)/shard_map/ppermute | solution.py:21
  5.8 8.6 %collective-permute-start.3 = (bf16[64,1024]{1,0:T(8,128)(2,1)}, bf16[64,1024]{1,0:T(8,128)(2,1)S(1)}, u32[]{:S(2)}, u32[]{:S(2)}) collective-permute-start(bf16[64,1024]{1,0:T(8,128)(2,1)} %own.1), channel_id=1, source_target_pairs={{0,128},{64,192},{128,0},{192,64},{1,129},{65,193},{129,1},{193,65... | collective-permute-start | bytes 393224 | tf_op jit(solution)/shard_map/ppermute | solution.py:21
  14.9 6.7 %collective-permute-start.4 = (bf16[256,1024]{1,0:T(8,128)(2,1)S(1)}, bf16[256,1024]{1,0:T(8,128)(2,1)S(1)}, u32[]{:S(2)}, u32[]{:S(2)}) collective-permute-start(bf16[256,1024]{1,0:T(8,128)(2,1)S(1)} %shard_map.76.own.refs_0_), channel_id=1, source_target_pairs={{0,1},{1,0},{2,3},{3,2},{4,5},{5,4},{6,7},{7,6},{8,9},{9,8},{10,11... | collective-permute-start | bytes 1572872 | tf_op jit(solution)/shard_map/ppermute | solution.py:21
  15.0 21.5 %collective-permute-start.8 = (bf16[256,1024]{1,0:T(8,128)(2,1)S(1)}, bf16[256,1024]{1,0:T(8,128)(2,1)S(1)}, u32[]{:S(2)}, u32[]{:S(2)}) collective-permute-start(bf16[256,1024]{1,0:T(8,128)(2,1)S(1)} %shard_map.76.own.refs_0_), channel_id=1, source_target_pairs={{0,64},{64,128},{128,192},{192,0},{1,65},{65,129},{129,193},{193,1... | collective-permute-start | bytes 1572872 | tf_op jit(solution)/shard_map/ppermute | solution.py:21
  15.8 21.0 %collective-permute-start.10 = (bf16[256,1024]{1,0:T(8,128)(2,1)S(1)}, bf16[256,1024]{1,0:T(8,128)(2,1)S(1)}, u32[]{:S(2)}, u32[]{:S(2)}) collective-permute-start(bf16[256,1024]{1,0:T(8,128)(2,1)S(1)} %shard_map.76.own.refs_0_), channel_id=1, source_target_pairs={{0,192},{64,0},{128,64},{192,128},{1,193},{65,1},{129,65},{193,129... | collective-permute-start | bytes 1572872 | tf_op jit(solution)/shard_map/ppermute | solution.py:21
  18.3 18.7 %collective-permute-start.12 = (bf16[64,1024]{1,0:T(8,128)(2,1)S(1)}, bf16[64,1024]{1,0:T(8,128)(2,1)S(1)}, u32[]{:S(2)}, u32[]{:S(2)}) collective-permute-start(bf16[64,1024]{1,0:T(8,128)(2,1)S(1)} %collective-permute-done.3.refs_1_.own), channel_id=1, source_target_pairs={{0,2},{2,4},{4,6},{6,0},{1,3},{3,5},{5,7},{7,1},{8,10},{10,12},{12... | collective-permute-start | bytes 393224 | tf_op jit(solution)/shard_map/ppermute | solution.py:21
  18.9 18.1 %collective-permute-start.13 = (bf16[64,1024]{1,0:T(8,128)(2,1)S(1)}, bf16[64,1024]{1,0:T(8,128)(2,1)S(1)}, u32[]{:S(2)}, u32[]{:S(2)}) collective-permute-start(bf16[64,1024]{1,0:T(8,128)(2,1)S(1)} %collective-permute-done.3.refs_1_.own), channel_id=1, source_target_pairs={{0,6},{2,0},{4,2},{6,4},{1,7},{3,1},{5,3},{7,5},{8,14},{10,8},{12,... | collective-permute-start | bytes 393224 | tf_op jit(solution)/shard_map/ppermute | solution.py:21
  21.6 15.5 %collective-permute-start.14 = (bf16[64,1024]{1,0:T(8,128)(2,1)S(1)}, bf16[64,1024]{1,0:T(8,128)(2,1)S(1)}, u32[]{:S(2)}, u32[]{:S(2)}) collective-permute-start(bf16[64,1024]{1,0:T(8,128)(2,1)S(1)} %collective-permute-done.3.refs_1_.own), channel_id=1, source_target_pairs={{0,4},{2,6},{4,0},{6,2},{1,5},{3,7},{5,1},{7,3},{8,12},{10,14},{12... | collective-permute-start | bytes 393224 | tf_op jit(solution)/shard_map/ppermute | solution.py:21
  29.3 12.2 %all-to-all-start = ((f32[32,4,128]{2,1,0:T(4,128)}), f32[32,4,128]{2,1,0:T(4,128)S(1)}, u32[]{:S(2)}, u32[]{:S(2)}) async-start(f32[32,4,128]{2,1,0:T(4,128)} %get-tuple-element.19.ahead), calls=%async_computation | async-start | bytes 131072 | tf_op jit(solution)/shard_map/all_to_all | solution.py:414
  36.5 13.7 %collective-permute-start.9 = (bf16[256,1024]{1,0:T(8,128)(2,1)S(1)}, bf16[256,1024]{1,0:T(8,128)(2,1)}, u32[]{:S(2)}, u32[]{:S(2)}) collective-permute-start(bf16[256,1024]{1,0:T(8,128)(2,1)S(1)} %collective-permute-done.8.refs_2_), channel_id=1, source_target_pairs={{0,1},{1,0},{2,3},{3,2},{4,5},{5,4},{6,7},{7,6},{8,9},{9,8},{10,11... | collective-permute-start | bytes 1572872 | tf_op jit(solution)/shard_map/ppermute | solution.py:21
  36.8 13.5 %collective-permute-start.11 = (bf16[256,1024]{1,0:T(8,128)(2,1)S(1)}, bf16[256,1024]{1,0:T(8,128)(2,1)}, u32[]{:S(2)}, u32[]{:S(2)}) collective-permute-start(bf16[256,1024]{1,0:T(8,128)(2,1)S(1)} %collective-permute-done.10.refs_4_), channel_id=1, source_target_pairs={{0,1},{1,0},{2,3},{3,2},{4,5},{5,4},{6,7},{7,6},{8,9},{9,8},{10,11... | collective-permute-start | bytes 1572872 | tf_op jit(solution)/shard_map/ppermute | solution.py:21
  42.1 8.2 %collective-permute-start.15 = (bf16[256,1024]{1,0:T(8,128)(2,1)S(1)}, bf16[256,1024]{1,0:T(8,128)(2,1)S(1)}, u32[]{:S(2)}, u32[]{:S(2)}) collective-permute-start(bf16[256,1024]{1,0:T(8,128)(2,1)S(1)} %shard_map.80.refs_6_), channel_id=1, source_target_pairs={{0,1},{1,0},{2,3},{3,2},{4,5},{5,4},{6,7},{7,6},{8,9},{9,8},{10,11... | collective-permute-start | bytes 1572872 | tf_op jit(solution)/shard_map/ppermute | solution.py:21
  46.7 12.6 %collective-permute-start.6 = (bf16[64,2048]{1,0:T(8,128)(2,1)S(1)}, bf16[64,2048]{1,0:T(8,128)(2,1)}, u32[]{:S(2)}, u32[]{:S(2)}) collective-permute-start(bf16[64,2048]{1,0:T(8,128)(2,1)S(1)} %get-tuple-element.22), channel_id=1, source_target_pairs={{0,2},{2,4},{4,6},{6,0},{1,3},{3,5},{5,7},{7,1},{8,10},{10,12},{12... | collective-permute-start | bytes 786440 | tf_op jit(solution)/shard_map/ppermute | solution.py:21
  47.6 11.7 %collective-permute-start.16 = (bf16[64,2048]{1,0:T(8,128)(2,1)S(1)}, bf16[64,2048]{1,0:T(8,128)(2,1)S(1)}, u32[]{:S(2)}, u32[]{:S(2)}) collective-permute-start(bf16[64,2048]{1,0:T(8,128)(2,1)S(1)} %get-tuple-element.24), channel_id=1, source_target_pairs={{0,6},{2,0},{4,2},{6,4},{1,7},{3,1},{5,3},{7,5},{8,14},{10,8},{12,... | collective-permute-start | bytes 786440 | tf_op jit(solution)/shard_map/ppermute | solution.py:21
  60.1 39.4 %all-to-all-start.1 = ((bf16[32,136,128]{2,1,0:T(8,128)(2,1)}), bf16[32,136,128]{2,1,0:T(8,128)(2,1)S(1)}, u32[]{:S(2)}, u32[]{:S(2)}) async-start(bf16[32,136,128]{2,1,0:T(8,128)(2,1)} %shard_map.82.refs_1_), calls=%async_computation.1 | async-start | bytes 2228224 | tf_op jit(solution)/shard_map/all_to_all | solution.py:428
  69.6 16.7 %collective-permute-start.17 = (bf16[128,2048]{1,0:T(8,128)(2,1)}, bf16[128,2048]{1,0:T(8,128)(2,1)S(1)}, u32[]{:S(2)}, u32[]{:S(2)}) collective-permute-start(bf16[128,2048]{1,0:T(8,128)(2,1)} %shard_map.83), channel_id=1, source_target_pairs={{0,4},{2,6},{4,0},{6,2},{1,5},{3,7},{5,1},{7,3},{8,12},{10,14},{12... | collective-permute-start | bytes 1572872 | tf_op jit(solution)/shard_map/ppermute | solution.py:21
  69.7 17.3 %collective-permute-start.5 = (bf16[64,2048]{1,0:T(8,128)(2,1)}, bf16[64,2048]{1,0:T(8,128)(2,1)S(1)}, u32[]{:S(2)}, u32[]{:S(2)}) collective-permute-start(bf16[64,2048]{1,0:T(8,128)(2,1)} %get-tuple-element.21.refs_8_), channel_id=1, source_target_pairs={{0,1},{1,0},{2,3},{3,2},{4,5},{5,4},{6,7},{7,6},{8,9},{9,8},{10,11... | collective-permute-start | bytes 786440 | tf_op jit(solution)/shard_map/ppermute | solution.py:21
  71.1 19.0 %collective-permute-start.20 = (bf16[64,2048]{1,0:T(8,128)(2,1)}, bf16[64,2048]{1,0:T(8,128)(2,1)S(1)}, u32[]{:S(2)}, u32[]{:S(2)}) collective-permute-start(bf16[64,2048]{1,0:T(8,128)(2,1)} %get-tuple-element.26), channel_id=1, source_target_pairs={{0,2},{2,4},{4,6},{6,0},{1,3},{3,5},{5,7},{7,1},{8,10},{10,12},{12... | collective-permute-start | bytes 786440 | tf_op jit(solution)/shard_map/ppermute | solution.py:21
  72.3 17.8 %collective-permute-start.21 = (bf16[64,2048]{1,0:T(8,128)(2,1)}, bf16[64,2048]{1,0:T(8,128)(2,1)S(1)}, u32[]{:S(2)}, u32[]{:S(2)}) collective-permute-start(bf16[64,2048]{1,0:T(8,128)(2,1)} %get-tuple-element.27), channel_id=1, source_target_pairs={{0,6},{2,0},{4,2},{6,4},{1,7},{3,1},{5,3},{7,5},{8,14},{10,8},{12,... | collective-permute-start | bytes 786440 | tf_op jit(solution)/shard_map/ppermute | solution.py:21
  74.5 15.7 %collective-permute-start.7 = (bf16[64,2048]{1,0:T(8,128)(2,1)}, bf16[64,2048]{1,0:T(8,128)(2,1)S(1)}, u32[]{:S(2)}, u32[]{:S(2)}) collective-permute-start(bf16[64,2048]{1,0:T(8,128)(2,1)} %collective-permute-done.6.refs_1_), channel_id=1, source_target_pairs={{0,1},{1,0},{2,3},{3,2},{4,5},{5,4},{6,7},{7,6},{8,9},{9,8},{10,11... | collective-permute-start | bytes 786440 | tf_op jit(solution)/shard_map/ppermute | solution.py:21
  86.4 3.8 %collective-permute-start.19 = (bf16[64,2048]{1,0:T(8,128)(2,1)}, bf16[64,2048]{1,0:T(8,128)(2,1)S(1)}, u32[]{:S(2)}, u32[]{:S(2)}) collective-permute-start(bf16[64,2048]{1,0:T(8,128)(2,1)} %copy-done.1), channel_id=1, source_target_pairs={{0,1},{1,0},{2,3},{3,2},{4,5},{5,4},{6,7},{7,6},{8,9},{9,8},{10,11... | collective-permute-start | bytes 786440 | tf_op jit(solution)/shard_map/ppermute | solution.py:21
  87.1 3.1 %collective-permute-start.18 = (bf16[64,2048]{1,0:T(8,128)(2,1)}, bf16[64,2048]{1,0:T(8,128)(2,1)}, u32[]{:S(2)}, u32[]{:S(2)}) collective-permute-start(bf16[64,2048]{1,0:T(8,128)(2,1)} %slice.4), channel_id=1, source_target_pairs={{0,1},{1,0},{2,3},{3,2},{4,5},{5,4},{6,7},{7,6},{8,9},{9,8},{10,11... | collective-permute-start | bytes 786440 | tf_op jit(solution)/shard_map/ppermute | solution.py:21
  (3 other events, 15.8 us)

commit v12 on v11

--- a/solution.py
+++ b/solution.py
@@ -140,7 +140,7 @@
 
 
 def scores(at, own, other, scaled, bias_row):
-    width = 512
+    width = 1024
     return pl.pallas_call(
         score_kernel,
         grid=(2048 // width,),

time: 102 us -> 101 us (level)
  no operation moved by 1% of the time
where the time goes in v12:
time: 101 us
  starting transfers between devices  38 us (38%)
  Pallas kernels  33.3 us (33%)
  waiting for transfers between devices  25.2 us (25%)
  local copies, waits for them, and re-layouts  1.58 us (2%)
  between operations  1.39 us (1%)
  other arithmetic  1.28 us (1%)
    ppermute x22, starting transfers between devices, shift(): return lax.ppermute(value, axis, [(i, (i + step) % n) for i in range(n)])  23.8 us
    ppermute x22, waiting for transfers between devices, shift(): return lax.ppermute(value, axis, [(i, (i + step) % n) for i in range(n)])  13.8 us
    all_to_all x1, starting transfers between devices, body(): lax.all_to_all(sums, ('y', 'h', 'l'), split_axis=0, concat_axis=0, tiled=...  9.54 us
    pallas_call x1, Pallas kernels, partial_sums(): pl.pallas_call(sums_kernel, grid_spec=pltpu.PrefetchScalarGridSpec(num_sc...  9.07 us
    all_to_all x1, waiting for transfers between devices, body(): lax.all_to_all(sums, ('y', 'h', 'l'), split_axis=0, concat_axis=0, tiled=...  6.95 us
    pallas_call x1, Pallas kernels, scores(): pl.pallas_call(score_kernel, grid=(2048 // width,), out_shape=(pltpu.HBM(...  6.68 us
    pallas_call x1, Pallas kernels, prepare(): pl.pallas_call(prepare_kernel, grid=(4,), in_specs=[pl.BlockSpec((512, 10...  5.26 us
    all_to_all x1, starting transfers between devices, body(): lax.all_to_all(share, ('y', 'x', 'c'), split_axis=0, concat_axis=0, tiled...  4.68 us
  transfers between devices with their start and end apart: 24, of which 4 were waited for; matrix products, arithmetic and copies ran while one was open for 2% of the time, Pallas kernels for 31%

profile of v12, /device:TPU:32, one launch (start us, length us, event | category | flops | bytes accessed | tf_op | source)
XLA Modules:
  0.0 100.7 jit_solution(11321589059732815552)
XLA Ops:
  0.6 1.6 %collective-permute-start = (bf16[64,1024]{1,0:T(8,128)(2,1)}, bf16[64,1024]{1,0:T(8,128)(2,1)S(1)}, u32[]{:S(2)}, u32[]{:S(2)}) collective-permute-start(bf16[64,1024]{1,0:T(8,128)(2,1)} %own.1), channel_id=1, source_target_pairs={{0,2},{2,4},{4,6},{6,0},{1,3},{3,5},{5,7},{7,1},{8,10},{10,12},{12... | collective-permute-start | bytes 393224 | tf_op jit(solution)/shard_map/ppermute | solution.py:21
  2.2 1.7 %collective-permute-start.1 = (bf16[64,1024]{1,0:T(8,128)(2,1)}, bf16[64,1024]{1,0:T(8,128)(2,1)S(1)}, u32[]{:S(2)}, u32[]{:S(2)}) collective-permute-start(bf16[64,1024]{1,0:T(8,128)(2,1)} %own.1), channel_id=1, source_target_pairs={{0,6},{2,0},{4,2},{6,4},{1,7},{3,1},{5,3},{7,5},{8,14},{10,8},{12,... | collective-permute-start | bytes 393224 | tf_op jit(solution)/shard_map/ppermute | solution.py:21
  3.9 1.8 %collective-permute-start.2 = (bf16[64,1024]{1,0:T(8,128)(2,1)}, bf16[64,1024]{1,0:T(8,128)(2,1)S(1)}, u32[]{:S(2)}, u32[]{:S(2)}) collective-permute-start(bf16[64,1024]{1,0:T(8,128)(2,1)} %own.1), channel_id=1, source_target_pairs={{0,4},{2,6},{4,0},{6,2},{1,5},{3,7},{5,1},{7,3},{8,12},{10,14},{12... | collective-permute-start | bytes 393224 | tf_op jit(solution)/shard_map/ppermute | solution.py:21
  5.8 3.2 %collective-permute-start.3 = (bf16[64,1024]{1,0:T(8,128)(2,1)}, bf16[64,1024]{1,0:T(8,128)(2,1)S(1)}, u32[]{:S(2)}, u32[]{:S(2)}) collective-permute-start(bf16[64,1024]{1,0:T(8,128)(2,1)} %own.1), channel_id=1, source_target_pairs={{0,128},{64,192},{128,0},{192,64},{1,129},{65,193},{129,1},{193,65... | collective-permute-start | bytes 393224 | tf_op jit(solution)/shard_map/ppermute | solution.py:21
  9.0 5.3 %shard_map.75 = (bf16[2048,1024]{1,0:T(8,128)(2,1)}, f32[1,2048]{1,0:T(1,128)S(1)}) custom-call(bf16[2048,1024]{1,0:T(8,128)(2,1)} %means.3, f32[1,1024]{1,0:T(1,128)} %bitcast.23, f32[1,2048]{1,0:T(1,128)} %bitcast.24), custom_call_target="tpu_custom_call" | custom-call | flops 12582912 | bytes 8388608 | tf_op jit(solution)/shard_map/pallas_call | solution.py:60
  15.0 0.8 collective-permute-start.8
  15.8 2.6 %collective-permute-start.10 = (bf16[256,1024]{1,0:T(8,128)(2,1)S(1)}, bf16[256,1024]{1,0:T(8,128)(2,1)S(1)}, u32[]{:S(2)}, u32[]{:S(2)}) collective-permute-start(bf16[256,1024]{1,0:T(8,128)(2,1)S(1)} %shard_map.76.own.refs_0_), channel_id=1, source_target_pairs={{0,192},{64,0},{128,64},{192,128},{1,193},{65,1},{129,65},{193,129... | collective-permute-start | bytes 1572872 | tf_op jit(solution)/shard_map/ppermute | solution.py:21
  18.9 2.6 %collective-permute-start.13 = (bf16[64,1024]{1,0:T(8,128)(2,1)S(1)}, bf16[64,1024]{1,0:T(8,128)(2,1)S(1)}, u32[]{:S(2)}, u32[]{:S(2)}) collective-permute-start(bf16[64,1024]{1,0:T(8,128)(2,1)S(1)} %collective-permute-done.3.refs_1_.own), channel_id=1, source_target_pairs={{0,6},{2,0},{4,2},{6,4},{1,7},{3,1},{5,3},{7,5},{8,14},{10,8},{12,... | collective-permute-start | bytes 393224 | tf_op jit(solution)/shard_map/ppermute | solution.py:21
  22.1 6.7 %shard_map.77 = (f32[512,2048]{1,0:T(8,128)}, f32[32,4,128]{2,1,0:T(4,128)}) custom-call(s32[5]{0:T(128)S(1)} %stack.23.at, bf16[256,1024]{1,0:T(8,128)(2,1)S(1)} %shard_map.76.own.refs_0_, bf16[256,1024]{1,0:T(8,128)(2,1)S(1)} %collective-permute-done.4.other.refs_1_, bf16[2048,1024]{1,0:T(8,128)(2,1)} %get-tuple-element.17.refs_0_.scaled, ...), custom_call_target="tpu_custom_call" | custom-call | flops 2147483648 | bytes 9437184 | tf_op jit(solution)/shard_map/pallas_call | solution.py:144
  28.8 4.7 %all-to-all-start = ((f32[32,4,128]{2,1,0:T(4,128)}), f32[32,4,128]{2,1,0:T(4,128)S(1)}, u32[]{:S(2)}, u32[]{:S(2)}) async-start(f32[32,4,128]{2,1,0:T(4,128)} %get-tuple-element.19.ahead), calls=%async_computation | async-start | bytes 131072 | tf_op jit(solution)/shard_map/all_to_all | solution.py:414
  33.5 2.5 %shard_map.79.refs_0_.means = f32[32,2048]{1,0:T(8,128)} custom-call(s32[5]{0:T(128)S(1)} %stack.23.at, bf16[2048,1024]{1,0:T(8,128)(2,1)} %means.3, f32[32,4,128]{2,1,0:T(4,128)} %get-tuple-element.19.ahead), custom_call_target="tpu_custom_call" | custom-call | tf_op jit(solution)/shard_map/pallas_call | solution.py:326
  36.5 4.4 %all-to-all-done.refs_1_ = f32[32,4,128]{2,1,0:T(4,128)S(1)} async-done(((f32[32,4,128]{2,1,0:T(4,128)}), f32[32,4,128]{2,1,0:T(4,128)S(1)}, u32[]{:S(2)}, u32[]{:S(2)}) %all-to-all-start) | async-done | bytes 65568 | tf_op jit(solution)/shard_map/all_to_all | solution.py:414
  41.9 4.4 %shard_map.78 = (bf16[64,2048]{1,0:T(8,128)(2,1)}, bf16[64,2048]{1,0:T(8,128)(2,1)S(1)}, bf16[64,2048]{1,0:T(8,128)(2,1)S(1)}, bf16[64,2048]{1,0:T(8,128)(2,1)},...) custom-call(s32[5]{0:T(128)S(1)} %stack.23.at, f32[4,8,4,128]{3,2,1,0:T(4,128)S(1)} %bitcast.19, ...), custom_call_target="tpu_custom_call" | custom-call | flops 2097152 | bytes 6291456 | tf_op jit(solution)/shard_map/pallas_call | solution.py:302
  47.1 2.6 %collective-permute-start.16 = (bf16[64,2048]{1,0:T(8,128)(2,1)S(1)}, bf16[64,2048]{1,0:T(8,128)(2,1)S(1)}, u32[]{:S(2)}, u32[]{:S(2)}) collective-permute-start(bf16[64,2048]{1,0:T(8,128)(2,1)S(1)} %get-tuple-element.24), channel_id=1, source_target_pairs={{0,6},{2,0},{4,2},{6,4},{1,7},{3,1},{5,3},{7,5},{8,14},{10,8},{12,... | collective-permute-start | bytes 786440 | tf_op jit(solution)/shard_map/ppermute | solution.py:21
  49.7 9.1 %shard_map.81.refs_0_ = bf16[32,136,128]{2,1,0:T(8,128)(2,1)} custom-call(s32[5]{0:T(128)S(1)} %stack.23.at, f32[4,8,4,128]{3,2,1,0:T(4,128)S(1)} %bitcast.20, bf16[2048,1024]{1,0:T(8,128)(2,1)} %get-tuple-element.17.refs_0_.scaled, f32[1,2048]{1,0:T(1,128)S(1)} %get-tuple-element.18.bias, bf16[256,1024]{1,0:T(8,128)(2,1)S(1)} %shard_map.76.own.refs_0_, ...), custom_call_target="tpu_custom_call" | custom-call | flops 4294967296 | bytes 8388608 | tf_op jit(solution)/shard_map/pallas_call | solution.py:243
  59.5 9.5 %all-to-all-start.1 = ((bf16[32,136,128]{2,1,0:T(8,128)(2,1)}), bf16[32,136,128]{2,1,0:T(8,128)(2,1)S(1)}, u32[]{:S(2)}, u32[]{:S(2)}) async-start(bf16[32,136,128]{2,1,0:T(8,128)(2,1)} %shard_map.82.refs_1_), calls=%async_computation.1 | async-start | bytes 2228224 | tf_op jit(solution)/shard_map/all_to_all | solution.py:428
  70.6 1.2 %collective-permute-start.20 = (bf16[64,2048]{1,0:T(8,128)(2,1)}, bf16[64,2048]{1,0:T(8,128)(2,1)S(1)}, u32[]{:S(2)}, u32[]{:S(2)}) collective-permute-start(bf16[64,2048]{1,0:T(8,128)(2,1)} %get-tuple-element.26), channel_id=1, source_target_pairs={{0,2},{2,4},{4,6},{6,0},{1,3},{3,5},{5,7},{7,1},{8,10},{10,12},{12... | collective-permute-start | bytes 786440 | tf_op jit(solution)/shard_map/ppermute | solution.py:21
  71.8 2.1 %collective-permute-start.21 = (bf16[64,2048]{1,0:T(8,128)(2,1)}, bf16[64,2048]{1,0:T(8,128)(2,1)S(1)}, u32[]{:S(2)}, u32[]{:S(2)}) collective-permute-start(bf16[64,2048]{1,0:T(8,128)(2,1)} %get-tuple-element.27), channel_id=1, source_target_pairs={{0,6},{2,0},{4,2},{6,4},{1,7},{3,1},{5,3},{7,5},{8,14},{10,8},{12,... | collective-permute-start | bytes 786440 | tf_op jit(solution)/shard_map/ppermute | solution.py:21
  74.0 11.8 %collective-permute-done.17.refs_6_ = bf16[128,2048]{1,0:T(8,128)(2,1)S(1)} collective-permute-done((bf16[128,2048]{1,0:T(8,128)(2,1)}, bf16[128,2048]{1,0:T(8,128)(2,1)S(1)}, u32[]{:S(2)}, u32[]{:S(2)}) %collective-permute-start.17) | collective-permute-done | bytes 524320 | tf_op jit(solution)/shard_map/ppermute | solution.py:21
  85.8 0.7 slice.4
  87.6 1.9 %collective-permute-done.20.refs_5_ = bf16[64,2048]{1,0:T(8,128)(2,1)S(1)} collective-permute-done((bf16[64,2048]{1,0:T(8,128)(2,1)}, bf16[64,2048]{1,0:T(8,128)(2,1)S(1)}, u32[]{:S(2)}, u32[]{:S(2)}) %collective-permute-start.20) | collective-permute-done | bytes 262176 | tf_op jit(solution)/shard_map/ppermute | solution.py:21
  89.6 2.3 %shard_map.84 = bf16[64,16384]{1,0:T(8,128)(2,1)} custom-call(s32[5]{0:T(128)S(1)} %stack.23.at, bf16[64,2048]{1,0:T(8,128)(2,1)S(1)} %collective-permute-done.5.refs_0_, bf16[64,2048]{1,0:T(8,128)(2,1)S(1)} %collective-permute-done.7.refs_1_, bf16[64,2048]{1,0:T(8,128)(2,1)} %collective-permute-done.18.refs_2_, ...), custom_call_target="tpu_custom_call" | custom-call | bytes 4194304 | tf_op jit(solution)/shard_map/pallas_call | solution.py:390
  92.0 7.0 %all-to-all-done.1.sent = bf16[32,136,128]{2,1,0:T(8,128)(2,1)S(1)} async-done(((bf16[32,136,128]{2,1,0:T(8,128)(2,1)}), bf16[32,136,128]{2,1,0:T(8,128)(2,1)S(1)}, u32[]{:S(2)}, u32[]{:S(2)}) %all-to-all-start.1) | async-done | bytes 1114144 | tf_op jit(solution)/shard_map/all_to_all | solution.py:428
  98.9 1.8 %shard_map.85 = (f32[32,2048]{1,0:T(8,128)}, f32[16,128]{1,0:T(8,128)}) custom-call(bf16[32,136,128]{2,1,0:T(8,128)(2,1)S(1)} %all-to-all-done.1.sent, f32[32,2048]{1,0:T(8,128)} %shard_map.79.refs_0_.means), custom_call_target="tpu_custom_call" | custom-call | tf_op jit(solution)/shard_map/pallas_call | solution.py:354
  (50 shorter events, 6.9 us)
Async XLA Ops:
  0.6 13.7 %collective-permute-start = (bf16[64,1024]{1,0:T(8,128)(2,1)}, bf16[64,1024]{1,0:T(8,128)(2,1)S(1)}, u32[]{:S(2)}, u32[]{:S(2)}) collective-permute-start(bf16[64,1024]{1,0:T(8,128)(2,1)} %own.1), channel_id=1, source_target_pairs={{0,2},{2,4},{4,6},{6,0},{1,3},{3,5},{5,7},{7,1},{8,10},{10,12},{12... | collective-permute-start | bytes 393224 | tf_op jit(solution)/shard_map/ppermute | solution.py:21
  2.2 12.1 %collective-permute-start.1 = (bf16[64,1024]{1,0:T(8,128)(2,1)}, bf16[64,1024]{1,0:T(8,128)(2,1)S(1)}, u32[]{:S(2)}, u32[]{:S(2)}) collective-permute-start(bf16[64,1024]{1,0:T(8,128)(2,1)} %own.1), channel_id=1, source_target_pairs={{0,6},{2,0},{4,2},{6,4},{1,7},{3,1},{5,3},{7,5},{8,14},{10,8},{12,... | collective-permute-start | bytes 393224 | tf_op jit(solution)/shard_map/ppermute | solution.py:21
  3.9 10.4 %collective-permute-start.2 = (bf16[64,1024]{1,0:T(8,128)(2,1)}, bf16[64,1024]{1,0:T(8,128)(2,1)S(1)}, u32[]{:S(2)}, u32[]{:S(2)}) collective-permute-start(bf16[64,1024]{1,0:T(8,128)(2,1)} %own.1), channel_id=1, source_target_pairs={{0,4},{2,6},{4,0},{6,2},{1,5},{3,7},{5,1},{7,3},{8,12},{10,14},{12... | collective-permute-start | bytes 393224 | tf_op jit(solution)/shard_map/ppermute | solution.py:21
  5.8 8.6 %collective-permute-start.3 = (bf16[64,1024]{1,0:T(8,128)(2,1)}, bf16[64,1024]{1,0:T(8,128)(2,1)S(1)}, u32[]{:S(2)}, u32[]{:S(2)}) collective-permute-start(bf16[64,1024]{1,0:T(8,128)(2,1)} %own.1), channel_id=1, source_target_pairs={{0,128},{64,192},{128,0},{192,64},{1,129},{65,193},{129,1},{193,65... | collective-permute-start | bytes 393224 | tf_op jit(solution)/shard_map/ppermute | solution.py:21
  14.9 6.7 %collective-permute-start.4 = (bf16[256,1024]{1,0:T(8,128)(2,1)S(1)}, bf16[256,1024]{1,0:T(8,128)(2,1)S(1)}, u32[]{:S(2)}, u32[]{:S(2)}) collective-permute-start(bf16[256,1024]{1,0:T(8,128)(2,1)S(1)} %shard_map.76.own.refs_0_), channel_id=1, source_target_pairs={{0,1},{1,0},{2,3},{3,2},{4,5},{5,4},{6,7},{7,6},{8,9},{9,8},{10,11... | collective-permute-start | bytes 1572872 | tf_op jit(solution)/shard_map/ppermute | solution.py:21
  15.0 20.9 %collective-permute-start.8 = (bf16[256,1024]{1,0:T(8,128)(2,1)S(1)}, bf16[256,1024]{1,0:T(8,128)(2,1)S(1)}, u32[]{:S(2)}, u32[]{:S(2)}) collective-permute-start(bf16[256,1024]{1,0:T(8,128)(2,1)S(1)} %shard_map.76.own.refs_0_), channel_id=1, source_target_pairs={{0,64},{64,128},{128,192},{192,0},{1,65},{65,129},{129,193},{193,1... | collective-permute-start | bytes 1572872 | tf_op jit(solution)/shard_map/ppermute | solution.py:21
  15.8 20.5 %collective-permute-start.10 = (bf16[256,1024]{1,0:T(8,128)(2,1)S(1)}, bf16[256,1024]{1,0:T(8,128)(2,1)S(1)}, u32[]{:S(2)}, u32[]{:S(2)}) collective-permute-start(bf16[256,1024]{1,0:T(8,128)(2,1)S(1)} %shard_map.76.own.refs_0_), channel_id=1, source_target_pairs={{0,192},{64,0},{128,64},{192,128},{1,193},{65,1},{129,65},{193,129... | collective-permute-start | bytes 1572872 | tf_op jit(solution)/shard_map/ppermute | solution.py:21
  18.3 18.1 %collective-permute-start.12 = (bf16[64,1024]{1,0:T(8,128)(2,1)S(1)}, bf16[64,1024]{1,0:T(8,128)(2,1)S(1)}, u32[]{:S(2)}, u32[]{:S(2)}) collective-permute-start(bf16[64,1024]{1,0:T(8,128)(2,1)S(1)} %collective-permute-done.3.refs_1_.own), channel_id=1, source_target_pairs={{0,2},{2,4},{4,6},{6,0},{1,3},{3,5},{5,7},{7,1},{8,10},{10,12},{12... | collective-permute-start | bytes 393224 | tf_op jit(solution)/shard_map/ppermute | solution.py:21
  18.9 17.6 %collective-permute-start.13 = (bf16[64,1024]{1,0:T(8,128)(2,1)S(1)}, bf16[64,1024]{1,0:T(8,128)(2,1)S(1)}, u32[]{:S(2)}, u32[]{:S(2)}) collective-permute-start(bf16[64,1024]{1,0:T(8,128)(2,1)S(1)} %collective-permute-done.3.refs_1_.own), channel_id=1, source_target_pairs={{0,6},{2,0},{4,2},{6,4},{1,7},{3,1},{5,3},{7,5},{8,14},{10,8},{12,... | collective-permute-start | bytes 393224 | tf_op jit(solution)/shard_map/ppermute | solution.py:21
  21.6 14.9 %collective-permute-start.14 = (bf16[64,1024]{1,0:T(8,128)(2,1)S(1)}, bf16[64,1024]{1,0:T(8,128)(2,1)S(1)}, u32[]{:S(2)}, u32[]{:S(2)}) collective-permute-start(bf16[64,1024]{1,0:T(8,128)(2,1)S(1)} %collective-permute-done.3.refs_1_.own), channel_id=1, source_target_pairs={{0,4},{2,6},{4,0},{6,2},{1,5},{3,7},{5,1},{7,3},{8,12},{10,14},{12... | collective-permute-start | bytes 393224 | tf_op jit(solution)/shard_map/ppermute | solution.py:21
  28.8 12.2 %all-to-all-start = ((f32[32,4,128]{2,1,0:T(4,128)}), f32[32,4,128]{2,1,0:T(4,128)S(1)}, u32[]{:S(2)}, u32[]{:S(2)}) async-start(f32[32,4,128]{2,1,0:T(4,128)} %get-tuple-element.19.ahead), calls=%async_computation | async-start | bytes 131072 | tf_op jit(solution)/shard_map/all_to_all | solution.py:414
  36.0 13.7 %collective-permute-start.9 = (bf16[256,1024]{1,0:T(8,128)(2,1)S(1)}, bf16[256,1024]{1,0:T(8,128)(2,1)}, u32[]{:S(2)}, u32[]{:S(2)}) collective-permute-start(bf16[256,1024]{1,0:T(8,128)(2,1)S(1)} %collective-permute-done.8.refs_2_), channel_id=1, source_target_pairs={{0,1},{1,0},{2,3},{3,2},{4,5},{5,4},{6,7},{7,6},{8,9},{9,8},{10,11... | collective-permute-start | bytes 1572872 | tf_op jit(solution)/shard_map/ppermute | solution.py:21
  36.3 13.5 %collective-permute-start.11 = (bf16[256,1024]{1,0:T(8,128)(2,1)S(1)}, bf16[256,1024]{1,0:T(8,128)(2,1)}, u32[]{:S(2)}, u32[]{:S(2)}) collective-permute-start(bf16[256,1024]{1,0:T(8,128)(2,1)S(1)} %collective-permute-done.10.refs_4_), channel_id=1, source_target_pairs={{0,1},{1,0},{2,3},{3,2},{4,5},{5,4},{6,7},{7,6},{8,9},{9,8},{10,11... | collective-permute-start | bytes 1572872 | tf_op jit(solution)/shard_map/ppermute | solution.py:21
  41.5 8.2 %collective-permute-start.15 = (bf16[256,1024]{1,0:T(8,128)(2,1)S(1)}, bf16[256,1024]{1,0:T(8,128)(2,1)S(1)}, u32[]{:S(2)}, u32[]{:S(2)}) collective-permute-start(bf16[256,1024]{1,0:T(8,128)(2,1)S(1)} %shard_map.80.refs_6_), channel_id=1, source_target_pairs={{0,1},{1,0},{2,3},{3,2},{4,5},{5,4},{6,7},{7,6},{8,9},{9,8},{10,11... | collective-permute-start | bytes 1572872 | tf_op jit(solution)/shard_map/ppermute | solution.py:21
  46.4 12.4 %collective-permute-start.6 = (bf16[64,2048]{1,0:T(8,128)(2,1)S(1)}, bf16[64,2048]{1,0:T(8,128)(2,1)}, u32[]{:S(2)}, u32[]{:S(2)}) collective-permute-start(bf16[64,2048]{1,0:T(8,128)(2,1)S(1)} %get-tuple-element.22), channel_id=1, source_target_pairs={{0,2},{2,4},{4,6},{6,0},{1,3},{3,5},{5,7},{7,1},{8,10},{10,12},{12... | collective-permute-start | bytes 786440 | tf_op jit(solution)/shard_map/ppermute | solution.py:21
  47.1 11.7 %collective-permute-start.16 = (bf16[64,2048]{1,0:T(8,128)(2,1)S(1)}, bf16[64,2048]{1,0:T(8,128)(2,1)S(1)}, u32[]{:S(2)}, u32[]{:S(2)}) collective-permute-start(bf16[64,2048]{1,0:T(8,128)(2,1)S(1)} %get-tuple-element.24), channel_id=1, source_target_pairs={{0,6},{2,0},{4,2},{6,4},{1,7},{3,1},{5,3},{7,5},{8,14},{10,8},{12,... | collective-permute-start | bytes 786440 | tf_op jit(solution)/shard_map/ppermute | solution.py:21
  59.5 39.4 %all-to-all-start.1 = ((bf16[32,136,128]{2,1,0:T(8,128)(2,1)}), bf16[32,136,128]{2,1,0:T(8,128)(2,1)S(1)}, u32[]{:S(2)}, u32[]{:S(2)}) async-start(bf16[32,136,128]{2,1,0:T(8,128)(2,1)} %shard_map.82.refs_1_), calls=%async_computation.1 | async-start | bytes 2228224 | tf_op jit(solution)/shard_map/all_to_all | solution.py:428
  69.1 16.7 %collective-permute-start.17 = (bf16[128,2048]{1,0:T(8,128)(2,1)}, bf16[128,2048]{1,0:T(8,128)(2,1)S(1)}, u32[]{:S(2)}, u32[]{:S(2)}) collective-permute-start(bf16[128,2048]{1,0:T(8,128)(2,1)} %shard_map.83), channel_id=1, source_target_pairs={{0,4},{2,6},{4,0},{6,2},{1,5},{3,7},{5,1},{7,3},{8,12},{10,14},{12... | collective-permute-start | bytes 1572872 | tf_op jit(solution)/shard_map/ppermute | solution.py:21
  69.2 17.3 %collective-permute-start.5 = (bf16[64,2048]{1,0:T(8,128)(2,1)}, bf16[64,2048]{1,0:T(8,128)(2,1)S(1)}, u32[]{:S(2)}, u32[]{:S(2)}) collective-permute-start(bf16[64,2048]{1,0:T(8,128)(2,1)} %get-tuple-element.21.refs_8_), channel_id=1, source_target_pairs={{0,1},{1,0},{2,3},{3,2},{4,5},{5,4},{6,7},{7,6},{8,9},{9,8},{10,11... | collective-permute-start | bytes 786440 | tf_op jit(solution)/shard_map/ppermute | solution.py:21
  70.6 19.0 %collective-permute-start.20 = (bf16[64,2048]{1,0:T(8,128)(2,1)}, bf16[64,2048]{1,0:T(8,128)(2,1)S(1)}, u32[]{:S(2)}, u32[]{:S(2)}) collective-permute-start(bf16[64,2048]{1,0:T(8,128)(2,1)} %get-tuple-element.26), channel_id=1, source_target_pairs={{0,2},{2,4},{4,6},{6,0},{1,3},{3,5},{5,7},{7,1},{8,10},{10,12},{12... | collective-permute-start | bytes 786440 | tf_op jit(solution)/shard_map/ppermute | solution.py:21
  71.8 17.8 %collective-permute-start.21 = (bf16[64,2048]{1,0:T(8,128)(2,1)}, bf16[64,2048]{1,0:T(8,128)(2,1)S(1)}, u32[]{:S(2)}, u32[]{:S(2)}) collective-permute-start(bf16[64,2048]{1,0:T(8,128)(2,1)} %get-tuple-element.27), channel_id=1, source_target_pairs={{0,6},{2,0},{4,2},{6,4},{1,7},{3,1},{5,3},{7,5},{8,14},{10,8},{12,... | collective-permute-start | bytes 786440 | tf_op jit(solution)/shard_map/ppermute | solution.py:21
  73.9 15.7 %collective-permute-start.7 = (bf16[64,2048]{1,0:T(8,128)(2,1)}, bf16[64,2048]{1,0:T(8,128)(2,1)S(1)}, u32[]{:S(2)}, u32[]{:S(2)}) collective-permute-start(bf16[64,2048]{1,0:T(8,128)(2,1)} %collective-permute-done.6.refs_1_), channel_id=1, source_target_pairs={{0,1},{1,0},{2,3},{3,2},{4,5},{5,4},{6,7},{7,6},{8,9},{9,8},{10,11... | collective-permute-start | bytes 786440 | tf_op jit(solution)/shard_map/ppermute | solution.py:21
  85.8 3.8 %collective-permute-start.19 = (bf16[64,2048]{1,0:T(8,128)(2,1)}, bf16[64,2048]{1,0:T(8,128)(2,1)S(1)}, u32[]{:S(2)}, u32[]{:S(2)}) collective-permute-start(bf16[64,2048]{1,0:T(8,128)(2,1)} %copy-done.1), channel_id=1, source_target_pairs={{0,1},{1,0},{2,3},{3,2},{4,5},{5,4},{6,7},{7,6},{8,9},{9,8},{10,11... | collective-permute-start | bytes 786440 | tf_op jit(solution)/shard_map/ppermute | solution.py:21
  86.5 3.1 %collective-permute-start.18 = (bf16[64,2048]{1,0:T(8,128)(2,1)}, bf16[64,2048]{1,0:T(8,128)(2,1)}, u32[]{:S(2)}, u32[]{:S(2)}) collective-permute-start(bf16[64,2048]{1,0:T(8,128)(2,1)} %slice.4), channel_id=1, source_target_pairs={{0,1},{1,0},{2,3},{3,2},{4,5},{5,4},{6,7},{7,6},{8,9},{9,8},{10,11... | collective-permute-start | bytes 786440 | tf_op jit(solution)/shard_map/ppermute | solution.py:21
  (3 other events, 15.8 us)
